TPU v7x, 32 devices: a whole 2x2x4 slice. The times are simulated.
32 devices in a mesh: dp: 8 (over z, core), tensor: 4 (over y, x).
Axes of the slice: x: 2, y: 2, z: 4, core: 2. Of those that a mesh axis runs over, the one named last changes fastest.
Arguments:
- hidden: bfloat16 [16, 1024, 2048], P('dp', 'tensor'), may hold values from -6 to 6
- cotangent: bfloat16 [16, 1024, 2048], P('dp', 'tensor'), may hold values from -6 to 6
- norm_gain: bfloat16 [2, 2048], P(None, 'dp'), may hold values from 0.5 to 1.5
- in_weights: bfloat16 [2, 2, 2048, 4096], P(None, None, 'dp', 'tensor'), may hold values from -0.125 to 0.125
- state_weight: bfloat16 [2, 2048, 256], P(None, 'dp'), may hold values from -0.125 to 0.125
- step_weight: bfloat16 [2, 2048, 64], P(None, 'dp', 'tensor'), may hold values from -0.0625 to 0.0625
- channel_taps: float32 [2, 5, 4096], P(None, None, 'tensor'), may hold values from -3 to 3
- state_taps: float32 [2, 5, 256], replicated, may hold values from -3 to 3
- step_bias: float32 [2, 64], P(None, 'tensor'), may hold values from -6 to -2
- decay_log: float32 [2, 64], P(None, 'tensor'), may hold values from -1 to 2
- skip_gain: float32 [2, 64], P(None, 'tensor'), may hold values from 0.5 to 1.5
- inner_gain: float32 [2, 4096], P(None, 'tensor'), may hold values from 0.5 to 1.5
- out_weight: bfloat16 [2, 4096, 2048], P(None, 'tensor', 'dp'), may hold values from -0.09375 to 0.09375
Outputs:
- mixed_out: float32 [16, 1024, 2048], P('dp', 'tensor')
- grad_hidden: float32 [16, 1024, 2048], P('dp', 'tensor')
- grad_norm_gain: float32 [2, 2048], P(None, 'dp')
- grad_in_weights: float32 [2, 2, 2048, 4096], P(None, None, 'dp', 'tensor')
- grad_state_weight: float32 [2, 2048, 256], P(None, 'dp')
- grad_step_weight: float32 [2, 2048, 64], P(None, 'dp', 'tensor')
- grad_channel_taps: float32 [2, 5, 4096], P(None, None, 'tensor')
- grad_state_taps: float32 [2, 5, 256], replicated
- grad_step_bias: float32 [2, 64], P(None, 'tensor')
- grad_decay_log: float32 [2, 64], P(None, 'tensor')
- grad_skip_gain: float32 [2, 64], P(None, 'tensor')
- grad_inner_gain: float32 [2, 4096], P(None, 'tensor')
- grad_out_weight: float32 [2, 4096, 2048], P(None, 'tensor', 'dp')
All inputs are finite; a program needn't handle non-finite values.
Results may differ from a plain program's by a relative error of at most 0.025.
Values may be sent and summed in bfloat16 or wider, within the bound.
A program may use at most 384 MiB of HBM per device.

v0:
```python
import jax
import jax.numpy as jnp
from jax import lax
from jax.sharding import PartitionSpec as P

GROUP = 256
INNER = 4096


EPSILON = 1e-05
HIGHEST = lax.Precision.HIGHEST


def causal_conv(signal, taps_table):
    tap_count = taps_table.shape[0] - 1
    length = signal.shape[0]
    padded = jnp.pad(signal, ((tap_count - 1, 0), (0, 0)))
    summed = jnp.broadcast_to(taps_table[tap_count], signal.shape)
    for offset in range(tap_count):
        summed = summed + taps_table[offset] * padded[offset : offset + length]
    return summed


def scan_block(state, segment):
    rates, inputs, key_rows, query_rows = segment
    length = rates.shape[0]
    running = jnp.cumsum(rates, axis=0)
    causal = jnp.tril(jnp.ones((length, length), jnp.float32))
    spread = running[:, None, :] - running[None, :, :]
    decay = jnp.exp(jnp.where(causal[:, :, None] > 0, spread, 0.0)) * causal[:, :, None]
    scores = jnp.dot(query_rows, key_rows.T, precision=HIGHEST)
    inside = jnp.einsum("tsh,shp->thp", scores[:, :, None] * decay, inputs, precision=HIGHEST)
    carried = (
        jnp.einsum("tn,hnp->thp", query_rows, state, precision=HIGHEST)
        * jnp.exp(running)[:, :, None]
    )
    remain = jnp.exp(running[-1][None, :] - running)
    fresh = jnp.einsum("sn,shp->hnp", key_rows, inputs * remain[:, :, None], precision=HIGHEST)
    return (state * jnp.exp(running[-1])[:, None, None] + fresh, inside + carried)


def state_scan(inputs, rates, key_rows, query_rows):
    length, head_count, head_width = inputs.shape
    blocks = length // GROUP
    segments = (
        rates.reshape(blocks, GROUP, head_count),
        inputs.reshape(blocks, GROUP, head_count, head_width),
        key_rows.reshape(blocks, GROUP, -1),
        query_rows.reshape(blocks, GROUP, -1),
    )
    initial = jnp.zeros((head_count, key_rows.shape[1], head_width), jnp.float32)
    _, pieces = lax.scan(jax.checkpoint(scan_block), initial, segments)
    return pieces.reshape(length, head_count, head_width)


def mixer(
    gate_in, conv_in, step_in, shared_in, channel_taps, state_taps, step_bias, decay_log, skip_gain
):
    length = gate_in.shape[0]
    head_count = step_in.shape[1]
    conv_out = jax.nn.silu(causal_conv(conv_in, channel_taps))
    shared = jax.nn.silu(causal_conv(shared_in, state_taps))
    half_width = shared.shape[1] // 2
    step_size = jax.nn.softplus(step_in + step_bias)
    values = conv_out.reshape(length, head_count, -1)
    rates = step_size * -jnp.exp(decay_log)
    scanned = state_scan(
        values * step_size[:, :, None], rates, shared[:, :half_width], shared[:, half_width:]
    )
    scanned = scanned + skip_gain[:, None] * values
    return scanned.reshape(length, -1) * jax.nn.silu(gate_in)


def prenorm(stream, gain_full):
    row_scale = lax.rsqrt(jnp.mean(stream * stream, axis=-1, keepdims=True) + EPSILON)
    return stream * row_scale * gain_full


def split_columns(columns, inner_local, heads_local):
    return (
        columns[:, :inner_local],
        columns[:, inner_local : 2 * inner_local],
        columns[:, 2 * inner_local : 2 * inner_local + heads_local],
        columns[:, 2 * inner_local + heads_local :],
    )


def fetch(in_weights, state_weight, step_weight, out_weight, norm_gain, layer_at):
    gathered = (
        lax.all_gather(in_weights[layer_at], "dp", axis=1, tiled=True),
        lax.all_gather(state_weight[layer_at], "dp", axis=0, tiled=True),
        lax.all_gather(step_weight[layer_at], "dp", axis=0, tiled=True),
        lax.all_gather(out_weight[layer_at], "dp", axis=1, tiled=True),
        lax.all_gather(norm_gain[layer_at], "dp", axis=0, tiled=True),
    )
    in_pair, shared_cols, step_cols, out_cols, gain_full = gathered
    joined = jnp.concatenate([in_pair[0], in_pair[1], step_cols, shared_cols], axis=1)
    return (joined, shared_cols, out_cols, gain_full.astype(jnp.float32))


def forward_layer(stream, weights, smalls):
    joined, shared_cols, out_cols, gain_full = weights
    inner_local = smalls[0].shape[1]
    heads_local = smalls[2].shape[0]
    normed = prenorm(stream, gain_full).astype(jnp.bfloat16)
    columns = jnp.dot(
        lax.all_gather(normed, "tensor", axis=0, tiled=True),
        joined,
        preferred_element_type=jnp.float32,
    )
    gated = mixer(*split_columns(columns, inner_local, heads_local), *smalls[:5])
    squares = lax.psum(jnp.sum(gated * gated, axis=-1), "tensor")
    inner_scale = lax.rsqrt(squares / INNER + EPSILON)[:, None]
    mixed = (gated * inner_scale * smalls[5]).astype(jnp.bfloat16)
    update = lax.psum_scatter(
        jnp.dot(mixed, out_cols, preferred_element_type=jnp.float32),
        "tensor",
        scatter_dimension=0,
        tiled=True,
    )
    return (stream + update, (stream, normed, columns, squares, mixed))


def backward_layer(grad_stream, weights, smalls, saved, totals):
    joined, shared_cols, out_cols, gain_full = weights
    stream, normed, columns, squares, mixed = saved
    inner_local = smalls[0].shape[1]
    heads_local = smalls[2].shape[0]
    main_width = 2 * inner_local + heads_local
    upstream = grad_stream.astype(jnp.bfloat16)
    gathered_up = lax.all_gather(upstream, "tensor", axis=0, tiled=True)
    grad_mixed = lax.dot_general(
        gathered_up, out_cols, (((1,), (1,)), ((), ())), preferred_element_type=jnp.float32
    )
    out_total = totals[2] + lax.dot_general(
        mixed, gathered_up, (((0,), (0,)), ((), ())), preferred_element_type=jnp.float32
    )
    gated, mix_pull = jax.vjp(mixer, *split_columns(columns, inner_local, heads_local), *smalls[:5])
    inner_scale = lax.rsqrt(squares / INNER + EPSILON)[:, None]
    weighted = grad_mixed * smalls[5]
    inner_sum = lax.psum(jnp.sum(weighted * gated, axis=-1), "tensor")
    grad_gated = weighted * inner_scale - gated * (inner_scale * inner_scale * inner_scale) * (
        inner_sum[:, None] / INNER
    )
    grad_inner_gain = jnp.sum(grad_mixed * gated * inner_scale, axis=0)
    mix_grads = mix_pull(grad_gated)
    lowered = jnp.concatenate([mix_grads[0], mix_grads[1], mix_grads[2]], axis=1).astype(
        jnp.bfloat16
    )
    grad_shared = mix_grads[3]
    shared_high = grad_shared.astype(jnp.bfloat16)
    shared_low = (grad_shared - shared_high.astype(jnp.float32)).astype(jnp.bfloat16)
    shard_rows = lax.all_gather(normed, "tensor", axis=0, tiled=True)
    main_acc = totals[0]
    shared_acc = totals[1]
    low_rows = lowered
    high_part = shared_high
    low_part = shared_low
    contract = (((0,), (0,)), ((), ()))
    main_acc = main_acc + lax.dot_general(
        shard_rows, low_rows, contract, preferred_element_type=jnp.float32
    )
    shared_acc = shared_acc + lax.dot_general(
        shard_rows, high_part, contract, preferred_element_type=jnp.float32
    )
    shared_acc = shared_acc + lax.dot_general(
        shard_rows, low_part, contract, preferred_element_type=jnp.float32
    )
    main_cols = joined[:, :main_width]
    low_rows = lowered
    high_part = shared_high
    low_part = shared_low
    contract = (((1,), (1,)), ((), ()))
    term = lax.dot_general(low_rows, main_cols, contract, preferred_element_type=jnp.float32)
    term = term + lax.dot_general(
        high_part, shared_cols, contract, preferred_element_type=jnp.float32
    )
    grad_normed = lax.psum_scatter(
        (
            term
            + lax.dot_general(low_part, shared_cols, contract, preferred_element_type=jnp.float32)
        ).astype(jnp.bfloat16),
        "tensor",
        scatter_dimension=0,
        tiled=True,
    ).astype(jnp.float32)
    _, norm_pull = jax.vjp(prenorm, stream, gain_full)
    grad_back, grad_gain = norm_pull(grad_normed)
    updated = [main_acc, shared_acc, out_total, totals[3] + grad_gain]
    updated = updated + [totals[4 + offset] + mix_grads[4 + offset] for offset in range(5)]
    updated = updated + [totals[9] + grad_inner_gain]
    return (grad_stream + grad_back, updated)


def reduce_grads(layer_totals):
    stacked = [jnp.stack([entry[position] for entry in layer_totals]) for position in range(10)]
    (
        main_all,
        shared_all,
        out_all,
        gain_all,
        channel_all,
        state_all,
        bias_all,
        decay_all,
        skip_all,
        inner_all,
    ) = stacked
    shared_all, gain_all, state_all = (
        lax.psum(shared_all.astype(jnp.bfloat16), "tensor").astype(jnp.float32),
        lax.psum(gain_all.astype(jnp.bfloat16), "tensor").astype(jnp.float32),
        lax.psum(state_all.astype(jnp.bfloat16), "tensor").astype(jnp.float32),
    )
    inner_local = inner_all.shape[1]
    in_pair = jnp.stack(
        [main_all[:, :, :inner_local], main_all[:, :, inner_local : 2 * inner_local]], axis=1
    )
    step_all = main_all[:, :, 2 * inner_local :]
    owned = (
        lax.psum_scatter(
            gain_all.astype(jnp.bfloat16), "dp", scatter_dimension=1, tiled=True
        ).astype(jnp.float32),
        lax.psum_scatter(
            in_pair.astype(jnp.bfloat16), "dp", scatter_dimension=2, tiled=True
        ).astype(jnp.float32),
        lax.psum_scatter(
            shared_all.astype(jnp.bfloat16), "dp", scatter_dimension=1, tiled=True
        ).astype(jnp.float32),
        lax.psum_scatter(
            step_all.astype(jnp.bfloat16), "dp", scatter_dimension=1, tiled=True
        ).astype(jnp.float32),
        lax.psum_scatter(
            out_all.astype(jnp.bfloat16), "dp", scatter_dimension=2, tiled=True
        ).astype(jnp.float32),
    )
    spread_out = (
        lax.psum(channel_all.astype(jnp.bfloat16), "dp").astype(jnp.float32),
        lax.psum(state_all.astype(jnp.bfloat16), "dp").astype(jnp.float32),
        lax.psum(bias_all.astype(jnp.bfloat16), "dp").astype(jnp.float32),
        lax.psum(decay_all.astype(jnp.bfloat16), "dp").astype(jnp.float32),
        lax.psum(skip_all.astype(jnp.bfloat16), "dp").astype(jnp.float32),
        lax.psum(inner_all.astype(jnp.bfloat16), "dp").astype(jnp.float32),
    )
    return (
        owned[0],
        owned[1],
        owned[2],
        owned[3],
        spread_out[0],
        spread_out[1],
        spread_out[2],
        spread_out[3],
        spread_out[4],
        spread_out[5],
        owned[4],
    )


def local(
    hidden,
    cotangent,
    norm_gain,
    in_weights,
    state_weight,
    step_weight,
    channel_taps,
    state_taps,
    step_bias,
    decay_log,
    skip_gain,
    inner_gain,
    out_weight,
):
    layer_total = in_weights.shape[0]
    batch_total = hidden.shape[0]
    d_model = norm_gain.shape[1] * lax.axis_size("dp")
    inner_local = inner_gain.shape[1]
    heads_local = step_bias.shape[1]
    shared_width = state_weight.shape[2]
    tap_rows = channel_taps.shape[1]
    main_width = 2 * inner_local + heads_local

    def layer_smalls(layer_at):
        return (
            channel_taps[layer_at],
            state_taps[layer_at],
            step_bias[layer_at],
            decay_log[layer_at],
            skip_gain[layer_at],
            inner_gain[layer_at],
        )

    def zero_layer():
        return [
            jnp.zeros((d_model, main_width), jnp.float32),
            jnp.zeros((d_model, shared_width), jnp.float32),
            jnp.zeros((inner_local, d_model), jnp.float32),
            jnp.zeros((d_model,), jnp.float32),
            jnp.zeros((tap_rows, inner_local), jnp.float32),
            jnp.zeros((tap_rows, shared_width), jnp.float32),
            jnp.zeros((heads_local,), jnp.float32),
            jnp.zeros((heads_local,), jnp.float32),
            jnp.zeros((heads_local,), jnp.float32),
            jnp.zeros((inner_local,), jnp.float32),
        ]

    def weights_for(layer_at):
        return fetch(in_weights, state_weight, step_weight, out_weight, norm_gain, layer_at)

    outputs = []
    input_grads = []
    layer_totals = [zero_layer() for layer_at in range(layer_total)]
    for batch_no in range(batch_total):
        stream = hidden[batch_no].astype(jnp.float32)
        saved_all = []
        for run_layer_at in range(layer_total):
            stream, saved = forward_layer(
                stream, weights_for(run_layer_at), layer_smalls(run_layer_at)
            )
            saved_all.append(saved)
        grad_stream = cotangent[batch_no].astype(jnp.float32)
        new_totals = list(layer_totals)
        for run_layer_at in reversed(range(layer_total)):
            grad_stream, new_totals[run_layer_at] = backward_layer(
                grad_stream,
                weights_for(run_layer_at),
                layer_smalls(run_layer_at),
                saved_all[run_layer_at],
                layer_totals[run_layer_at],
            )
        stream, grad_stream, layer_totals = (stream, grad_stream, new_totals)
        outputs.append(stream)
        input_grads.append(grad_stream)
    reduced = reduce_grads(layer_totals)
    return (
        jnp.stack(outputs),
        jnp.stack(input_grads),
        reduced[0],
        reduced[1],
        reduced[2],
        reduced[3],
        reduced[4],
        reduced[5],
        reduced[6],
        reduced[7],
        reduced[8],
        reduced[9],
        reduced[10],
    )


def solution(mesh):
    placed = (
        P("dp", "tensor", None),
        P("dp", "tensor", None),
        P(None, "dp"),
        P(None, None, "dp", "tensor"),
        P(None, "dp", None),
        P(None, "dp", "tensor"),
        P(None, None, "tensor"),
        P(),
        P(None, "tensor"),
        P(None, "tensor"),
        P(None, "tensor"),
        P(None, "tensor"),
        P(None, "tensor", "dp"),
    )
    return jax.shard_map(
        local,
        mesh=mesh,
        in_specs=placed,
        out_specs=(
            P("dp", "tensor", None),
            P("dp", "tensor", None),
            P(None, "dp"),
            P(None, None, "dp", "tensor"),
            P(None, "dp", None),
            P(None, "dp", "tensor"),
            P(None, None, "tensor"),
            P(),
            P(None, "tensor"),
            P(None, "tensor"),
            P(None, "tensor"),
            P(None, "tensor"),
            P(None, "tensor", "dp"),
        ),
        check_vma=False,
    )
```

profile of v0, /device:TPU:0, one launch (start us, length us, event | category | flops | bytes accessed | tf_op | source)
XLA Modules:
  0.0 4368.1 jit_solution(1932637840819663472)
XLA Ops:
  50.5 45.3 %all-gather.39.cloned.1.call-done = bf16[1,2,2048,1024]{3,2,1,0:T(8,128)(2,1)} async-done(((bf16[1,2,256,1024]{3,2,1,0:T(8,128)(2,1)}), bf16[1,2,2048,1024]{3,2,1,0:T(8,128)(2,1)}) %all-gather.39.cloned.1.call-update) | async-done | bytes 8388624 | tf_op jit(solution)/shard_map/all_gather | solution.py:90
  133.4 38.9 all-gather.31.cloned.1.call-done
  195.3 32.0 all-gather.27.cloned.1.call-done
  283.4 149.7 %while.210 = (s32[]{:T(128)}, f32[16,128,64]{1,2,0:T(8,128)S(1)}, f32[4,256,16,64]{1,0,3,2:T(4,128)}, f32[4,256,16]{1,2,0:T(8,128)S(1)}, f32[4,256,16,64]{1,3,2,...) while((s32[]{:T(128)}, f32[16,128,64]{1,2,0:T(8,128)S(1)}, ...), condition=%wide.region_20.21_spmd.clone, body=%wide.region_17.20_spmd.clone.sunk | while | flops 1717510144 | bytes 13980223 | solution.py:52
  448.9 149.8 %while.208 = (s32[]{:T(128)}, f32[16,128,64]{1,2,0:T(8,128)S(1)}, f32[4,256,16,64]{1,0,3,2:T(4,128)}, f32[4,256,16]{1,2,0:T(8,128)S(1)}, f32[4,256,16,64]{1,3,2,...) while((s32[]{:T(128)}, f32[16,128,64]{1,2,0:T(8,128)S(1)}, ...), condition=%wide.region_4.5_spmd.clone, body=%wide.region_1.4_spmd.clone.sunk | while | flops 1717510144 | bytes 13980223 | solution.py:52
  667.1 56.4 %reduce-scatter.20.cloned.1.call-done = f32[256,2048]{1,0:T(8,128)} async-done(((f32[1024,2048]{1,0:T(8,128)}), f32[256,2048]{1,0:T(8,128)}) %reduce-scatter.20.cloned.1.call-update) | async-done | bytes 2097168 | tf_op jit(solution)/shard_map/reduce_scatter | solution.py:115
  723.6 89.8 %reduce-scatter.16.cloned.1.call-done = f32[256,2048]{1,0:T(8,128)} async-done(((f32[1024,2048]{1,0:T(8,128)}), f32[256,2048]{1,0:T(8,128)}) %reduce-scatter.16.cloned.1.call-update) | async-done | bytes 2097168 | tf_op jit(solution)/shard_map/reduce_scatter | solution.py:115
  836.4 31.5 all-gather.51.cloned.1.call-done
  867.9 49.4 %all-gather.49.cloned.1.call-done = bf16[1,1024,2048]{2,1,0:T(8,128)(2,1)} async-done(((bf16[1,1024,256]{2,1,0:T(8,128)(2,1)}), bf16[1,1024,2048]{2,1,0:T(8,128)(2,1)}) %all-gather.49.cloned.1.call-update) | async-done | bytes 4194320 | tf_op jit(solution)/shard_map/all_gather | solution.py:93
  927.5 72.2 %all-gather.45.cloned.1.call-done = bf16[1,2,2048,1024]{3,2,1,0:T(8,128)(2,1)} async-done(((bf16[1,2,256,1024]{3,2,1,0:T(8,128)(2,1)}), bf16[1,2,2048,1024]{3,2,1,0:T(8,128)(2,1)}) %all-gather.45.cloned.1.call-update) | async-done | bytes 8388624 | tf_op jit(solution)/shard_map/all_gather | solution.py:90
  1037.2 38.8 all-gather.33.cloned.1.call-done
  1099.5 31.7 all-gather.29.cloned.1.call-done
  1160.4 24.3 fusion.617
  1199.9 149.8 %while.211 = (s32[]{:T(128)}, f32[16,128,64]{1,2,0:T(8,128)S(1)}, f32[4,256,16,64]{1,0,3,2:T(4,128)}, f32[4,256,16]{1,2,0:T(8,128)S(1)}, f32[4,256,16,64]{1,3,2,...) while((s32[]{:T(128)}, f32[16,128,64]{1,2,0:T(8,128)S(1)}, ...), condition=%wide.region_28.29_spmd.clone, body=%wide.region_25.28_spmd.clone.sunk | while | flops 1717510144 | bytes 13980223 | solution.py:52
  1364.8 150.0 %while.209 = (s32[]{:T(128)}, f32[16,128,64]{1,2,0:T(8,128)S(1)}, f32[4,256,16,64]{1,0,3,2:T(4,128)}, f32[4,256,16]{1,2,0:T(8,128)S(1)}, f32[4,256,16,64]{1,3,2,...) while((s32[]{:T(128)}, f32[16,128,64]{1,2,0:T(8,128)S(1)}, ...), condition=%wide.region_12.13_spmd.clone, body=%wide.region_9.12_spmd.clone.sunk | while | flops 1717510144 | bytes 13980671 | solution.py:52
  1519.3 153.0 %while.212 = (s32[]{:T(128)}, f32[16,128,64]{1,2,0:T(8,128)S(1)}, f32[4,256,16,64]{1,0,3,2:T(4,128)}, f32[4,16,128,64]{2,3,1,0:T(8,128)}, f32[4,256,16]{1,2,0:T(...) while((s32[]{:T(128)}, f32[16,128,64]{1,2,0:T(8,128)S(1)}, ...), condition=%wide.region_35.37_spmd.clone, body=%wide.region_32.36_spmd.clone.sunk | while | flops 1717313536 | bytes 14439951 | solution.py:52
  1676.8 153.3 %while.216 = (s32[]{:T(128)}, f32[16,128,64]{1,2,0:T(8,128)S(1)}, f32[4,256,16,64]{1,0,3,2:T(4,128)}, f32[4,16,128,64]{2,3,1,0:T(8,128)}, f32[4,256,16]{1,2,0:T(...) while((s32[]{:T(128)}, f32[16,128,64]{1,2,0:T(8,128)S(1)}, ...), condition=%wide.region_79.81_spmd.clone, body=%wide.region_76.80_spmd.clone.sunk | while | flops 1717313536 | bytes 14439503 | solution.py:52
  1922.7 260.4 %while.213 = (s32[]{:T(128)}, f32[16,128,64]{1,2,0:T(8,128)}, f32[4,256,16]{1,0,2:T(4,128)}, f32[4,256,16,64]{1,0,3,2:T(4,128)}, f32[4,256,128]{2,1,0:T(8,128)},...) while((s32[]{:T(128)}, f32[16,128,64]{1,2,0:T(8,128)}, ...), condition=%wide.region_50.52_spmd.clone, body=%wide.region_38.51_spmd.clone.sunk | while | flops 3946033152 | bytes 42112128 | solution.py:52
  2198.1 241.0 %while.217 = (s32[]{:T(128)}, f32[16,128,64]{1,2,0:T(8,128)}, f32[4,256,16]{1,0,2:T(4,128)}, f32[4,256,16,64]{1,0,3,2:T(4,128)}, f32[4,256,128]{2,1,0:T(8,128)},...) while((s32[]{:T(128)}, f32[16,128,64]{1,2,0:T(8,128)}, ...), condition=%wide.region_94.96_spmd.clone, body=%wide.region_82.95_spmd.clone.sunk | while | flops 3946033152 | bytes 37916088 | solution.py:52
  2605.4 56.4 %reduce-scatter.28.cloned.1.call-done = bf16[256,2048]{1,0:T(8,128)(2,1)} async-done(((bf16[1024,2048]{1,0:T(8,128)(2,1)}), bf16[256,2048]{1,0:T(8,128)(2,1)}) %reduce-scatter.28.cloned.1.call-update) | async-done | bytes 1048592 | tf_op jit(solution)/shard_map/reduce_scatter | solution.py:178
  2665.9 85.2 %reduce-scatter.18.cloned.1.call-done = f32[256,2048]{1,0:T(8,128)} async-done(((f32[1024,2048]{1,0:T(8,128)}), f32[256,2048]{1,0:T(8,128)}) %reduce-scatter.18.cloned.1.call-update) | async-done | bytes 2097168 | tf_op jit(solution)/shard_map/reduce_scatter | solution.py:115
  2761.6 153.1 %while.214 = (s32[]{:T(128)}, f32[16,128,64]{1,2,0:T(8,128)S(1)}, f32[4,256,16,64]{1,0,3,2:T(4,128)}, f32[4,16,128,64]{2,3,1,0:T(8,128)}, f32[4,256,16]{1,2,0:T(...) while((s32[]{:T(128)}, f32[16,128,64]{1,2,0:T(8,128)S(1)}, ...), condition=%wide.region_57.59_spmd.clone, body=%wide.region_54.58_spmd.clone.sunk | while | flops 1717313536 | bytes 14439503 | solution.py:52
  2919.3 155.9 %while.218 = (s32[]{:T(128)}, f32[16,128,64]{1,2,0:T(8,128)S(1)}, f32[4,256,16,64]{1,0,3,2:T(4,128)}, f32[4,16,128,64]{2,3,1,0:T(8,128)}, f32[4,256,16]{1,2,0:T(...) while((s32[]{:T(128)}, f32[16,128,64]{1,2,0:T(8,128)S(1)}, ...), condition=%wide.region_101.103_spmd.clone, body=%wide.region_98.102_spmd.clone.sunk | while | flops 1717313536 | bytes 14440011 | solution.py:52
  2932.6 23.5 dynamic_update_slice.291
  3161.6 246.4 %while.215 = (s32[]{:T(128)}, f32[16,128,64]{1,2,0:T(8,128)}, f32[4,256,16]{1,0,2:T(4,128)}, f32[4,256,16,64]{1,0,3,2:T(4,128)}, f32[4,256,128]{2,1,0:T(8,128)},...) while((s32[]{:T(128)}, f32[16,128,64]{1,2,0:T(8,128)}, ...), condition=%wide.region_72.74_spmd.clone, body=%wide.region_60.73_spmd.clone.sunk | while | flops 3946033152 | bytes 37917768 | solution.py:52
  3430.9 241.1 %while.219 = (s32[]{:T(128)}, f32[16,128,64]{1,2,0:T(8,128)}, f32[4,256,16]{1,0,2:T(4,128)}, f32[4,256,16,64]{1,0,3,2:T(4,128)}, f32[4,256,128]{2,1,0:T(8,128)},...) while((s32[]{:T(128)}, f32[16,128,64]{1,2,0:T(8,128)}, ...), condition=%wide.region_116.118_spmd.clone, body=%wide.region_104.117_spmd.clone.sunk | while | flops 3946033152 | bytes 37916088 | solution.py:52
  3714.2 24.1 multiply_reduce_fusion.39
  3987.6 75.1 %reduce-scatter.22.cloned.1.call-done = f32[256,2048]{1,0:T(8,128)} async-done(((f32[1024,2048]{1,0:T(8,128)}), f32[256,2048]{1,0:T(8,128)}) %reduce-scatter.22.cloned.1.call-update) | async-done | bytes 2097168 | tf_op jit(solution)/shard_map/reduce_scatter | solution.py:115
  4072.0 24.3 reduce-scatter.40.cloned.1.call-done
  4107.6 28.6 all-reduce.100
  4140.4 47.4 %reduce-scatter.36.cloned.1.call-done = bf16[2,1024,256]{2,1,0:T(8,128)(2,1)} async-done(((bf16[2,1024,2048]{2,1,0:T(8,128)(2,1)}), bf16[2,1024,256]{2,1,0:T(8,128)(2,1)}) %reduce-scatter.36.cloned.1.call-update) | async-done | bytes 1048592 | tf_op jit(solution)/shard_map/reduce_scatter | solution.py:232
  4190.5 166.4 %reduce-scatter.32.cloned.1.call-done = bf16[2,2,256,1024]{2,3,0,1:T(8,128)(2,1)} async-done(((bf16[2,2,2048,1024]{2,3,0,1:T(8,128)(2,1)}), bf16[2,2,256,1024]{2,3,0,1:T(8,128)(2,1)}) %reduce-scatter.32.cloned.1.call-update) | async-done | bytes 2097168 | tf_op jit(solution)/shard_map/reduce_scatter | solution.py:223
  (2195 shorter events, 3286.1 us)
Async XLA Ops:
  7.2 88.6 %all-gather.39.cloned.1.call-start = ((), (), s32[]{:S(2)}) async-start(), calls=%async_computation.30 | async-start | bytes 9437184 | tf_op jit(solution)/shard_map/all_gather | solution.py:90
  10.5 107.6 %all-gather.41.cloned.1.call-start = ((), (), s32[]{:S(2)}) async-start(), calls=%async_computation.31 | async-start | bytes 1179648 | tf_op jit(solution)/shard_map/all_gather | solution.py:91
  11.3 161.0 %all-gather.31.cloned.1.call-start = ((), (), s32[]{:S(2)}) async-start(), calls=%async_computation.17 | async-start | bytes 5242880 | tf_op jit(solution)/shard_map/all_gather | solution.py:107
  28.4 198.9 %all-gather.27.cloned.1.call-start = ((), (), s32[]{:S(2)}) async-start(), calls=%async_computation.13 | async-start | bytes 5242880 | tf_op jit(solution)/shard_map/all_gather | solution.py:107
  29.0 596.7 %all-gather.43.cloned.1.call-start = ((), (), s32[]{:S(2)}) async-start(), calls=%async_computation.32 | async-start | bytes 4718592 | tf_op jit(solution)/shard_map/all_gather | solution.py:93
  30.1 693.5 %reduce-scatter.20.cloned.1.call-start = ((), (), s32[]{:S(2)}) async-start(), calls=%async_computation.18 | async-start | bytes 10485760 | tf_op jit(solution)/shard_map/reduce_scatter | solution.py:115
  47.4 219.3 %copy-start.232 = (f32[16]{0:T(128)}, f32[16]{0:T(128)S(1)}, u32[]{:S(2)}) copy-start(f32[16]{0:T(128)S(1)} %get-tuple-element.3226) | copy-start | bytes 196
  48.6 219.2 %copy-start.209 = (f32[1,1,256]{2,0,1:T(1,128)}, f32[1,1,256]{2,0,1:T(1,128)S(1)}, u32[]{:S(2)}) copy-start(f32[1,1,256]{2,0,1:T(1,128)S(1)} %get-tuple-element.3153) | copy-start | bytes 3076
  48.6 219.2 %copy-start.211 = (f32[1,1,256]{2,0,1:T(1,128)}, f32[1,1,256]{2,0,1:T(1,128)S(1)}, u32[]{:S(2)}) copy-start(f32[1,1,256]{2,0,1:T(1,128)S(1)} %get-tuple-element.3154) | copy-start | bytes 3076
  48.6 219.2 %copy-start.213 = (f32[1,1,256]{2,0,1:T(1,128)}, f32[1,1,256]{2,0,1:T(1,128)S(1)}, u32[]{:S(2)}) copy-start(f32[1,1,256]{2,0,1:T(1,128)S(1)} %get-tuple-element.3155) | copy-start | bytes 3076
  637.1 176.3 %reduce-scatter.16.cloned.1.call-start = ((), (), s32[]{:S(2)}) async-start(), calls=%async_computation.14 | async-start | bytes 10485760 | tf_op jit(solution)/shard_map/reduce_scatter | solution.py:115
  649.7 218.2 %all-gather.51.cloned.1.call-start = ((), (), s32[]{:S(2)}) async-start(), calls=%async_computation.36 | async-start | bytes 5242880 | tf_op jit(solution)/shard_map/all_gather | solution.py:131
  653.3 264.1 %all-gather.49.cloned.1.call-start = ((), (), s32[]{:S(2)}) async-start(), calls=%async_computation.35 | async-start | bytes 4718592 | tf_op jit(solution)/shard_map/all_gather | solution.py:93
  654.0 345.7 %all-gather.45.cloned.1.call-start = ((), (), s32[]{:S(2)}) async-start(), calls=%async_computation.33 | async-start | bytes 9437184 | tf_op jit(solution)/shard_map/all_gather | solution.py:90
  654.6 367.4 %all-gather.47.cloned.1.call-start = ((), (), s32[]{:S(2)}) async-start(), calls=%async_computation.34 | async-start | bytes 1179648 | tf_op jit(solution)/shard_map/all_gather | solution.py:91
  655.3 420.7 %all-gather.33.cloned.1.call-start = ((), (), s32[]{:S(2)}) async-start(), calls=%async_computation.19 | async-start | bytes 5242880 | tf_op jit(solution)/shard_map/all_gather | solution.py:107
  819.3 311.9 %all-gather.29.cloned.1.call-start = ((), (), s32[]{:S(2)}) async-start(), calls=%async_computation.15 | async-start | bytes 5242880 | tf_op jit(solution)/shard_map/all_gather | solution.py:107
  820.0 1043.2 %all-gather.53.cloned.1.call-start = ((), (), s32[]{:S(2)}) async-start(), calls=%async_computation.37 | async-start | bytes 5242880 | tf_op jit(solution)/shard_map/all_gather | solution.py:131
  820.6 1784.8 %reduce-scatter.24.cloned.1.call-start = ((), (), s32[]{:S(2)}) async-start(), calls=%async_computation.21 | async-start | bytes 5242880 | tf_op jit(solution)/shard_map/reduce_scatter | solution.py:178
  2552.5 109.3 %reduce-scatter.28.cloned.1.call-start = ((), (), s32[]{:S(2)}) async-start(), calls=%async_computation.24 | async-start | bytes 5242880 | tf_op jit(solution)/shard_map/reduce_scatter | solution.py:178
  2581.4 169.7 %reduce-scatter.18.cloned.1.call-start = ((), (), s32[]{:S(2)}) async-start(), calls=%async_computation.16 | async-start | bytes 10485760 | tf_op jit(solution)/shard_map/reduce_scatter | solution.py:115
  2593.6 498.1 %all-gather.35.cloned.1.call-start = ((), (), s32[]{:S(2)}) async-start(), calls=%async_computation.22 | async-start | bytes 5242880 | tf_op jit(solution)/shard_map/all_gather | solution.py:131
  2756.6 345.0 %all-gather.37.cloned.1.call-start = ((), (), s32[]{:S(2)}) async-start(), calls=%async_computation.25 | async-start | bytes 5242880 | tf_op jit(solution)/shard_map/all_gather | solution.py:131
  2914.7 974.0 %reduce-scatter.38.cloned.1.call-start = ((), (), s32[]{:S(2)}) async-start(), calls=%async_computation.38 | async-start | bytes 2359296 | tf_op jit(solution)/shard_map/reduce_scatter | solution.py:226
  3714.1 223.4 %reduce-scatter.26.cloned.1.call-start = ((), (), s32[]{:S(2)}) async-start(), calls=%async_computation.23 | async-start | bytes 5242880 | tf_op jit(solution)/shard_map/reduce_scatter | solution.py:178
  3787.0 150.4 %reduce-scatter.30.cloned.1.call-start = ((), (), s32[]{:S(2)}) async-start(), calls=%async_computation.26 | async-start | bytes 5242880 | tf_op jit(solution)/shard_map/reduce_scatter | solution.py:178
  3822.4 156.2 %reduce-scatter.34.cloned.1.call-start = ((), (), s32[]{:S(2)}) async-start(), calls=%async_computation.28 | async-start | bytes 147456 | tf_op jit(solution)/shard_map/reduce_scatter | solution.py:229
  3888.6 91.4 %all-reduce.104.cloned.1.call-start = ((), (), s32[]{:S(2)}) async-start(), calls=%async_computation.39 | async-start | bytes 524288 | tf_op jit(solution)/shard_map/psum | solution.py:210
  3889.1 173.6 %reduce-scatter.22.cloned.1.call-start = ((), (), s32[]{:S(2)}) async-start(), calls=%async_computation.20 | async-start | bytes 10485760 | tf_op jit(solution)/shard_map/reduce_scatter | solution.py:115
  3900.7 195.7 %reduce-scatter.40.cloned.1.call-start = ((), (), s32[]{:S(2)}) async-start(), calls=%async_computation.40 | async-start | bytes 589824
  3941.8 246.0 %reduce-scatter.36.cloned.1.call-start = ((), (), s32[]{:S(2)}) async-start(), calls=%async_computation.29 | async-start | bytes 9437184 | tf_op jit(solution)/shard_map/reduce_scatter | solution.py:232
  3949.4 407.6 %reduce-scatter.32.cloned.1.call-start = ((), (), s32[]{:S(2)}) async-start(), calls=%async_computation.27 | async-start | bytes 18874368 | tf_op jit(solution)/shard_map/reduce_scatter | solution.py:223
  (307 other events, 5508.0 us)
Sparse Core Ops, SparseCore 0:
  10.6 85.2 all-gather.38
  97.5 20.5 all-gather.40
  119.9 52.3 all-gather.30
  174.6 52.6 all-gather.26
  228.8 47.7 all-gather.42
  637.2 86.3 reduce-scatter.19
  726.9 86.3 reduce-scatter.15
  815.2 52.7 all-gather.50
  869.5 47.7 all-gather.48
  919.4 80.2 all-gather.44
  1001.3 20.6 all-gather.46
  1023.7 52.3 all-gather.32
  1078.5 52.6 all-gather.28
  1132.9 52.6 all-gather.52
  2552.6 52.7 reduce-scatter.23
  2609.0 52.6 reduce-scatter.27
  2664.7 86.3 reduce-scatter.17
  2756.7 52.6 all-gather.34
  2914.8 52.7 all-gather.36
  3714.2 35.6 reduce-scatter.37
  3787.1 52.5 reduce-scatter.25
  3843.2 52.6 reduce-scatter.29
  3898.8 30.1 reduce-scatter.33
  3931.8 41.1 all-reduce.103
  3976.3 86.3 reduce-scatter.21
  4065.4 30.8 reduce-scatter.39
  4098.6 89.1 reduce-scatter.35
  4190.3 166.6 reduce-scatter.31
where the time goes:
time: 4410 us; the launch traced here: 4370 us
  local copies, waits for them, and re-layouts  1640 us (37%)
  matrix products  1100 us (25%)
  waiting for transfers between devices  989 us (22%)
  other arithmetic  475 us (11%)
  blocking collectives  130 us (3%)
    dynamic_update_slice x128, local copies, waits for them, and re-layouts, state_scan(): _, pieces = lax.scan(jax.checkpoint(scan_block), initial, segments)  1200 us
    dot_general x64, matrix products, scan_block(): jnp.einsum('tsh,shp->thp', scores[:, :, None] * decay, inputs, precision=...  357 us
    reduce_scatter x4, waiting for transfers between devices, forward_layer(): lax.psum_scatter(jnp.dot(mixed, out_cols, preferred_element_type=jnp.floa...  307 us
    reduce_scatter x1, waiting for transfers between devices, reduce_grads(): lax.psum_scatter(in_pair.astype(jnp.bfloat16), 'dp', scatter_dimension=2,...  166 us
    all_gather x4, waiting for transfers between devices, forward_layer(): lax.all_gather(normed, 'tensor', axis=0, tiled=True)  141 us
    dot_general x64, matrix products, scan_block(): jnp.einsum('sn,shp->hnp', key_rows, inputs * remain[:, :, None], precisio...  132 us
    another operation x185, other arithmetic  120 us
    all_gather x2, waiting for transfers between devices, fetch(): lax.all_gather(in_weights[layer_at], 'dp', axis=1, tiled=True)  118 us
  transfers between devices with their start and end apart: 28, of which 19 were waited for; matrix products, arithmetic and copies ran while one was open for 44% of the time, Pallas kernels for 0%

commit v1 on v0

v1 whole, which is shorter than its diff:
```python
import functools

import jax
import jax.numpy as jnp
from jax import lax
from jax.experimental import pallas as pl
from jax.experimental.pallas import tpu as pltpu
from jax.sharding import PartitionSpec as P

EPSILON = 1e-05
CHUNK = 128
GROUP_LANES = 256
LOG2E = 1.4426950408889634
F32 = jnp.float32
BF16 = jnp.bfloat16
NN = (((1,), (0,)), ((), ()))
NT = (((1,), (1,)), ((), ()))
TN = (((0,), (0,)), ((), ()))


def mm(a, b, dims=NN):
    return lax.dot_general(a, b, dims, preferred_element_type=F32)


def sigmoid(v):
    return 0.5 * jnp.tanh(0.5 * v) + 0.5


def softplus(v):
    return jnp.maximum(v, 0.0) + jnp.log(1.0 + jnp.exp(-jnp.abs(v)))


def split3(v):
    high = v.astype(BF16)
    rest = v - high.astype(F32)
    mid = rest.astype(BF16)
    return high, mid, (rest - mid.astype(F32)).astype(BF16)


def spread(v, expand, heads):
    high = v.astype(BF16)
    low = (v - high.astype(F32)).astype(BF16)
    lane = lax.broadcasted_iota(jnp.int32, v.shape, 1)
    parts = jnp.where(lane < heads, high, jnp.where(lane < 2 * heads, low, jnp.zeros_like(low)))
    return mm(parts, expand)


def conv_rows(window, table, length):
    total = table[4:5] + table[3:4] * window[8 : 8 + length]
    for back in range(1, 4):
        total = total + table[3 - back : 4 - back] * pltpu.roll(window, back, 0)[8 : 8 + length]
    return total


def causal(length, flip):
    row = lax.broadcasted_iota(jnp.int32, (length, length), 0)
    col = lax.broadcasted_iota(jnp.int32, (length, length), 1)
    return (row <= col) if flip else (row >= col)


def head_masks(lanes, width):
    lane = lax.broadcasted_iota(jnp.int32, (1, lanes), 1)
    return [(lane >= j * width) & (lane < (j + 1) * width) for j in range(lanes // width)]


def gate_lanes(start, part):
    at = start // part * 2 * part + start % part
    return slice(at, at + GROUP_LANES), slice(at + part, at + part + GROUP_LANES)


def forward_kernel(heads, part, columns_ref, small_ref, chan_ref, taps_ref, head_ref, expand_ref, tri_ref,
                   mixed_ref, square_ref, y_ref, saved_ref, state, xbuf, sbuf):
    length, channels = y_ref.shape
    width = channels // heads
    shared = taps_ref.shape[1]
    half = shared // 2

    @pl.when(pl.program_id(0) == 0)
    def _():
        state[...] = jnp.zeros_like(state)
        xbuf[0:8] = jnp.zeros((8, channels), F32)
        sbuf[0:8] = jnp.zeros((8, shared), F32)

    sbuf[8:] = small_ref[:, :shared]
    tri = tri_ref[...]
    expand = expand_ref[...]
    dt = softplus(small_ref[:, shared:] + head_ref[0:1])
    running = sum(mm(tri, piece) for piece in split3(dt * (head_ref[1:2] * LOG2E)))
    running_t = running.T
    decay_in = jnp.exp2(running)
    decay_out = jnp.exp2(running[length - 1 :] - running)
    dt_wide = spread(dt, expand, heads)
    in_wide = spread(decay_in, expand, heads)
    out_wide = spread(dt * decay_out, expand, heads)

    taps = taps_ref[...]
    bc = conv_rows(sbuf[...], taps, length)
    bc = (bc * sigmoid(bc)).astype(BF16)
    keys, queries = bc[:, :half], bc[:, half:]
    scores = jnp.where(causal(length, False), mm(queries, keys, NT), 0.0)
    squares = jnp.zeros((length, 128), F32)
    masks = head_masks(GROUP_LANES, width)
    for start in range(0, channels, GROUP_LANES):
        lanes = slice(start, start + GROUP_LANES)
        gate_at, conv_at = gate_lanes(start, part)
        table = chan_ref[:, lanes]
        xbuf[8:, lanes] = columns_ref[:, conv_at].astype(F32)
        c = conv_rows(xbuf[:, lanes], table, length)
        xbuf[0:8, lanes] = xbuf[length:, lanes]
        xs = c * sigmoid(c)
        values = (xs * dt_wide[:, lanes]).astype(BF16)
        weights, parts = [], []
        for j in range(GROUP_LANES // width):
            h = start // width + j
            gap = jnp.minimum(running[:, h : h + 1] - running_t[h : h + 1, :], 0.0)
            weights.append((scores * jnp.exp2(gap)).astype(BF16))
            parts.append(jnp.where(masks[j], values, jnp.zeros_like(values)))
        before = state[:, lanes]
        before_low = before.astype(BF16)
        saved_ref[0, :, lanes] = before_low
        y = mm(jnp.concatenate(weights, axis=1), jnp.concatenate(parts, axis=0))
        y = y + mm(queries, before_low) * in_wide[:, lanes]
        y_ref[:, lanes] = y
        z = columns_ref[:, gate_at].astype(F32)
        gated = (y + table[5:6] * xs) * (z * sigmoid(z))
        mixed_ref[:, lanes] = (gated * table[6:7]).astype(BF16)
        power = gated * gated
        for at in range(0, GROUP_LANES, 128):
            squares = squares + power[:, at : at + 128]
        fresh = mm(keys, (xs * out_wide[:, lanes]).astype(BF16), TN)
        state[:, lanes] = before * in_wide[length - 1 :, lanes] + fresh
    square_ref[...] = jnp.sum(squares, axis=1, keepdims=True)
    sbuf[0:8] = sbuf[length:]


def backward_kernel(heads, part, columns_ref, halo_ref, small_ref, shalo_ref, y_ref, saved_ref, up_ref, pull_ref,
                    chan_ref, taps_ref, head_ref, expand_ref, tri_ref,
                    dcolumns_ref, dsmall_ref, gchan_ref, gtaps_ref, ghead_ref,
                    dstate, xbuf, sbuf, dxbuf, dsbuf):
    length, channels = y_ref.shape
    width = channels // heads
    shared = taps_ref.shape[1]
    half = shared // 2
    step_no = pl.program_id(0)
    first_block = step_no == pl.num_programs(0) - 1

    @pl.when(step_no == 0)
    def _():
        dstate[...] = jnp.zeros_like(dstate)
        dxbuf[length:] = jnp.zeros((8, channels), F32)
        dsbuf[length:] = jnp.zeros((8, shared), F32)
        gchan_ref[...] = jnp.zeros_like(gchan_ref)
        gtaps_ref[...] = jnp.zeros_like(gtaps_ref)
        ghead_ref[...] = jnp.zeros_like(ghead_ref)

    sbuf[8:] = small_ref[:, :shared]
    sbuf[0:8] = jnp.where(first_block, 0.0, shalo_ref[:, :shared])
    tri = tri_ref[...]
    expand = expand_ref[...]
    step = small_ref[:, shared:] + head_ref[0:1]
    dt = softplus(step)
    rate = dt * head_ref[1:2]
    running = sum(mm(tri, piece) for piece in split3(rate * LOG2E))
    running_t = running.T
    decay_in = jnp.exp2(running)
    decay_out = jnp.exp2(running[length - 1 :] - running)
    dt_wide = spread(dt, expand, heads)
    in_wide = spread(decay_in, expand, heads)
    out_wide = spread(decay_out, expand, heads)

    taps = taps_ref[...]
    bc_in = conv_rows(sbuf[...], taps, length)
    bc_sig = sigmoid(bc_in)
    bc = (bc_in * bc_sig).astype(BF16)
    keys, queries = bc[:, :half], bc[:, half:]
    keep = causal(length, True)
    scores = jnp.where(keep, mm(keys, queries, NT), 0.0)
    pull = pull_ref[...]
    masks = head_masks(GROUP_LANES, width)
    dscores = jnp.zeros((length, length), F32)
    dkeys = jnp.zeros((length, half), F32)
    dqueries = jnp.zeros((length, half), F32)
    drun = jnp.zeros((length, 128), F32)
    ddt = jnp.zeros((length, 128), F32)
    last_row = lax.broadcasted_iota(jnp.int32, (length, 1), 0) == length - 1
    per_group = GROUP_LANES // width
    for start in range(0, channels, GROUP_LANES):
        lanes = slice(start, start + GROUP_LANES)
        gate_at, conv_at = gate_lanes(start, part)
        table = chan_ref[:, lanes]
        xbuf[8:, lanes] = columns_ref[:, conv_at].astype(F32)
        xbuf[0:8, lanes] = jnp.where(first_block, 0.0, halo_ref[:, conv_at].astype(F32)[-8:])
        c = conv_rows(xbuf[:, lanes], table, length)
        c_sig = sigmoid(c)
        xs = c * c_sig
        z = columns_ref[:, gate_at].astype(F32)
        z_sig = sigmoid(z)
        z_silu = z * z_sig
        y = y_ref[:, lanes]
        total = y + table[5:6] * xs
        gated = total * z_silu
        up = up_ref[:, lanes].astype(F32)
        gchan_ref[6:7, lanes] += jnp.sum(up * gated, axis=0, keepdims=True)
        dgated = table[6:7] * up - gated * pull
        dcolumns_ref[:, gate_at] = (dgated * total * (z_sig + z_silu * (1.0 - z_sig))).astype(BF16)
        dy = dgated * z_silu
        gchan_ref[5:6, lanes] += jnp.sum(dy * xs, axis=0, keepdims=True)
        dy_low = dy.astype(BF16)
        dt_lanes = dt_wide[:, lanes]
        values = (xs * dt_lanes).astype(BF16)
        weights, dparts, vparts, decays = [], [], [], []
        for j in range(per_group):
            h = start // width + j
            decay = jnp.exp2(jnp.minimum(running_t[h : h + 1, :] - running[:, h : h + 1], 0.0))
            decays.append(decay)
            weights.append((scores * decay).astype(BF16))
            dparts.append(jnp.where(masks[j], dy_low, jnp.zeros_like(dy_low)))
            vparts.append(jnp.where(masks[j], values, jnp.zeros_like(values)))
        outer = mm(jnp.concatenate(vparts, axis=0), dy_low, NT)
        for j in range(per_group):
            dscores = dscores + outer[j * length : (j + 1) * length] * decays[j]
        dvalues = mm(jnp.concatenate(weights, axis=1), jnp.concatenate(dparts, axis=0))
        before = saved_ref[0, :, lanes]
        dafter = dstate[:, lanes]
        dafter_low = dafter.astype(BF16)
        out_lanes = out_wide[:, lanes]
        carried = mm(keys, dafter_low) * out_lanes
        dvalues = dvalues + carried
        values_f = values.astype(F32)
        dkeys = dkeys + mm((values_f * out_lanes).astype(BF16), dafter_low, NT)
        in_lanes = in_wide[:, lanes]
        dy_in = (dy * in_lanes).astype(BF16)
        dqueries = dqueries + mm(dy_in, before, NT)
        end_decay = in_lanes[length - 1 :]
        at_end = jnp.sum(values_f * carried, axis=0, keepdims=True) + end_decay * jnp.sum(
            before.astype(F32) * dafter, axis=0, keepdims=True
        )
        dstate[:, lanes] = end_decay * dafter + mm(queries, dy_in, TN)
        turn = dy_low.astype(F32) * y - values_f * dvalues + jnp.where(last_row, at_end, 0.0)
        turn_high = turn.astype(BF16)
        turn_low = (turn - turn_high.astype(F32)).astype(BF16)
        group_expand = expand[:, lanes]
        drun = drun + mm(turn_high, group_expand, NT) + mm(turn_low, group_expand, NT)
        ddt = ddt + mm((dvalues * xs).astype(BF16), group_expand, NT)
        dxs = dvalues * dt_lanes + table[5:6] * dy
        dc = dxs * (c_sig + xs * (1.0 - c_sig))
        dxbuf[0:length, lanes] = dc
        window = dxbuf[:, lanes]
        here = xbuf[8:, lanes]
        gchan_ref[4:5, lanes] += jnp.sum(dc, axis=0, keepdims=True)
        gchan_ref[3:4, lanes] += jnp.sum(dc * here, axis=0, keepdims=True)
        dconv = table[3:4] * dc
        for ahead in range(1, 4):
            moved = pltpu.roll(window, length + 8 - ahead, 0)[:length]
            gchan_ref[3 - ahead : 4 - ahead, lanes] += jnp.sum(moved * here, axis=0, keepdims=True)
            dconv = dconv + table[3 - ahead : 4 - ahead] * moved
        dcolumns_ref[:, conv_at] = dconv.astype(BF16)
        dxbuf[length:, lanes] = dxbuf[0:8, lanes]

    dscores_low = jnp.where(keep, dscores, 0.0).astype(BF16)
    dkeys = dkeys + mm(dscores_low, queries)
    dqueries = dqueries + mm(dscores_low, keys, TN)
    dbc = jnp.concatenate([dkeys, dqueries], axis=1) * (bc_sig + bc_in * bc_sig * (1.0 - bc_sig))
    dsbuf[0:length] = dbc
    window = dsbuf[...]
    here = sbuf[8:]
    gtaps_ref[4:5] += jnp.sum(dbc, axis=0, keepdims=True)
    gtaps_ref[3:4] += jnp.sum(dbc * here, axis=0, keepdims=True)
    dshared = taps[3:4] * dbc
    for ahead in range(1, 4):
        moved = pltpu.roll(window, length + 8 - ahead, 0)[:length]
        gtaps_ref[3 - ahead : 4 - ahead] += jnp.sum(moved * here, axis=0, keepdims=True)
        dshared = dshared + taps[3 - ahead : 4 - ahead] * moved
    dsmall_ref[:, :shared] = dshared.astype(dsmall_ref.dtype)
    dsbuf[length:] = dsbuf[0:8]

    high, mid, low = split3(drun)
    drate = mm(tri, high, TN) + mm(tri, mid, TN) + mm(tri, low, TN)
    dstep = (ddt + drate * head_ref[1:2]) * sigmoid(step)
    ghead_ref[0:1] += jnp.sum(dstep, axis=0, keepdims=True)
    ghead_ref[1:2] += jnp.sum(drate * rate, axis=0, keepdims=True)
    lane = lax.broadcasted_iota(jnp.int32, dstep.shape, 1)
    dsmall_ref[:, shared:] = jnp.where(lane < heads, dstep, 0.0).astype(dsmall_ref.dtype)


def scan_tables(heads, channels):
    row = lax.broadcasted_iota(jnp.int32, (128, channels), 0) % heads
    col = lax.broadcasted_iota(jnp.int32, (128, channels), 1) // (channels // heads)
    return (row == col).astype(BF16), jnp.tril(jnp.ones((CHUNK, CHUNK), BF16))


def whole(array):
    return pl.BlockSpec(array.shape, lambda i: (0,) * array.ndim)


def mixer_forward(columns, small, tables, heads):
    tokens, channels = columns.shape[0], columns.shape[1] // 2
    shared = tables[1].shape[1]
    blocks = tokens // CHUNK

    def rows(cols):
        return pl.BlockSpec((CHUNK, cols), lambda i: (i, 0))

    return pl.pallas_call(
        functools.partial(forward_kernel, heads, channels // 2),
        grid=(blocks,),
        in_specs=[rows(2 * channels), rows(small.shape[1])] + [whole(table) for table in tables],
        out_specs=[
            rows(channels),
            rows(1),
            rows(channels),
            pl.BlockSpec((1, shared // 2, channels), lambda i: (i, 0, 0)),
        ],
        out_shape=[
            jax.ShapeDtypeStruct((tokens, channels), BF16),
            jax.ShapeDtypeStruct((tokens, 1), F32),
            jax.ShapeDtypeStruct((tokens, channels), F32),
            jax.ShapeDtypeStruct((blocks, shared // 2, channels), BF16),
        ],
        scratch_shapes=[
            pltpu.VMEM((shared // 2, channels), F32),
            pltpu.VMEM((CHUNK + 8, channels), F32),
            pltpu.VMEM((CHUNK + 8, shared), F32),
        ],
        compiler_params=pltpu.CompilerParams(vmem_limit_bytes=48 * 1024 * 1024),
        cost_estimate=pl.CostEstimate(
            flops=tokens * channels * 6000, bytes_accessed=tokens * channels * 14, transcendentals=tokens * channels * 6
        ),
        name="mixer_forward",
    )(columns, small, *tables)


def mixer_backward(columns, small, y, saved, up, pull, tables, heads):
    tokens, channels = columns.shape[0], columns.shape[1] // 2
    shared = tables[1].shape[1]
    blocks = tokens // CHUNK

    def rows(cols):
        return pl.BlockSpec((CHUNK, cols), lambda i: (blocks - 1 - i, 0))

    def earlier(count, cols):
        per_block = CHUNK // count
        return pl.BlockSpec((count, cols), lambda i: (jnp.maximum((blocks - 1 - i) * per_block - 1, 0), 0))

    def fixed(r, c):
        return pl.BlockSpec((r, c), lambda i: (0, 0))

    return pl.pallas_call(
        functools.partial(backward_kernel, heads, channels // 2),
        grid=(blocks,),
        in_specs=[
            rows(2 * channels),
            earlier(8 if columns.dtype == F32 else 16, 2 * channels),
            rows(small.shape[1]),
            earlier(8, small.shape[1]),
            rows(channels),
            pl.BlockSpec((1, shared // 2, channels), lambda i: (blocks - 1 - i, 0, 0)),
            rows(channels),
            rows(1),
        ]
        + [whole(table) for table in tables],
        out_specs=[rows(2 * channels), rows(small.shape[1]), fixed(8, channels), fixed(8, shared), fixed(8, 128)],
        out_shape=[
            jax.ShapeDtypeStruct((tokens, 2 * channels), BF16),
            jax.ShapeDtypeStruct((tokens, small.shape[1]), BF16),
            jax.ShapeDtypeStruct((8, channels), F32),
            jax.ShapeDtypeStruct((8, shared), F32),
            jax.ShapeDtypeStruct((8, 128), F32),
        ],
        scratch_shapes=[
            pltpu.VMEM((shared // 2, channels), F32),
            pltpu.VMEM((CHUNK + 8, channels), F32),
            pltpu.VMEM((CHUNK + 8, shared), F32),
            pltpu.VMEM((CHUNK + 8, channels), F32),
            pltpu.VMEM((CHUNK + 8, shared), F32),
        ],
        compiler_params=pltpu.CompilerParams(vmem_limit_bytes=56 * 1024 * 1024),
        cost_estimate=pl.CostEstimate(
            flops=tokens * channels * 14000, bytes_accessed=tokens * channels * 20, transcendentals=tokens * channels * 6
        ),
        name="mixer_backward",
    )(columns, columns, small, small, y, saved, up, pull, *tables)


class Place:
    def __init__(self):
        self.members = lax.axis_size("tensor")
        self.groups = self.members // 2
        self.at = lax.axis_index("tensor")
        self.sequence = self.at % 2
        self.group = self.at // 2
        self.core = lax.axis_index("dp") % 2

    def to_pair(self, v):
        return lax.ppermute(v, "tensor", [(t, t ^ 1) for t in range(self.members)])

    def to_core(self, v):
        return lax.ppermute(v, "dp", [(t, t ^ 1) for t in range(lax.axis_size("dp"))])

    def to_group(self, v, hop):
        return lax.ppermute(
            v, "tensor", [(t, (t + 2 * hop) % self.members) for t in range(self.members)]
        )

    def rows_of(self, v, hop):
        count = v.shape[0] // self.groups
        return lax.dynamic_slice_in_dim(v, (self.group + hop) % self.groups * count, count, 0)

    def gather_rows(self, v):
        count = v.shape[0]
        total = jnp.zeros((count * self.groups,) + v.shape[1:], v.dtype)
        total = lax.dynamic_update_slice_in_dim(total, v, self.group * count, 0)
        for hop in range(1, self.groups):
            start = (self.group - hop) % self.groups * count
            total = lax.dynamic_update_slice_in_dim(total, self.to_group(v, hop), start, 0)
        return total

    def add_groups(self, v):
        return v + sum(self.to_group(v, hop) for hop in range(1, self.groups))

    def scatter_rows(self, product):
        arrived = [
            self.to_group(product(hop).astype(BF16), hop) for hop in range(1, self.groups)
        ]
        return product(0) + sum(piece.astype(F32) for piece in arrived)

    def in_order(self, mine, other, first):
        return jnp.where(first == 0, jnp.concatenate([mine, other]), jnp.concatenate([other, mine]))

    def take_sequence(self, v):
        mine = jnp.where(self.sequence == 0, v[0], v[1])
        other = self.to_pair(jnp.where(self.sequence == 0, v[1], v[0]))
        return self.in_order(mine, other, self.sequence)

    def give_sequence(self, v):
        count = v.shape[0] // 2
        mine = lax.dynamic_slice_in_dim(v, self.sequence * count, count, 0)
        other = self.to_pair(lax.dynamic_slice_in_dim(v, (1 - self.sequence) * count, count, 0))
        return jnp.where(
            self.sequence == 0, jnp.stack([mine, other]), jnp.stack([other, mine])
        )

    def other_shard(self, v):
        fetched = self.to_pair(lax.dynamic_index_in_dim(v, self.core, 0, keepdims=False))
        swapped = self.to_core(fetched)
        first = jnp.where(self.core == 0, fetched, swapped)
        return first, jnp.where(self.core == 0, swapped, fetched)

    def fold_other(self, own, other):
        arrived = self.to_core(lax.dynamic_index_in_dim(other, 1 - self.core, 0, keepdims=False))
        kept = lax.dynamic_index_in_dim(other, self.core, 0, keepdims=False)
        summed = (kept.astype(F32) + arrived.astype(F32)).astype(BF16)
        landed = self.to_pair(summed)
        lane = lax.broadcasted_iota(jnp.int32, own.shape, 0)
        return own + jnp.where(lane == self.core, landed[None], jnp.zeros_like(own))


def norm_scale(stream):
    return lax.rsqrt(jnp.mean(stream * stream, axis=-1, keepdims=True) + EPSILON)


def block_forward(place, stream, weights, tables, heads, inner):
    big, small_cols, out_cols, gain = weights
    row_scale = norm_scale(stream)
    normed = place.gather_rows((stream * row_scale * gain).astype(BF16))
    columns = mm(normed, big).astype(BF16)
    small = mm(normed, small_cols)
    mixed, square, y, saved = mixer_forward(columns, small, tables, heads)
    scale = lax.rsqrt(place.add_groups(square) / inner + EPSILON)
    update = place.scatter_rows(lambda hop: mm(place.rows_of(mixed, hop), out_cols))
    after = stream + update * place.rows_of(scale, 0)
    return after, (stream, normed, columns, small, mixed, y, saved, scale, update)


def block_backward(place, grad, last_up, weights, tables, heads, inner, kept):
    big, small_cols, out_cols, gain = weights
    stream, normed, columns, small, mixed, y, saved, scale, update = kept
    if last_up is None:
        own_scale = place.rows_of(scale, 0)
        own_up = (grad * own_scale).astype(BF16)
        own_pull = jnp.sum(own_up.astype(F32) * update, axis=-1, keepdims=True) * (own_scale * own_scale / inner)
        up = place.gather_rows(own_up)
        pull = place.gather_rows(own_pull)
        grad_mixed = mm(up, out_cols, NT)
    else:
        up = (last_up.astype(F32) * scale).astype(BF16)
        grad_mixed = mm(up, out_cols, NT)
        product = jnp.sum(grad_mixed * mixed.astype(F32), axis=-1, keepdims=True)
        pull = place.add_groups(product) * (scale * scale / inner)
    grad_out = mm(mixed, up, TN).astype(BF16)
    dcolumns, dsmall, gchan, gtaps, ghead = mixer_backward(
        columns, small, y, saved, grad_mixed, pull, tables, heads
    )
    grad_normed = place.scatter_rows(
        lambda hop: mm(place.rows_of(dcolumns, hop), big, NT) + mm(place.rows_of(dsmall, hop), small_cols, NT)
    )
    own_cols = dcolumns.shape[1] // 4

    def grad_part(at):
        return mm(normed, dcolumns[:, at * own_cols : (at + 1) * own_cols], TN).astype(BF16)

    grad_other = jnp.stack([grad_part(2), grad_part(3)])
    grad_own = jnp.stack([grad_part(0), grad_part(1)])
    grad_small = mm(normed, dsmall, TN)
    row_scale = norm_scale(stream)
    unit = stream * row_scale
    grad_gain = jnp.sum(grad_normed * unit, axis=0)
    lifted = grad_normed * gain
    grad = grad + row_scale * (lifted - unit * jnp.mean(lifted * unit, axis=-1, keepdims=True))
    return grad, (grad_own, grad_other, grad_small, grad_out, grad_gain, gchan, gtaps, ghead)


def local(
    hidden,
    cotangent,
    norm_gain,
    in_weights,
    state_weight,
    step_weight,
    channel_taps,
    state_taps,
    step_bias,
    decay_log,
    skip_gain,
    inner_gain,
    out_weight,
):
    place = Place()
    layers = in_weights.shape[0]
    own_heads = step_bias.shape[1]
    heads = 2 * own_heads
    own_cols = in_weights.shape[3]
    channels = 2 * own_cols
    width = own_cols // own_heads
    inner = own_cols * place.members
    shared = state_weight.shape[2]
    copies = 128 // heads
    expand, tri = scan_tables(heads, channels)

    stream = place.take_sequence(hidden).astype(F32)
    last_up = place.gather_rows(place.take_sequence(cotangent))

    per_channel = jnp.concatenate([channel_taps, inner_gain[:, None]], axis=1)
    per_head = jnp.stack([step_bias, decay_log, skip_gain], axis=1)
    packed = jnp.concatenate([per_channel.reshape(layers, -1), per_head.reshape(layers, -1)], axis=1)
    arrived = place.to_pair(packed)
    split_at = per_channel[0].size
    per_channel = jnp.concatenate([per_channel, arrived[:, :split_at].reshape(per_channel.shape)], axis=2)
    per_head = jnp.concatenate([per_head, arrived[:, split_at:].reshape(per_head.shape)], axis=2)

    thin = jnp.concatenate([state_weight, step_weight, norm_gain[:, :, None]], axis=2)
    thin = lax.all_gather(thin, "dp", axis=1, tiled=True)
    state_cols = thin[:, :, :shared]
    step_cols = thin[:, :, shared : shared + own_heads]
    step_cols = jnp.concatenate([step_cols, place.to_pair(step_cols)], axis=2)
    gains = thin[:, :, -1].astype(F32)

    weights, tables = [], []
    for layer in range(layers):
        pair = lax.all_gather(in_weights[layer], "dp", axis=1, tiled=True)
        other = place.other_shard(pair)
        big = jnp.concatenate([pair[0], pair[1], other[0], other[1]], axis=1)
        out_own = lax.all_gather(out_weight[layer], "dp", axis=1, tiled=True)
        halves = out_own.reshape(2, out_own.shape[0] // 2, out_own.shape[1])
        out_cols = jnp.concatenate([out_own, *place.other_shard(halves)], axis=0)
        small_cols = jnp.concatenate([state_cols[layer]] + [step_cols[layer]] * copies, axis=1)
        weights.append((big, small_cols, out_cols, gains[layer]))
        wide_skip = jnp.repeat(per_head[layer, 2], width)[None]
        blank = jnp.zeros((1, channels), F32)
        chan = jnp.concatenate([per_channel[layer, :5], wide_skip, per_channel[layer, 5:6], blank], axis=0)
        taps = jnp.concatenate([state_taps[layer], jnp.zeros((3, shared), F32)], axis=0)
        head = jnp.stack([per_head[layer, 0], -jnp.exp(per_head[layer, 1])])
        head = jnp.concatenate([jnp.tile(head, (1, copies)), jnp.zeros((6, 128), F32)], axis=0)
        tables.append((chan, taps, head, expand, tri))

    kept = []
    for layer in range(layers):
        stream, saved = block_forward(place, stream, weights[layer], tables[layer], heads, inner)
        kept.append(saved)
    mixed_out = place.give_sequence(stream)

    grad = lax.dynamic_slice_in_dim(last_up, place.group * stream.shape[0], stream.shape[0], 0).astype(F32)
    grads = [None] * layers
    for layer in reversed(range(layers)):
        grad, grads[layer] = block_backward(
            place,
            grad,
            last_up if layer == layers - 1 else None,
            weights[layer],
            tables[layer],
            heads,
            inner,
            kept[layer],
        )
    grad_hidden = place.give_sequence(grad.astype(BF16)).astype(F32)

    big_grads, out_grads, thin_grads, channel_grads, taps_grads = [], [], [], [], []
    for layer in range(layers):
        grad_own, grad_other, grad_small, grad_out, grad_gain, gchan, gtaps, ghead = grads[layer]
        folded = place.fold_other(grad_own, grad_other)
        big_grads.append(lax.psum_scatter(folded, "dp", scatter_dimension=1, tiled=True).astype(F32))
        quarters = grad_out.reshape(2, 2, own_cols // 2, grad_out.shape[1])
        folded = place.fold_other(quarters[0], quarters[1]).reshape(own_cols, -1)
        out_grads.append(lax.psum_scatter(folded, "dp", scatter_dimension=1, tiled=True).astype(F32))
        step_own = grad_small[:, shared : shared + own_heads]
        step_own = step_own + place.to_pair(grad_small[:, shared + own_heads : shared + heads])
        thin_grads.append(jnp.concatenate([grad_small[:, :shared], step_own, grad_gain[:, None]], axis=1).astype(BF16))
        skips = gchan[5].reshape(heads, width).sum(axis=1)
        per_channel_grad = jnp.concatenate([gchan[:5], gchan[6:7]], axis=0)
        per_head_grad = jnp.stack([ghead[0, :heads], ghead[1, :heads], skips])

        def half_of(at):
            return jnp.concatenate(
                [
                    per_channel_grad[:, at * own_cols : (at + 1) * own_cols].reshape(-1),
                    per_head_grad[:, at * own_heads : (at + 1) * own_heads].reshape(-1),
                ]
            )

        channel_grads.append(half_of(0) + place.to_pair(half_of(1)))
        taps_grads.append(gtaps[:5])

    thin_total = lax.psum_scatter(jnp.stack(thin_grads), "dp", scatter_dimension=1, tiled=True)
    step_total = thin_total[:, :, shared : shared + own_heads].astype(F32)
    joint = jnp.concatenate([thin_total[:, :, :shared], thin_total[:, :, -1:]], axis=2)
    joint = lax.psum(joint, "tensor").astype(F32)
    channel_total = lax.psum(jnp.stack(channel_grads), "dp")
    taps_total = lax.psum(jnp.stack(taps_grads), ("dp", "tensor"))
    channel_part = channel_total[:, :split_at].reshape(layers, 6, own_cols)
    head_part = channel_total[:, split_at:].reshape(layers, 3, own_heads)
    return (
        mixed_out,
        grad_hidden,
        joint[:, :, shared],
        jnp.stack(big_grads),
        joint[:, :, :shared],
        step_total,
        channel_part[:, :5],
        taps_total,
        head_part[:, 0],
        head_part[:, 1],
        head_part[:, 2],
        channel_part[:, 5],
        jnp.stack(out_grads),
    )


def solution(mesh):
    placed = (
        P("dp", "tensor", None),
        P("dp", "tensor", None),
        P(None, "dp"),
        P(None, None, "dp", "tensor"),
        P(None, "dp", None),
        P(None, "dp", "tensor"),
        P(None, None, "tensor"),
        P(),
        P(None, "tensor"),
        P(None, "tensor"),
        P(None, "tensor"),
        P(None, "tensor"),
        P(None, "tensor", "dp"),
    )
    return jax.shard_map(
        local,
        mesh=mesh,
        in_specs=placed,
        out_specs=(
            P("dp", "tensor", None),
            P("dp", "tensor", None),
            P(None, "dp"),
            P(None, None, "dp", "tensor"),
            P(None, "dp", None),
            P(None, "dp", "tensor"),
            P(None, None, "tensor"),
            P(),
            P(None, "tensor"),
            P(None, "tensor"),
            P(None, "tensor"),
            P(None, "tensor"),
            P(None, "tensor", "dp"),
        ),
        check_vma=False,
    )
```

time: 4410 us -> 1520 us (0.34)
  local copies, waits for them, and re-layouts: 1640 us -> 74.8 us
  matrix products: 1100 us -> 276 us
  other arithmetic: 475 us -> 121 us
  waiting for transfers between devices: 989 us -> 765 us
  Pallas kernels: 0 us -> 151 us
  blocking collectives: 130 us -> 66.4 us
    dynamic_update_slice x128 -> x6, local copies, waits for them, and re-layouts: 1200 us -> 7.33 us  [the longest x5 7.06 us: gather_rows(): lax.dynamic_update_slice_in_dim(total, self.to_group(v, hop), start, 0)]
    dot_general x280 -> x30, matrix products: 1020 us -> 276 us  [mm(): return lax.dot_general(a, b, dims, preferred_element_type=F32)]
    ppermute x0 -> x38, waiting for transfers between devices: none -> 596 us  [the longest x18 368 us: to_pair(): return lax.ppermute(v, 'tensor', [(t, t ^ 1) for t in range(self.members)])]
    reduce_scatter x12 -> x5, waiting for transfers between devices: 589 us -> 24.2 us  [the longest x1 24.2 us: local(): lax.psum_scatter(jnp.stack(thin_grads), 'dp', scatter_dimension=1, tiled=...]
    all_gather x14 -> x5, waiting for transfers between devices: 372 us -> 143 us  [the longest x2 80.4 us: local(): pair = lax.all_gather(in_weights[layer], 'dp', axis=1, tiled=True)]
    another operation x219 -> x10, other arithmetic: 168 us -> 8.17 us  [the longest x1 3.83 us: local(): jnp.stack(big_grads)]
    pallas_call x0 -> x4, Pallas kernels: none -> 151 us  [the longest x2 105 us: mixer_backward(): pl.pallas_call(functools.partial(backward_kernel, heads, channels // 2),...]
    reduce_sum x54 -> x6, other arithmetic: 145 us -> 14.1 us  [the longest x2 7.74 us: block_backward(): grad_gain = jnp.sum(grad_normed * unit, axis=0)]
  transfers between devices with their start and end apart: 28 -> 49, of which waited for: 19 -> 24; matrix products, arithmetic and copies ran while one was open for 44% -> 28% of each run, Pallas kernels for 0% -> 10%
where the time goes in v1:
time: 1520 us; the launch traced here: 1510 us
  waiting for transfers between devices  765 us (50%)
  matrix products  276 us (18%)
  Pallas kernels  151 us (10%)
  other arithmetic  121 us (8%)
  local copies, waits for them, and re-layouts  74.8 us (5%)
  blocking collectives  66.4 us (4%)
  starting transfers between devices  40.4 us (3%)
  between operations  16.1 us (1%)
    ppermute x18, waiting for transfers between devices, to_pair(): return lax.ppermute(v, 'tensor', [(t, t ^ 1) for t in range(self.members)])  368 us
    dot_general x30, matrix products, mm(): return lax.dot_general(a, b, dims, preferred_element_type=F32)  276 us
    ppermute x12, waiting for transfers between devices, to_group(): lax.ppermute(v, 'tensor', [(t, (t + 2 * hop) % self.members) for t in ran...  228 us
    pallas_call x2, Pallas kernels, mixer_backward(): pl.pallas_call(functools.partial(backward_kernel, heads, channels // 2),...  105 us
    all_gather x2, waiting for transfers between devices, local(): pair = lax.all_gather(in_weights[layer], 'dp', axis=1, tiled=True)  80.4 us
    pallas_call x2, Pallas kernels, mixer_forward(): pl.pallas_call(functools.partial(forward_kernel, heads, channels // 2), g...  45.9 us
    psum x1, blocking collectives, local(): taps_total = lax.psum(jnp.stack(taps_grads), ('dp', 'tensor'))  40 us
    all_gather x2, waiting for transfers between devices, local(): out_own = lax.all_gather(out_weight[layer], 'dp', axis=1, tiled=True)  35.2 us
  transfers between devices with their start and end apart: 49, of which 24 were waited for; matrix products, arithmetic and copies ran while one was open for 28% of the time, Pallas kernels for 10%

profile of v1, /device:TPU:0, one launch (start us, length us, event | category | flops | bytes accessed | tf_op | source)
XLA Modules:
  0.0 1509.9 jit_solution(11659726709686701619)
XLA Ops:
  19.4 75.9 %all-gather.12.cloned.1.call-done = bf16[1,2,2048,1024]{3,2,1,0:T(8,128)(2,1)} async-done(((bf16[1,2,256,1024]{3,2,1,0:T(8,128)(2,1)}), bf16[1,2,2048,1024]{3,2,1,0:T(8,128)(2,1)}) %all-gather.12.cloned.1.call-update) | async-done | bytes 8388624 | tf_op jit(solution)/shard_map/all_gather | solution.py:560
  108.1 35.2 %all-gather.14.cloned.1.call-done = bf16[1,1024,2048]{2,1,0:T(8,128)(2,1)} async-done(((bf16[1,1024,256]{2,1,0:T(8,128)(2,1)}), bf16[1,1024,2048]{2,1,0:T(8,128)(2,1)}) %all-gather.14.cloned.1.call-update) | async-done | bytes 4194320 | tf_op jit(solution)/shard_map/all_gather | solution.py:563
  147.9 27.5 %all-gather.10.cloned.1.call-done = bf16[2,2048,273]{1,2,0:T(8,128)(2,1)} async-done(((bf16[2,256,273]{1,2,0:T(8,128)(2,1)}), bf16[2,2048,273]{1,2,0:T(8,128)(2,1)}) %all-gather.10.cloned.1.call-update) | async-done | bytes 2236432 | tf_op jit(solution)/shard_map/all_gather | solution.py:552
  179.2 19.3 %collective-permute-done.2 = bf16[2048,1024]{1,0:T(8,128)(2,1)} collective-permute-done((bf16[2048,1024]{1,0:T(8,128)(2,1)}, bf16[2048,1024]{1,0:T(8,128)(2,1)}, u32[]{:S(2)}, u32[]{:S(2)}) %collective-permute-start.2) | collective-permute-done | bytes 4194336 | tf_op jit(solution)/shard_map/ppermute | solution.py:395
  200.1 43.3 %collective-permute-done.6 = bf16[512,2048]{1,0:T(8,128)(2,1)} collective-permute-done((bf16[512,2048]{1,0:T(8,128)(2,1)}, bf16[512,2048]{1,0:T(8,128)(2,1)}, u32[]{:S(2)}, u32[]{:S(2)}) %collective-permute-start.6) | collective-permute-done | bytes 2097184 | tf_op jit(solution)/shard_map/ppermute | solution.py:395
  274.7 23.8 %convolution_convert_fusion.3.columns_ref.halo_ref = bf16[1024,4096]{1,0:T(8,128)(2,1)} fusion(bf16[1024,2048]{1,0:T(8,128)(2,1)} %copy-done.41, bf16[2048,1024]{1,0:T(8,128)(2,1)} %get-tuple-element.134, bf16[2048,1024]{1,0:T(8,128)(2,1)} %get-tuple-element.133, bf16[2048,1024]{1,0:T(8,128)(2,1)} %get-tuple-element.131, ...), kind=kOutput, calls=%fused_computation.23 | convolution fusion | flops 17251172352 | bytes 29360128 | tf_op jit(solution)/shard_map/dot_general | solution.py:22
  298.6 22.9 %mixer_forward.2 = (bf16[1024,2048]{1,0:T(8,128)(2,1)}, f32[1024,1]{1,0:T(8,128)S(1)}, f32[1024,2048]{1,0:T(8,128)}, bf16[8,128,2048]{2,1,0:T(8,128)(2,1)}) custom-call(bf16[1024,4096]{1,0:T(8,128)(2,1)} %convolution_convert_fusion.3.columns_ref.halo_ref, f32[1024,384]{1,0:T(8,128)S(1)} %fusion.110.small_ref.shalo_ref, ...), custom_call_target="tpu_custom_call" | custom-call | flops 12582912000 | bytes 29360128 | tf_op jit(solution)/shard_map/mixer_forward/pallas_call | solution.py:304
  332.5 50.3 %collective-permute-done.18 = bf16[256,2048]{1,0:T(8,128)(2,1)S(1)} collective-permute-done((bf16[256,2048]{1,0:T(8,128)(2,1)S(1)}, bf16[256,2048]{1,0:T(8,128)(2,1)S(1)}, u32[]{:S(2)}, u32[]{:S(2)}) %collective-permute-start.18) | collective-permute-done | bytes 1048608 | tf_op jit(solution)/shard_map/ppermute | solution.py:395
  396.2 50.1 %collective-permute-done.9 = f32[1024,1]{1,0:T(8,128)} collective-permute-done((f32[1024,1]{1,0:T(8,128)S(1)}, f32[1024,1]{1,0:T(8,128)}, u32[]{:S(2)}, u32[]{:S(2)}) %collective-permute-start.9) | collective-permute-done | bytes 4128 | tf_op jit(solution)/shard_map/ppermute | solution.py:401
  474.6 34.0 %collective-permute-done.10 = bf16[512,2048]{1,0:T(8,128)(2,1)S(1)} collective-permute-done((bf16[512,2048]{1,0:T(8,128)(2,1)}, bf16[512,2048]{1,0:T(8,128)(2,1)S(1)}, u32[]{:S(2)}, u32[]{:S(2)}) %collective-permute-start.10) | collective-permute-done | bytes 2097184 | tf_op jit(solution)/shard_map/ppermute | solution.py:401
  510.1 24.1 %convolution_convert_fusion.2.columns_ref.halo_ref = bf16[1024,4096]{1,0:T(8,128)(2,1)} fusion(bf16[1024,2048]{1,0:T(8,128)(2,1)} %constant_dynamic-update-slice_fusion.14, bf16[2048,1024]{1,0:T(8,128)(2,1)} %get-tuple-element.129, bf16[2048,1024]{1,0:T(8,128)(2,1)} %get-tuple-element.128, bf16[2048,1024]{1,0:T(8,128)(2,1)} %get-tuple-element.126, ...), kind=kOutput, calls=%fused_computation.22 | convolution fusion | flops 17251172352 | bytes 29360128 | tf_op jit(solution)/shard_map/dot_general | solution.py:22
  539.3 23.0 %mixer_forward.3 = (bf16[1024,2048]{1,0:T(8,128)(2,1)}, f32[1024,1]{1,0:T(8,128)S(1)}, f32[1024,2048]{1,0:T(8,128)}, bf16[8,128,2048]{2,1,0:T(8,128)(2,1)}) custom-call(bf16[1024,4096]{1,0:T(8,128)(2,1)} %convolution_convert_fusion.2.columns_ref.halo_ref, f32[1024,384]{1,0:T(8,128)S(1)} %fusion.111.small_ref.shalo_ref, ...), custom_call_target="tpu_custom_call" | custom-call | flops 12582912000 | bytes 29360128 | tf_op jit(solution)/shard_map/mixer_forward/pallas_call | solution.py:304
  586.3 14.8 multiply_reduce_fusion
  612.7 52.7 %mixer_backward.2 = (bf16[1024,4096]{1,0:T(8,128)(2,1)}, bf16[1024,384]{1,0:T(8,128)(2,1)}, f32[8,2048]{1,0:T(8,128)}, f32[8,256]{1,0:T(8,128)}, f32[8,128]{1,0:T(8,128)}) custom-call(bf16[1024,4096]{1,0:T(8,128)(2,1)} %convolution_convert_fusion.2.columns_ref.halo_ref, bf16[1024,4096]{1,0:T(8,128)(2,1)} %convolution_convert_fusion.2.columns_ref.halo_ref, ...), custom_call_target="tpu_custom_call" | custom-call | flops 29360128000 | bytes 41943040 | tf_op jit(solution)/shard_map/mixer_backward/pallas_call | solution.py:348
  673.1 13.9 add_convert_fusion.1
  688.6 14.1 fusion.30
  702.7 29.8 %collective-permute-done.21 = bf16[512,2048]{1,0:T(8,128)(2,1)S(1)} collective-permute-done((bf16[512,2048]{1,0:T(8,128)(2,1)}, bf16[512,2048]{1,0:T(8,128)(2,1)S(1)}, u32[]{:S(2)}, u32[]{:S(2)}) %collective-permute-start.21) | collective-permute-done | bytes 2097184 | tf_op jit(solution)/shard_map/ppermute | solution.py:401
  755.0 36.5 %collective-permute-done.23 = f32[512,1]{1,0:T(8,128)S(1)} collective-permute-done((f32[512,1]{1,0:T(8,128)S(1)}, f32[512,1]{1,0:T(8,128)S(1)}, u32[]{:S(2)}, u32[]{:S(2)}) %collective-permute-start.23) | collective-permute-done | bytes 2080 | tf_op jit(solution)/shard_map/ppermute | solution.py:401
  793.6 15.9 %fusion.96.up_ref = f32[1024,2048]{1,0:T(8,128)} fusion(bf16[1024,2048]{1,0:T(8,128)(2,1)S(1)} %constant_dynamic-update-slice_fusion.10, bf16[512,2048]{1,0:T(8,128)(2,1)S(1)} %copy-done.57, bf16[512,2048]{1,0:T(8,128)(2,1)S(1)} %copy-done.55, bf16[1024,2048]{1,0:T(8,128)(2,1)} %bitcast.202), kind=kOutput, calls=%fused_computation.270 | convolution fusion | flops 8615100416 | bytes 20971520 | tf_op jit(solution)/shard_map/dot_general | solution.py:22
  809.5 52.6 %mixer_backward.3 = (bf16[1024,4096]{1,0:T(8,128)(2,1)}, bf16[1024,384]{1,0:T(8,128)(2,1)}, f32[8,2048]{1,0:T(8,128)}, f32[8,256]{1,0:T(8,128)}, f32[8,128]{1,0:T(8,128)}) custom-call(bf16[1024,4096]{1,0:T(8,128)(2,1)} %convolution_convert_fusion.3.columns_ref.halo_ref, bf16[1024,4096]{1,0:T(8,128)(2,1)} %convolution_convert_fusion.3.columns_ref.halo_ref, ...), custom_call_target="tpu_custom_call" | custom-call | flops 29360128000 | bytes 41943040 | tf_op jit(solution)/shard_map/mixer_backward/pallas_call | solution.py:348
  866.5 13.8 fusion.26
  880.3 12.7 add_convert_fusion
  913.1 23.4 %collective-permute-done.24 = bf16[512,2048]{1,0:T(8,128)(2,1)S(1)} collective-permute-done((bf16[512,2048]{1,0:T(8,128)(2,1)S(1)}, bf16[512,2048]{1,0:T(8,128)(2,1)S(1)}, u32[]{:S(2)}, u32[]{:S(2)}) %collective-permute-start.24) | collective-permute-done | bytes 2097184 | tf_op jit(solution)/shard_map/ppermute | solution.py:401
  952.2 24.2 %reduce-scatter.6.cloned.1.call-done = bf16[2,256,273]{1,2,0:T(8,128)(2,1)} async-done(((bf16[2,2048,273]{1,2,0:T(8,128)(2,1)}), bf16[2,256,273]{1,2,0:T(8,128)(2,1)}) %reduce-scatter.6.cloned.1.call-update) | async-done | bytes 279568 | tf_op jit(solution)/shard_map/reduce_scatter | solution.py:623
  978.9 20.2 %collective-permute-done.37 = bf16[512,2048]{1,0:T(8,128)(2,1)} collective-permute-done((bf16[512,2048]{1,0:T(8,128)(2,1)S(1)}, bf16[512,2048]{1,0:T(8,128)(2,1)}, u32[]{:S(2)}, u32[]{:S(2)}) %collective-permute-start.37) | collective-permute-done | bytes 2097184 | tf_op jit(solution)/shard_map/ppermute | solution.py:395
  999.1 45.2 %collective-permute-done.35 = bf16[512,2048]{1,0:T(8,128)(2,1)} collective-permute-done((bf16[512,2048]{1,0:T(8,128)(2,1)}, bf16[512,2048]{1,0:T(8,128)(2,1)}, u32[]{:S(2)}, u32[]{:S(2)}) %collective-permute-start.35) | collective-permute-done | bytes 2097184 | tf_op jit(solution)/shard_map/ppermute | solution.py:395
  1132.4 54.1 %collective-permute-done.31 = bf16[2048,1024]{1,0:T(8,128)(2,1)S(1)} collective-permute-done((bf16[2048,1024]{1,0:T(8,128)(2,1)S(1)}, bf16[2048,1024]{1,0:T(8,128)(2,1)S(1)}, u32[]{:S(2)}, u32[]{:S(2)}) %collective-permute-start.31) | collective-permute-done | bytes 4194336 | tf_op jit(solution)/shard_map/ppermute | solution.py:395
  1186.5 89.5 %collective-permute-done.29 = bf16[2048,1024]{1,0:T(8,128)(2,1)S(1)} collective-permute-done((bf16[2048,1024]{1,0:T(8,128)(2,1)S(1)}, bf16[2048,1024]{1,0:T(8,128)(2,1)S(1)}, u32[]{:S(2)}, u32[]{:S(2)}) %collective-permute-start.29) | collective-permute-done | bytes 4194336 | tf_op jit(solution)/shard_map/ppermute | solution.py:395
  1296.8 46.9 %collective-permute-done.15 = bf16[512,2048]{1,0:T(8,128)(2,1)} collective-permute-done((bf16[512,2048]{1,0:T(8,128)(2,1)}, bf16[512,2048]{1,0:T(8,128)(2,1)}, u32[]{:S(2)}, u32[]{:S(2)}) %collective-permute-start.15) | collective-permute-done | bytes 2097184 | tf_op jit(solution)/shard_map/ppermute | solution.py:401
  1356.9 43.1 %collective-permute-done.33 = f32[6192]{0:T(1024)S(1)} collective-permute-done((f32[6192]{0:T(1024)S(1)}, f32[6192]{0:T(1024)S(1)}, u32[]{:S(2)}, u32[]{:S(2)}) %collective-permute-start.33) | collective-permute-done | bytes 24800 | tf_op jit(solution)/shard_map/ppermute | solution.py:395
  1410.1 40.0 %psum.23 = f32[2,5,256]{2,1,0:T(8,128)S(1)} all-reduce(f32[2,5,256]{2,1,0:T(8,128)S(1)} %pad_maximum_fusion.14), channel_id=1, replica_groups=mesh['dp'=8,'tensor'=4] {'dp','tensor'}, use_global_device_ids=true, to_apply=%region_15.16 | all-reduce | flops 2560 | bytes 20480 | tf_op jit(solution)/shard_map/psum | solution.py:628
  1461.3 26.4 %psum.22 = f32[2,6192]{1,0:T(2,128)S(1)} all-reduce(f32[2,6192]{1,0:T(2,128)S(1)} %pad_maximum_fusion.9), channel_id=1, replica_groups=mesh['dp'=8,'tensor'=4] {'dp'}, use_global_device_ids=true, to_apply=%region_14.15 | all-reduce | flops 12384 | bytes 99072 | tf_op jit(solution)/shard_map/psum | solution.py:627
  (482 shorter events, 394.6 us)
Async XLA Ops:
  7.2 88.1 %all-gather.12.cloned.1.call-start = ((), (), s32[]{:S(2)}) async-start(), calls=%async_computation.12 | async-start | bytes 9437184 | tf_op jit(solution)/shard_map/all_gather | solution.py:560
  10.5 132.8 %all-gather.14.cloned.1.call-start = ((), (), s32[]{:S(2)}) async-start(), calls=%async_computation.13 | async-start | bytes 4718592 | tf_op jit(solution)/shard_map/all_gather | solution.py:563
  11.6 163.8 %all-gather.10.cloned.1.call-start = ((), (), s32[]{:S(2)}) async-start(), calls=%async_computation.5 | async-start | bytes 2580480 | tf_op jit(solution)/shard_map/all_gather | solution.py:552
  12.6 245.3 %all-gather.16.cloned.1.call-start = ((), (), s32[]{:S(2)}) async-start(), calls=%async_computation.14 | async-start | bytes 9437184 | tf_op jit(solution)/shard_map/all_gather | solution.py:560
  13.2 378.2 %all-gather.18.cloned.1.call-start = ((), (), s32[]{:S(2)}) async-start(), calls=%async_computation.15 | async-start | bytes 4718592 | tf_op jit(solution)/shard_map/all_gather | solution.py:563
  15.9 91.3 %collective-permute-start = (bf16[256,2048]{1,0:T(8,128)(2,1)}, bf16[256,2048]{1,0:T(8,128)(2,1)S(1)}, u32[]{:S(2)}, u32[]{:S(2)}) collective-permute-start(bf16[256,2048]{1,0:T(8,128)(2,1)} %get-tuple-element.149), channel_id=1, source_target_pairs={{0,1},{1,0},{2,3},{3,2},{4,5},{5,4},{6,7},{7,6},{8,9},{9,8},{10,11... | collective-permute-start | bytes 3145736 | tf_op jit(solution)/shard_map/ppermute | solution.py:395
  19.1 87.4 %collective-permute-start.5 = (f32[2,6192]{1,0:T(2,128)S(1)}, f32[2,6192]{1,0:T(2,128)S(1)}, u32[]{:S(2)}, u32[]{:S(2)}) collective-permute-start(f32[2,6192]{1,0:T(2,128)S(1)} %pad_maximum_fusion.8), channel_id=1, source_target_pairs={{0,1},{1,0},{2,3},{3,2},{4,5},{5,4},{6,7},{7,6},{8,9},{9,8},{10,11... | collective-permute-start | bytes 148616 | tf_op jit(solution)/shard_map/ppermute | solution.py:395
  19.3 957.1 %reduce-scatter.6.cloned.1.call-start = ((), (), s32[]{:S(2)}) async-start(), calls=%async_computation.6 | async-start | bytes 2580480 | tf_op jit(solution)/shard_map/reduce_scatter | solution.py:623
  104.7 93.8 %collective-permute-start.2 = (bf16[2048,1024]{1,0:T(8,128)(2,1)}, bf16[2048,1024]{1,0:T(8,128)(2,1)}, u32[]{:S(2)}, u32[]{:S(2)}) collective-permute-start(bf16[2048,1024]{1,0:T(8,128)(2,1)} %get-tuple-element.132), channel_id=1, source_target_pairs={{0,1},{1,0},{2,3},{3,2},{4,5},{5,4},{6,7},{7,6},{8,9},{9,8},{10,11... | collective-permute-start | bytes 12582920 | tf_op jit(solution)/shard_map/ppermute | solution.py:395
  146.4 97.0 %collective-permute-start.6 = (bf16[512,2048]{1,0:T(8,128)(2,1)}, bf16[512,2048]{1,0:T(8,128)(2,1)}, u32[]{:S(2)}, u32[]{:S(2)}) collective-permute-start(bf16[512,2048]{1,0:T(8,128)(2,1)} %dynamic-slice_bitcast_fusion.6), channel_id=1, source_target_pairs={{0,1},{1,0},{2,3},{3,2},{4,5},{5,4},{6,7},{7,6},{8,9},{9,8},{10,11... | collective-permute-start | bytes 6291464 | tf_op jit(solution)/shard_map/ppermute | solution.py:395
  177.8 68.5 %collective-permute-start.1 = (bf16[512,2048]{1,0:T(8,128)(2,1)S(1)}, bf16[512,2048]{1,0:T(8,128)(2,1)S(1)}, u32[]{:S(2)}, u32[]{:S(2)}) collective-permute-start(bf16[512,2048]{1,0:T(8,128)(2,1)S(1)} %get-tuple-element.124), channel_id=1, source_target_pairs={{0,2},{1,3},{2,0},{3,1},{4,6},{5,7},{6,4},{7,5},{8,10},{9,11},{10,... | collective-permute-start | bytes 6291464 | tf_op jit(solution)/shard_map/ppermute | solution.py:401
  198.5 70.5 %collective-permute-start.3 = (bf16[2048,1024]{1,0:T(8,128)(2,1)}, bf16[2048,1024]{1,0:T(8,128)(2,1)}, u32[]{:S(2)}, u32[]{:S(2)}) collective-permute-start(bf16[2048,1024]{1,0:T(8,128)(2,1)} %collective-permute-done.2), channel_id=1, source_target_pairs={{0,4},{4,0},{8,12},{12,8},{16,20},{20,16},{24,28},{28,24},{1,5},{5... | collective-permute-start | bytes 12582920 | tf_op jit(solution)/shard_map/ppermute | solution.py:398
  267.5 128.7 %collective-permute-start.11 = (bf16[2048,1024]{1,0:T(8,128)(2,1)}, bf16[2048,1024]{1,0:T(8,128)(2,1)}, u32[]{:S(2)}, u32[]{:S(2)}) collective-permute-start(bf16[2048,1024]{1,0:T(8,128)(2,1)} %get-tuple-element.127), channel_id=1, source_target_pairs={{0,1},{1,0},{2,3},{3,2},{4,5},{5,4},{6,7},{7,6},{8,9},{9,8},{10,11... | collective-permute-start | bytes 12582920 | tf_op jit(solution)/shard_map/ppermute | solution.py:395
  329.3 118.2 %collective-permute-start.8 = (bf16[512,2048]{1,0:T(8,128)(2,1)}, bf16[512,2048]{1,0:T(8,128)(2,1)}, u32[]{:S(2)}, u32[]{:S(2)}) collective-permute-start(bf16[512,2048]{1,0:T(8,128)(2,1)} %convolution_convert_fusion.5), channel_id=1, source_target_pairs={{0,2},{1,3},{2,0},{3,1},{4,6},{5,7},{6,4},{7,5},{8,10},{9,11},{10,... | collective-permute-start | bytes 6291464 | tf_op jit(solution)/shard_map/ppermute | solution.py:401
  331.9 50.9 %collective-permute-start.18 = (bf16[256,2048]{1,0:T(8,128)(2,1)S(1)}, bf16[256,2048]{1,0:T(8,128)(2,1)S(1)}, u32[]{:S(2)}, u32[]{:S(2)}) collective-permute-start(bf16[256,2048]{1,0:T(8,128)(2,1)S(1)} %get-tuple-element.145), channel_id=1, source_target_pairs={{0,1},{1,0},{2,3},{3,2},{4,5},{5,4},{6,7},{7,6},{8,9},{9,8},{10,11... | collective-permute-start | bytes 3145736 | tf_op jit(solution)/shard_map/ppermute | solution.py:395
  387.9 76.2 %collective-permute-start.19 = (bf16[512,2048]{1,0:T(8,128)(2,1)}, bf16[512,2048]{1,0:T(8,128)(2,1)}, u32[]{:S(2)}, u32[]{:S(2)}) collective-permute-start(bf16[512,2048]{1,0:T(8,128)(2,1)} %get-tuple-element.114), channel_id=1, source_target_pairs={{0,2},{1,3},{2,0},{3,1},{4,6},{5,7},{6,4},{7,5},{8,10},{9,11},{10,... | collective-permute-start | bytes 6291464 | tf_op jit(solution)/shard_map/ppermute | solution.py:401
  389.9 56.4 %collective-permute-start.9 = (f32[1024,1]{1,0:T(8,128)S(1)}, f32[1024,1]{1,0:T(8,128)}, u32[]{:S(2)}, u32[]{:S(2)}) collective-permute-start(f32[1024,1]{1,0:T(8,128)S(1)} %get-tuple-element.32), channel_id=1, source_target_pairs={{0,2},{1,3},{2,0},{3,1},{4,6},{5,7},{6,4},{7,5},{8,10},{9,11},{10,... | collective-permute-start | bytes 12296 | tf_op jit(solution)/shard_map/ppermute | solution.py:401
  394.7 73.9 %collective-permute-start.13 = (bf16[512,2048]{1,0:T(8,128)(2,1)}, bf16[512,2048]{1,0:T(8,128)(2,1)}, u32[]{:S(2)}, u32[]{:S(2)}) collective-permute-start(bf16[512,2048]{1,0:T(8,128)(2,1)} %dynamic-slice_bitcast_fusion.5), channel_id=1, source_target_pairs={{0,1},{1,0},{2,3},{3,2},{4,5},{5,4},{6,7},{7,6},{8,9},{9,8},{10,11... | collective-permute-start | bytes 6291464 | tf_op jit(solution)/shard_map/ppermute | solution.py:395
  396.2 72.4 %collective-permute-start.12 = (bf16[2048,1024]{1,0:T(8,128)(2,1)}, bf16[2048,1024]{1,0:T(8,128)(2,1)}, u32[]{:S(2)}, u32[]{:S(2)}) collective-permute-start(bf16[2048,1024]{1,0:T(8,128)(2,1)} %collective-permute-done.11), channel_id=1, source_target_pairs={{0,4},{4,0},{8,12},{12,8},{16,20},{20,16},{24,28},{28,24},{1,5},{5... | collective-permute-start | bytes 12582920 | tf_op jit(solution)/shard_map/ppermute | solution.py:398
  468.6 95.2 %collective-permute-start.14 = (bf16[512,2048]{1,0:T(8,128)(2,1)}, bf16[512,2048]{1,0:T(8,128)(2,1)}, u32[]{:S(2)}, u32[]{:S(2)}) collective-permute-start(bf16[512,2048]{1,0:T(8,128)(2,1)} %collective-permute-done.13), channel_id=1, source_target_pairs={{0,4},{4,0},{8,12},{12,8},{16,20},{20,16},{24,28},{28,24},{1,5},{5... | collective-permute-start | bytes 6291464 | tf_op jit(solution)/shard_map/ppermute | solution.py:398
  608.9 335.4 %collective-permute-start.36 = (bf16[512,2048]{1,0:T(8,128)(2,1)}, bf16[512,2048]{1,0:T(8,128)(2,1)}, u32[]{:S(2)}, u32[]{:S(2)}) collective-permute-start(bf16[512,2048]{1,0:T(8,128)(2,1)} %dynamic-slice_bitcast_fusion.2), channel_id=1, source_target_pairs={{0,4},{4,0},{8,12},{12,8},{16,20},{20,16},{24,28},{28,24},{1,5},{5... | collective-permute-start | bytes 6291464 | tf_op jit(solution)/shard_map/ppermute | solution.py:398
  741.6 49.9 %collective-permute-start.22 = (bf16[512,2048]{1,0:T(8,128)(2,1)S(1)}, bf16[512,2048]{1,0:T(8,128)(2,1)}, u32[]{:S(2)}, u32[]{:S(2)}) collective-permute-start(bf16[512,2048]{1,0:T(8,128)(2,1)S(1)} %get-tuple-element.109), channel_id=1, source_target_pairs={{0,2},{1,3},{2,0},{3,1},{4,6},{5,7},{6,4},{7,5},{8,10},{9,11},{10,... | collective-permute-start | bytes 6291464 | tf_op jit(solution)/shard_map/ppermute | solution.py:401
  942.2 551.1 %all-reduce.6.cloned.1.call-start = ((), (), s32[]{:S(2)}) async-start(), calls=%async_computation.7 | async-start | bytes 540672 | tf_op jit(solution)/shard_map/psum | solution.py:626
  948.0 51.1 %collective-permute-start.37 = (bf16[512,2048]{1,0:T(8,128)(2,1)S(1)}, bf16[512,2048]{1,0:T(8,128)(2,1)}, u32[]{:S(2)}, u32[]{:S(2)}) collective-permute-start(bf16[512,2048]{1,0:T(8,128)(2,1)S(1)} %fusion.22), channel_id=1, source_target_pairs={{0,1},{1,0},{2,3},{3,2},{4,5},{5,4},{6,7},{7,6},{8,9},{9,8},{10,11... | collective-permute-start | bytes 6291464 | tf_op jit(solution)/shard_map/ppermute | solution.py:395
  951.6 92.7 %collective-permute-start.35 = (bf16[512,2048]{1,0:T(8,128)(2,1)}, bf16[512,2048]{1,0:T(8,128)(2,1)}, u32[]{:S(2)}, u32[]{:S(2)}) collective-permute-start(bf16[512,2048]{1,0:T(8,128)(2,1)} %fusion.23), channel_id=1, source_target_pairs={{0,1},{1,0},{2,3},{3,2},{4,5},{5,4},{6,7},{7,6},{8,9},{9,8},{10,11... | collective-permute-start | bytes 6291464 | tf_op jit(solution)/shard_map/ppermute | solution.py:395
  978.7 517.9 %reduce-scatter.14.cloned.1.call-start = ((), (), s32[]{:S(2)}) async-start(), calls=%async_computation.11 | async-start | bytes 4718592 | tf_op jit(solution)/shard_map/reduce_scatter | solution.py:604
  1052.2 444.4 %reduce-scatter.12.cloned.1.call-start = ((), (), s32[]{:S(2)}) async-start(), calls=%async_computation.10 | async-start | bytes 4718592 | tf_op jit(solution)/shard_map/reduce_scatter | solution.py:604
  1087.3 412.0 %reduce-scatter.10.cloned.1.call-start = ((), (), s32[]{:S(2)}) async-start(), calls=%async_computation.9 | async-start | bytes 9437184 | tf_op jit(solution)/shard_map/reduce_scatter | solution.py:601
  1093.1 93.4 %collective-permute-start.31 = (bf16[2048,1024]{1,0:T(8,128)(2,1)S(1)}, bf16[2048,1024]{1,0:T(8,128)(2,1)S(1)}, u32[]{:S(2)}, u32[]{:S(2)}) collective-permute-start(bf16[2048,1024]{1,0:T(8,128)(2,1)S(1)} %fusion), channel_id=1, source_target_pairs={{0,1},{1,0},{2,3},{3,2},{4,5},{5,4},{6,7},{7,6},{8,9},{9,8},{10,11... | collective-permute-start | bytes 12582920 | tf_op jit(solution)/shard_map/ppermute | solution.py:395
  1100.1 175.9 %collective-permute-start.29 = (bf16[2048,1024]{1,0:T(8,128)(2,1)S(1)}, bf16[2048,1024]{1,0:T(8,128)(2,1)S(1)}, u32[]{:S(2)}, u32[]{:S(2)}) collective-permute-start(bf16[2048,1024]{1,0:T(8,128)(2,1)S(1)} %fusion.1), channel_id=1, source_target_pairs={{0,1},{1,0},{2,3},{3,2},{4,5},{5,4},{6,7},{7,6},{8,9},{9,8},{10,11... | collective-permute-start | bytes 12582920 | tf_op jit(solution)/shard_map/ppermute | solution.py:395
  1286.1 213.2 %reduce-scatter.8.cloned.1.call-start = ((), (), s32[]{:S(2)}) async-start(), calls=%async_computation.8 | async-start | bytes 9437184 | tf_op jit(solution)/shard_map/reduce_scatter | solution.py:601
  1296.6 47.0 %collective-permute-start.15 = (bf16[512,2048]{1,0:T(8,128)(2,1)}, bf16[512,2048]{1,0:T(8,128)(2,1)}, u32[]{:S(2)}, u32[]{:S(2)}) collective-permute-start(bf16[512,2048]{1,0:T(8,128)(2,1)} %convolution_convert_fusion.4), channel_id=1, source_target_pairs={{0,2},{1,3},{2,0},{3,1},{4,6},{5,7},{6,4},{7,5},{8,10},{9,11},{10,... | collective-permute-start | bytes 6291464 | tf_op jit(solution)/shard_map/ppermute | solution.py:401
  (114 other events, 4675.7 us)
Sparse Core Ops, SparseCore 0:
  10.5 84.7 all-gather.11
  96.9 46.3 all-gather.13
  144.9 30.5 all-gather.9
  176.9 80.9 all-gather.15
  259.9 46.3 all-gather.17
  942.3 33.9 reduce-scatter.5
  979.3 44.5 all-reduce.5
  1052.3 47.5 reduce-scatter.13
  1102.4 48.8 reduce-scatter.11
  1286.2 87.2 reduce-scatter.9
  1375.9 89.0 reduce-scatter.7

commit v2 on v1

v2 whole, which is shorter than its diff:
```python
import functools

import jax
import jax.numpy as jnp
from jax import lax
from jax.experimental import pallas as pl
from jax.experimental.pallas import tpu as pltpu
from jax.sharding import PartitionSpec as P

EPSILON = 1e-05
CHUNK = 128
PIECES = 2
GROUP_LANES = 256
LOG2E = 1.4426950408889634
F32 = jnp.float32
BF16 = jnp.bfloat16
NN = (((1,), (0,)), ((), ()))
NT = (((1,), (1,)), ((), ()))
TN = (((0,), (0,)), ((), ()))


def mm(a, b, dims=NN):
    return lax.dot_general(a, b, dims, preferred_element_type=F32)


def sigmoid(v):
    return 0.5 * jnp.tanh(0.5 * v) + 0.5


def softplus(v):
    return jnp.maximum(v, 0.0) + jnp.log(1.0 + jnp.exp(-jnp.abs(v)))


def split3(v):
    high = v.astype(BF16)
    rest = v - high.astype(F32)
    mid = rest.astype(BF16)
    return high, mid, (rest - mid.astype(F32)).astype(BF16)


def spread(v, expand, heads):
    high = v.astype(BF16)
    low = (v - high.astype(F32)).astype(BF16)
    lane = lax.broadcasted_iota(jnp.int32, v.shape, 1)
    parts = jnp.where(lane < heads, high, jnp.where(lane < 2 * heads, low, jnp.zeros_like(low)))
    return mm(parts, expand)


def conv_rows(window, table, length):
    total = table[4:5] + table[3:4] * window[8 : 8 + length]
    for back in range(1, 4):
        total = total + table[3 - back : 4 - back] * pltpu.roll(window, back, 0)[8 : 8 + length]
    return total


def causal(length, flip):
    row = lax.broadcasted_iota(jnp.int32, (length, length), 0)
    col = lax.broadcasted_iota(jnp.int32, (length, length), 1)
    return (row <= col) if flip else (row >= col)


def head_masks(lanes, width):
    lane = lax.broadcasted_iota(jnp.int32, (1, lanes), 1)
    return [(lane >= j * width) & (lane < (j + 1) * width) for j in range(lanes // width)]


def forward_kernel(first, heads, half_no, *refs):
    columns_ref, small_ref, chan_ref, taps_ref, head_ref, expand_ref, tri_ref = refs[:7]
    refs = refs[7:]
    if not first:
        start_ref, tail_ref, stail_ref = refs[:3]
        refs = refs[3:]
    mixed_ref, square_ref, y_ref, saved_ref, state, xbuf, sbuf = refs[-7:]
    length, channels = y_ref.shape
    width = channels // heads
    shared = taps_ref.shape[1]
    half = shared // 2
    step_lanes = slice(half_no * (half + 128) + half, (half_no + 1) * (half + 128))

    def shared_of(ref):
        return jnp.concatenate([ref[:, :half], ref[:, half + 128 : shared + 128]], axis=1)

    @pl.when(pl.program_id(0) == 0)
    def _():
        if first:
            state[...] = jnp.zeros_like(state)
            xbuf[0:8] = jnp.zeros((8, channels), F32)
            sbuf[0:8] = jnp.zeros((8, shared), F32)
        else:
            state[...] = start_ref[...]
            xbuf[0:8] = tail_ref[:, channels:].astype(F32)[-8:]
            sbuf[0:8] = shared_of(stail_ref)

    sbuf[8:] = shared_of(small_ref)
    tri = tri_ref[...]
    expand = expand_ref[...]
    head = head_ref[8 * half_no : 8 * half_no + 8]
    dt = softplus(small_ref[:, step_lanes] + head[0:1])
    running = sum(mm(tri, piece) for piece in split3(dt * (head[1:2] * LOG2E)))
    running_t = running.T
    decay_in = jnp.exp2(running)
    decay_out = jnp.exp2(running[length - 1 :] - running)
    dt_wide = spread(dt, expand, heads)
    in_wide = spread(decay_in, expand, heads)
    out_wide = spread(dt * decay_out, expand, heads)

    taps = taps_ref[...]
    bc = conv_rows(sbuf[...], taps, length)
    bc = (bc * sigmoid(bc)).astype(BF16)
    keys, queries = bc[:, :half], bc[:, half:]
    scores = jnp.where(causal(length, False), mm(queries, keys, NT), 0.0)
    squares = jnp.zeros((length, 128), F32)
    masks = head_masks(GROUP_LANES, width)
    for start in range(0, channels, GROUP_LANES):
        lanes = slice(start, start + GROUP_LANES)
        conv_at = slice(channels + start, channels + start + GROUP_LANES)
        table = chan_ref[:, half_no * channels + start : half_no * channels + start + GROUP_LANES]
        xbuf[8:, lanes] = columns_ref[:, conv_at].astype(F32)
        c = conv_rows(xbuf[:, lanes], table, length)
        xbuf[0:8, lanes] = xbuf[length:, lanes]
        xs = c * sigmoid(c)
        values = (xs * dt_wide[:, lanes]).astype(BF16)
        weights, parts = [], []
        for j in range(GROUP_LANES // width):
            h = start // width + j
            gap = jnp.minimum(running[:, h : h + 1] - running_t[h : h + 1, :], 0.0)
            weights.append((scores * jnp.exp2(gap)).astype(BF16))
            parts.append(jnp.where(masks[j], values, jnp.zeros_like(values)))
        before = state[:, lanes]
        before_low = before.astype(BF16)
        saved_ref[0, :, lanes] = before_low
        y = mm(jnp.concatenate(weights, axis=1), jnp.concatenate(parts, axis=0))
        y = y + mm(queries, before_low) * in_wide[:, lanes]
        y_ref[:, lanes] = y
        z = columns_ref[:, lanes].astype(F32)
        gated = (y + table[5:6] * xs) * (z * sigmoid(z))
        mixed_ref[:, lanes] = (gated * table[6:7]).astype(BF16)
        power = gated * gated
        for at in range(0, GROUP_LANES, 128):
            squares = squares + power[:, at : at + 128]
        fresh = mm(keys, (xs * out_wide[:, lanes]).astype(BF16), TN)
        state[:, lanes] = before * in_wide[length - 1 :, lanes] + fresh
    square_ref[...] = jnp.sum(squares, axis=1, keepdims=True)
    sbuf[0:8] = sbuf[length:]


def backward_kernel(first, last, heads, *refs):
    columns_refs, small_ref, y_refs, saved_refs, up_refs = refs[:2], refs[2], refs[3:5], refs[5:7], refs[7:9]
    pull_ref, chan_ref, taps_ref, head_ref, expand_ref, tri_ref, halo0, halo1, shalo_ref, early0, early1, searly_ref = refs[9:21]
    halo_refs, early_refs = (halo0, halo1), (early0, early1)
    refs = refs[21:]
    if not last:
        carried_refs = refs[:6]
    dcolumns_ref, dstate, dtail_ref, dstail_ref, gchan_ref, gtaps_ref, ghead_ref, xbuf, sbuf, dxbuf, dsbuf = refs[-11:]
    length, channels = y_refs[0].shape
    width = channels // heads
    shared = taps_ref.shape[1]
    half = shared // 2
    step_no = pl.program_id(0)
    first_block = step_no == pl.num_programs(0) - 1

    @pl.when(step_no == 0)
    def _():
        if last:
            dstate[...] = jnp.zeros_like(dstate)
            dxbuf[length:] = jnp.zeros((8, 2 * channels), F32)
            dsbuf[length:] = jnp.zeros((8, shared), F32)
            gchan_ref[...] = jnp.zeros_like(gchan_ref)
            gtaps_ref[...] = jnp.zeros_like(gtaps_ref)
            ghead_ref[...] = jnp.zeros_like(ghead_ref)
        else:
            dstate[...] = carried_refs[0][...]
            dxbuf[length:] = carried_refs[1][...]
            dsbuf[length:] = carried_refs[2][...]
            gchan_ref[...] = carried_refs[3][...]
            gtaps_ref[...] = carried_refs[4][...]
            ghead_ref[...] = carried_refs[5][...]

    def outside(rows):
        return jnp.zeros_like(rows) if first else rows

    def shared_of(ref):
        return jnp.concatenate([ref[:, :half], ref[:, half + 128 : shared + 128]], axis=1)

    sbuf[8:] = shared_of(small_ref)
    sbuf[0:8] = jnp.where(first_block, outside(shared_of(searly_ref)), shared_of(shalo_ref))
    tri = tri_ref[...]
    expand = expand_ref[...]
    taps = taps_ref[...]
    bc_in = conv_rows(sbuf[...], taps, length)
    bc_sig = sigmoid(bc_in)
    bc = (bc_in * bc_sig).astype(BF16)
    keys, queries = bc[:, :half], bc[:, half:]
    keep = causal(length, True)
    scores = jnp.where(keep, mm(keys, queries, NT), 0.0)
    pull = pull_ref[...]
    masks = head_masks(GROUP_LANES, width)
    dscores = jnp.zeros((length, length), F32)
    dkeys = jnp.zeros((length, half), F32)
    dqueries = jnp.zeros((length, half), F32)
    last_row = lax.broadcasted_iota(jnp.int32, (length, 1), 0) == length - 1
    lane = lax.broadcasted_iota(jnp.int32, (length, 128), 1)
    per_group = GROUP_LANES // width
    for half_no in range(2):
        columns_ref, halo_ref, early_ref = columns_refs[half_no], halo_refs[half_no], early_refs[half_no]
        y_ref, saved_ref, up_ref = y_refs[half_no], saved_refs[half_no], up_refs[half_no]
        step_lanes = slice(half_no * (half + 128) + half, (half_no + 1) * (half + 128))
        head = head_ref[8 * half_no : 8 * half_no + 8]
        step = small_ref[:, step_lanes] + head[0:1]
        dt = softplus(step)
        rate = dt * head[1:2]
        running = sum(mm(tri, piece) for piece in split3(rate * LOG2E))
        running_t = running.T
        decay_in = jnp.exp2(running)
        decay_out = jnp.exp2(running[length - 1 :] - running)
        dt_wide = spread(dt, expand, heads)
        in_wide = spread(decay_in, expand, heads)
        out_wide = spread(decay_out, expand, heads)
        drun = jnp.zeros((length, 128), F32)
        ddt = jnp.zeros((length, 128), F32)
        for start in range(0, channels, GROUP_LANES):
            lanes = slice(start, start + GROUP_LANES)
            conv_at = slice(channels + start, channels + start + GROUP_LANES)
            at = half_no * channels + start
            wide = slice(at, at + GROUP_LANES)
            table = chan_ref[:, wide]
            xbuf[8:, lanes] = columns_ref[:, conv_at].astype(F32)
            xbuf[0:8, lanes] = jnp.where(first_block, outside(early_ref[:, conv_at].astype(F32)[-8:]), halo_ref[:, conv_at].astype(F32)[-8:])
            c = conv_rows(xbuf[:, lanes], table, length)
            c_sig = sigmoid(c)
            xs = c * c_sig
            z = columns_ref[:, lanes].astype(F32)
            z_sig = sigmoid(z)
            z_silu = z * z_sig
            y = y_ref[:, lanes]
            total = y + table[5:6] * xs
            gated = total * z_silu
            up = up_ref[:, lanes].astype(F32)
            gchan_ref[6:7, wide] += jnp.sum(up * gated, axis=0, keepdims=True)
            dgated = table[6:7] * up - gated * pull
            out_at = half_no * (2 * channels + half + 128) + start
            dcolumns_ref[:, out_at : out_at + GROUP_LANES] = (
                dgated * total * (z_sig + z_silu * (1.0 - z_sig))
            ).astype(BF16)
            dy = dgated * z_silu
            gchan_ref[5:6, wide] += jnp.sum(dy * xs, axis=0, keepdims=True)
            dy_low = dy.astype(BF16)
            dt_lanes = dt_wide[:, lanes]
            values = (xs * dt_lanes).astype(BF16)
            weights, dparts, vparts, decays = [], [], [], []
            for j in range(per_group):
                h = start // width + j
                decay = jnp.exp2(jnp.minimum(running_t[h : h + 1, :] - running[:, h : h + 1], 0.0))
                decays.append(decay)
                weights.append((scores * decay).astype(BF16))
                dparts.append(jnp.where(masks[j], dy_low, jnp.zeros_like(dy_low)))
                vparts.append(jnp.where(masks[j], values, jnp.zeros_like(values)))
            outer = mm(jnp.concatenate(vparts, axis=0), dy_low, NT)
            for j in range(per_group):
                dscores = dscores + outer[j * length : (j + 1) * length] * decays[j]
            dvalues = mm(jnp.concatenate(weights, axis=1), jnp.concatenate(dparts, axis=0))
            before = saved_ref[0, :, lanes]
            dafter = dstate[:, wide]
            dafter_low = dafter.astype(BF16)
            out_lanes = out_wide[:, lanes]
            carried = mm(keys, dafter_low) * out_lanes
            dvalues = dvalues + carried
            values_f = values.astype(F32)
            dkeys = dkeys + mm((values_f * out_lanes).astype(BF16), dafter_low, NT)
            in_lanes = in_wide[:, lanes]
            dy_in = (dy * in_lanes).astype(BF16)
            dqueries = dqueries + mm(dy_in, before, NT)
            end_decay = in_lanes[length - 1 :]
            at_end = jnp.sum(values_f * carried, axis=0, keepdims=True) + end_decay * jnp.sum(
                before.astype(F32) * dafter, axis=0, keepdims=True
            )
            dstate[:, wide] = end_decay * dafter + mm(queries, dy_in, TN)
            turn = dy_low.astype(F32) * y - values_f * dvalues + jnp.where(last_row, at_end, 0.0)
            turn_high = turn.astype(BF16)
            turn_low = (turn - turn_high.astype(F32)).astype(BF16)
            group_expand = expand[:, lanes]
            drun = drun + mm(turn_high, group_expand, NT) + mm(turn_low, group_expand, NT)
            ddt = ddt + mm((dvalues * xs).astype(BF16), group_expand, NT)
            dxs = dvalues * dt_lanes + table[5:6] * dy
            dc = dxs * (c_sig + xs * (1.0 - c_sig))
            dxbuf[0:length, wide] = dc
            window = dxbuf[:, wide]
            here = xbuf[8:, lanes]
            gchan_ref[4:5, wide] += jnp.sum(dc, axis=0, keepdims=True)
            gchan_ref[3:4, wide] += jnp.sum(dc * here, axis=0, keepdims=True)
            dconv = table[3:4] * dc
            for ahead in range(1, 4):
                moved = pltpu.roll(window, length + 8 - ahead, 0)[:length]
                gchan_ref[3 - ahead : 4 - ahead, wide] += jnp.sum(moved * here, axis=0, keepdims=True)
                dconv = dconv + table[3 - ahead : 4 - ahead] * moved
            out_at = out_at + channels
            dcolumns_ref[:, out_at : out_at + GROUP_LANES] = dconv.astype(BF16)
            dxbuf[length:, wide] = dxbuf[0:8, wide]

        drate = sum(mm(tri, piece, TN) for piece in split3(drun))
        dstep = (ddt + drate * head[1:2]) * sigmoid(step)
        ghead_ref[8 * half_no : 8 * half_no + 1] += jnp.sum(dstep, axis=0, keepdims=True)
        ghead_ref[8 * half_no + 1 : 8 * half_no + 2] += jnp.sum(drate * rate, axis=0, keepdims=True)
        out_at = half_no * (2 * channels + half + 128) + 2 * channels + half
        dcolumns_ref[:, out_at : out_at + 128] = jnp.where(lane < heads, dstep, 0.0).astype(BF16)

    dscores_low = jnp.where(keep, dscores, 0.0).astype(BF16)
    dkeys = dkeys + mm(dscores_low, queries)
    dqueries = dqueries + mm(dscores_low, keys, TN)
    dbc = jnp.concatenate([dkeys, dqueries], axis=1) * (bc_sig + bc_in * bc_sig * (1.0 - bc_sig))
    dsbuf[0:length] = dbc
    window = dsbuf[...]
    here = sbuf[8:]
    gtaps_ref[4:5] += jnp.sum(dbc, axis=0, keepdims=True)
    gtaps_ref[3:4] += jnp.sum(dbc * here, axis=0, keepdims=True)
    dshared = taps[3:4] * dbc
    for ahead in range(1, 4):
        moved = pltpu.roll(window, length + 8 - ahead, 0)[:length]
        gtaps_ref[3 - ahead : 4 - ahead] += jnp.sum(moved * here, axis=0, keepdims=True)
        dshared = dshared + taps[3 - ahead : 4 - ahead] * moved
    for half_no in range(2):
        out_at = half_no * (2 * channels + half + 128) + 2 * channels
        dcolumns_ref[:, out_at : out_at + half] = dshared[:, half_no * half : (half_no + 1) * half].astype(BF16)
    dsbuf[length:] = dsbuf[0:8]
    dtail_ref[...] = dxbuf[0:8]
    dstail_ref[...] = dsbuf[0:8]


def scan_tables(heads, channels):
    row = lax.broadcasted_iota(jnp.int32, (128, channels), 0) % heads
    col = lax.broadcasted_iota(jnp.int32, (128, channels), 1) // (channels // heads)
    return (row == col).astype(BF16), jnp.tril(jnp.ones((CHUNK, CHUNK), BF16))


def whole(array):
    return pl.BlockSpec(array.shape, lambda i: (0,) * array.ndim)


def last_rows(array, count):
    at = array.shape[0] // count - 1
    return pl.BlockSpec((count,) + array.shape[1:], lambda i: (at, 0))


def unread(arrays):
    return [pl.BlockSpec(memory_space=pl.ANY) for _ in arrays]


def mixer_forward(columns, small, tables, heads, half_no, earlier=None, after=()):
    tokens, channels = columns.shape[0], columns.shape[1] // 2
    shared = tables[1].shape[1]
    blocks = tokens // CHUNK

    def rows(cols):
        return pl.BlockSpec((CHUNK, cols), lambda i: (i, 0))

    operands = [columns, small, *tables]
    specs = [rows(2 * channels), rows(small.shape[1])] + [whole(table) for table in tables]
    if earlier is not None:
        operands += list(earlier)
        specs += [whole(earlier[0]), last_rows(earlier[1], 16), last_rows(earlier[2], 8)]
    operands += list(after)
    specs += unread(after)
    return pl.pallas_call(
        functools.partial(forward_kernel, earlier is None, heads, half_no),
        grid=(blocks,),
        in_specs=specs,
        out_specs=[
            rows(channels),
            rows(1),
            rows(channels),
            pl.BlockSpec((1, shared // 2, channels), lambda i: (i, 0, 0)),
            pl.BlockSpec((shared // 2, channels), lambda i: (0, 0)),
        ],
        out_shape=[
            jax.ShapeDtypeStruct((tokens, channels), BF16),
            jax.ShapeDtypeStruct((tokens, 1), F32),
            jax.ShapeDtypeStruct((tokens, channels), F32),
            jax.ShapeDtypeStruct((blocks, shared // 2, channels), BF16),
            jax.ShapeDtypeStruct((shared // 2, channels), F32),
        ],
        scratch_shapes=[
            pltpu.VMEM((CHUNK + 8, channels), F32),
            pltpu.VMEM((CHUNK + 8, shared), F32),
        ],
        compiler_params=pltpu.CompilerParams(vmem_limit_bytes=48 * 1024 * 1024),
        cost_estimate=pl.CostEstimate(
            flops=tokens * channels * 6000, bytes_accessed=tokens * channels * 14, transcendentals=tokens * channels * 6
        ),
        name="mixer_forward",
    )(*operands)


def mixer_backward(columns, small, y, saved, up, pull, tables, heads, early, carried, after=()):
    tokens, channels = y[0].shape
    shared = tables[1].shape[1]
    blocks = tokens // CHUNK
    small_width = small.shape[1]

    def rows(cols):
        return pl.BlockSpec((CHUNK, cols), lambda i: (blocks - 1 - i, 0))

    def halo(count, cols):
        per_block = CHUNK // count
        return pl.BlockSpec((count, cols), lambda i: (jnp.maximum((blocks - 1 - i) * per_block - 1, 0), 0))

    def fixed(r, c):
        return pl.BlockSpec((r, c), lambda i: (0, 0))

    saved_spec = pl.BlockSpec((1, shared // 2, channels), lambda i: (blocks - 1 - i, 0, 0))
    before = (columns[0], columns[1], small) if early is None else early
    operands = [*columns, small, *y, *saved, *up, pull, *tables, *columns, small, *before]
    specs = [rows(2 * channels)] * 2 + [rows(small_width)] + [rows(channels)] * 2 + [saved_spec] * 2 + [rows(channels)] * 2
    specs += [rows(1)] + [whole(table) for table in tables]
    specs += [halo(16, 2 * channels)] * 2 + [halo(8, small_width)]
    specs += [last_rows(before[0], 16), last_rows(before[1], 16), last_rows(before[2], 8)]
    if carried is not None:
        operands += list(carried)
        specs += [whole(array) for array in carried]
    operands += list(after)
    specs += unread(after)
    fixed_shapes = [(shared // 2, 2 * channels), (8, 2 * channels), (8, shared), (8, 2 * channels), (8, shared), (16, 128)]
    return pl.pallas_call(
        functools.partial(backward_kernel, early is None, carried is None, heads),
        grid=(blocks,),
        in_specs=specs,
        out_specs=[rows(4 * channels + shared + 256)] + [fixed(*shape) for shape in fixed_shapes],
        out_shape=[
            jax.ShapeDtypeStruct((tokens, 4 * channels + shared + 256), BF16),
        ]
        + [jax.ShapeDtypeStruct(shape, F32) for shape in fixed_shapes],
        scratch_shapes=[
            pltpu.VMEM((CHUNK + 8, channels), F32),
            pltpu.VMEM((CHUNK + 8, shared), F32),
            pltpu.VMEM((CHUNK + 8, 2 * channels), F32),
            pltpu.VMEM((CHUNK + 8, shared), F32),
        ],
        compiler_params=pltpu.CompilerParams(vmem_limit_bytes=56 * 1024 * 1024),
        cost_estimate=pl.CostEstimate(
            flops=tokens * channels * 28000, bytes_accessed=tokens * channels * 40, transcendentals=tokens * channels * 12
        ),
        name="mixer_backward",
    )(*operands)


class Place:
    def __init__(self):
        self.members = lax.axis_size("tensor")
        self.groups = self.members // 2
        self.sequence = lax.axis_index("tensor") % 2
        self.group = lax.axis_index("tensor") // 2
        copies = lax.axis_size("dp")
        self.owners = [
            [d * self.members + 2 * g + s for s in range(2) for d in range(copies)] for g in range(self.groups)
        ]

    def to_pair(self, v):
        return lax.ppermute(v, "tensor", [(t, t ^ 1) for t in range(self.members)])

    def to_group(self, v, hop):
        return lax.ppermute(v, "tensor", [(t, (t + 2 * hop) % self.members) for t in range(self.members)])

    def gather_owners(self, v):
        return lax.all_gather(v, ("dp", "tensor"), axis=0, axis_index_groups=self.owners, tiled=True)

    def scatter_owners(self, v):
        return lax.psum_scatter(v, ("dp", "tensor"), scatter_dimension=0, axis_index_groups=self.owners, tiled=True)

    def add_groups(self, v):
        return v + sum(self.to_group(v, hop) for hop in range(1, self.groups))

    def sum_groups(self, v):
        return v.astype(F32) + sum(self.to_group(v, hop).astype(F32) for hop in range(1, self.groups))

    def both(self, v, axis):
        other = self.to_pair(v)
        return jnp.where(
            self.sequence == 0, jnp.concatenate([v, other], axis=axis), jnp.concatenate([other, v], axis=axis)
        )

    def rows_of(self, chunks, hop):
        at = (self.group + hop) % self.groups
        if len(chunks) == self.groups == 2:
            return jnp.where(at == 0, chunks[0], chunks[1])
        total = jnp.concatenate(chunks)
        count = total.shape[0] // self.groups
        return lax.dynamic_slice_in_dim(total, at * count, count, 0)

    def gather_chunks(self, v, chunks):
        if chunks == self.groups == 2:
            other = self.to_group(v, 1)
            return [jnp.where(self.group == at, v, other) for at in range(2)]
        count = v.shape[0]
        total = jnp.zeros((count * self.groups,) + v.shape[1:], v.dtype)
        total = lax.dynamic_update_slice_in_dim(total, v, self.group * count, 0)
        for hop in range(1, self.groups):
            start = (self.group - hop) % self.groups * count
            total = lax.dynamic_update_slice_in_dim(total, self.to_group(v, hop), start, 0)
        return jnp.split(total, chunks)

    def scatter_rows(self, chunks):
        arrived = [self.to_group(self.rows_of(chunks, hop), hop) for hop in range(1, self.groups)]
        return self.rows_of(chunks, 0).astype(F32) + sum(piece.astype(F32) for piece in arrived)

    def take_sequence(self, v):
        mine = jnp.where(self.sequence == 0, v[0], v[1])
        other = self.to_pair(jnp.where(self.sequence == 0, v[1], v[0]))
        return jnp.where(self.sequence == 0, jnp.concatenate([mine, other]), jnp.concatenate([other, mine]))

    def give_sequence(self, v):
        first, second = jnp.split(v, 2)
        mine = jnp.where(self.sequence == 0, first, second)
        other = self.to_pair(jnp.where(self.sequence == 0, second, first))
        return jnp.where(self.sequence == 0, jnp.stack([mine, other]), jnp.stack([other, mine]))


def norm_scale(stream):
    return lax.rsqrt(jnp.mean(stream * stream, axis=-1, keepdims=True) + EPSILON)


def block_forward(place, streams, weights, tables, heads, inner, final):
    in_cols, small_cols, out_rows, gain = weights
    main = small_cols[0].shape[1]
    kept = {"stream": streams, "columns": [], "y": [], "saved": [], "mixed": [], "scale": [], "update": []}
    normed = [(stream * norm_scale(stream) * gain).astype(BF16) for stream in streams]
    small = [mm(part, jnp.concatenate(small_cols, axis=1)) for part in normed]
    halves = []
    for half_no, cols in enumerate(in_cols):
        results, earlier = [], None
        for at, part in enumerate(normed):
            columns = mm(part, cols[:, :-main]).astype(BF16)
            mixed, square, y, saved, state = mixer_forward(columns, small[at], tables, heads, half_no, earlier)
            earlier = (state, columns, small[at])
            results.append((columns, mixed, square, y, saved))
        halves.append(results)
    shares, scales = [], []
    for at in range(len(streams)):
        first, second = halves[0][at], halves[1][at]
        shares.append((mm(first[1], out_rows[0], NT) + mm(second[1], out_rows[1], NT)).astype(BF16))
        scales.append(lax.rsqrt(place.add_groups(first[2] + second[2]) / inner + EPSILON))
        for key, position in (("columns", 0), ("mixed", 1), ("y", 3), ("saved", 4)):
            kept[key].append((first[position], second[position]))
    kept.update(normed=normed, small=small, scale=scales)
    if final:
        after = place.rows_of(streams, 0) + place.scatter_rows(shares) * place.rows_of(scales, 0)
    else:
        kept["update"] = [place.sum_groups(share) for share in shares]
        after = [stream + update * scale for stream, update, scale in zip(streams, kept["update"], scales)]
    return after, kept


def block_backward(place, grads, weights, tables, heads, inner, kept, final, first, after):
    in_cols, small_cols, out_rows, gain = weights
    chunks = len(grads)
    scales = kept["scale"]
    ups = [(grad * scale).astype(BF16) for grad, scale in zip(grads, scales)]
    grad_mixed = [[mm(up, rows) for rows in out_rows] for up in ups]
    if final:
        pulls = [
            sum(jnp.sum(g * m.astype(F32), axis=-1, keepdims=True) for g, m in zip(*pairs))
            for pairs in zip(grad_mixed, kept["mixed"])
        ]
        pulls = [place.add_groups(pull) for pull in pulls]
    else:
        pulls = [jnp.sum(up.astype(F32) * u, axis=-1, keepdims=True) for up, u in zip(ups, kept["update"])]
    pulls = [pull * (scale * scale / inner) for pull, scale in zip(pulls, scales)]
    up = jnp.concatenate(ups)
    mixed = [jnp.concatenate([part[half_no] for part in kept["mixed"]]) for half_no in range(2)]
    grad_out = jnp.concatenate([mm(up, part, TN).astype(BF16) for part in mixed])
    out_owned = place.scatter_owners(grad_out)

    dcolumns, shares = [None] * chunks, [None] * chunks
    carried = None
    for at in reversed(range(chunks)):
        early = (*kept["columns"][at - 1], kept["small"][at - 1]) if at else None
        result = mixer_backward(
            kept["columns"][at],
            kept["small"][at],
            kept["y"][at],
            kept["saved"][at],
            grad_mixed[at],
            pulls[at],
            tables,
            heads,
            early,
            carried,
            after[at],
        )
        dcolumns[at], carried = jnp.split(result[0], 2, axis=1), result[1:]
        shares[at] = sum(mm(part, cols, NT) for part, cols in zip(dcolumns[at], in_cols)).astype(BF16)
    normed = jnp.concatenate(kept["normed"])
    joined = [jnp.concatenate([part[half_no] for part in dcolumns]) for half_no in range(2)]
    grad_in = jnp.concatenate([mm(normed, part, TN).astype(BF16) for part in joined])
    in_owned = place.scatter_owners(grad_in)

    streams = kept["stream"]
    if first:
        streams, grads = [place.rows_of(streams, 0)], [place.rows_of(grads, 0)]
        sums = [place.scatter_rows(shares)]
    else:
        sums = [place.sum_groups(share) for share in shares]
    grad_gain, results = 0.0, []
    for stream, grad, grad_normed in zip(streams, grads, sums):
        row_scale = norm_scale(stream)
        unit = stream * row_scale
        grad_gain = grad_gain + jnp.sum(grad_normed * unit, axis=0)
        lifted = grad_normed * gain
        results.append(grad + row_scale * (lifted - unit * jnp.mean(lifted * unit, axis=-1, keepdims=True)))
    if not first:
        grad_gain = jnp.where(place.group == 0, grad_gain, 0.0)
    return results, (in_owned, out_owned, grad_gain, carried[3:], grad_in)


def local(
    hidden,
    cotangent,
    norm_gain,
    in_weights,
    state_weight,
    step_weight,
    channel_taps,
    state_taps,
    step_bias,
    decay_log,
    skip_gain,
    inner_gain,
    out_weight,
):
    place = Place()
    layers = in_weights.shape[0]
    rows = in_weights.shape[2]
    heads = step_bias.shape[1]
    own_cols = in_weights.shape[3]
    width = own_cols // heads
    inner = own_cols * place.members
    shared = state_weight.shape[2]
    half = shared // 2
    copies = 128 // heads
    main = 2 * own_cols
    expand, tri = scan_tables(heads, own_cols)

    weights = []
    for layer in range(layers):
        state_half = lax.dynamic_slice_in_dim(state_weight[layer], place.sequence * half, half, 1)
        thin = [step_weight[layer]] * 2
        blank = jnp.zeros((rows, 127 - 2 * heads), BF16)
        block = [in_weights[layer, 0], in_weights[layer, 1], state_half, *thin, blank, norm_gain[layer][:, None]]
        block = jnp.concatenate(block + [out_weight[layer].T], axis=1)
        both = place.gather_owners(block)
        shards = jnp.split(both, 2)
        thin_end = main + half + 128
        in_cols = [shard[:, :thin_end] for shard in shards]
        small_cols = [shard[:, main:thin_end] for shard in shards]
        out_rows = [shard[:, thin_end:] for shard in shards]
        gain = shards[0][:, thin_end - 1].astype(F32)
        weights.append((in_cols, small_cols, out_rows, gain))

    streams = place.gather_chunks(place.take_sequence(hidden), PIECES)
    streams = [stream.astype(F32) for stream in streams]
    per_channel = place.both(jnp.concatenate([channel_taps, inner_gain[:, None]], axis=1), 2)
    per_head = jnp.stack([step_bias, decay_log, skip_gain], axis=1)
    per_head = place.both(per_head[:, None], 1)
    tables = []
    for layer in range(layers):
        wide_skip = jnp.repeat(per_head[layer, :, 2].reshape(-1), width)[None]
        blank = jnp.zeros((1, main), F32)
        chan = jnp.concatenate([per_channel[layer, :5], wide_skip, per_channel[layer, 5:6], blank], axis=0)
        taps = jnp.concatenate([state_taps[layer], jnp.zeros((3, shared), F32)], axis=0)
        head = []
        for part in range(2):
            pair = jnp.stack([per_head[layer, part, 0], -jnp.exp(per_head[layer, part, 1])])
            pair = jnp.concatenate([pair, pair, jnp.zeros((2, 128 - 2 * heads), F32)], axis=1)
            head += [pair, jnp.zeros((6, 128), F32)]
        tables.append((chan, taps, jnp.concatenate(head), expand, tri))

    last_up = place.gather_chunks(place.take_sequence(cotangent), PIECES)
    kept = []
    for layer in range(layers):
        streams, saved = block_forward(
            place, streams, weights[layer], tables[layer], heads, inner, layer == layers - 1
        )
        kept.append(saved)
    mixed_out = place.give_sequence(streams)

    grads = [part.astype(F32) for part in last_up]
    taken = [None] * layers
    after = [()] * PIECES
    for layer in reversed(range(layers)):
        grads, taken[layer] = block_backward(
            place,
            grads,
            weights[layer],
            tables[layer],
            heads,
            inner,
            kept[layer],
            layer == layers - 1,
            layer == 0,
            after,
        )
        after = [()] * (PIECES - 1) + [(taken[layer][-1],)]
    grad_hidden = place.give_sequence(grads[0].astype(BF16)).astype(F32)

    slots, sizes = [], []
    for layer in range(layers):
        gchan, gtaps, ghead = taken[layer][3]
        skips = gchan[5].reshape(2, heads, width).sum(axis=2)
        mine = jnp.stack([ghead[0, :heads], ghead[8, :heads], ghead[1, :heads], ghead[9, :heads], skips[0], skips[1]])
        channels = jnp.concatenate([gchan[:5].reshape(-1), gchan[6], mine.reshape(-1)])
        slot = lax.broadcasted_iota(jnp.int32, (place.groups, 1), 0) == place.group
        slotted = jnp.where(slot, channels[None], 0.0).reshape(-1)
        slots.append(jnp.concatenate([slotted, gtaps[:5].reshape(-1), taken[layer][2]]))
        sizes = [channels.size, gtaps[:5].size]
    totals = [lax.psum(slot, ("dp", "tensor")) for slot in slots]

    outs = []
    for layer in range(layers):
        total = totals[layer]
        count = sizes[0] * place.groups
        channels = lax.dynamic_slice_in_dim(total, place.group * sizes[0], sizes[0], 0)
        taps_part = total[count : count + sizes[1]].reshape(5, shared)
        gain_part = lax.dynamic_slice_in_dim(total, count + sizes[1] + lax.axis_index("dp") * rows, rows, 0)
        per_channel_part = channels[: 6 * main].reshape(6, 2, own_cols)
        per_channel_part = lax.dynamic_index_in_dim(per_channel_part, place.sequence, 1, keepdims=False)
        per_head_part = channels[6 * main :].reshape(3, 2, heads)
        per_head_part = lax.dynamic_index_in_dim(per_head_part, place.sequence, 1, keepdims=False)
        in_owned, out_owned = taken[layer][:2]
        in_owned = in_owned.astype(F32)
        state_part = place.both(place.add_groups(in_owned[:, main : main + half]), 1)
        outs.append(
            (
                gain_part,
                jnp.stack([in_owned[:, :own_cols], in_owned[:, own_cols:main]]),
                state_part,
                in_owned[:, main + half : main + half + heads],
                per_channel_part[:5],
                taps_part,
                per_head_part[0],
                per_head_part[1],
                per_head_part[2],
                per_channel_part[5],
                out_owned.astype(F32).T,
            )
        )
    return (mixed_out, grad_hidden) + tuple(jnp.stack(parts) for parts in zip(*outs))


def solution(mesh):
    placed = (
        P("dp", "tensor", None),
        P("dp", "tensor", None),
        P(None, "dp"),
        P(None, None, "dp", "tensor"),
        P(None, "dp", None),
        P(None, "dp", "tensor"),
        P(None, None, "tensor"),
        P(),
        P(None, "tensor"),
        P(None, "tensor"),
        P(None, "tensor"),
        P(None, "tensor"),
        P(None, "tensor", "dp"),
    )
    return jax.shard_map(
        local,
        mesh=mesh,
        in_specs=placed,
        out_specs=(
            P("dp", "tensor", None),
            P("dp", "tensor", None),
            P(None, "dp"),
            P(None, None, "dp", "tensor"),
            P(None, "dp", None),
            P(None, "dp", "tensor"),
            P(None, None, "tensor"),
            P(),
            P(None, "tensor"),
            P(None, "tensor"),
            P(None, "tensor"),
            P(None, "tensor"),
            P(None, "tensor", "dp"),
        ),
        check_vma=False,
    )
```

time: 1520 us -> 1750 us (1.15)
  waiting for transfers between devices: 765 us -> 986 us
  blocking collectives: 66.4 us -> 0 us
  matrix products: 276 us -> 337 us
  Pallas kernels: 151 us -> 172 us
  other arithmetic: 121 us -> 141 us
    reduce_scatter x5 -> x4, waiting for transfers between devices: 24.2 us -> 552 us  [scatter_owners(): lax.psum_scatter(v, ('dp', 'tensor'), scatter_dimension=0, axis_index_gro...]
    ppermute x18 -> x8, waiting for transfers between devices: 368 us -> 100 us  [to_pair(): return lax.ppermute(v, 'tensor', [(t, t ^ 1) for t in range(self.members)])]
    psum x2 -> x0, blocking collectives: 66.4 us -> none  [the longest x1 40 us: local(): taps_total = lax.psum(jnp.stack(taps_grads), ('dp', 'tensor'))]
    dot_general x30 -> x44, matrix products: 276 us -> 337 us  [mm(): return lax.dot_general(a, b, dims, preferred_element_type=F32)]
    concatenate x11 -> x9, other arithmetic: 1.68 us -> 39.8 us  [the longest x2 23.4 us: block_backward(): jnp.concatenate([mm(normed, part, TN).astype(BF16) for part in joined])]
    squeeze x7 -> x2, local copies, waits for them, and re-layouts: 29.4 us -> 0.02 us  [the longest x1 0.02 us: local(): per_channel[layer, 5:6]]
    all_gather x5 -> x2, waiting for transfers between devices: 143 us -> 114 us  [gather_owners(): lax.all_gather(v, ('dp', 'tensor'), axis=0, axis_index_groups=self.owners...]
    pallas_call x4 -> x12, Pallas kernels: 151 us -> 172 us  [the longest x4 108 us: mixer_backward(): pl.pallas_call(functools.partial(backward_kernel, early is None, carried...]
  transfers between devices with their start and end apart: 49 -> 31, of which waited for: 24 -> 18; matrix products, arithmetic and copies ran while one was open for 28% -> 23% of each run, Pallas kernels for 10% -> 7%
where the time goes in v2:
time: 1750 us
  waiting for transfers between devices  986 us (56%)
  matrix products  337 us (19%)
  Pallas kernels  172 us (10%)
  other arithmetic  141 us (8%)
  local copies, waits for them, and re-layouts  64.1 us (4%)
  starting transfers between devices  31 us (2%)
    reduce_scatter x4, waiting for transfers between devices, scatter_owners(): lax.psum_scatter(v, ('dp', 'tensor'), scatter_dimension=0, axis_index_gro...  552 us
    dot_general x44, matrix products, mm(): return lax.dot_general(a, b, dims, preferred_element_type=F32)  337 us
    ppermute x16, waiting for transfers between devices, to_group(): lax.ppermute(v, 'tensor', [(t, (t + 2 * hop) % self.members) for t in ran...  218 us
    all_gather x2, waiting for transfers between devices, gather_owners(): lax.all_gather(v, ('dp', 'tensor'), axis=0, axis_index_groups=self.owners...  114 us
    pallas_call x4, Pallas kernels, mixer_backward(): pl.pallas_call(functools.partial(backward_kernel, early is None, carried...  108 us
    ppermute x8, waiting for transfers between devices, to_pair(): return lax.ppermute(v, 'tensor', [(t, t ^ 1) for t in range(self.members)])  100 us
    pallas_call x8, Pallas kernels, mixer_forward(): pl.pallas_call(functools.partial(forward_kernel, earlier is None, heads,...  63.1 us
  transfers between devices with their start and end apart: 31, of which 18 were waited for; matrix products, arithmetic and copies ran while one was open for 23% of the time, Pallas kernels for 7%

profile of v2, /device:TPU:0, one launch (start us, length us, event | category | flops | bytes accessed | tf_op | source)
XLA Modules:
  0.0 1745.5 jit_solution(6336341174318270320)
XLA Ops:
  40.6 44.7 %collective-permute-done.3 = f32[2,1,3,16]{3,0,2,1:T(2,128)S(1)} collective-permute-done((f32[2,1,3,16]{3,0,2,1:T(2,128)S(1)}, f32[2,1,3,16]{3,0,2,1:T(2,128)S(1)}, u32[]{:S(2)}, u32[]{:S(2)}) %collective-permute-start.3) | collective-permute-done | bytes 416 | tf_op jit(solution)/shard_map/ppermute | solution.py:457
  91.0 43.8 %collective-permute-done.1 = bf16[512,2048]{1,0:T(8,128)(2,1)} collective-permute-done((bf16[512,2048]{1,0:T(8,128)(2,1)S(1)}, bf16[512,2048]{1,0:T(8,128)(2,1)}, u32[]{:S(2)}, u32[]{:S(2)}) %collective-permute-start.1) | collective-permute-done | bytes 2097184 | tf_op jit(solution)/shard_map/ppermute | solution.py:460
  140.2 76.6 %all-gather.3.cloned.1.call-done = bf16[4096,3328]{0,1:T(8,128)(2,1)} async-done(((bf16[256,3328]{0,1:T(8,128)(2,1)}), bf16[4096,3328]{0,1:T(8,128)(2,1)}) %all-gather.3.cloned.1.call-update) | async-done | bytes 27262992 | tf_op jit(solution)/shard_map/all_gather | solution.py:463
  222.0 10.3 fusion.64.refs_0_.refs_8_.refs_18_.refs_15_
  239.9 9.9 fusion.70.refs_0_.refs_8_.refs_19_.refs_1_.refs_16_
  276.4 9.9 fusion.73.refs_0_.refs_1_.refs_16_
  326.1 37.9 %all-gather.5.cloned.1.call-done = bf16[4096,3328]{0,1:T(8,128)(2,1)} async-done(((bf16[256,3328]{0,1:T(8,128)(2,1)}), bf16[4096,3328]{0,1:T(8,128)(2,1)}) %all-gather.5.cloned.1.call-update) | async-done | bytes 27262992 | tf_op jit(solution)/shard_map/all_gather | solution.py:463
  366.5 83.4 %collective-permute-done.7 = f32[512,1]{1,0:T(8,128)S(1)} collective-permute-done((f32[512,1]{1,0:T(8,128)S(1)}, f32[512,1]{1,0:T(8,128)S(1)}, u32[]{:S(2)}, u32[]{:S(2)}) %collective-permute-start.7) | collective-permute-done | bytes 2080 | tf_op jit(solution)/shard_map/ppermute | solution.py:460
  468.6 9.6 fusion.76.refs_0_.refs_8_.refs_18_.refs_15_
  521.4 9.9 fusion.85.refs_0_.refs_1_.refs_16_
  584.5 26.8 %mixer_backward.4 = (bf16[512,4608]{1,0:T(8,128)(2,1)}, f32[128,2048]{1,0:T(8,128)}, f32[8,2048]{1,0:T(8,128)}, f32[8,256]{1,0:T(8,128)}, f32[8,2048]{1,0:T(8,12...) custom-call(bf16[512,2048]{1,0:T(8,128)(2,1)} %fusion.79.refs_0_.refs_15_, bf16[512,2048]{1,0:T(8,128)(2,1)} %fusion.85.refs_0_.refs_1_.refs_16_, ...), custom_call_target="tpu_custom_call" | custom-call | flops 14680064000 | bytes 20971520 | tf_op jit(solution)/shard_map/mixer_backward/pallas_call | solution.py:422
  635.3 40.1 %collective-permute-done.17 = bf16[512,2048]{1,0:T(8,128)(2,1)S(1)} collective-permute-done((bf16[512,2048]{1,0:T(8,128)(2,1)S(1)}, bf16[512,2048]{1,0:T(8,128)(2,1)S(1)}, u32[]{:S(2)}, u32[]{:S(2)}) %collective-permute-start.17) | collective-permute-done | bytes 2097184 | tf_op jit(solution)/shard_map/ppermute | solution.py:460
  729.7 27.4 %mixer_backward.5 = (bf16[512,4608]{1,0:T(8,128)(2,1)}, f32[128,2048]{1,0:T(8,128)}, f32[8,2048]{1,0:T(8,128)}, f32[8,256]{1,0:T(8,128)}, f32[8,2048]{1,0:T(8,12...) custom-call(bf16[512,2048]{1,0:T(8,128)(2,1)} %fusion.76.refs_0_.refs_8_.refs_18_.refs_15_, ...), custom_call_target="tpu_custom_call" | custom-call | flops 14680064000 | bytes 20971520 | tf_op jit(solution)/shard_map/mixer_backward/pallas_call | solution.py:422
  769.9 9.5 add_convert_fusion.4
  779.8 13.3 convolution_convert_fusion.2
  793.1 14.9 convolution_convert_fusion.3
  808.0 11.6 pad_maximum_fusion.refs_21_
  819.6 27.0 %mixer_backward.6 = (bf16[512,4608]{1,0:T(8,128)(2,1)}, f32[128,2048]{1,0:T(8,128)}, f32[8,2048]{1,0:T(8,128)}, f32[8,256]{1,0:T(8,128)}, f32[8,2048]{1,0:T(8,12...) custom-call(bf16[512,2048]{1,0:T(8,128)(2,1)} %fusion.67.refs_0_.refs_15_, bf16[512,2048]{1,0:T(8,128)(2,1)} %fusion.73.refs_0_.refs_1_.refs_16_, ...), custom_call_target="tpu_custom_call" | custom-call | flops 14680064000 | bytes 20971520 | tf_op jit(solution)/shard_map/mixer_backward/pallas_call | solution.py:422
  846.6 9.7 fusion
  857.4 10.1 add_convert_fusion.1
  891.4 27.2 %mixer_backward.7 = (bf16[512,4608]{1,0:T(8,128)(2,1)}, f32[128,2048]{1,0:T(8,128)}, f32[8,2048]{1,0:T(8,128)}, f32[8,256]{1,0:T(8,128)}, f32[8,2048]{1,0:T(8,12...) custom-call(bf16[512,2048]{1,0:T(8,128)(2,1)} %fusion.64.refs_0_.refs_8_.refs_18_.refs_15_, ...), custom_call_target="tpu_custom_call" | custom-call | flops 14680064000 | bytes 20971520 | tf_op jit(solution)/shard_map/mixer_backward/pallas_call | solution.py:422
  927.8 10.5 broadcast_select_fusion
  942.3 40.8 %collective-permute-done.18 = bf16[512,2048]{1,0:T(8,128)(2,1)} collective-permute-done((bf16[512,2048]{1,0:T(8,128)(2,1)}, bf16[512,2048]{1,0:T(8,128)(2,1)}, u32[]{:S(2)}, u32[]{:S(2)}) %collective-permute-start.18) | collective-permute-done | bytes 2097184 | tf_op jit(solution)/shard_map/ppermute | solution.py:460
  1027.3 12.9 convolution_convert_fusion
  1040.2 14.7 convolution_convert_fusion.1
  1054.9 11.8 pad_maximum_fusion.1
  1073.4 42.9 %collective-permute-done.11 = f32[256,2048]{1,0:T(8,128)} collective-permute-done((f32[256,2048]{1,0:T(8,128)}, f32[256,2048]{1,0:T(8,128)}, u32[]{:S(2)}, u32[]{:S(2)}) %collective-permute-start.11) | collective-permute-done | bytes 2097184 | tf_op jit(solution)/shard_map/ppermute | solution.py:457
  1143.4 10.3 collective-permute-done.19
  1156.1 63.3 %reduce-scatter.11.cloned.1.call-done = bf16[256,1024]{1,0:T(8,128)(2,1)} async-done(((bf16[4096,1024]{1,0:T(8,128)(2,1)}), bf16[256,1024]{1,0:T(8,128)(2,1)}) %reduce-scatter.11.cloned.1.call-update) | async-done | bytes 524304 | tf_op jit(solution)/shard_map/reduce_scatter | solution.py:466
  1219.4 108.3 %reduce-scatter.9.cloned.1.call-done = bf16[256,1024]{1,0:T(8,128)(2,1)} async-done(((bf16[4096,1024]{1,0:T(8,128)(2,1)}), bf16[256,1024]{1,0:T(8,128)(2,1)}) %reduce-scatter.9.cloned.1.call-update) | async-done | bytes 524304 | tf_op jit(solution)/shard_map/reduce_scatter | solution.py:466
  1330.8 195.5 %reduce-scatter.7.cloned.1.call-done = bf16[256,2304]{1,0:T(8,128)(2,1)} async-done(((bf16[4096,2304]{1,0:T(8,128)(2,1)}), bf16[256,2304]{1,0:T(8,128)(2,1)}) %reduce-scatter.7.cloned.1.call-update) | async-done | bytes 1179664 | tf_op jit(solution)/shard_map/reduce_scatter | solution.py:466
  1539.4 185.1 %reduce-scatter.5.cloned.1.call-done = bf16[256,2304]{1,0:T(8,128)(2,1)} async-done(((bf16[4096,2304]{1,0:T(8,128)(2,1)}), bf16[256,2304]{1,0:T(8,128)(2,1)}) %reduce-scatter.5.cloned.1.call-update) | async-done | bytes 1179664 | tf_op jit(solution)/shard_map/reduce_scatter | solution.py:466
  (483 shorter events, 479.7 us)
Async XLA Ops:
  7.2 209.7 %all-gather.3.cloned.1.call-start = ((), (), s32[]{:S(2)}) async-start(), calls=%async_computation.4 | async-start | bytes 28966912 | tf_op jit(solution)/shard_map/all_gather | solution.py:463
  21.4 342.5 %all-gather.5.cloned.1.call-start = ((), (), s32[]{:S(2)}) async-start(), calls=%async_computation.5 | async-start | bytes 28966912 | tf_op jit(solution)/shard_map/all_gather | solution.py:463
  30.1 1102.3 %all-reduce.5.cloned.1.call-start = ((), (), s32[]{:S(2)}) async-start(), calls=%async_computation.10 | async-start | bytes 458752 | tf_op jit(solution)/shard_map/psum | solution.py:713
  33.4 51.9 %collective-permute-start = (bf16[256,2048]{1,0:T(8,128)(2,1)}, bf16[256,2048]{1,0:T(8,128)(2,1)}, u32[]{:S(2)}, u32[]{:S(2)}) collective-permute-start(bf16[256,2048]{1,0:T(8,128)(2,1)} %get-tuple-element.225), channel_id=1, source_target_pairs={{0,1},{1,0},{2,3},{3,2},{4,5},{5,4},{6,7},{7,6},{8,9},{9,8},{10,11... | collective-permute-start | bytes 3145736 | tf_op jit(solution)/shard_map/ppermute | solution.py:457
  36.6 53.2 %collective-permute-start.2 = (f32[2,6,1024]{2,1,0:T(8,128)}, f32[2,6,1024]{2,1,0:T(8,128)}, u32[]{:S(2)}, u32[]{:S(2)}) collective-permute-start(f32[2,6,1024]{2,1,0:T(8,128)} %pad_maximum_fusion.24), channel_id=1, source_target_pairs={{0,1},{1,0},{2,3},{3,2},{4,5},{5,4},{6,7},{7,6},{8,9},{9,8},{10,11... | collective-permute-start | bytes 147464 | tf_op jit(solution)/shard_map/ppermute | solution.py:457
  36.7 48.7 %collective-permute-start.3 = (f32[2,1,3,16]{3,0,2,1:T(2,128)S(1)}, f32[2,1,3,16]{3,0,2,1:T(2,128)S(1)}, u32[]{:S(2)}, u32[]{:S(2)}) collective-permute-start(f32[2,1,3,16]{3,0,2,1:T(2,128)S(1)} %maximum_bitcast_fusion.2), channel_id=1, source_target_pairs={{0,1},{1,0},{2,3},{3,2},{4,5},{5,4},{6,7},{7,6},{8,9},{9,8},{10,11... | collective-permute-start | bytes 1160 | tf_op jit(solution)/shard_map/ppermute | solution.py:457
  40.2 278.4 %collective-permute-start.12 = (bf16[256,2048]{1,0:T(8,128)(2,1)}, bf16[256,2048]{1,0:T(8,128)(2,1)}, u32[]{:S(2)}, u32[]{:S(2)}) collective-permute-start(bf16[256,2048]{1,0:T(8,128)(2,1)} %get-tuple-element.219), channel_id=1, source_target_pairs={{0,1},{1,0},{2,3},{3,2},{4,5},{5,4},{6,7},{7,6},{8,9},{9,8},{10,11... | collective-permute-start | bytes 3145736 | tf_op jit(solution)/shard_map/ppermute | solution.py:457
  40.4 490.9 %copy-start.3 = (bf16[128,128]{1,0:T(8,128)(2,1)}, bf16[128,128]{1,0:T(8,128)(2,1)S(1)}, u32[]{:S(2)}) copy-start(bf16[128,128]{1,0:T(8,128)(2,1)S(1)} %fusion.136.refs_6_.refs_14_) | copy-start | bytes 98308
  87.8 46.9 %collective-permute-start.1 = (bf16[512,2048]{1,0:T(8,128)(2,1)S(1)}, bf16[512,2048]{1,0:T(8,128)(2,1)}, u32[]{:S(2)}, u32[]{:S(2)}) collective-permute-start(bf16[512,2048]{1,0:T(8,128)(2,1)S(1)} %maximum_select_fusion.1), channel_id=1, source_target_pairs={{0,2},{1,3},{2,0},{3,1},{4,6},{5,7},{6,4},{7,5},{8,10},{9,11},{10,... | collective-permute-start | bytes 6291464 | tf_op jit(solution)/shard_map/ppermute | solution.py:460
  305.8 149.2 %collective-permute-start.6 = (bf16[512,2048]{1,0:T(8,128)(2,1)}, bf16[512,2048]{1,0:T(8,128)(2,1)}, u32[]{:S(2)}, u32[]{:S(2)}) collective-permute-start(bf16[512,2048]{1,0:T(8,128)(2,1)} %add_convert_fusion.7), channel_id=1, source_target_pairs={{0,2},{1,3},{2,0},{3,1},{4,6},{5,7},{6,4},{7,5},{8,10},{9,11},{10,... | collective-permute-start | bytes 6291464 | tf_op jit(solution)/shard_map/ppermute | solution.py:460
  317.8 140.7 %collective-permute-start.4 = (bf16[512,2048]{1,0:T(8,128)(2,1)}, bf16[512,2048]{1,0:T(8,128)(2,1)}, u32[]{:S(2)}, u32[]{:S(2)}) collective-permute-start(bf16[512,2048]{1,0:T(8,128)(2,1)} %add_convert_fusion.8), channel_id=1, source_target_pairs={{0,2},{1,3},{2,0},{3,1},{4,6},{5,7},{6,4},{7,5},{8,10},{9,11},{10,... | collective-permute-start | bytes 6291464 | tf_op jit(solution)/shard_map/ppermute | solution.py:460
  322.6 236.3 %collective-permute-start.13 = (bf16[512,2048]{1,0:T(8,128)(2,1)}, bf16[512,2048]{1,0:T(8,128)(2,1)}, u32[]{:S(2)}, u32[]{:S(2)}) collective-permute-start(bf16[512,2048]{1,0:T(8,128)(2,1)} %maximum_select_fusion.2), channel_id=1, source_target_pairs={{0,2},{1,3},{2,0},{3,1},{4,6},{5,7},{6,4},{7,5},{8,10},{9,11},{10,... | collective-permute-start | bytes 6291464 | tf_op jit(solution)/shard_map/ppermute | solution.py:460
  323.9 126.1 %collective-permute-start.7 = (f32[512,1]{1,0:T(8,128)S(1)}, f32[512,1]{1,0:T(8,128)S(1)}, u32[]{:S(2)}, u32[]{:S(2)}) collective-permute-start(f32[512,1]{1,0:T(8,128)S(1)} %add.289), channel_id=1, source_target_pairs={{0,2},{1,3},{2,0},{3,1},{4,6},{5,7},{6,4},{7,5},{8,10},{9,11},{10,... | collective-permute-start | bytes 6152 | tf_op jit(solution)/shard_map/ppermute | solution.py:460
  324.8 130.0 %collective-permute-start.5 = (f32[512,1]{1,0:T(8,128)S(1)}, f32[512,1]{1,0:T(8,128)S(1)}, u32[]{:S(2)}, u32[]{:S(2)}) collective-permute-start(f32[512,1]{1,0:T(8,128)S(1)} %add.282), channel_id=1, source_target_pairs={{0,2},{1,3},{2,0},{3,1},{4,6},{5,7},{6,4},{7,5},{8,10},{9,11},{10,... | collective-permute-start | bytes 6152 | tf_op jit(solution)/shard_map/ppermute | solution.py:460
  539.5 19.1 %collective-permute-start.10 = (f32[512,1]{1,0:T(8,128)S(1)}, f32[512,1]{1,0:T(8,128)S(1)}, u32[]{:S(2)}, u32[]{:S(2)}) collective-permute-start(f32[512,1]{1,0:T(8,128)S(1)} %add.303), channel_id=1, source_target_pairs={{0,2},{1,3},{2,0},{3,1},{4,6},{5,7},{6,4},{7,5},{8,10},{9,11},{10,... | collective-permute-start | bytes 6152 | tf_op jit(solution)/shard_map/ppermute | solution.py:460
  541.0 17.5 %collective-permute-start.9 = (f32[512,1]{1,0:T(8,128)S(1)}, f32[512,1]{1,0:T(8,128)S(1)}, u32[]{:S(2)}, u32[]{:S(2)}) collective-permute-start(f32[512,1]{1,0:T(8,128)S(1)} %add.300), channel_id=1, source_target_pairs={{0,2},{1,3},{2,0},{3,1},{4,6},{5,7},{6,4},{7,5},{8,10},{9,11},{10,... | collective-permute-start | bytes 6152 | tf_op jit(solution)/shard_map/ppermute | solution.py:460
  574.2 9.5 collective-permute-start.15
  583.7 51.6 %collective-permute-start.8 = (bf16[512,2048]{1,0:T(8,128)(2,1)}, bf16[512,2048]{1,0:T(8,128)(2,1)S(1)}, u32[]{:S(2)}, u32[]{:S(2)}) collective-permute-start(bf16[512,2048]{1,0:T(8,128)(2,1)} %get-tuple-element.278), channel_id=1, source_target_pairs={{0,2},{1,3},{2,0},{3,1},{4,6},{5,7},{6,4},{7,5},{8,10},{9,11},{10,... | collective-permute-start | bytes 6291464 | tf_op jit(solution)/shard_map/ppermute | solution.py:460
  629.4 46.0 %collective-permute-start.17 = (bf16[512,2048]{1,0:T(8,128)(2,1)S(1)}, bf16[512,2048]{1,0:T(8,128)(2,1)S(1)}, u32[]{:S(2)}, u32[]{:S(2)}) collective-permute-start(bf16[512,2048]{1,0:T(8,128)(2,1)S(1)} %add_convert_fusion.3), channel_id=1, source_target_pairs={{0,2},{1,3},{2,0},{3,1},{4,6},{5,7},{6,4},{7,5},{8,10},{9,11},{10,... | collective-permute-start | bytes 6291464 | tf_op jit(solution)/shard_map/ppermute | solution.py:460
  713.4 14.5 collective-permute-start.14
  779.4 88.1 %collective-permute-start.16 = (bf16[512,2048]{1,0:T(8,128)(2,1)S(1)}, bf16[512,2048]{1,0:T(8,128)(2,1)}, u32[]{:S(2)}, u32[]{:S(2)}) collective-permute-start(bf16[512,2048]{1,0:T(8,128)(2,1)S(1)} %add_convert_fusion.4), channel_id=1, source_target_pairs={{0,2},{1,3},{2,0},{3,1},{4,6},{5,7},{6,4},{7,5},{8,10},{9,11},{10,... | collective-permute-start | bytes 6291464 | tf_op jit(solution)/shard_map/ppermute | solution.py:460
  938.2 44.8 %collective-permute-start.18 = (bf16[512,2048]{1,0:T(8,128)(2,1)}, bf16[512,2048]{1,0:T(8,128)(2,1)}, u32[]{:S(2)}, u32[]{:S(2)}) collective-permute-start(bf16[512,2048]{1,0:T(8,128)(2,1)} %get-tuple-element.284), channel_id=1, source_target_pairs={{0,2},{1,3},{2,0},{3,1},{4,6},{5,7},{6,4},{7,5},{8,10},{9,11},{10,... | collective-permute-start | bytes 6291464 | tf_op jit(solution)/shard_map/ppermute | solution.py:460
  988.0 231.4 %reduce-scatter.11.cloned.1.call-start = ((), (), s32[]{:S(2)}) async-start(), calls=%async_computation.9 | async-start | bytes 8912896 | tf_op jit(solution)/shard_map/reduce_scatter | solution.py:466
  995.8 331.9 %reduce-scatter.9.cloned.1.call-start = ((), (), s32[]{:S(2)}) async-start(), calls=%async_computation.8 | async-start | bytes 8912896 | tf_op jit(solution)/shard_map/reduce_scatter | solution.py:466
  1019.9 506.4 %reduce-scatter.7.cloned.1.call-start = ((), (), s32[]{:S(2)}) async-start(), calls=%async_computation.7 | async-start | bytes 20054016 | tf_op jit(solution)/shard_map/reduce_scatter | solution.py:466
  1020.5 704.1 %reduce-scatter.5.cloned.1.call-start = ((), (), s32[]{:S(2)}) async-start(), calls=%async_computation.6 | async-start | bytes 20054016 | tf_op jit(solution)/shard_map/reduce_scatter | solution.py:466
  1071.7 44.6 %collective-permute-start.11 = (f32[256,2048]{1,0:T(8,128)}, f32[256,2048]{1,0:T(8,128)}, u32[]{:S(2)}, u32[]{:S(2)}) collective-permute-start(f32[256,2048]{1,0:T(8,128)} %get-tuple-element.211), channel_id=1, source_target_pairs={{0,1},{1,0},{2,3},{3,2},{4,5},{5,4},{6,7},{7,6},{8,9},{9,8},{10,11... | collective-permute-start | bytes 6291464 | tf_op jit(solution)/shard_map/ppermute | solution.py:457
  1130.6 23.1 %collective-permute-start.19 = (bf16[256,2048]{1,0:T(8,128)(2,1)S(1)}, bf16[256,2048]{1,0:T(8,128)(2,1)S(1)}, u32[]{:S(2)}, u32[]{:S(2)}) collective-permute-start(bf16[256,2048]{1,0:T(8,128)(2,1)S(1)} %get-tuple-element.217), channel_id=1, source_target_pairs={{0,1},{1,0},{2,3},{3,2},{4,5},{5,4},{6,7},{7,6},{8,9},{9,8},{10,11... | collective-permute-start | bytes 3145736 | tf_op jit(solution)/shard_map/ppermute | solution.py:457
  1527.9 5.6 collective-permute-start.22
  1534.4 5.0 collective-permute-start.23
  1727.2 5.4 collective-permute-start.20
  1732.5 5.0 collective-permute-start.21
  (105 other events, 5020.7 us)
Sparse Core Ops, SparseCore 0:
  21.5 195.2 all-gather.2
  218.9 144.9 all-gather.4
  988.1 121.8 all-reduce.4
  1113.9 105.4 reduce-scatter.10
  1223.3 104.3 reduce-scatter.8
  1331.6 194.6 reduce-scatter.6
  1530.5 194.0 reduce-scatter.4

commit v3 on v2

--- a/solution.py
+++ b/solution.py
@@ -16,6 +16,7 @@
 BF16 = jnp.bfloat16
 NN = (((1,), (0,)), ((), ()))
 NT = (((1,), (1,)), ((), ()))
+MESH = pl.DeviceIdType.MESH
 TN = (((0,), (0,)), ((), ()))
 
 
@@ -442,12 +443,231 @@
     )(*operands)
 
 
+def stacked_product(lhs, rhs, shards):
+    features, tokens = lhs[0].shape
+    columns = sum(part.shape[1] for part in rhs[0]) // shards
+    whole_rows = len(rhs[0]) == 1
+    row_tile = min(512, features)
+    tile = columns // 2 if columns % 256 == 0 else columns
+    tiles = columns // tile
+    chunks = len(lhs)
+
+    def kernel(*refs):
+        out_ref = refs[-1]
+        shard = pl.program_id(0)
+        total = 0.0
+        for at in range(chunks):
+            rows = refs[at][...]
+            if whole_rows:
+                total = total + mm(rows, refs[chunks + at][...])
+            else:
+                pair = refs[chunks + 2 * at : chunks + 2 * at + 2]
+                total = total + mm(rows, jnp.where(shard == 0, pair[0][...], pair[1][...]))
+        out_ref[0] = total.astype(BF16)
+
+    lhs_spec = pl.BlockSpec((row_tile, tokens), lambda s, n, m: (m, 0))
+    if whole_rows:
+        rhs_spec = pl.BlockSpec((tokens, tile), lambda s, n, m: (0, s * tiles + n))
+    else:
+        rhs_spec = pl.BlockSpec((tokens, tile), lambda s, n, m: (0, n))
+    parts = [part for chunk in rhs for part in chunk]
+    return pl.pallas_call(
+        kernel,
+        grid=(shards, tiles, features // row_tile),
+        in_specs=[lhs_spec] * chunks + [rhs_spec] * len(parts),
+        out_specs=pl.BlockSpec((1, row_tile, tile), lambda s, n, m: (s, m, n)),
+        out_shape=jax.ShapeDtypeStruct((shards, features, columns), BF16),
+        compiler_params=pltpu.CompilerParams(vmem_limit_bytes=48 * 1024 * 1024),
+        cost_estimate=pl.CostEstimate(
+            flops=2 * shards * features * columns * tokens * chunks,
+            bytes_accessed=2 * shards * (features * columns + chunks * tokens * columns + chunks * features * tokens),
+            transcendentals=0,
+        ),
+        name="stacked_product",
+    )(*lhs, *parts)
+
+
+def reduce_kernel(chips, groups, hops, parts, *refs):
+    lhs, rhs, vec_ref = refs[:parts], refs[parts : 2 * parts], refs[2 * parts]
+    (out_ref, vec_out, pair_out, pair_in, own, chip_out, chip_in, vec_send, vec_recv,
+     pair_send_sem, pair_recv_sem, chip_send_sem, chip_recv_sem, vec_send_sem, vec_recv_sem) = refs[2 * parts + 1 :]
+    rows, columns = out_ref.shape
+    dp, tensor = lax.axis_index("dp"), lax.axis_index("tensor")
+    chip, core = dp // 2, dp % 2
+    shard, group = tensor % 2, tensor // 2
+    tile = columns // 3 if columns % 384 == 0 else columns
+
+    def core_device():
+        return (dp + 1 - 2 * core, tensor)
+
+    def pair_device():
+        return (dp, tensor + 1 - 2 * shard)
+
+    def chip_device(hop):
+        return ((chip + hop) % chips * 2 + core, tensor)
+
+    def group_device(hop):
+        return (dp, (group + hop) % groups * 2 + shard)
+
+    partners = [core_device(), pair_device()]
+    partners += [chip_device(hop) for hop in range(1, chips)] + [group_device(hop) for hop in range(1, groups)]
+    barrier = pltpu.get_barrier_semaphore()
+    for partner in partners:
+        pl.semaphore_signal(barrier, inc=1, device_id=partner, device_id_type=MESH)
+    pl.semaphore_wait(barrier, len(partners))
+
+    def copy(src, dst, send_sem, recv_sem, device):
+        return pltpu.make_async_remote_copy(
+            src_ref=src, dst_ref=dst, send_sem=send_sem, recv_sem=recv_sem, device_id=device, device_id_type=MESH
+        )
+
+    stages = [[core_device()], [pair_device()], [chip_device(hop) for hop in range(1, chips)]]
+    stages.append([group_device(hop) for hop in range(1, groups)])
+    firsts = [sum(len(stage) for stage in stages[:at]) for at in range(4)]
+
+    def vec_copies(stage):
+        return [
+            copy(vec_send.at[stage], vec_recv.at[firsts[stage] + at], vec_send_sem.at[firsts[stage] + at],
+                 vec_recv_sem.at[firsts[stage] + at], device)
+            for at, device in enumerate(stages[stage])
+        ]
+
+    def vec_start(stage):
+        for each in vec_copies(stage):
+            each.start()
+
+    def vec_finish(stage):
+        total = vec_send[stage]
+        for at, each in enumerate(vec_copies(stage)):
+            each.wait()
+            total = total + vec_recv[firsts[stage] + at]
+        if stage < 3:
+            vec_send[stage + 1] = total
+            vec_start(stage + 1)
+        else:
+            vec_out[...] = total
+
+    vec_send[0] = vec_ref[...]
+    vec_start(0)
+
+    def product(piece_rows, at):
+        total = 0.0
+        for part in range(parts):
+            total = total + mm(lhs[part][piece_rows, :], rhs[part][:, pl.ds(at, tile)])
+        return total
+
+    def pair_copy(piece):
+        return copy(pair_out.at[piece % 2], pair_in.at[piece], pair_send_sem.at[piece], pair_recv_sem.at[piece], pair_device())
+
+    def chip_copy(hop):
+        return copy(chip_out.at[hop - 1], chip_in.at[hop - 1], chip_send_sem.at[hop - 1], chip_recv_sem.at[hop - 1], chip_device(hop))
+
+    def take_pair(piece):
+        pair_copy(piece).wait_recv()
+        hop = hops[piece]
+
+        @pl.loop(0, columns // tile)
+        def _(step):
+            at = pl.ds(pl.multiple_of(step * tile, 128), tile)
+            total = own[piece % 2, :, at] + pair_in[piece, :, at].astype(F32)
+            if hop:
+                chip_out[hop - 1, :, at] = total.astype(BF16)
+            else:
+                own[piece % 2, :, at] = total
+
+        if hop:
+            chip_copy(hop).start()
+
+    for piece, hop in enumerate(hops):
+        piece_rows = pl.ds(pl.multiple_of((chip + hop) % chips * rows, rows), rows)
+        if piece >= 2:
+            pair_copy(piece - 2).wait_send()
+
+        @pl.loop(0, columns // tile)
+        def _(step):
+            at = pl.multiple_of(step * tile, 128)
+            column = pl.multiple_of((1 - shard) * columns + at, 128)
+            pair_out[piece % 2, :, pl.ds(at, tile)] = product(piece_rows, column).astype(BF16)
+
+        pair_copy(piece).start()
+
+        @pl.loop(0, columns // tile)
+        def _(step):
+            at = pl.multiple_of(step * tile, 128)
+            column = pl.multiple_of(shard * columns + at, 128)
+            own[piece % 2, :, pl.ds(at, tile)] = product(piece_rows, column)
+
+        if piece:
+            take_pair(piece - 1)
+        if piece < 4:
+            vec_finish(piece)
+    last = len(hops) - 1
+    for stage in range(len(hops), 4):
+        vec_finish(stage)
+    take_pair(last)
+    for hop in range(1, chips):
+        chip_copy(hop).wait_recv()
+
+    @pl.loop(0, columns // tile)
+    def _(step):
+        at = pl.ds(pl.multiple_of(step * tile, 128), tile)
+        total = own[last % 2, :, at]
+        for hop in range(1, chips):
+            total = total + chip_in[hop - 1, :, at].astype(F32)
+        out_ref[:, at] = total
+
+    for piece in range(max(0, last - 1), last + 1):
+        pair_copy(piece).wait_send()
+    for hop in range(1, chips):
+        chip_copy(hop).wait_send()
+
+
+def reduced_product(place, lhs, rhs, vec):
+    chips, groups = place.chips, place.groups
+    rows, columns = lhs[0].shape[0] // chips, rhs[0].shape[1] // 2
+    hops = sorted(range(chips), key=lambda hop: -min(hop, chips - hop))
+    parts = len(lhs)
+    vecs = 1 + 1 + (chips - 1) + (groups - 1)
+    vmem = pl.BlockSpec(memory_space=pltpu.VMEM)
+    return pl.pallas_call(
+        functools.partial(reduce_kernel, chips, groups, hops, parts),
+        in_specs=[vmem] * (2 * parts + 1),
+        out_specs=[vmem] * 2,
+        out_shape=[jax.ShapeDtypeStruct((rows, columns), F32), jax.ShapeDtypeStruct(vec.shape, F32)],
+        scratch_shapes=[
+            pltpu.VMEM((2, rows, columns), BF16),
+            pltpu.VMEM((chips, rows, columns), BF16),
+            pltpu.VMEM((2, rows, columns), F32),
+            pltpu.VMEM((chips - 1, rows, columns), BF16),
+            pltpu.VMEM((chips - 1, rows, columns), BF16),
+            pltpu.VMEM((4,) + vec.shape, F32),
+            pltpu.VMEM((vecs,) + vec.shape, F32),
+            pltpu.SemaphoreType.DMA((chips,)),
+            pltpu.SemaphoreType.DMA((chips,)),
+            pltpu.SemaphoreType.DMA((chips - 1,)),
+            pltpu.SemaphoreType.DMA((chips - 1,)),
+            pltpu.SemaphoreType.DMA((vecs,)),
+            pltpu.SemaphoreType.DMA((vecs,)),
+        ],
+        compiler_params=pltpu.CompilerParams(
+            collective_id=0, has_side_effects=True, vmem_limit_bytes=58 * 1024 * 1024
+        ),
+        cost_estimate=pl.CostEstimate(
+            flops=4 * chips * rows * columns * parts * lhs[0].shape[1], bytes_accessed=100 * 1024 * 1024, transcendentals=0
+        ),
+        name="reduced_product",
+    )(*lhs, *rhs, vec)
+
+
 class Place:
     def __init__(self):
         self.members = lax.axis_size("tensor")
         self.groups = self.members // 2
         self.sequence = lax.axis_index("tensor") % 2
         self.group = lax.axis_index("tensor") // 2
+        self.chips = lax.axis_size("dp") // 2
+        self.chip = lax.axis_index("dp") // 2
+        self.core = lax.axis_index("dp") % 2
         copies = lax.axis_size("dp")
         self.owners = [
             [d * self.members + 2 * g + s for s in range(2) for d in range(copies)] for g in range(self.groups)
@@ -459,11 +679,25 @@
     def to_group(self, v, hop):
         return lax.ppermute(v, "tensor", [(t, (t + 2 * hop) % self.members) for t in range(self.members)])
 
+    def to_core(self, v):
+        return lax.ppermute(v, "dp", [(t, t ^ 1) for t in range(2 * self.chips)])
+
+    def to_chip(self, v, hop):
+        count = 2 * self.chips
+        return lax.ppermute(v, "dp", [(t, (t + 2 * hop) % count) for t in range(count)])
+
+    def core_rows(self, v):
+        parts = v.reshape(self.chips, 2, -1, v.shape[1])
+        near = lax.dynamic_index_in_dim(parts, self.core, 1, keepdims=False)
+        far = lax.dynamic_index_in_dim(parts, 1 - self.core, 1, keepdims=False)
+        return near.reshape(-1, v.shape[1]), far.reshape(-1, v.shape[1])
+
+    def scatter_owners(self, v):
+        v = v.reshape(-1, v.shape[-1])
+        return lax.psum_scatter(v, ("dp", "tensor"), scatter_dimension=0, axis_index_groups=self.owners, tiled=True)
+
     def gather_owners(self, v):
         return lax.all_gather(v, ("dp", "tensor"), axis=0, axis_index_groups=self.owners, tiled=True)
-
-    def scatter_owners(self, v):
-        return lax.psum_scatter(v, ("dp", "tensor"), scatter_dimension=0, axis_index_groups=self.owners, tiled=True)
 
     def add_groups(self, v):
         return v + sum(self.to_group(v, hop) for hop in range(1, self.groups))
@@ -511,6 +745,44 @@
         mine = jnp.where(self.sequence == 0, first, second)
         other = self.to_pair(jnp.where(self.sequence == 0, second, first))
         return jnp.where(self.sequence == 0, jnp.stack([mine, other]), jnp.stack([other, mine]))
+
+
+def then(v, *earlier):
+    return lax.optimization_barrier((v, earlier))[0]
+
+
+class LastSum:
+
+    def __init__(self, place, features, columns):
+        self.place = place
+        rows = [place.core_rows(part) for part in features]
+        self.lhs = [near for near, far in rows] + [place.to_core(far) for near, far in rows]
+        self.rhs = [part for part in columns] + [[place.to_core(shard) for shard in part] for part in columns]
+
+    def by_permutes(self):
+        self.stack = stacked_product(self.lhs, self.rhs, 2)
+        return self.stack
+
+    def to_pair(self):
+        other = lax.dynamic_index_in_dim(self.stack, 1 - self.place.sequence, 0, keepdims=False)
+        self.landed = self.place.to_pair(other)
+        return other
+
+    def to_chips(self):
+        place = self.place
+        own = lax.dynamic_index_in_dim(self.stack, place.sequence, 0, keepdims=False)
+        total = (own.astype(F32) + self.landed.astype(F32)).astype(BF16)
+        pieces = total.reshape(place.chips, -1, total.shape[1])
+        self.kept = lax.dynamic_index_in_dim(pieces, place.chip, 0, keepdims=False)
+        hops = range(1, place.chips)
+        self.sent = [
+            lax.dynamic_index_in_dim(pieces, (place.chip + hop) % place.chips, 0, keepdims=False) for hop in hops
+        ]
+        self.arrived = [place.to_chip(piece, hop) for piece, hop in zip(self.sent, hops)]
+        return self.sent
+
+    def total(self):
+        return self.kept.astype(F32) + sum(piece.astype(F32) for piece in self.arrived)
 
 
 def norm_scale(stream):
@@ -535,8 +807,9 @@
     shares, scales = [], []
     for at in range(len(streams)):
         first, second = halves[0][at], halves[1][at]
-        shares.append((mm(first[1], out_rows[0], NT) + mm(second[1], out_rows[1], NT)).astype(BF16))
         scales.append(lax.rsqrt(place.add_groups(first[2] + second[2]) / inner + EPSILON))
+        share = (mm(first[1], out_rows[0], NT) + mm(second[1], out_rows[1], NT)).astype(BF16)
+        shares.append(then(share, scales[at]))
         for key, position in (("columns", 0), ("mixed", 1), ("y", 3), ("saved", 4)):
             kept[key].append((first[position], second[position]))
     kept.update(normed=normed, small=small, scale=scales)
@@ -548,66 +821,54 @@
     return after, kept
 
 
-def block_backward(place, grads, weights, tables, heads, inner, kept, final, first, after):
-    in_cols, small_cols, out_rows, gain = weights
-    chunks = len(grads)
-    scales = kept["scale"]
-    ups = [(grad * scale).astype(BF16) for grad, scale in zip(grads, scales)]
-    grad_mixed = [[mm(up, rows) for rows in out_rows] for up in ups]
-    if final:
-        pulls = [
-            sum(jnp.sum(g * m.astype(F32), axis=-1, keepdims=True) for g, m in zip(*pairs))
-            for pairs in zip(grad_mixed, kept["mixed"])
-        ]
-        pulls = [place.add_groups(pull) for pull in pulls]
-    else:
-        pulls = [jnp.sum(up.astype(F32) * u, axis=-1, keepdims=True) for up, u in zip(ups, kept["update"])]
-    pulls = [pull * (scale * scale / inner) for pull, scale in zip(pulls, scales)]
-    up = jnp.concatenate(ups)
-    mixed = [jnp.concatenate([part[half_no] for part in kept["mixed"]]) for half_no in range(2)]
-    grad_out = jnp.concatenate([mm(up, part, TN).astype(BF16) for part in mixed])
-    out_owned = place.scatter_owners(grad_out)
-
-    dcolumns, shares = [None] * chunks, [None] * chunks
-    carried = None
-    for at in reversed(range(chunks)):
-        early = (*kept["columns"][at - 1], kept["small"][at - 1]) if at else None
+def norm_backward(stream, grad, grad_normed, gain):
+    row_scale = norm_scale(stream)
+    unit = stream * row_scale
+    lifted = grad_normed * gain
+    back = grad + row_scale * (lifted - unit * jnp.mean(lifted * unit, axis=-1, keepdims=True))
+    return back, jnp.sum(grad_normed * unit, axis=0)
+
+
+class Backward:
+    def __init__(self, place, weights, tables, heads, inner, kept):
+        self.place, self.weights, self.tables, self.heads, self.inner, self.kept = place, weights, tables, heads, inner, kept
+        chunks = len(kept["normed"])
+        self.ups, self.grad_mixed, self.pulls = [None] * chunks, [None] * chunks, [None] * chunks
+        self.dcolumns, self.shares = [None] * chunks, [None] * chunks
+        self.carried = None
+
+    def enter(self, at, grad):
+        scale = self.kept["scale"][at]
+        self.ups[at] = (grad * scale).astype(BF16)
+        self.grad_mixed[at] = [mm(self.ups[at], rows) for rows in self.weights[2]]
+        if self.kept["update"]:
+            pull = jnp.sum(self.ups[at].astype(F32) * self.kept["update"][at], axis=-1, keepdims=True)
+        else:
+            pairs = zip(self.grad_mixed[at], self.kept["mixed"][at])
+            pull = sum(jnp.sum(g * m.astype(F32), axis=-1, keepdims=True) for g, m in pairs)
+            pull = self.place.add_groups(pull)
+        self.pulls[at] = pull * (scale * scale / self.inner)
+
+    def mix(self, at, after=()):
+        kept = self.kept
         result = mixer_backward(
             kept["columns"][at],
             kept["small"][at],
             kept["y"][at],
             kept["saved"][at],
-            grad_mixed[at],
-            pulls[at],
-            tables,
-            heads,
-            early,
-            carried,
-            after[at],
+            self.grad_mixed[at],
+            self.pulls[at],
+            self.tables,
+            self.heads,
+            (*kept["columns"][at - 1], kept["small"][at - 1]) if at else None,
+            self.carried,
+            after,
         )
-        dcolumns[at], carried = jnp.split(result[0], 2, axis=1), result[1:]
-        shares[at] = sum(mm(part, cols, NT) for part, cols in zip(dcolumns[at], in_cols)).astype(BF16)
-    normed = jnp.concatenate(kept["normed"])
-    joined = [jnp.concatenate([part[half_no] for part in dcolumns]) for half_no in range(2)]
-    grad_in = jnp.concatenate([mm(normed, part, TN).astype(BF16) for part in joined])
-    in_owned = place.scatter_owners(grad_in)
-
-    streams = kept["stream"]
-    if first:
-        streams, grads = [place.rows_of(streams, 0)], [place.rows_of(grads, 0)]
-        sums = [place.scatter_rows(shares)]
-    else:
-        sums = [place.sum_groups(share) for share in shares]
-    grad_gain, results = 0.0, []
-    for stream, grad, grad_normed in zip(streams, grads, sums):
-        row_scale = norm_scale(stream)
-        unit = stream * row_scale
-        grad_gain = grad_gain + jnp.sum(grad_normed * unit, axis=0)
-        lifted = grad_normed * gain
-        results.append(grad + row_scale * (lifted - unit * jnp.mean(lifted * unit, axis=-1, keepdims=True)))
-    if not first:
-        grad_gain = jnp.where(place.group == 0, grad_gain, 0.0)
-    return results, (in_owned, out_owned, grad_gain, carried[3:], grad_in)
+        self.dcolumns[at], self.carried = result[0], result[1:]
+
+    def share(self, columns):
+        parts = jnp.split(columns, 2, axis=1)
+        return sum(mm(part, cols, NT) for part, cols in zip(parts, self.weights[0])).astype(BF16)
 
 
 def local(
@@ -672,45 +933,79 @@
             head += [pair, jnp.zeros((6, 128), F32)]
         tables.append((chan, taps, jnp.concatenate(head), expand, tri))
 
-    last_up = place.gather_chunks(place.take_sequence(cotangent), PIECES)
     kept = []
     for layer in range(layers):
-        streams, saved = block_forward(
-            place, streams, weights[layer], tables[layer], heads, inner, layer == layers - 1
-        )
+        final = layer == layers - 1
+        if layer == 0:
+            last_up = place.take_sequence(then(cotangent, streams))
+            last_up = place.gather_chunks(last_up, PIECES)
+        streams, saved = block_forward(place, streams, weights[layer], tables[layer], heads, inner, final)
         kept.append(saved)
-    mixed_out = place.give_sequence(streams)
+    mixed_out = place.give_sequence(streams.astype(BF16)).astype(F32)
 
     grads = [part.astype(F32) for part in last_up]
-    taken = [None] * layers
-    after = [()] * PIECES
+    in_grads, out_grads, gain_grads, carried = [None] * layers, [None] * layers, [None] * layers, [None] * layers
     for layer in reversed(range(layers)):
-        grads, taken[layer] = block_backward(
-            place,
-            grads,
-            weights[layer],
-            tables[layer],
-            heads,
-            inner,
-            kept[layer],
-            layer == layers - 1,
-            layer == 0,
-            after,
-        )
-        after = [()] * (PIECES - 1) + [(taken[layer][-1],)]
-    grad_hidden = place.give_sequence(grads[0].astype(BF16)).astype(F32)
+        back = Backward(place, weights[layer], tables[layer], heads, inner, kept[layer])
+        for at in reversed(range(PIECES)):
+            back.enter(at, grads[at])
+        streams, gain, mixed = kept[layer]["stream"], weights[layer][3], kept[layer]["mixed"]
+        turned = [part.T for part in kept[layer]["normed"]]
+        ups = [part.T for part in back.ups]
+        if layer:
+            out_stack = stacked_product(ups, mixed, 2)
+            out_grads[layer] = place.scatter_owners(out_stack)
+            held = (out_stack,)
+            for at in reversed(range(PIECES)):
+                back.mix(at, held)
+                back.shares[at] = back.share(back.dcolumns[at])
+                held = (back.shares[at],)
+            in_stack = stacked_product(then(tuple(turned), *back.shares), [[part] for part in back.dcolumns], 2)
+            in_grads[layer] = place.scatter_owners(in_stack)
+            sums = then(tuple(place.sum_groups(share) for share in back.shares), in_stack)
+            results = [norm_backward(*parts, gain) for parts in zip(streams, grads, sums)]
+            grads = [result[0] for result in results]
+            gain_grads[layer] = jnp.where(place.group == 0, sum(result[1] for result in results), 0.0)
+        else:
+            out_sum = LastSum(place, ups, mixed)
+            held = (out_sum.by_permutes(), out_sum.to_pair())
+            for at in reversed(range(PIECES)):
+                back.mix(at, held)
+                held = ()
+            if len(back.dcolumns) == place.groups:
+                sent = [back.share(place.rows_of(back.dcolumns, hop)) for hop in range(1, place.groups)]
+                own = back.share(then(place.rows_of(back.dcolumns, 0), *sent))
+            else:
+                shares = [back.share(columns) for columns in back.dcolumns]
+                sent = [place.rows_of(shares, hop) for hop in range(1, place.groups)]
+                own = place.rows_of(shares, 0)
+            arrived = [place.to_group(piece, hop) for hop, piece in enumerate(sent, 1)]
+            in_sum = LastSum(place, turned, [[part] for part in back.dcolumns])
+            out_sent = out_sum.to_chips()
+            grad_normed = own.astype(F32) + sum(piece.astype(F32) for piece in arrived)
+            grad, gain_grads[layer] = norm_backward(
+                place.rows_of(streams, 0), place.rows_of(grads, 0), grad_normed, gain
+            )
+        carried[layer] = back.carried[3:]
+    grad_hidden = place.give_sequence(grad.astype(BF16)).astype(F32)
 
     slots, sizes = [], []
     for layer in range(layers):
-        gchan, gtaps, ghead = taken[layer][3]
+        gchan, gtaps, ghead = carried[layer]
         skips = gchan[5].reshape(2, heads, width).sum(axis=2)
         mine = jnp.stack([ghead[0, :heads], ghead[8, :heads], ghead[1, :heads], ghead[9, :heads], skips[0], skips[1]])
         channels = jnp.concatenate([gchan[:5].reshape(-1), gchan[6], mine.reshape(-1)])
         slot = lax.broadcasted_iota(jnp.int32, (place.groups, 1), 0) == place.group
         slotted = jnp.where(slot, channels[None], 0.0).reshape(-1)
-        slots.append(jnp.concatenate([slotted, gtaps[:5].reshape(-1), taken[layer][2]]))
+        slots.append(jnp.concatenate([slotted, gtaps[:5].reshape(-1), gain_grads[layer]]))
         sizes = [channels.size, gtaps[:5].size]
-    totals = [lax.psum(slot, ("dp", "tensor")) for slot in slots]
+    vec = jnp.concatenate(slots)
+    count = -(-vec.size // 1024) * 1024
+    vec = jnp.concatenate([vec, jnp.zeros((count - vec.size,), F32)]).reshape(-1, 128)
+    vec = then(vec, *out_sent)
+    in_grads[0], vec = reduced_product(place, in_sum.lhs, [part for (part,) in in_sum.rhs], vec)
+    out_grads[0] = out_sum.total()
+    totals = jnp.split(vec.reshape(-1)[: layers * slots[0].size], layers)
 
     outs = []
     for layer in range(layers):
@@ -723,8 +1018,7 @@
         per_channel_part = lax.dynamic_index_in_dim(per_channel_part, place.sequence, 1, keepdims=False)
         per_head_part = channels[6 * main :].reshape(3, 2, heads)
         per_head_part = lax.dynamic_index_in_dim(per_head_part, place.sequence, 1, keepdims=False)
-        in_owned, out_owned = taken[layer][:2]
-        in_owned = in_owned.astype(F32)
+        in_owned, out_owned = in_grads[layer].astype(F32), out_grads[layer].astype(F32)
         state_part = place.both(place.add_groups(in_owned[:, main : main + half]), 1)
         outs.append(
             (
@@ -738,7 +1032,7 @@
                 per_head_part[1],
                 per_head_part[2],
                 per_channel_part[5],
-                out_owned.astype(F32).T,
+                out_owned.T,
             )
         )
     return (mixed_out, grad_hidden) + tuple(jnp.stack(parts) for parts in zip(*outs))

time: 1750 us -> 1240 us (0.71)
  waiting for transfers between devices: 986 us -> 291 us
  Pallas kernels: 172 us -> 414 us
  matrix products: 337 us -> 262 us
  local copies, waits for them, and re-layouts: 64.1 us -> 100 us
  other arithmetic: 141 us -> 112 us
    reduce_scatter x4 -> x2, waiting for transfers between devices: 552 us -> 0.02 us  [scatter_owners(): lax.psum_scatter(v, ('dp', 'tensor'), scatter_dimension=0, axis_index_gro...]
    pallas_call x0 -> x4, Pallas kernels: none -> 241 us  [the longest x1 176 us: reduced_product(): pl.pallas_call(functools.partial(reduce_kernel, chips, groups, hops, part...]
    ppermute x16, waiting for transfers between devices: 218 us -> 76.6 us  [to_group(): lax.ppermute(v, 'tensor', [(t, (t + 2 * hop) % self.members) for t in ran...]
    dot_general x44 -> x36, matrix products: 337 us -> 262 us  [mm(): return lax.dot_general(a, b, dims, preferred_element_type=F32)]
    concatenate x4 -> x0, other arithmetic: 38.9 us -> none  [the longest x2 23.4 us: block_backward(): jnp.concatenate([mm(normed, part, TN).astype(BF16) for part in joined])]
    ppermute x8 -> x9, waiting for transfers between devices: 100 us -> 91.3 us  [to_pair(): return lax.ppermute(v, 'tensor', [(t, t ^ 1) for t in range(self.members)])]
  transfers between devices with their start and end apart: 31 -> 42, of which waited for: 18 -> 13; matrix products, arithmetic and copies ran while one was open for 23% -> 37% of each run, Pallas kernels for 7% -> 34%
where the time goes in v3:
time: 1240 us; the launch traced here: 1230 us
  Pallas kernels  414 us (33%)
  waiting for transfers between devices  291 us (23%)
  matrix products  262 us (21%)
  other arithmetic  112 us (9%)
  local copies, waits for them, and re-layouts  100 us (8%)
  starting transfers between devices  30.5 us (2%)
  between operations  15.8 us (1%)
    dot_general x36, matrix products, mm(): return lax.dot_general(a, b, dims, preferred_element_type=F32)  262 us
    pallas_call x1, Pallas kernels, reduced_product(): pl.pallas_call(functools.partial(reduce_kernel, chips, groups, hops, part...  176 us
    all_gather x2, waiting for transfers between devices, gather_owners(): lax.all_gather(v, ('dp', 'tensor'), axis=0, axis_index_groups=self.owners...  114 us
    pallas_call x4, Pallas kernels, mixer_backward(): pl.pallas_call(functools.partial(backward_kernel, early is None, carried...  110 us
    ppermute x9, waiting for transfers between devices, to_pair(): return lax.ppermute(v, 'tensor', [(t, t ^ 1) for t in range(self.members)])  91.3 us
    ppermute x16, waiting for transfers between devices, to_group(): lax.ppermute(v, 'tensor', [(t, (t + 2 * hop) % self.members) for t in ran...  76.6 us
    pallas_call x3, Pallas kernels, stacked_product(): pl.pallas_call(kernel, grid=(shards, tiles, features // row_tile), in_spe...  65.1 us
    pallas_call x8, Pallas kernels, mixer_forward(): pl.pallas_call(functools.partial(forward_kernel, earlier is None, heads,...  63.6 us
  transfers between devices with their start and end apart: 42, of which 13 were waited for; matrix products, arithmetic and copies ran while one was open for 37% of the time, Pallas kernels for 34%

profile of v3, /device:TPU:0, one launch (start us, length us, event | category | flops | bytes accessed | tf_op | source)
XLA Modules:
  0.0 1225.2 jit_solution(17741601251109378888)
XLA Ops:
  43.0 41.6 %collective-permute-done.3 = f32[2,1,3,16]{3,0,2,1:T(2,128)S(1)} collective-permute-done((f32[2,1,3,16]{3,0,2,1:T(2,128)S(1)}, f32[2,1,3,16]{3,0,2,1:T(2,128)S(1)}, u32[]{:S(2)}, u32[]{:S(2)}) %collective-permute-start.3) | collective-permute-done | bytes 416 | tf_op jit(solution)/shard_map/ppermute | solution.py:677
  89.7 39.8 %collective-permute-done.12 = bf16[256,2048]{0,1:T(8,128)(2,1)} collective-permute-done((bf16[256,2048]{0,1:T(8,128)(2,1)}, bf16[256,2048]{0,1:T(8,128)(2,1)}, u32[]{:S(2)}, u32[]{:S(2)}) %collective-permute-start.12) | collective-permute-done | bytes 1048608 | tf_op jit(solution)/shard_map/ppermute | solution.py:677
  139.1 76.2 %all-gather.3.cloned.1.call-done = bf16[4096,3328]{0,1:T(8,128)(2,1)} async-done(((bf16[256,3328]{0,1:T(8,128)(2,1)}), bf16[4096,3328]{0,1:T(8,128)(2,1)}) %all-gather.3.cloned.1.call-update) | async-done | bytes 27262992 | tf_op jit(solution)/shard_map/all_gather | solution.py:700
  220.4 10.4 fusion.51.refs_0_.refs_8_.refs_19_.refs_1_.refs_16_
  238.7 9.7 fusion.45.refs_0_.refs_8_.refs_18_.refs_15_
  259.0 9.7 fusion.54.refs_0_.refs_1_.refs_16_
  276.6 9.7 fusion.48.refs_0_.refs_15_
  325.0 37.5 %all-gather.5.cloned.1.call-done = bf16[4096,3328]{0,1:T(8,128)(2,1)} async-done(((bf16[256,3328]{0,1:T(8,128)(2,1)}), bf16[4096,3328]{0,1:T(8,128)(2,1)}) %all-gather.5.cloned.1.call-update) | async-done | bytes 27262992 | tf_op jit(solution)/shard_map/all_gather | solution.py:700
  368.7 35.8 %collective-permute-done.7 = bf16[512,2048]{0,1:T(8,128)(2,1)} collective-permute-done((bf16[512,2048]{0,1:T(8,128)(2,1)}, bf16[512,2048]{0,1:T(8,128)(2,1)}, u32[]{:S(2)}, u32[]{:S(2)}) %collective-permute-start.7) | collective-permute-done | bytes 2097184 | tf_op jit(solution)/shard_map/ppermute | solution.py:680
  412.5 9.7 fusion.57.refs_0_.refs_8_.refs_18_.refs_15_
  430.0 10.1 fusion.63.refs_0_.refs_8_.refs_19_.refs_1_.refs_16_
  449.4 9.3 fusion.60.refs_0_.refs_15_
  466.7 10.1 fusion.66.refs_0_.refs_1_.refs_16_
  531.8 18.9 %stacked_product.3.refs_21_ = bf16[2,2048,1024]{2,1,0:T(8,128)(2,1)} custom-call(bf16[2048,512]{1,0:T(8,128)(2,1)} %get-tuple-element.237.refs_0_, bf16[2048,512]{1,0:T(8,128)(2,1)} %get-tuple-element.212.refs_1_, bf16[512,1024]{1,0:T(8,128)(2,1)S(1)} %copy-done.31, bf16[512,1024]{1,0:T(8,128)(2,1)S(1)} %copy-done.21, bf16[512,1024]{1,0:T(8,128)(2,1)S(1)} %copy-done.29, ...), custom_call_target="tpu_custom_call" | custom-call | flops 8589934592 | bytes 20971520 | tf_op jit(solution)/shard_map/stacked_product/pallas_call | solution.py:474
  550.8 11.8 copy.176
  578.9 27.6 %mixer_backward.4 = (bf16[512,4608]{1,0:T(8,128)(2,1)}, f32[128,2048]{1,0:T(8,128)}, f32[8,2048]{1,0:T(8,128)}, f32[8,256]{1,0:T(8,128)}, f32[8,2048]{1,0:T(8,12...) custom-call(bf16[512,2048]{1,0:T(8,128)(2,1)} %fusion.60.refs_0_.refs_15_, bf16[512,2048]{1,0:T(8,128)(2,1)} %fusion.66.refs_0_.refs_1_.refs_16_, ...), custom_call_target="tpu_custom_call" | custom-call | flops 14680064000 | bytes 20971520 | tf_op jit(solution)/shard_map/mixer_backward/pallas_call | solution.py:423
  606.5 8.6 fusion.10
  615.2 12.9 %add_convert_fusion.4 = bf16[512,2048]{0,1:T(8,128)(2,1)} fusion(f32[512,2048]{0,1:T(8,128)S(1)} %fusion.10, bf16[4096,3328]{0,1:T(8,128)(2,1)} %all-gather.5.cloned.1.call-done, bf16[512,4608]{1,0:T(8,128)(2,1)S(1)} %copy-done.93), kind=kOutput, calls=%fused_computation.61 | convolution fusion | flops 4833935360 | bytes 18087936 | tf_op jit(solution)/shard_map/dot_general | solution.py:24
  633.7 27.2 %mixer_backward.5 = (bf16[512,4608]{1,0:T(8,128)(2,1)}, f32[128,2048]{1,0:T(8,128)}, f32[8,2048]{1,0:T(8,128)}, f32[8,256]{1,0:T(8,128)}, f32[8,2048]{1,0:T(8,12...) custom-call(bf16[512,2048]{1,0:T(8,128)(2,1)} %fusion.57.refs_0_.refs_8_.refs_18_.refs_15_, ...), custom_call_target="tpu_custom_call" | custom-call | flops 14680064000 | bytes 20971520 | tf_op jit(solution)/shard_map/mixer_backward/pallas_call | solution.py:423
  661.0 8.8 fusion.8
  669.8 12.8 %add_convert_fusion.3 = bf16[512,2048]{0,1:T(8,128)(2,1)} fusion(f32[512,2048]{0,1:T(8,128)S(1)} %fusion.8, bf16[4096,3328]{0,1:T(8,128)(2,1)} %all-gather.5.cloned.1.call-done, bf16[512,4608]{1,0:T(8,128)(2,1)S(1)} %copy-done.94), kind=kOutput, calls=%fused_computation.60 | convolution fusion | flops 4833935360 | bytes 18087936 | tf_op jit(solution)/shard_map/dot_general | solution.py:24
  686.5 29.1 %stacked_product.4 = bf16[2,2048,2304]{2,1,0:T(8,128)(2,1)} custom-call(bf16[2048,512]{1,0:T(8,128)(2,1)S(1)} %bitcast.218, bf16[2048,512]{1,0:T(8,128)(2,1)S(1)} %bitcast.217, bf16[512,4608]{1,0:T(8,128)(2,1)} %get-tuple-element.124.refs_2_, bf16[512,4608]{1,0:T(8,128)(2,1)} %get-tuple-element.123.refs_3_), custom_call_target="tpu_custom_call" | custom-call | flops 19327352832 | bytes 36700160 | tf_op jit(solution)/shard_map/stacked_product/pallas_call | solution.py:474
  737.1 10.4 multiply_reduce_fusion.4
  785.7 17.0 %stacked_product.5.refs_21_ = bf16[2,1024,1024]{2,1,0:T(8,128)(2,1)} custom-call(bf16[1024,512]{1,0:T(8,128)(2,1)S(1)} %bitcast.219, bf16[1024,512]{1,0:T(8,128)(2,1)S(1)} %bitcast.220, bf16[1024,512]{1,0:T(8,128)(2,1)} %collective-permute-done.18.refs_2_, bf16[1024,512]{1,0:T(8,128)(2,1)S(1)} %collective-permute-done.19.refs_3_, ...), custom_call_target="tpu_custom_call" | custom-call | flops 8589934592 | bytes 20971520 | tf_op jit(solution)/shard_map/stacked_product/pallas_call | solution.py:474
  806.7 27.0 %mixer_backward.6 = (bf16[512,4608]{1,0:T(8,128)(2,1)}, f32[128,2048]{1,0:T(8,128)}, f32[8,2048]{1,0:T(8,128)}, f32[8,256]{1,0:T(8,128)}, f32[8,2048]{1,0:T(8,12...) custom-call(bf16[512,2048]{1,0:T(8,128)(2,1)} %fusion.48.refs_0_.refs_15_, bf16[512,2048]{1,0:T(8,128)(2,1)} %fusion.54.refs_0_.refs_1_.refs_16_, ...), custom_call_target="tpu_custom_call" | custom-call | flops 14680064000 | bytes 20971520 | tf_op jit(solution)/shard_map/mixer_backward/pallas_call | solution.py:423
  833.7 27.7 %mixer_backward.7 = (bf16[512,4608]{1,0:T(8,128)(2,1)}, f32[128,2048]{1,0:T(8,128)}, f32[8,2048]{1,0:T(8,128)}, f32[8,256]{1,0:T(8,128)}, f32[8,2048]{1,0:T(8,12...) custom-call(bf16[512,2048]{1,0:T(8,128)(2,1)} %fusion.45.refs_0_.refs_8_.refs_18_.refs_15_, ...), custom_call_target="tpu_custom_call" | custom-call | flops 14680064000 | bytes 20971520 | tf_op jit(solution)/shard_map/mixer_backward/pallas_call | solution.py:423
  876.3 12.6 %add_convert_fusion.2 = bf16[512,2048]{0,1:T(8,128)(2,1)} fusion(f32[512,2048]{0,1:T(8,128)S(1)} %fusion.2, bf16[4096,3328]{0,1:T(8,128)(2,1)} %all-gather.3.cloned.1.call-done, bf16[512,4608]{1,0:T(8,128)(2,1)S(1)} %get-tuple-element.233), kind=kOutput, calls=%fused_computation.50 | convolution fusion | flops 4833935360 | bytes 18087936 | tf_op jit(solution)/shard_map/dot_general | solution.py:24
  891.0 10.7 fusion
  908.3 28.6 %collective-permute-done.24 = bf16[512,2048]{0,1:T(8,128)(2,1)} collective-permute-done((bf16[512,2048]{0,1:T(8,128)(2,1)}, bf16[512,2048]{0,1:T(8,128)(2,1)}, u32[]{:S(2)}, u32[]{:S(2)}) %collective-permute-start.24) | collective-permute-done | bytes 2097184 | tf_op jit(solution)/shard_map/ppermute | solution.py:680
  936.9 12.2 multiply_reduce_fusion.2
  952.5 11.0 add_convert_fusion
  1007.0 175.7 %reduced_product.1 = (f32[256,2304]{1,0:T(8,128)}, f32[440,128]{1,0:T(8,128)}) custom-call(bf16[1024,512]{1,0:T(8,128)(2,1)} %bitcast.232, bf16[1024,512]{1,0:T(8,128)(2,1)} %bitcast.233, bf16[1024,512]{1,0:T(8,128)(2,1)} %collective-permute-done.26.refs_2_, bf16[1024,512]{1,0:T(8,128)(2,1)} %collective-permute-done.27.refs_3_, ...), custom_call_target="tpu_custom_call" | custom-call | flops 19327352832 | bytes 104857600 | tf_op jit(solution)/shard_map/reduced_product/pallas_call | solution.py:632
  (491 shorter events, 409.2 us)
Async XLA Ops:
  7.2 208.1 %all-gather.3.cloned.1.call-start = ((), (), s32[]{:S(2)}) async-start(), calls=%async_computation.2 | async-start | bytes 28966912 | tf_op jit(solution)/shard_map/all_gather | solution.py:700
  19.9 342.5 %all-gather.5.cloned.1.call-start = ((), (), s32[]{:S(2)}) async-start(), calls=%async_computation.3 | async-start | bytes 28966912 | tf_op jit(solution)/shard_map/all_gather | solution.py:700
  28.5 1173.9 %reduce-scatter.5.cloned.1.call-start = ((), (), s32[]{:S(2)}) async-start(), calls=%async_computation.5 | async-start | bytes 8912896 | tf_op jit(solution)/shard_map/reduce_scatter | solution.py:697
  33.0 51.7 %collective-permute-start = (bf16[256,2048]{0,1:T(8,128)(2,1)S(1)}, bf16[256,2048]{0,1:T(8,128)(2,1)}, u32[]{:S(2)}, u32[]{:S(2)}) collective-permute-start(bf16[256,2048]{0,1:T(8,128)(2,1)S(1)} %get-tuple-element.266), channel_id=1, source_target_pairs={{0,1},{1,0},{2,3},{3,2},{4,5},{5,4},{6,7},{7,6},{8,9},{9,8},{10,11... | collective-permute-start | bytes 3145736 | tf_op jit(solution)/shard_map/ppermute | solution.py:677
  35.5 54.0 %collective-permute-start.2 = (f32[2,6,1024]{2,1,0:T(8,128)S(1)}, f32[2,6,1024]{2,1,0:T(8,128)S(1)}, u32[]{:S(2)}, u32[]{:S(2)}) collective-permute-start(f32[2,6,1024]{2,1,0:T(8,128)S(1)} %pad_maximum_fusion.9), channel_id=1, source_target_pairs={{0,1},{1,0},{2,3},{3,2},{4,5},{5,4},{6,7},{7,6},{8,9},{9,8},{10,11... | collective-permute-start | bytes 147464 | tf_op jit(solution)/shard_map/ppermute | solution.py:677
  35.6 49.0 %collective-permute-start.3 = (f32[2,1,3,16]{3,0,2,1:T(2,128)S(1)}, f32[2,1,3,16]{3,0,2,1:T(2,128)S(1)}, u32[]{:S(2)}, u32[]{:S(2)}) collective-permute-start(f32[2,1,3,16]{3,0,2,1:T(2,128)S(1)} %maximum_bitcast_fusion.2), channel_id=1, source_target_pairs={{0,1},{1,0},{2,3},{3,2},{4,5},{5,4},{6,7},{7,6},{8,9},{9,8},{10,11... | collective-permute-start | bytes 1160 | tf_op jit(solution)/shard_map/ppermute | solution.py:677
  42.0 87.4 %collective-permute-start.12 = (bf16[256,2048]{0,1:T(8,128)(2,1)}, bf16[256,2048]{0,1:T(8,128)(2,1)}, u32[]{:S(2)}, u32[]{:S(2)}) collective-permute-start(bf16[256,2048]{0,1:T(8,128)(2,1)} %get-tuple-element.258), channel_id=1, source_target_pairs={{0,1},{1,0},{2,3},{3,2},{4,5},{5,4},{6,7},{7,6},{8,9},{9,8},{10,11... | collective-permute-start | bytes 3145736 | tf_op jit(solution)/shard_map/ppermute | solution.py:677
  87.5 47.3 %collective-permute-start.1 = (bf16[512,2048]{0,1:T(8,128)(2,1)S(1)}, bf16[512,2048]{0,1:T(8,128)(2,1)}, u32[]{:S(2)}, u32[]{:S(2)}) collective-permute-start(bf16[512,2048]{0,1:T(8,128)(2,1)S(1)} %maximum_select_fusion), channel_id=1, source_target_pairs={{0,2},{1,3},{2,0},{3,1},{4,6},{5,7},{6,4},{7,5},{8,10},{9,11},{10,... | collective-permute-start | bytes 6291464 | tf_op jit(solution)/shard_map/ppermute | solution.py:680
  133.7 375.8 %collective-permute-start.13 = (bf16[512,2048]{0,1:T(8,128)(2,1)}, bf16[512,2048]{0,1:T(8,128)(2,1)}, u32[]{:S(2)}, u32[]{:S(2)}) collective-permute-start(bf16[512,2048]{0,1:T(8,128)(2,1)} %maximum_select_fusion.2), channel_id=1, source_target_pairs={{0,2},{1,3},{2,0},{3,1},{4,6},{5,7},{6,4},{7,5},{8,10},{9,11},{10,... | collective-permute-start | bytes 6291464 | tf_op jit(solution)/shard_map/ppermute | solution.py:680
  256.1 54.8 %collective-permute-start.4 = (f32[512,1]{1,0:T(8,128)S(1)}, f32[512,1]{1,0:T(8,128)S(1)}, u32[]{:S(2)}, u32[]{:S(2)}) collective-permute-start(f32[512,1]{1,0:T(8,128)S(1)} %add.340), channel_id=1, source_target_pairs={{0,2},{1,3},{2,0},{3,1},{4,6},{5,7},{6,4},{7,5},{8,10},{9,11},{10,... | collective-permute-start | bytes 6152 | tf_op jit(solution)/shard_map/ppermute | solution.py:680
  311.7 53.4 %collective-permute-start.5 = (bf16[512,2048]{0,1:T(8,128)(2,1)}, bf16[512,2048]{0,1:T(8,128)(2,1)}, u32[]{:S(2)}, u32[]{:S(2)}) collective-permute-start(bf16[512,2048]{0,1:T(8,128)(2,1)} %add_convert_fusion.9), channel_id=1, source_target_pairs={{0,2},{1,3},{2,0},{3,1},{4,6},{5,7},{6,4},{7,5},{8,10},{9,11},{10,... | collective-permute-start | bytes 6291464 | tf_op jit(solution)/shard_map/ppermute | solution.py:680
  320.3 84.2 %collective-permute-start.7 = (bf16[512,2048]{0,1:T(8,128)(2,1)}, bf16[512,2048]{0,1:T(8,128)(2,1)}, u32[]{:S(2)}, u32[]{:S(2)}) collective-permute-start(bf16[512,2048]{0,1:T(8,128)(2,1)} %add_convert_fusion.8), channel_id=1, source_target_pairs={{0,2},{1,3},{2,0},{3,1},{4,6},{5,7},{6,4},{7,5},{8,10},{9,11},{10,... | collective-permute-start | bytes 6291464 | tf_op jit(solution)/shard_map/ppermute | solution.py:680
  321.5 455.3 %collective-permute-start.23 = (bf16[512,1024]{1,0:T(8,128)(2,1)}, bf16[512,1024]{1,0:T(8,128)(2,1)}, u32[]{:S(2)}, u32[]{:S(2)}) collective-permute-start(bf16[512,1024]{1,0:T(8,128)(2,1)} %get-tuple-element.92.refs_7_), channel_id=1, source_target_pairs={{0,4},{4,0},{8,12},{12,8},{16,20},{20,16},{24,28},{28,24},{1,5},{5... | collective-permute-start | bytes 3145736 | tf_op jit(solution)/shard_map/ppermute | solution.py:683
  321.5 462.8 %collective-permute-start.21 = (bf16[512,1024]{1,0:T(8,128)(2,1)}, bf16[512,1024]{1,0:T(8,128)(2,1)}, u32[]{:S(2)}, u32[]{:S(2)}) collective-permute-start(bf16[512,1024]{1,0:T(8,128)(2,1)} %get-tuple-element.85.refs_5_), channel_id=1, source_target_pairs={{0,4},{4,0},{8,12},{12,8},{16,20},{20,16},{24,28},{28,24},{1,5},{5... | collective-permute-start | bytes 3145736 | tf_op jit(solution)/shard_map/ppermute | solution.py:683
  448.2 57.0 %collective-permute-start.8 = (f32[512,1]{1,0:T(8,128)S(1)}, f32[512,1]{1,0:T(8,128)S(1)}, u32[]{:S(2)}, u32[]{:S(2)}) collective-permute-start(f32[512,1]{1,0:T(8,128)S(1)} %add.354), channel_id=1, source_target_pairs={{0,2},{1,3},{2,0},{3,1},{4,6},{5,7},{6,4},{7,5},{8,10},{9,11},{10,... | collective-permute-start | bytes 6152 | tf_op jit(solution)/shard_map/ppermute | solution.py:680
  508.4 224.9 %collective-permute-start.10 = (bf16[512,2048]{0,1:T(8,128)(2,1)}, bf16[512,2048]{0,1:T(8,128)(2,1)}, u32[]{:S(2)}, u32[]{:S(2)}) collective-permute-start(bf16[512,2048]{0,1:T(8,128)(2,1)} %broadcast_select_fusion.2), channel_id=1, source_target_pairs={{0,2},{1,3},{2,0},{3,1},{4,6},{5,7},{6,4},{7,5},{8,10},{9,11},{10,... | collective-permute-start | bytes 6291464 | tf_op jit(solution)/shard_map/ppermute | solution.py:680
  529.6 47.5 %collective-permute-start.15 = (f32[512,1]{1,0:T(8,128)S(1)}, f32[512,1]{1,0:T(8,128)}, u32[]{:S(2)}, u32[]{:S(2)}) collective-permute-start(f32[512,1]{1,0:T(8,128)S(1)} %copy.150), channel_id=1, source_target_pairs={{0,2},{1,3},{2,0},{3,1},{4,6},{5,7},{6,4},{7,5},{8,10},{9,11},{10,... | collective-permute-start | bytes 6152 | tf_op jit(solution)/shard_map/ppermute | solution.py:680
  562.6 642.3 %reduce-scatter.3.cloned.1.call-start = ((), (), s32[]{:S(2)}) async-start(), calls=%async_computation.4 | async-start | bytes 20054016 | tf_op jit(solution)/shard_map/reduce_scatter | solution.py:697
  575.9 57.0 %collective-permute-start.14 = (f32[512,1]{1,0:T(8,128)S(1)}, f32[512,1]{1,0:T(8,128)S(1)}, u32[]{:S(2)}, u32[]{:S(2)}) collective-permute-start(f32[512,1]{1,0:T(8,128)S(1)} %copy.148), channel_id=1, source_target_pairs={{0,2},{1,3},{2,0},{3,1},{4,6},{5,7},{6,4},{7,5},{8,10},{9,11},{10,... | collective-permute-start | bytes 6152 | tf_op jit(solution)/shard_map/ppermute | solution.py:680
  632.1 84.8 %collective-permute-start.17 = (bf16[512,2048]{0,1:T(8,128)(2,1)}, bf16[512,2048]{0,1:T(8,128)(2,1)}, u32[]{:S(2)}, u32[]{:S(2)}) collective-permute-start(bf16[512,2048]{0,1:T(8,128)(2,1)} %add_convert_fusion.4), channel_id=1, source_target_pairs={{0,2},{1,3},{2,0},{3,1},{4,6},{5,7},{6,4},{7,5},{8,10},{9,11},{10,... | collective-permute-start | bytes 6291464 | tf_op jit(solution)/shard_map/ppermute | solution.py:680
  682.6 45.4 %collective-permute-start.16 = (bf16[512,2048]{0,1:T(8,128)(2,1)}, bf16[512,2048]{0,1:T(8,128)(2,1)}, u32[]{:S(2)}, u32[]{:S(2)}) collective-permute-start(bf16[512,2048]{0,1:T(8,128)(2,1)} %add_convert_fusion.3), channel_id=1, source_target_pairs={{0,2},{1,3},{2,0},{3,1},{4,6},{5,7},{6,4},{7,5},{8,10},{9,11},{10,... | collective-permute-start | bytes 6291464 | tf_op jit(solution)/shard_map/ppermute | solution.py:680
  716.9 68.8 %collective-permute-start.22 = (bf16[512,1024]{1,0:T(8,128)(2,1)S(1)}, bf16[512,1024]{1,0:T(8,128)(2,1)}, u32[]{:S(2)}, u32[]{:S(2)}) collective-permute-start(bf16[512,1024]{1,0:T(8,128)(2,1)S(1)} %copy-done.15), channel_id=1, source_target_pairs={{0,4},{4,0},{8,12},{12,8},{16,20},{20,16},{24,28},{28,24},{1,5},{5... | collective-permute-start | bytes 3145736 | tf_op jit(solution)/shard_map/ppermute | solution.py:683
  728.0 57.7 %collective-permute-start.20 = (bf16[512,1024]{1,0:T(8,128)(2,1)S(1)}, bf16[512,1024]{1,0:T(8,128)(2,1)}, u32[]{:S(2)}, u32[]{:S(2)}) collective-permute-start(bf16[512,1024]{1,0:T(8,128)(2,1)S(1)} %copy-done.13), channel_id=1, source_target_pairs={{0,4},{4,0},{8,12},{12,8},{16,20},{20,16},{24,28},{28,24},{1,5},{5... | collective-permute-start | bytes 3145736 | tf_op jit(solution)/shard_map/ppermute | solution.py:683
  754.4 31.3 %collective-permute-start.18 = (bf16[1024,512]{1,0:T(8,128)(2,1)}, bf16[1024,512]{1,0:T(8,128)(2,1)}, u32[]{:S(2)}, u32[]{:S(2)}) collective-permute-start(bf16[1024,512]{1,0:T(8,128)(2,1)} %bitcast.55), channel_id=1, source_target_pairs={{0,4},{4,0},{8,12},{12,8},{16,20},{20,16},{24,28},{28,24},{1,5},{5... | collective-permute-start | bytes 3145736 | tf_op jit(solution)/shard_map/ppermute | solution.py:683
  784.2 165.9 %collective-permute-start.11 = (bf16[256,2048]{0,1:T(8,128)(2,1)}, bf16[256,2048]{0,1:T(8,128)(2,1)}, u32[]{:S(2)}, u32[]{:S(2)}) collective-permute-start(bf16[256,2048]{0,1:T(8,128)(2,1)} %get-tuple-element.260), channel_id=1, source_target_pairs={{0,1},{1,0},{2,3},{3,2},{4,5},{5,4},{6,7},{7,6},{8,9},{9,8},{10,11... | collective-permute-start | bytes 3145736 | tf_op jit(solution)/shard_map/ppermute | solution.py:677
  805.8 95.9 %collective-permute-start.30 = (bf16[1024,1024]{1,0:T(8,128)(2,1)}, bf16[1024,1024]{1,0:T(8,128)(2,1)S(1)}, u32[]{:S(2)}, u32[]{:S(2)}) collective-permute-start(bf16[1024,1024]{1,0:T(8,128)(2,1)} %dynamic-slice_bitcast_fusion.refs_22_), channel_id=1, source_target_pairs={{0,1},{1,0},{2,3},{3,2},{4,5},{5,4},{6,7},{7,6},{8,9},{9,8},{10,11... | collective-permute-start | bytes 6291464 | tf_op jit(solution)/shard_map/ppermute | solution.py:677
  861.4 145.5 %collective-permute-start.28 = (bf16[512,4608]{1,0:T(8,128)(2,1)}, bf16[512,4608]{1,0:T(8,128)(2,1)}, u32[]{:S(2)}, u32[]{:S(2)}) collective-permute-start(bf16[512,4608]{1,0:T(8,128)(2,1)} %get-tuple-element.143.refs_4_), channel_id=1, source_target_pairs={{0,4},{4,0},{8,12},{12,8},{16,20},{20,16},{24,28},{28,24},{1,5},{5... | collective-permute-start | bytes 14155784 | tf_op jit(solution)/shard_map/ppermute | solution.py:683
  861.5 145.4 %collective-permute-start.29 = (bf16[512,4608]{1,0:T(8,128)(2,1)}, bf16[512,4608]{1,0:T(8,128)(2,1)}, u32[]{:S(2)}, u32[]{:S(2)}) collective-permute-start(bf16[512,4608]{1,0:T(8,128)(2,1)} %get-tuple-element.144.refs_5_), channel_id=1, source_target_pairs={{0,4},{4,0},{8,12},{12,8},{16,20},{20,16},{24,28},{28,24},{1,5},{5... | collective-permute-start | bytes 14155784 | tf_op jit(solution)/shard_map/ppermute | solution.py:683
  888.9 48.0 %collective-permute-start.24 = (bf16[512,2048]{0,1:T(8,128)(2,1)}, bf16[512,2048]{0,1:T(8,128)(2,1)}, u32[]{:S(2)}, u32[]{:S(2)}) collective-permute-start(bf16[512,2048]{0,1:T(8,128)(2,1)} %add_convert_fusion.2), channel_id=1, source_target_pairs={{0,2},{1,3},{2,0},{3,1},{4,6},{5,7},{6,4},{7,5},{8,10},{9,11},{10,... | collective-permute-start | bytes 6291464 | tf_op jit(solution)/shard_map/ppermute | solution.py:680
  906.0 58.7 %collective-permute-start.35 = (bf16[256,1024]{0,1:T(8,128)(2,1)}, bf16[256,1024]{0,1:T(8,128)(2,1)}, u32[]{:S(2)}, u32[]{:S(2)}) collective-permute-start(bf16[256,1024]{0,1:T(8,128)(2,1)} %bitcast.238), channel_id=1, source_target_pairs={{0,8},{4,12},{8,16},{12,20},{16,24},{20,28},{24,0},{28,4},{1,9},{5... | collective-permute-start | bytes 1572872 | tf_op jit(solution)/shard_map/ppermute | solution.py:687
  964.7 42.3 %collective-permute-start.26 = (bf16[1024,512]{1,0:T(8,128)(2,1)}, bf16[1024,512]{1,0:T(8,128)(2,1)}, u32[]{:S(2)}, u32[]{:S(2)}) collective-permute-start(bf16[1024,512]{1,0:T(8,128)(2,1)} %bitcast.68), channel_id=1, source_target_pairs={{0,4},{4,0},{8,12},{12,8},{16,20},{20,16},{24,28},{28,24},{1,5},{5... | collective-permute-start | bytes 3145736 | tf_op jit(solution)/shard_map/ppermute | solution.py:683
  967.2 39.8 %collective-permute-start.27 = (bf16[1024,512]{1,0:T(8,128)(2,1)}, bf16[1024,512]{1,0:T(8,128)(2,1)}, u32[]{:S(2)}, u32[]{:S(2)}) collective-permute-start(bf16[1024,512]{1,0:T(8,128)(2,1)} %bitcast.70), channel_id=1, source_target_pairs={{0,4},{4,0},{8,12},{12,8},{16,20},{20,16},{24,28},{28,24},{1,5},{5... | collective-permute-start | bytes 3145736 | tf_op jit(solution)/shard_map/ppermute | solution.py:683
  (105 other events, 4546.1 us)
Sparse Core Ops, SparseCore 0:
  20.0 195.2 all-gather.2
  217.4 144.9 all-gather.4
  562.7 102.5 reduce-scatter.4
  715.8 243.5 reduce-scatter.2

commit v4 on v2

v4 whole, which is shorter than its diff:
```python
import functools

import jax
import jax.numpy as jnp
from jax import lax
from jax.experimental import pallas as pl
from jax.experimental.pallas import tpu as pltpu
from jax.sharding import PartitionSpec as P

EPSILON = 1e-05
CHUNK = 128
PIECES = 2
GROUP_LANES = 256
LOG2E = 1.4426950408889634
F32 = jnp.float32
BF16 = jnp.bfloat16
NN = (((1,), (0,)), ((), ()))
NT = (((1,), (1,)), ((), ()))
MESH = pl.DeviceIdType.MESH
TN = (((0,), (0,)), ((), ()))


def mm(a, b, dims=NN):
    return lax.dot_general(a, b, dims, preferred_element_type=F32)


def sigmoid(v):
    return 0.5 * jnp.tanh(0.5 * v) + 0.5


def softplus(v):
    return jnp.maximum(v, 0.0) + jnp.log(1.0 + jnp.exp(-jnp.abs(v)))


def split3(v):
    high = v.astype(BF16)
    rest = v - high.astype(F32)
    mid = rest.astype(BF16)
    return high, mid, (rest - mid.astype(F32)).astype(BF16)


def spread(v, expand, heads):
    high = v.astype(BF16)
    low = (v - high.astype(F32)).astype(BF16)
    lane = lax.broadcasted_iota(jnp.int32, v.shape, 1)
    parts = jnp.where(lane < heads, high, jnp.where(lane < 2 * heads, low, jnp.zeros_like(low)))
    return mm(parts, expand)


def conv_rows(window, table, length):
    total = table[4:5] + table[3:4] * window[8 : 8 + length]
    for back in range(1, 4):
        total = total + table[3 - back : 4 - back] * pltpu.roll(window, back, 0)[8 : 8 + length]
    return total


def causal(length, flip):
    row = lax.broadcasted_iota(jnp.int32, (length, length), 0)
    col = lax.broadcasted_iota(jnp.int32, (length, length), 1)
    return (row <= col) if flip else (row >= col)


def head_masks(lanes, width):
    lane = lax.broadcasted_iota(jnp.int32, (1, lanes), 1)
    return [(lane >= j * width) & (lane < (j + 1) * width) for j in range(lanes // width)]


def both_halves(ref):
    half = ref.shape[2] - 128
    return jnp.concatenate([ref[0, :, :half], ref[1, :, :half]], axis=1)


def forward_kernel(first, heads, *refs):
    columns_ref, small_ref, chan_ref, taps_ref, head_ref, expand_ref, tri_ref = refs[:7]
    refs = refs[7:]
    if not first:
        start_ref, tail_ref, stail_ref = refs[:3]
    mixed_ref, square_ref, y_ref, saved_ref, state, xbuf, sbuf = refs[-7:]
    length, channels = y_ref.shape[1:]
    width = channels // heads
    shared = taps_ref.shape[1]
    half = shared // 2

    @pl.when(pl.program_id(0) == 0)
    def _():
        if first:
            state[...] = jnp.zeros_like(state)
            xbuf[0:8] = jnp.zeros((8, 2 * channels), F32)
            sbuf[0:8] = jnp.zeros((8, shared), F32)
        else:
            state[...] = start_ref[...]
            for half_no in range(2):
                xbuf[0:8, half_no * channels : (half_no + 1) * channels] = tail_ref[half_no, :, channels:].astype(F32)[-8:]
            sbuf[0:8] = both_halves(stail_ref)

    sbuf[8:] = both_halves(small_ref)
    tri = tri_ref[...]
    expand = expand_ref[...]
    taps = taps_ref[...]
    bc = conv_rows(sbuf[...], taps, length)
    bc = (bc * sigmoid(bc)).astype(BF16)
    keys, queries = bc[:, :half], bc[:, half:]
    scores = jnp.where(causal(length, False), mm(queries, keys, NT), 0.0)
    squares = jnp.zeros((length, 128), F32)
    masks = head_masks(GROUP_LANES, width)
    for half_no in range(2):
        head = head_ref[8 * half_no : 8 * half_no + 8]
        dt = softplus(small_ref[half_no, :, half:] + head[0:1])
        running = sum(mm(tri, piece) for piece in split3(dt * (head[1:2] * LOG2E)))
        running_t = running.T
        decay_in = jnp.exp2(running)
        decay_out = jnp.exp2(running[length - 1 :] - running)
        dt_wide = spread(dt, expand, heads)
        in_wide = spread(decay_in, expand, heads)
        out_wide = spread(dt * decay_out, expand, heads)
        for start in range(0, channels, GROUP_LANES):
            lanes = slice(start, start + GROUP_LANES)
            conv_at = slice(channels + start, channels + start + GROUP_LANES)
            wide = slice(half_no * channels + start, half_no * channels + start + GROUP_LANES)
            table = chan_ref[:, wide]
            xbuf[8:, wide] = columns_ref[half_no, :, conv_at].astype(F32)
            c = conv_rows(xbuf[:, wide], table, length)
            xbuf[0:8, wide] = xbuf[length:, wide]
            xs = c * sigmoid(c)
            values = (xs * dt_wide[:, lanes]).astype(BF16)
            weights, parts = [], []
            for j in range(GROUP_LANES // width):
                h = start // width + j
                gap = jnp.minimum(running[:, h : h + 1] - running_t[h : h + 1, :], 0.0)
                weights.append((scores * jnp.exp2(gap)).astype(BF16))
                parts.append(jnp.where(masks[j], values, jnp.zeros_like(values)))
            before = state[:, wide]
            before_low = before.astype(BF16)
            saved_ref[half_no, 0, :, lanes] = before_low
            y = mm(jnp.concatenate(weights, axis=1), jnp.concatenate(parts, axis=0))
            y = y + mm(queries, before_low) * in_wide[:, lanes]
            y_ref[half_no, :, lanes] = y
            z = columns_ref[half_no, :, lanes].astype(F32)
            gated = (y + table[5:6] * xs) * (z * sigmoid(z))
            mixed_ref[half_no, :, lanes] = (gated * table[6:7]).astype(BF16)
            power = gated * gated
            for at in range(0, GROUP_LANES, 128):
                squares = squares + power[:, at : at + 128]
            fresh = mm(keys, (xs * out_wide[:, lanes]).astype(BF16), TN)
            state[:, wide] = before * in_wide[length - 1 :, lanes] + fresh
    square_ref[...] = jnp.sum(squares, axis=1, keepdims=True)
    sbuf[0:8] = sbuf[length:]


def backward_kernel(first, last, heads, *refs):
    columns_ref, small_ref, y_ref, saved_ref, up_ref, pull_ref = refs[:6]
    chan_ref, taps_ref, head_ref, expand_ref, tri_ref, halo_ref, shalo_ref, early_ref, searly_ref = refs[6:15]
    refs = refs[15:]
    if not last:
        carried_refs = refs[:6]
    dcolumns_ref, dstate, dtail_ref, dstail_ref, gchan_ref, gtaps_ref, ghead_ref, xbuf, sbuf, dxbuf, dsbuf = refs[-11:]
    length, channels = y_ref.shape[1:]
    width = channels // heads
    shared = taps_ref.shape[1]
    half = shared // 2
    step_no = pl.program_id(0)
    first_block = step_no == pl.num_programs(0) - 1

    @pl.when(step_no == 0)
    def _():
        if last:
            dstate[...] = jnp.zeros_like(dstate)
            dxbuf[length:] = jnp.zeros((8, 2 * channels), F32)
            dsbuf[length:] = jnp.zeros((8, shared), F32)
            gchan_ref[...] = jnp.zeros_like(gchan_ref)
            gtaps_ref[...] = jnp.zeros_like(gtaps_ref)
            ghead_ref[...] = jnp.zeros_like(ghead_ref)
        else:
            dstate[...] = carried_refs[0][...]
            dxbuf[length:] = carried_refs[1][...]
            dsbuf[length:] = carried_refs[2][...]
            gchan_ref[...] = carried_refs[3][...]
            gtaps_ref[...] = carried_refs[4][...]
            ghead_ref[...] = carried_refs[5][...]

    def outside(rows):
        return jnp.zeros_like(rows) if first else rows

    sbuf[8:] = both_halves(small_ref)
    sbuf[0:8] = jnp.where(first_block, outside(both_halves(searly_ref)), both_halves(shalo_ref))
    tri = tri_ref[...]
    expand = expand_ref[...]
    taps = taps_ref[...]
    bc_in = conv_rows(sbuf[...], taps, length)
    bc_sig = sigmoid(bc_in)
    bc = (bc_in * bc_sig).astype(BF16)
    keys, queries = bc[:, :half], bc[:, half:]
    keep = causal(length, True)
    scores = jnp.where(keep, mm(keys, queries, NT), 0.0)
    pull = pull_ref[...]
    masks = head_masks(GROUP_LANES, width)
    dscores = jnp.zeros((length, length), F32)
    dkeys = jnp.zeros((length, half), F32)
    dqueries = jnp.zeros((length, half), F32)
    last_row = lax.broadcasted_iota(jnp.int32, (length, 1), 0) == length - 1
    lane = lax.broadcasted_iota(jnp.int32, (length, 128), 1)
    per_group = GROUP_LANES // width
    for half_no in range(2):
        head = head_ref[8 * half_no : 8 * half_no + 8]
        step = small_ref[half_no, :, half:] + head[0:1]
        dt = softplus(step)
        rate = dt * head[1:2]
        running = sum(mm(tri, piece) for piece in split3(rate * LOG2E))
        running_t = running.T
        decay_in = jnp.exp2(running)
        decay_out = jnp.exp2(running[length - 1 :] - running)
        dt_wide = spread(dt, expand, heads)
        in_wide = spread(decay_in, expand, heads)
        out_wide = spread(decay_out, expand, heads)
        drun = jnp.zeros((length, 128), F32)
        ddt = jnp.zeros((length, 128), F32)
        for start in range(0, channels, GROUP_LANES):
            lanes = slice(start, start + GROUP_LANES)
            conv_at = slice(channels + start, channels + start + GROUP_LANES)
            at = half_no * channels + start
            wide = slice(at, at + GROUP_LANES)
            table = chan_ref[:, wide]
            xbuf[8:, lanes] = columns_ref[half_no, :, conv_at].astype(F32)
            xbuf[0:8, lanes] = jnp.where(first_block, outside(early_ref[half_no, :, conv_at].astype(F32)[-8:]), halo_ref[half_no, :, conv_at].astype(F32)[-8:])
            c = conv_rows(xbuf[:, lanes], table, length)
            c_sig = sigmoid(c)
            xs = c * c_sig
            z = columns_ref[half_no, :, lanes].astype(F32)
            z_sig = sigmoid(z)
            z_silu = z * z_sig
            y = y_ref[half_no, :, lanes]
            total = y + table[5:6] * xs
            gated = total * z_silu
            up = up_ref[half_no, :, lanes].astype(F32)
            gchan_ref[6:7, wide] += jnp.sum(up * gated, axis=0, keepdims=True)
            dgated = table[6:7] * up - gated * pull
            out_at = half_no * (2 * channels + half + 128) + start
            dcolumns_ref[:, out_at : out_at + GROUP_LANES] = (
                dgated * total * (z_sig + z_silu * (1.0 - z_sig))
            ).astype(BF16)
            dy = dgated * z_silu
            gchan_ref[5:6, wide] += jnp.sum(dy * xs, axis=0, keepdims=True)
            dy_low = dy.astype(BF16)
            dt_lanes = dt_wide[:, lanes]
            values = (xs * dt_lanes).astype(BF16)
            weights, dparts, vparts, decays = [], [], [], []
            for j in range(per_group):
                h = start // width + j
                decay = jnp.exp2(jnp.minimum(running_t[h : h + 1, :] - running[:, h : h + 1], 0.0))
                decays.append(decay)
                weights.append((scores * decay).astype(BF16))
                dparts.append(jnp.where(masks[j], dy_low, jnp.zeros_like(dy_low)))
                vparts.append(jnp.where(masks[j], values, jnp.zeros_like(values)))
            outer = mm(jnp.concatenate(vparts, axis=0), dy_low, NT)
            for j in range(per_group):
                dscores = dscores + outer[j * length : (j + 1) * length] * decays[j]
            dvalues = mm(jnp.concatenate(weights, axis=1), jnp.concatenate(dparts, axis=0))
            before = saved_ref[half_no, 0, :, lanes]
            dafter = dstate[:, wide]
            dafter_low = dafter.astype(BF16)
            out_lanes = out_wide[:, lanes]
            carried = mm(keys, dafter_low) * out_lanes
            dvalues = dvalues + carried
            values_f = values.astype(F32)
            dkeys = dkeys + mm((values_f * out_lanes).astype(BF16), dafter_low, NT)
            in_lanes = in_wide[:, lanes]
            dy_in = (dy * in_lanes).astype(BF16)
            dqueries = dqueries + mm(dy_in, before, NT)
            end_decay = in_lanes[length - 1 :]
            at_end = jnp.sum(values_f * carried, axis=0, keepdims=True) + end_decay * jnp.sum(
                before.astype(F32) * dafter, axis=0, keepdims=True
            )
            dstate[:, wide] = end_decay * dafter + mm(queries, dy_in, TN)
            turn = dy_low.astype(F32) * y - values_f * dvalues + jnp.where(last_row, at_end, 0.0)
            turn_high = turn.astype(BF16)
            turn_low = (turn - turn_high.astype(F32)).astype(BF16)
            group_expand = expand[:, lanes]
            drun = drun + mm(turn_high, group_expand, NT) + mm(turn_low, group_expand, NT)
            ddt = ddt + mm((dvalues * xs).astype(BF16), group_expand, NT)
            dxs = dvalues * dt_lanes + table[5:6] * dy
            dc = dxs * (c_sig + xs * (1.0 - c_sig))
            dxbuf[0:length, wide] = dc
            window = dxbuf[:, wide]
            here = xbuf[8:, lanes]
            gchan_ref[4:5, wide] += jnp.sum(dc, axis=0, keepdims=True)
            gchan_ref[3:4, wide] += jnp.sum(dc * here, axis=0, keepdims=True)
            dconv = table[3:4] * dc
            for ahead in range(1, 4):
                moved = pltpu.roll(window, length + 8 - ahead, 0)[:length]
                gchan_ref[3 - ahead : 4 - ahead, wide] += jnp.sum(moved * here, axis=0, keepdims=True)
                dconv = dconv + table[3 - ahead : 4 - ahead] * moved
            out_at = out_at + channels
            dcolumns_ref[:, out_at : out_at + GROUP_LANES] = dconv.astype(BF16)
            dxbuf[length:, wide] = dxbuf[0:8, wide]

        drate = sum(mm(tri, piece, TN) for piece in split3(drun))
        dstep = (ddt + drate * head[1:2]) * sigmoid(step)
        ghead_ref[8 * half_no : 8 * half_no + 1] += jnp.sum(dstep, axis=0, keepdims=True)
        ghead_ref[8 * half_no + 1 : 8 * half_no + 2] += jnp.sum(drate * rate, axis=0, keepdims=True)
        out_at = half_no * (2 * channels + half + 128) + 2 * channels + half
        dcolumns_ref[:, out_at : out_at + 128] = jnp.where(lane < heads, dstep, 0.0).astype(BF16)

    dscores_low = jnp.where(keep, dscores, 0.0).astype(BF16)
    dkeys = dkeys + mm(dscores_low, queries)
    dqueries = dqueries + mm(dscores_low, keys, TN)
    dbc = jnp.concatenate([dkeys, dqueries], axis=1) * (bc_sig + bc_in * bc_sig * (1.0 - bc_sig))
    dsbuf[0:length] = dbc
    window = dsbuf[...]
    here = sbuf[8:]
    gtaps_ref[4:5] += jnp.sum(dbc, axis=0, keepdims=True)
    gtaps_ref[3:4] += jnp.sum(dbc * here, axis=0, keepdims=True)
    dshared = taps[3:4] * dbc
    for ahead in range(1, 4):
        moved = pltpu.roll(window, length + 8 - ahead, 0)[:length]
        gtaps_ref[3 - ahead : 4 - ahead] += jnp.sum(moved * here, axis=0, keepdims=True)
        dshared = dshared + taps[3 - ahead : 4 - ahead] * moved
    for half_no in range(2):
        out_at = half_no * (2 * channels + half + 128) + 2 * channels
        dcolumns_ref[:, out_at : out_at + half] = dshared[:, half_no * half : (half_no + 1) * half].astype(BF16)
    dsbuf[length:] = dsbuf[0:8]
    dtail_ref[...] = dxbuf[0:8]
    dstail_ref[...] = dsbuf[0:8]


def scan_tables(heads, channels):
    row = lax.broadcasted_iota(jnp.int32, (128, channels), 0) % heads
    col = lax.broadcasted_iota(jnp.int32, (128, channels), 1) // (channels // heads)
    return (row == col).astype(BF16), jnp.tril(jnp.ones((CHUNK, CHUNK), BF16))


def whole(array):
    return pl.BlockSpec(array.shape, lambda i: (0,) * array.ndim)


def last_rows(array, count):
    at = array.shape[1] // count - 1
    return pl.BlockSpec((2, count, array.shape[2]), lambda i: (0, at, 0))


def unread(arrays):
    return [pl.BlockSpec(memory_space=pl.ANY) for _ in arrays]


def mixer_forward(columns, small, tables, heads, earlier=None):
    _, tokens, channels = columns.shape
    channels = channels // 2
    shared = tables[1].shape[1]
    blocks = tokens // CHUNK

    def rows(cols):
        return pl.BlockSpec((2, CHUNK, cols), lambda i: (0, i, 0))

    operands = [columns, small, *tables]
    specs = [rows(2 * channels), rows(small.shape[2])] + [whole(table) for table in tables]
    if earlier is not None:
        operands += list(earlier)
        specs += [whole(earlier[0]), last_rows(earlier[1], 16), last_rows(earlier[2], 8)]
    return pl.pallas_call(
        functools.partial(forward_kernel, earlier is None, heads),
        grid=(blocks,),
        in_specs=specs,
        out_specs=[
            rows(channels),
            pl.BlockSpec((CHUNK, 1), lambda i: (i, 0)),
            rows(channels),
            pl.BlockSpec((2, 1, shared // 2, channels), lambda i: (0, i, 0, 0)),
            pl.BlockSpec((shared // 2, 2 * channels), lambda i: (0, 0)),
        ],
        out_shape=[
            jax.ShapeDtypeStruct((2, tokens, channels), BF16),
            jax.ShapeDtypeStruct((tokens, 1), F32),
            jax.ShapeDtypeStruct((2, tokens, channels), F32),
            jax.ShapeDtypeStruct((2, blocks, shared // 2, channels), BF16),
            jax.ShapeDtypeStruct((shared // 2, 2 * channels), F32),
        ],
        scratch_shapes=[
            pltpu.VMEM((CHUNK + 8, 2 * channels), F32),
            pltpu.VMEM((CHUNK + 8, shared), F32),
        ],
        compiler_params=pltpu.CompilerParams(vmem_limit_bytes=48 * 1024 * 1024),
        cost_estimate=pl.CostEstimate(
            flops=tokens * channels * 12000, bytes_accessed=tokens * channels * 28, transcendentals=tokens * channels * 12
        ),
        name="mixer_forward",
    )(*operands)


def mixer_backward(columns, small, y, saved, up, pull, tables, heads, early, carried, after=()):
    _, tokens, channels = y.shape
    shared = tables[1].shape[1]
    blocks = tokens // CHUNK
    thin = small.shape[2]

    def rows(cols):
        return pl.BlockSpec((2, CHUNK, cols), lambda i: (0, blocks - 1 - i, 0))

    def flat_rows(cols):
        return pl.BlockSpec((CHUNK, cols), lambda i: (blocks - 1 - i, 0))

    def halo(count, cols):
        per_block = CHUNK // count
        return pl.BlockSpec((2, count, cols), lambda i: (0, jnp.maximum((blocks - 1 - i) * per_block - 1, 0), 0))

    def fixed(r, c):
        return pl.BlockSpec((r, c), lambda i: (0, 0))

    saved_spec = pl.BlockSpec((2, 1, shared // 2, channels), lambda i: (0, blocks - 1 - i, 0, 0))
    before = (columns, small) if early is None else early
    operands = [columns, small, y, saved, up, pull, *tables, columns, small, *before]
    specs = [rows(2 * channels), rows(thin), rows(channels), saved_spec, rows(channels), flat_rows(1)]
    specs += [whole(table) for table in tables] + [halo(16, 2 * channels), halo(8, thin)]
    specs += [last_rows(before[0], 16), last_rows(before[1], 8)]
    if carried is not None:
        operands += list(carried)
        specs += [whole(array) for array in carried]
    operands += list(after)
    specs += unread(after)
    fixed_shapes = [(shared // 2, 2 * channels), (8, 2 * channels), (8, shared), (8, 2 * channels), (8, shared), (16, 128)]
    return pl.pallas_call(
        functools.partial(backward_kernel, early is None, carried is None, heads),
        grid=(blocks,),
        in_specs=specs,
        out_specs=[flat_rows(4 * channels + 2 * thin)] + [fixed(*shape) for shape in fixed_shapes],
        out_shape=[jax.ShapeDtypeStruct((tokens, 4 * channels + 2 * thin), BF16)]
        + [jax.ShapeDtypeStruct(shape, F32) for shape in fixed_shapes],
        scratch_shapes=[
            pltpu.VMEM((CHUNK + 8, channels), F32),
            pltpu.VMEM((CHUNK + 8, shared), F32),
            pltpu.VMEM((CHUNK + 8, 2 * channels), F32),
            pltpu.VMEM((CHUNK + 8, shared), F32),
        ],
        compiler_params=pltpu.CompilerParams(vmem_limit_bytes=56 * 1024 * 1024),
        cost_estimate=pl.CostEstimate(
            flops=tokens * channels * 28000, bytes_accessed=tokens * channels * 40, transcendentals=tokens * channels * 12
        ),
        name="mixer_backward",
    )(*operands)


def product_call(kernel, grid, specs, outs, out_specs, operands, flops, name):
    moved = sum(array.size * array.dtype.itemsize for array in operands[:1]) + flops // 512
    return pl.pallas_call(
        kernel,
        grid=grid,
        in_specs=specs,
        out_specs=out_specs,
        out_shape=outs,
        compiler_params=pltpu.CompilerParams(vmem_limit_bytes=60 * 1024 * 1024),
        cost_estimate=pl.CostEstimate(flops=flops, bytes_accessed=moved, transcendentals=0),
        name=name,
    )(*operands)


def in_projection(normed, gathered, own, thin):
    tokens, features = normed.shape

    def kernel(normed_ref, main_ref, thin_ref, columns_ref, small_ref):
        rows = normed_ref[...]
        columns_ref[0] = mm(rows, main_ref[...]).astype(BF16)

        @pl.when(pl.program_id(1) == 0)
        def _():
            small_ref[0] = mm(rows, thin_ref[...])

    return product_call(
        kernel,
        (2, 2),
        [
            pl.BlockSpec((tokens, features), lambda s, n: (0, 0)),
            pl.BlockSpec((features, own), lambda s, n: (s, 1 + n)),
            pl.BlockSpec((features, thin), lambda s, n: (s, 3 * own // thin)),
        ],
        [jax.ShapeDtypeStruct((2, tokens, 2 * own), BF16), jax.ShapeDtypeStruct((2, tokens, thin), F32)],
        [
            pl.BlockSpec((1, tokens, own), lambda s, n: (s, 0, n)),
            pl.BlockSpec((1, tokens, thin), lambda s, n: (s, 0, 0)),
        ],
        (normed, gathered, gathered),
        4 * tokens * features * (2 * own + thin),
        "in_projection",
    )


def out_projection(mixed, gathered, own):
    _, tokens, _ = mixed.shape
    features = gathered.shape[0] // 2
    tile = min(512, features)
    tiles = features // tile

    def kernel(mixed_ref, first_ref, second_ref, share_ref):
        share_ref[...] = (mm(mixed_ref[0], first_ref[...], NT) + mm(mixed_ref[1], second_ref[...], NT)).astype(BF16)

    return product_call(
        kernel,
        (tiles,),
        [
            pl.BlockSpec((2, tokens, own), lambda n: (0, 0, 0)),
            pl.BlockSpec((tile, own), lambda n: (n, 0)),
            pl.BlockSpec((tile, own), lambda n: (tiles + n, 0)),
        ],
        jax.ShapeDtypeStruct((tokens, features), BF16),
        pl.BlockSpec((tokens, tile), lambda n: (0, n)),
        (mixed, gathered, gathered),
        4 * tokens * features * own,
        "out_projection",
    )


def mixed_gradient(up, gathered, own, mixed):
    tokens, features = up.shape

    def kernel(up_ref, weight_ref, mixed_ref, grad_ref, pull_ref):
        grad = mm(up_ref[...], weight_ref[...])
        grad_ref[0] = grad.astype(BF16)
        pull = jnp.sum(grad * mixed_ref[0].astype(F32), axis=1, keepdims=True)

        @pl.when(pl.program_id(0) == 0)
        def _():
            pull_ref[...] = pull

        @pl.when(pl.program_id(0) == 1)
        def _():
            pull_ref[...] += pull

    return product_call(
        kernel,
        (2,),
        [
            pl.BlockSpec((tokens, features), lambda s: (0, 0)),
            pl.BlockSpec((features, own), lambda s: (s, 0)),
            pl.BlockSpec((1, tokens, own), lambda s: (s, 0, 0)),
        ],
        [jax.ShapeDtypeStruct((2, tokens, own), BF16), jax.ShapeDtypeStruct((tokens, 1), F32)],
        [pl.BlockSpec((1, tokens, own), lambda s: (s, 0, 0)), pl.BlockSpec((tokens, 1), lambda s: (0, 0))],
        (up, gathered, mixed),
        4 * tokens * features * own,
        "mixed_gradient",
    )


def normed_gradient(dcolumns, gathered, own, thin):
    tokens, columns = dcolumns.shape
    features = gathered.shape[0] // 2
    tile = min(512, features)
    tiles = features // tile

    def kernel(dcolumns_ref, *refs):
        total, at = 0.0, 0
        for ref in refs[:-1]:
            total = total + mm(dcolumns_ref[:, at : at + ref.shape[1]], ref[...], NT)
            at += ref.shape[1]
        refs[-1][...] = total.astype(BF16)

    specs = [pl.BlockSpec((tokens, columns), lambda n: (0, 0))]
    for shard in range(2):
        specs.append(pl.BlockSpec((tile, own), lambda n, s=shard: (s * tiles + n, 1)))
        specs.append(pl.BlockSpec((tile, own), lambda n, s=shard: (s * tiles + n, 2)))
        specs.append(pl.BlockSpec((tile, thin), lambda n, s=shard: (s * tiles + n, 3 * own // thin)))
    return product_call(
        kernel,
        (tiles,),
        specs,
        jax.ShapeDtypeStruct((tokens, features), BF16),
        pl.BlockSpec((tokens, tile), lambda n: (0, n)),
        (dcolumns,) + (gathered,) * 6,
        2 * tokens * features * columns,
        "normed_gradient",
    )


def stacked_product(lhs, rhs, block=None):
    tokens, features = lhs[0].shape
    chunks = len(lhs)
    split = rhs[0].ndim == 3
    columns = rhs[0].shape[-1] if split else rhs[0].shape[1] // 2
    row_tile, core = (min(256, features), jnp.zeros((1,), jnp.int32)) if block is None else block
    stride = 1 if block is None else 2
    steps = features // (row_tile * stride)

    def kernel(core_ref, *refs):
        out_ref = refs[-1]
        for shard in range(2):
            total = 0.0
            for at in range(chunks):
                ref = refs[chunks + at]
                part = ref[shard] if split else ref[:, shard * columns : (shard + 1) * columns]
                total = total + mm(refs[at][...], part, TN)
            out_ref[shard] = total.astype(BF16)

    return pl.pallas_call(
        kernel,
        grid_spec=pltpu.PrefetchScalarGridSpec(
            num_scalar_prefetch=1,
            grid=(steps,),
            in_specs=[pl.BlockSpec((tokens, row_tile), lambda m, core_ref: (0, stride * m + core_ref[0]))] * chunks
            + [pl.BlockSpec(part.shape, lambda m, core_ref, n=part.ndim: (0,) * n) for part in rhs],
            out_specs=pl.BlockSpec((2, row_tile, columns), lambda m, core_ref: (0, m, 0)),
        ),
        out_shape=jax.ShapeDtypeStruct((2, steps * row_tile, columns), BF16),
        compiler_params=pltpu.CompilerParams(vmem_limit_bytes=60 * 1024 * 1024),
        cost_estimate=pl.CostEstimate(
            flops=4 * steps * row_tile * columns * tokens * chunks,
            bytes_accessed=4 * steps * row_tile * columns + 2 * chunks * tokens * (2 * columns + features),
            transcendentals=0,
        ),
        name="stacked_product",
    )(core, *lhs, *rhs)


class Where:
    def __init__(self, chips, groups):
        self.chips, self.groups = chips, groups
        self.dp, self.tensor = lax.axis_index("dp"), lax.axis_index("tensor")
        self.chip, self.core = self.dp // 2, self.dp % 2
        self.shard, self.group = self.tensor % 2, self.tensor // 2

    def other_core(self):
        return (self.dp + 1 - 2 * self.core, self.tensor)

    def pair(self):
        return (self.dp, self.tensor + 1 - 2 * self.shard)

    def chip_at(self, chip):
        return (chip * 2 + self.core, self.tensor)

    def chip_hop(self, hop):
        return self.chip_at((self.chip + hop) % self.chips)

    def group_hop(self, hop):
        return (self.dp, (self.group + hop) % self.groups * 2 + self.shard)

    def meet(self):
        partners = [self.other_core(), self.pair()]
        partners += [self.chip_hop(hop) for hop in range(1, self.chips)]
        partners += [self.group_hop(hop) for hop in range(1, self.groups)]
        barrier = pltpu.get_barrier_semaphore()
        for partner in partners:
            pl.semaphore_signal(barrier, inc=1, device_id=partner, device_id_type=MESH)
        pl.semaphore_wait(barrier, len(partners))


def remote(src, dst, send_sem, recv_sem, device):
    return pltpu.make_async_remote_copy(
        src_ref=src, dst_ref=dst, send_sem=send_sem, recv_sem=recv_sem, device_id=device, device_id_type=MESH
    )


def gather_kernel(chips, groups, block_ref, hidden_ref, all_ref, stream_ref, left_sem, right_sem, pair_sem, core_sem,
                  chain_recv, pair_recv, core_recv, hidden_send, hidden_recv, local_sem):
    at = Where(chips, groups)
    at.meet()
    mine = pltpu.make_async_copy(block_ref, all_ref.at[at.shard, at.dp], local_sem.at[0])
    mine.start()
    rows = pltpu.make_async_copy(hidden_ref.at[at.shard], stream_ref.at[at.tensor], local_sem.at[1])
    rows.start()

    def hidden_copies():
        slot = stream_ref.at[at.tensor]
        copies = [remote(hidden_ref.at[1 - at.shard], slot, hidden_send.at[0], hidden_recv.at[at.tensor], at.pair())]
        for hop in range(1, groups):
            copies.append(
                remote(hidden_ref.at[at.shard], slot, hidden_send.at[hop], hidden_recv.at[at.tensor], at.group_hop(hop))
            )
        return copies

    def hidden_passed():
        other = at.tensor + 1 - 2 * at.shard
        slot = stream_ref.at[other]
        return [
            remote(slot, slot, hidden_send.at[groups - 1 + hop], hidden_recv.at[other], at.group_hop(hop))
            for hop in range(1, groups)
        ]

    def source(chip):
        return chip * 2 + at.core

    def own_or(chip):
        return all_ref.at[at.shard, source(chip)]

    def to_left(chip, src):
        return remote(src, own_or(chip), left_sem.at[chip], chain_recv.at[chip], at.chip_at(jnp.maximum(at.chip - 1, 0)))

    def to_right(chip, src):
        neighbour = at.chip_at(jnp.minimum(at.chip + 1, chips - 1))
        return remote(src, own_or(chip), right_sem.at[chip], chain_recv.at[chip], neighbour)

    def to_pair(chip, src):
        return remote(src, own_or(chip), pair_sem.at[chip], pair_recv.at[chip], at.pair())

    def to_core(shard, chip, src):
        place = all_ref.at[shard, source(chip)]
        return remote(src, place, core_sem.at[shard, chip], core_recv.at[shard, chip], at.other_core())

    has_left, has_right = at.chip > 0, at.chip < chips - 1
    for copy in hidden_copies():
        copy.start()
    to_pair(at.chip, block_ref).start()

    @pl.when(has_left)
    def _():
        to_left(at.chip, block_ref).start()

    @pl.when(has_right)
    def _():
        to_right(at.chip, block_ref).start()

    to_core(at.shard, at.chip, block_ref).start()

    def from_left(step):
        chip = jnp.maximum(at.chip - step, 0)
        return at.chip >= step, chip

    def from_right(step):
        chip = jnp.minimum(at.chip + step, chips - 1)
        return at.chip + step < chips, chip

    for step in range(1, chips):
        there, chip = from_left(step)

        @pl.when(there)
        def _():
            block = own_or(chip)
            to_right(chip, block).wait_recv()

            @pl.when(has_right)
            def _():
                to_right(chip, block).start()

            to_pair(chip, block).start()
            to_core(at.shard, chip, block).start()

        there, chip = from_right(step)

        @pl.when(there)
        def _():
            block = own_or(chip)
            to_left(chip, block).wait_recv()

            @pl.when(has_left)
            def _():
                to_left(chip, block).start()

            to_pair(chip, block).start()
            to_core(at.shard, chip, block).start()

        if step == 1:
            hidden_copies()[0].wait_send()
            other = at.tensor + 1 - 2 * at.shard
            arrived = stream_ref.at[other]
            remote(arrived, arrived, hidden_send.at[0], hidden_recv.at[other], at.pair()).wait_recv()
            for copy in hidden_passed():
                copy.start()

    def pair_block(chip):
        return all_ref.at[1 - at.shard, source(chip)]

    def pass_pair(chip):
        block = pair_block(chip)
        remote(block, block, pair_sem.at[chip], pair_recv.at[chip], at.pair()).wait_recv()
        to_core(1 - at.shard, chip, block).start()

    pass_pair(at.chip)
    for step in range(1, chips):
        there, chip = from_left(step)

        @pl.when(there)
        def _():
            pass_pair(chip)

        there, chip = from_right(step)

        @pl.when(there)
        def _():
            pass_pair(chip)

    mine.wait()
    rows.wait()
    for copy in hidden_copies()[1:]:
        copy.wait_send()
    for copy in hidden_passed():
        copy.wait_send()
    for hop in range(1, groups):
        for shard in range(2):
            member = (at.group + hop) % groups * 2 + shard
            arrived = stream_ref.at[member]
            remote(arrived, arrived, hidden_send.at[0], hidden_recv.at[member], at.pair()).wait_recv()
    far_core = 1 - at.core
    for chip in range(chips):
        block = own_or(chip)
        to_pair(chip, block).wait_send()
        for shard in range(2):
            to_core(shard, chip, all_ref.at[shard, source(chip)]).wait_send()
            arrived = all_ref.at[shard, chip * 2 + far_core]
            remote(arrived, arrived, core_sem.at[shard, chip], core_recv.at[shard, chip], at.other_core()).wait_recv()

        @pl.when(has_right & (at.chip >= chip))
        def _():
            to_right(chip, block).wait_send()

        @pl.when(has_left & (at.chip <= chip))
        def _():
            to_left(chip, block).wait_send()


def gathered_first(place, block, hidden):
    chips, groups, members = place.chips, place.groups, place.members
    anywhere = pl.BlockSpec(memory_space=pl.ANY)
    dma = pltpu.SemaphoreType.DMA
    both, stream = pl.pallas_call(
        functools.partial(gather_kernel, chips, groups),
        in_specs=[anywhere] * 2,
        out_specs=[anywhere] * 2,
        out_shape=[
            jax.ShapeDtypeStruct((2, 2 * chips) + block.shape, BF16),
            jax.ShapeDtypeStruct((members,) + hidden.shape[1:], BF16),
        ],
        scratch_shapes=[
            dma((chips,)), dma((chips,)), dma((chips,)), dma((2, chips)),
            dma((chips,)), dma((chips,)), dma((2, chips)),
            dma((2 * groups,)), dma((members,)), dma((2,)),
        ],
        compiler_params=pltpu.CompilerParams(collective_id=1, has_side_effects=True),
        cost_estimate=pl.CostEstimate(flops=0, bytes_accessed=300 * 1024 * 1024, transcendentals=0),
        name="gathered_first",
    )(block, hidden)
    return both.reshape(-1, block.shape[1]), stream.reshape(-1, hidden.shape[2])


def reduce_kernel(chips, groups, orders, parts, *refs):
    lhs, rhs, halves_ref, common_ref = refs[:parts], refs[parts : 2 * parts], refs[2 * parts], refs[2 * parts + 1]
    (out_ref, half_out, common_out, pair_out, pair_in, own, chain_in, half_buf, half_in, common_buf, common_in,
     pair_send, pair_recv, chain_send, chain_recv, half_send, half_recv, common_send, common_recv) = refs[2 * parts + 2 :]
    rows, columns = out_ref.shape
    tile = columns // 2 if columns % 256 == 0 else columns
    at = Where(chips, groups)
    at.meet()

    stages = [[at.other_core()], [at.pair()], [at.chip_hop(hop) for hop in range(1, chips)]]
    stages.append([at.group_hop(hop) for hop in range(1, groups)])
    firsts = [sum(len(stage) for stage in stages[:no]) for no in range(4)]

    def small_copies(stage):
        copies = []
        for step, device in enumerate(stages[stage]):
            slot = firsts[stage] + step
            copies.append(
                remote(common_buf.at[stage], common_in.at[slot], common_send.at[slot], common_recv.at[slot], device)
            )
            if stage == 0:
                for shard in range(2):
                    copies.append(
                        remote(half_buf.at[0, shard], half_in.at[shard], half_send.at[shard], half_recv.at[shard], device)
                    )
            elif stage == 1:
                copies.append(
                    remote(half_buf.at[1, 1 - at.shard], half_in.at[2], half_send.at[2], half_recv.at[2], device)
                )
            elif stage == 2:
                copies.append(
                    remote(half_buf.at[2, 0], half_in.at[3 + step], half_send.at[3 + step], half_recv.at[3 + step], device)
                )
        return copies

    def small_start(stage):
        for copy in small_copies(stage):
            copy.start()

    def small_finish(stage):
        for copy in small_copies(stage):
            copy.wait()
        total = common_buf[stage]
        for step in range(len(stages[stage])):
            total = total + common_in[firsts[stage] + step]
        if stage < 3:
            common_buf[stage + 1] = total
        else:
            common_out[...] = total
        if stage == 0:
            for shard in range(2):
                half_buf[1, shard] = half_buf[0, shard] + half_in[shard]
        elif stage == 1:
            half_buf[2, 0] = jnp.where(at.shard == 0, half_buf[1, 0], half_buf[1, 1]) + half_in[2]
        elif stage == 2:
            total = half_buf[2, 0]
            for step in range(chips - 1):
                total = total + half_in[3 + step]
            half_out[...] = total
        if stage < 3:
            small_start(stage + 1)

    half_buf[0] = halves_ref[...]
    common_buf[0] = common_ref[...]
    small_start(0)

    def target(step):
        chip = 0
        for number, order in enumerate(orders):
            chip = chip + jnp.where(at.chip == number, order[step], 0)
        return chip

    def pair_copy(step):
        return remote(pair_out.at[step], pair_in.at[step], pair_send.at[step], pair_recv.at[step], at.pair())

    def chain_copy(step):
        chip = target(step)
        right = chip > at.chip
        neighbour = jnp.clip(jnp.where(right, at.chip + 1, at.chip - 1), 0, chips - 1)
        slot = jnp.where(right | (neighbour != chip), chip, chips)
        return remote(pair_out.at[step], chain_in.at[slot], chain_send.at[step], chain_recv.at[slot], at.chip_at(neighbour))

    def arrival(slot):
        block = chain_in.at[slot]
        return remote(block, block, chain_send.at[0], chain_recv.at[slot], at.pair())

    def multiply(step):
        chip = target(step)
        features = pl.ds(pl.multiple_of((2 * chip + at.core) * rows, 128), rows)

        def product(column):
            total = 0.0
            for part in range(parts):
                total = total + mm(lhs[part][:, features], rhs[part][:, pl.ds(column, tile)], TN)
            return total

        @pl.loop(0, columns // tile)
        def _(tile_no):
            first = pl.multiple_of(tile_no * tile, 128)
            column = pl.multiple_of((1 - at.shard) * columns + first, 128)
            pair_out[step, :, pl.ds(first, tile)] = product(column).astype(BF16)

        pair_copy(step).start()

        @pl.loop(0, columns // tile)
        def _(tile_no):
            first = pl.multiple_of(tile_no * tile, 128)
            column = pl.multiple_of(at.shard * columns + first, 128)
            own[step % 3, :, pl.ds(first, tile)] = product(column)

    def in_tiles(body):
        @pl.loop(0, columns // 128)
        def _(tile_no):
            body(pl.ds(pl.multiple_of(tile_no * 128, 128), 128))

    def add_to_own(step, block, slot):
        def body(lanes):
            own[step % 3, :, lanes] = own[step % 3, :, lanes] + block[slot, :, lanes].astype(F32)

        in_tiles(body)

    def pass_on(step):
        pair_copy(step).wait()
        add_to_own(step, pair_in, step)
        chip = target(step)
        if step < chips - 1:

            @pl.when(((chip > at.chip) & (at.chip > 0)) | ((chip < at.chip) & (at.chip < chips - 1)))
            def _():
                arrival(chip).wait_recv()
                add_to_own(step, chain_in, chip)

            def body(lanes):
                pair_out[step, :, lanes] = own[step % 3, :, lanes].astype(BF16)

            in_tiles(body)
            chain_copy(step).start()
        else:

            @pl.when(at.chip > 0)
            def _():
                arrival(at.chip).wait_recv()
                add_to_own(step, chain_in, at.chip)

            @pl.when(at.chip < chips - 1)
            def _():
                arrival(chips).wait_recv()
                add_to_own(step, chain_in, chips)

            def body(lanes):
                out_ref[:, lanes] = own[step % 3, :, lanes]

            in_tiles(body)

    for step in range(chips):
        multiply(step)
        if step >= 2:
            pass_on(step - 2)
        if step < 4:
            small_finish(step)
    for stage in range(chips, 4):
        small_finish(stage)
    for step in range(max(0, chips - 2), chips):
        pass_on(step)
    for step in range(chips - 1):
        chain_copy(step).wait_send()


def reduced_product(place, lhs, rhs, halves, common, number):
    chips, groups = place.chips, place.groups
    rows, columns = lhs[0].shape[1] // (2 * chips), rhs[0].shape[1] // 2
    orders = []
    for chip in range(chips):
        due = {to: chip + chips - 1 - to if to > chip else chips - 1 - chip + to for to in range(chips) if to != chip}
        orders.append(sorted(due, key=due.get) + [chip])
    parts = len(lhs)
    slots = 1 + 1 + (chips - 1) + (groups - 1)
    vmem = pl.BlockSpec(memory_space=pltpu.VMEM)
    dma = pltpu.SemaphoreType.DMA
    half = halves.shape[1:]
    return pl.pallas_call(
        functools.partial(reduce_kernel, chips, groups, orders, parts),
        in_specs=[vmem] * (2 * parts + 2),
        out_specs=[vmem] * 3,
        out_shape=[
            jax.ShapeDtypeStruct((rows, columns), F32),
            jax.ShapeDtypeStruct(half, F32),
            jax.ShapeDtypeStruct(common.shape, F32),
        ],
        scratch_shapes=[
            pltpu.VMEM((chips, rows, columns), BF16),
            pltpu.VMEM((chips, rows, columns), BF16),
            pltpu.VMEM((3, rows, columns), F32),
            pltpu.VMEM((chips + 1, rows, columns), BF16),
            pltpu.VMEM((3, 2) + half, F32),
            pltpu.VMEM((2 + chips,) + half, F32),
            pltpu.VMEM((4,) + common.shape, F32),
            pltpu.VMEM((slots,) + common.shape, F32),
            dma((chips,)), dma((chips,)), dma((chips,)), dma((chips + 1,)),
            dma((2 + chips,)), dma((2 + chips,)), dma((slots,)), dma((slots,)),
        ],
        compiler_params=pltpu.CompilerParams(
            collective_id=2 + number, has_side_effects=True, vmem_limit_bytes=60 * 1024 * 1024
        ),
        cost_estimate=pl.CostEstimate(
            flops=24 * chips * rows * columns * parts * lhs[0].shape[0], bytes_accessed=100 * 1024 * 1024, transcendentals=0
        ),
        name="reduced_product",
    )(*lhs, *rhs, halves, common)


class Place:
    def __init__(self):
        self.members = lax.axis_size("tensor")
        self.groups = self.members // 2
        self.sequence = lax.axis_index("tensor") % 2
        self.group = lax.axis_index("tensor") // 2
        self.chips = lax.axis_size("dp") // 2
        self.chip = lax.axis_index("dp") // 2
        self.core = lax.axis_index("dp") % 2
        copies = lax.axis_size("dp")
        self.owners = [
            [d * self.members + 2 * g + s for s in range(2) for d in range(copies)] for g in range(self.groups)
        ]

    def to_pair(self, v):
        return lax.ppermute(v, "tensor", [(t, t ^ 1) for t in range(self.members)])

    def to_group(self, v, hop):
        return lax.ppermute(v, "tensor", [(t, (t + 2 * hop) % self.members) for t in range(self.members)])

    def to_core(self, v):
        return lax.ppermute(v, "dp", [(t, t ^ 1) for t in range(2 * self.chips)])

    def to_chip(self, v, hop):
        count = 2 * self.chips
        return lax.ppermute(v, "dp", [(t, (t + 2 * hop) % count) for t in range(count)])

    def gather_owners(self, v):
        return lax.all_gather(v, ("dp", "tensor"), axis=0, axis_index_groups=self.owners, tiled=True)

    def add_groups(self, v):
        return v + sum(self.to_group(v, hop) for hop in range(1, self.groups))

    def sent_to_groups(self, v):
        return [self.to_group(v, hop) for hop in range(1, self.groups)]

    def both(self, v, axis):
        other = self.to_pair(v)
        return jnp.where(
            self.sequence == 0, jnp.concatenate([v, other], axis=axis), jnp.concatenate([other, v], axis=axis)
        )

    def rows_of(self, chunks, hop):
        at = (self.group + hop) % self.groups
        if len(chunks) == self.groups == 2:
            return jnp.where(at == 0, chunks[0], chunks[1])
        total = jnp.concatenate(chunks)
        count = total.shape[0] // self.groups
        return lax.dynamic_slice_in_dim(total, at * count, count, 0)

    def gather_chunks(self, v, chunks):
        if chunks == self.groups == 2:
            other = self.to_group(v, 1)
            return [jnp.where(self.group == at, v, other) for at in range(2)]
        count = v.shape[0]
        total = jnp.zeros((count * self.groups,) + v.shape[1:], v.dtype)
        total = lax.dynamic_update_slice_in_dim(total, v, self.group * count, 0)
        for hop in range(1, self.groups):
            start = (self.group - hop) % self.groups * count
            total = lax.dynamic_update_slice_in_dim(total, self.to_group(v, hop), start, 0)
        return jnp.split(total, chunks)

    def scatter_rows(self, chunks):
        arrived = [self.to_group(self.rows_of(chunks, hop), hop) for hop in range(1, self.groups)]
        return self.rows_of(chunks, 0).astype(F32) + sum(piece.astype(F32) for piece in arrived)

    def take_sequence(self, v):
        mine = jnp.where(self.sequence == 0, v[0], v[1])
        other = self.to_pair(jnp.where(self.sequence == 0, v[1], v[0]))
        return jnp.where(self.sequence == 0, jnp.concatenate([mine, other]), jnp.concatenate([other, mine]))

    def give_sequence(self, v):
        first, second = jnp.split(v.astype(BF16), 2)
        mine = jnp.where(self.sequence == 0, first, second)
        other = self.to_pair(jnp.where(self.sequence == 0, second, first))
        return mine, other

    def both_sequences(self, given, *earlier):
        mine, other = then(given, *earlier)
        mine, other = mine.astype(F32), other.astype(F32)
        return jnp.where(self.sequence == 0, jnp.stack([mine, other]), jnp.stack([other, mine]))


def then(v, *earlier):
    return lax.optimization_barrier((v, earlier))[0]


def added(v, arrived):
    return v.astype(F32) + sum(piece.astype(F32) for piece in arrived)


class WeightSum:

    def __init__(self, place, features, columns):
        self.place = place
        self.lhs = list(features) + [place.to_core(part) for part in features]
        self.rhs = list(columns) + [place.to_core(part) for part in columns]

    def to_pair(self, *earlier):
        place = self.place
        self.lhs = list(then(tuple(self.lhs), *earlier))
        rows = self.lhs[0].shape[1] // (2 * place.chips)
        self.stack = stacked_product(self.lhs, self.rhs, (rows, place.core.astype(jnp.int32)[None]))
        other = lax.dynamic_index_in_dim(self.stack, 1 - self.place.sequence, 0, keepdims=False)
        self.landed = self.place.to_pair(other)
        return other

    def to_chips(self):
        place = self.place
        own = lax.dynamic_index_in_dim(self.stack, place.sequence, 0, keepdims=False)
        total = (own.astype(F32) + self.landed.astype(F32)).astype(BF16)
        pieces = total.reshape(place.chips, -1, total.shape[1])
        self.kept = lax.dynamic_index_in_dim(pieces, place.chip, 0, keepdims=False)
        hops = range(1, place.chips)
        self.sent = [
            lax.dynamic_index_in_dim(pieces, (place.chip + hop) % place.chips, 0, keepdims=False) for hop in hops
        ]
        self.arrived = [place.to_chip(piece, hop) for piece, hop in zip(self.sent, hops)]
        return self.sent

    def total(self, *earlier):
        kept, arrived = then((self.kept, tuple(self.arrived)), *earlier)
        return added(kept, arrived)


def norm_scale(stream):
    return lax.rsqrt(jnp.mean(stream * stream, axis=-1, keepdims=True) + EPSILON)


def block_forward(place, incoming, weights, tables, heads, inner, final):
    gathered, gain, own, thin = weights
    kept = {"update": []}
    for key in ("stream", "normed", "columns", "small", "mixed", "y", "saved", "scale", "share"):
        kept[key] = []
    earlier = None
    for at in range(PIECES):
        stream = incoming(at, *kept["share"][-1:])
        part = (stream * norm_scale(stream) * gain).astype(BF16)
        if at:
            part = then(part, kept["share"][at - 1])
        columns, small = in_projection(part, gathered, own, thin)
        mixed, square, y, saved, state = mixer_forward(columns, small, tables, heads, earlier)
        earlier = (state, columns, small)
        scale = lax.rsqrt(place.add_groups(square) / inner + EPSILON)
        share = then(out_projection(mixed, gathered, own), scale)
        results = (stream, part, columns, small, mixed, y, saved, scale, share)
        names = ("stream", "normed", "columns", "small", "mixed", "y", "saved", "scale", "share")
        for key, value in zip(names, results):
            kept[key].append(value)
    shares, scales = kept["share"], kept["scale"]
    if final:
        after = place.rows_of(kept["stream"], 0) + place.scatter_rows(shares) * place.rows_of(scales, 0)
    else:
        arrived = [place.sent_to_groups(share) for share in shares]

        def after(at, *earlier):
            update = added(shares[at], then(tuple(arrived[at]), *earlier) if earlier else arrived[at])
            kept["update"].append(update)
            return kept["stream"][at] + update * scales[at]

    return after, kept


def norm_backward(stream, grad, grad_normed, gain):
    row_scale = norm_scale(stream)
    unit = stream * row_scale
    lifted = grad_normed * gain
    back = grad + row_scale * (lifted - unit * jnp.mean(lifted * unit, axis=-1, keepdims=True))
    return back, jnp.sum(grad_normed * unit, axis=0)


class Backward:
    def __init__(self, place, weights, tables, heads, inner, kept, final):
        self.final = final
        self.place, self.weights, self.tables, self.heads, self.inner, self.kept = place, weights, tables, heads, inner, kept
        chunks = len(kept["normed"])
        self.ups, self.grad_mixed, self.pulls = [None] * chunks, [None] * chunks, [None] * chunks
        self.dcolumns, self.shares = [None] * chunks, [None] * chunks
        self.carried = None

    def enter(self, at, grad):
        gathered, _, own, _ = self.weights
        scale = self.kept["scale"][at]
        self.ups[at] = (grad * scale).astype(BF16)
        self.grad_mixed[at], pull = mixed_gradient(self.ups[at], gathered, own, self.kept["mixed"][at])
        if not self.final:
            pull = jnp.sum(self.ups[at].astype(F32) * self.kept["update"][at], axis=-1, keepdims=True)
        else:
            pull = self.place.add_groups(pull)
        self.pulls[at] = pull * (scale * scale / self.inner)

    def mix(self, at, after=()):
        kept = self.kept
        result = mixer_backward(
            kept["columns"][at],
            kept["small"][at],
            kept["y"][at],
            kept["saved"][at],
            self.grad_mixed[at],
            self.pulls[at],
            self.tables,
            self.heads,
            (kept["columns"][at - 1], kept["small"][at - 1]) if at else None,
            self.carried,
            after,
        )
        self.dcolumns[at], self.carried = result[0], result[1:]

    def share(self, columns):
        gathered, _, own, thin = self.weights
        return normed_gradient(columns, gathered, own, thin)


def local(
    hidden,
    cotangent,
    norm_gain,
    in_weights,
    state_weight,
    step_weight,
    channel_taps,
    state_taps,
    step_bias,
    decay_log,
    skip_gain,
    inner_gain,
    out_weight,
):
    place = Place()
    layers = in_weights.shape[0]
    rows = in_weights.shape[2]
    heads = step_bias.shape[1]
    own_cols = in_weights.shape[3]
    width = own_cols // heads
    inner = own_cols * place.members
    shared = state_weight.shape[2]
    half = shared // 2
    copies = 128 // heads
    main = 2 * own_cols
    expand, tri = scan_tables(heads, own_cols)

    weights = []
    for layer in range(layers):
        if layer == 1:
            in_weights = then(in_weights, gathered)
        state_half = lax.dynamic_slice_in_dim(state_weight[layer], place.sequence * half, half, 1)
        thin = [step_weight[layer]] * 2
        blank = jnp.zeros((rows, 127 - 2 * heads), BF16)
        block = [out_weight[layer].T, in_weights[layer, 0], in_weights[layer, 1], state_half, *thin, blank]
        block = jnp.concatenate(block + [norm_gain[layer][:, None]], axis=1)
        if layer:
            gathered = place.gather_owners(block)
        else:
            gathered, sequence_rows = gathered_first(place, block, hidden)
        gain = gathered[: gathered.shape[0] // 2, -1].astype(F32)
        weights.append((gathered, gain, own_cols, half + 128))

    chunks = [stream.astype(F32) for stream in jnp.split(sequence_rows, PIECES)]

    def streams(at, *earlier):
        return chunks[at]

    per_channel = place.both(jnp.concatenate([channel_taps, inner_gain[:, None]], axis=1), 2)
    per_head = jnp.stack([step_bias, decay_log, skip_gain], axis=1)
    per_head = place.both(per_head[:, None], 1)
    tables = []
    for layer in range(layers):
        wide_skip = jnp.repeat(per_head[layer, :, 2].reshape(-1), width)[None]
        blank = jnp.zeros((1, main), F32)
        chan = jnp.concatenate([per_channel[layer, :5], wide_skip, per_channel[layer, 5:6], blank], axis=0)
        taps = jnp.concatenate([state_taps[layer], jnp.zeros((3, shared), F32)], axis=0)
        head = []
        for part in range(2):
            pair = jnp.stack([per_head[layer, part, 0], -jnp.exp(per_head[layer, part, 1])])
            pair = jnp.concatenate([pair, pair, jnp.zeros((2, 128 - 2 * heads), F32)], axis=1)
            head += [pair, jnp.zeros((6, 128), F32)]
        tables.append((chan, taps, jnp.concatenate(head), expand, tri))

    kept = []
    for layer in range(layers):
        final = layer == layers - 1
        if layer == 0:
            last_up = place.take_sequence(then(cotangent, chunks))
            last_up = place.gather_chunks(last_up, PIECES)
        streams, saved = block_forward(place, streams, weights[layer], tables[layer], heads, inner, final)
        kept.append(saved)
    mixed_out = place.give_sequence(streams)

    grads = [part.astype(F32) for part in last_up]
    in_sums, out_sums, gain_grads, carried = [None] * layers, [None] * layers, [0.0] * layers, [None] * layers
    half_totals, common_totals = [None] * layers, [None] * layers
    pending, held = None, ()

    def small_sums(layer):
        gchan, gtaps, ghead = carried[layer]
        blank = jnp.zeros((1, own_cols - 256), F32)
        parts = []
        for part in range(2):
            per_head_row = jnp.concatenate([ghead[8 * part : 8 * part + 1], ghead[8 * part + 1 : 8 * part + 2], blank], axis=1)
            parts.append(jnp.concatenate([gchan[:7, part * own_cols : (part + 1) * own_cols], per_head_row]))
        return jnp.stack(parts), gtaps

    for layer in reversed(range(layers)):
        final = layer == layers - 1
        back = Backward(place, weights[layer], tables[layer], heads, inner, kept[layer], final)
        for at in reversed(range(PIECES)):
            if not final:
                share, arrived = pending[at]
                before = (in_sums[layer + 1].owned,) if at == PIECES - 1 else (back.ups[at + 1],)
                grad_normed = added(share, then(tuple(arrived), *before))
                grads[at], gain_grad = norm_backward(
                    kept[layer + 1]["stream"][at], grads[at], grad_normed, weights[layer + 1][1]
                )
                gain_grads[layer + 1] = gain_grads[layer + 1] + jnp.where(place.group == 0, gain_grad, 0.0)
            back.enter(at, grads[at])
        normed, mixed = kept[layer]["normed"], kept[layer]["mixed"]
        out_sum = out_sums[layer] = WeightSum(place, back.ups, mixed)
        held += (out_sum.to_pair(),)
        for at in reversed(range(PIECES)):
            back.mix(at, held)
            held = ()
            if layer:
                back.shares[at] = back.share(back.dcolumns[at])
                held = (back.shares[at],)
                if at == PIECES - 1:
                    held += tuple(out_sum.to_chips())
        carried[layer] = back.carried[3:]
        in_sum = in_sums[layer] = WeightSum(place, normed, back.dcolumns)
        if layer:
            pending = [(share, place.sent_to_groups(share)) for share in back.shares]
            halves, common = small_sums(layer)
            halves = then(halves, *back.shares)
            in_sum.owned, half_totals[layer], common_totals[layer] = reduced_product(
                place, in_sum.lhs, in_sum.rhs, halves, common, layer
            )
            continue
        if PIECES == place.groups:
            sent = [back.share(place.rows_of(back.dcolumns, hop)) for hop in range(1, place.groups)]
            own = back.share(then(place.rows_of(back.dcolumns, 0), *sent))
        else:
            shares = [back.share(columns) for columns in back.dcolumns]
            sent = [place.rows_of(shares, hop) for hop in range(1, place.groups)]
            own = place.rows_of(shares, 0)
        arrived = [place.to_group(piece, hop) for hop, piece in enumerate(sent, 1)]
        out_sent = out_sum.to_chips()
        grad, gain_grads[layer] = norm_backward(
            place.rows_of(kept[layer]["stream"], 0), place.rows_of(grads, 0), added(own, arrived), weights[layer][1]
        )
    grad_hidden = place.give_sequence(grad)

    halves, common = small_sums(0)
    gains = jnp.stack(gain_grads).reshape(-1, shared)
    common = jnp.concatenate([common, gains, jnp.zeros((-gains.shape[0] % 8, shared), F32)])
    common = then(common, *out_sent)
    in_sums[0].owned, half_totals[0], common_totals[0] = reduced_product(
        place, in_sum.lhs, in_sum.rhs, halves, common, 0
    )
    gain_total = common_totals[0][8 : 8 + gains.shape[0]].reshape(layers, -1)

    outs = []
    for layer in range(layers):
        per_channel_part = half_totals[layer]
        gain_part = lax.dynamic_slice_in_dim(gain_total[layer], lax.axis_index("dp") * rows, rows, 0)
        taps_part = common_totals[layer][:5]
        in_owned, out_owned = in_sums[layer].owned, out_sums[layer].total(in_sums[layer].owned)
        state_part = place.both(place.add_groups(in_owned[:, main : main + half]), 1)
        outs.append(
            (
                gain_part,
                jnp.stack([in_owned[:, :own_cols], in_owned[:, own_cols:main]]),
                state_part,
                in_owned[:, main + half : main + half + heads],
                per_channel_part[:5],
                taps_part,
                per_channel_part[7, :heads],
                per_channel_part[7, 128 : 128 + heads],
                per_channel_part[5].reshape(heads, width).sum(axis=1),
                per_channel_part[6],
                out_owned.T,
            )
        )
    mixed_out = place.both_sequences(mixed_out, in_sums[-1].owned)
    grad_hidden = place.both_sequences(grad_hidden, in_sums[0].owned)
    return (mixed_out, grad_hidden) + tuple(jnp.stack(parts) for parts in zip(*outs))


def solution(mesh):
    placed = (
        P("dp", "tensor", None),
        P("dp", "tensor", None),
        P(None, "dp"),
        P(None, None, "dp", "tensor"),
        P(None, "dp", None),
        P(None, "dp", "tensor"),
        P(None, None, "tensor"),
        P(),
        P(None, "tensor"),
        P(None, "tensor"),
        P(None, "tensor"),
        P(None, "tensor"),
        P(None, "tensor", "dp"),
    )
    return jax.shard_map(
        local,
        mesh=mesh,
        in_specs=placed,
        out_specs=(
            P("dp", "tensor", None),
            P("dp", "tensor", None),
            P(None, "dp"),
            P(None, None, "dp", "tensor"),
            P(None, "dp", None),
            P(None, "dp", "tensor"),
            P(None, None, "tensor"),
            P(),
            P(None, "tensor"),
            P(None, "tensor"),
            P(None, "tensor"),
            P(None, "tensor"),
            P(None, "tensor", "dp"),
        ),
        check_vma=False,
    )
```

time: 1750 us -> 1220 us (0.70)
  waiting for transfers between devices: 986 us -> 90.9 us
  Pallas kernels: 172 us -> 867 us
  matrix products: 337 us -> 0 us
    pallas_call x8 -> x25, Pallas kernels: 63.1 us -> 759 us  [the longest x2 296 us: reduced_product(): pl.pallas_call(functools.partial(reduce_kernel, chips, groups, orders, pa...]
    reduce_scatter x4 -> x0, waiting for transfers between devices: 552 us -> none  [scatter_owners(): lax.psum_scatter(v, ('dp', 'tensor'), scatter_dimension=0, axis_index_gro...]
    dot_general x44 -> x0, matrix products: 337 us -> none  [mm(): return lax.dot_general(a, b, dims, preferred_element_type=F32)]
    ppermute x16 -> x15, waiting for transfers between devices: 218 us -> 45.7 us  [to_group(): lax.ppermute(v, 'tensor', [(t, (t + 2 * hop) % self.members) for t in ran...]
    ppermute x8 -> x9, waiting for transfers between devices: 100 us -> 5.15 us  [to_pair(): return lax.ppermute(v, 'tensor', [(t, t ^ 1) for t in range(self.members)])]
    all_gather x2 -> x1, waiting for transfers between devices: 114 us -> 34.1 us  [gather_owners(): lax.all_gather(v, ('dp', 'tensor'), axis=0, axis_index_groups=self.owners...]
    concatenate x6 -> x1, other arithmetic: 39 us -> 0.61 us  [local(): jnp.concatenate([common, gains, jnp.zeros((-gains.shape[0] % 8, shared),...]
    ppermute x0 -> x22, starting transfers between devices: none -> 20.2 us  [the longest x6 17.2 us: to_chip(): lax.ppermute(v, 'dp', [(t, (t + 2 * hop) % count) for t in range(count)])]
  transfers between devices with their start and end apart: 31 -> 47, of which waited for: 18 -> 11; matrix products, arithmetic and copies ran while one was open for 23% -> 13% of each run, Pallas kernels for 7% -> 56%
where the time goes in v4:
time: 1220 us; the launch traced here: 1210 us
  Pallas kernels  867 us (71%)
  other arithmetic  132 us (11%)
  waiting for transfers between devices  90.9 us (7%)
  local copies, waits for them, and re-layouts  59.1 us (5%)
  starting transfers between devices  47 us (4%)
  between operations  15.7 us (1%)
    pallas_call x2, Pallas kernels, reduced_product(): pl.pallas_call(functools.partial(reduce_kernel, chips, groups, orders, pa...  296 us
    pallas_call x16, Pallas kernels, product_call(): pl.pallas_call(kernel, grid=grid, in_specs=specs, out_specs=out_specs, ou...  201 us
    pallas_call x1, Pallas kernels, gathered_first(): pl.pallas_call(functools.partial(gather_kernel, chips, groups), in_specs=...  180 us
    pallas_call x4, Pallas kernels, mixer_backward(): pl.pallas_call(functools.partial(backward_kernel, early is None, carried...  109 us
    pallas_call x4, Pallas kernels, mixer_forward(): pl.pallas_call(functools.partial(forward_kernel, earlier is None, heads),...  52.2 us
    ppermute x15, waiting for transfers between devices, to_group(): lax.ppermute(v, 'tensor', [(t, (t + 2 * hop) % self.members) for t in ran...  45.7 us
    all_gather x1, waiting for transfers between devices, gather_owners(): lax.all_gather(v, ('dp', 'tensor'), axis=0, axis_index_groups=self.owners...  34.1 us
    pallas_call x2, Pallas kernels, stacked_product(): pl.pallas_call(kernel, grid_spec=pltpu.PrefetchScalarGridSpec(num_scalar_...  29.2 us
  transfers between devices with their start and end apart: 47, of which 11 were waited for; matrix products, arithmetic and copies ran while one was open for 13% of the time, Pallas kernels for 56%

profile of v4, /device:TPU:0, one launch (start us, length us, event | category | flops | bytes accessed | tf_op | source)
XLA Modules:
  0.0 1212.1 jit_solution(2415894848902468334)
XLA Ops:
  16.7 179.8 %gathered_first.1 = (bf16[2,8,256,3328]{3,2,1,0:T(8,128)(2,1)}, bf16[4,256,2048]{2,1,0:T(8,128)(2,1)}) custom-call(bf16[256,3328]{1,0:T(8,128)(2,1)} %concatenate.132.block_ref, bf16[2,256,2048]{2,1,0:T(8,128)(2,1)} %hidden_ref.1), custom_call_target="tpu_custom_call" | custom-call | bytes 314572800 | tf_op jit(solution)/shard_map/gathered_first/pallas_call | solution.py:809
  219.9 16.0 %in_projection.4 = (bf16[2,512,2048]{2,1,0:T(8,128)(2,1)}, f32[2,512,256]{2,1,0:T(8,128)}) custom-call(bf16[512,2048]{1,0:T(8,128)(2,1)} %get-tuple-element.338.normed_ref.refs_0_, bf16[4096,3328]{1,0:T(8,128)(2,1)} %bitcast.184, bf16[4096,3328]{1,0:T(8,128)(2,1)} %bitcast.185), custom_call_target="tpu_custom_call" | custom-call | flops 9663676416 | bytes 20971520 | tf_op jit(solution)/shard_map/in_projection/pallas_call | solution.py:442
  238.3 12.8 %mixer_forward.4 = (bf16[2,512,1024]{2,1,0:T(8,128)(2,1)}, f32[512,1]{1,0:T(8,128)S(1)}, f32[2,512,1024]{2,1,0:T(8,128)}, bf16[2,4,128,1024]{3,2,1,0:T(8,128)(2,1)}, f32[128,2048]{1,0:T(8,128)S(1)}) custom-call(bf16[2,512,2048]{2,1,0:T(8,128)(2,1)} %get-tuple-element.111.refs_0_.refs_8_.refs_13_.refs_11_, f32[2,512,256]{2,1,0:T(8,128)S(1)} %copy-done.10, ...), custom_call_target="tpu_custom_call" | custom-call | flops 6291456000 | bytes 14680064 | tf_op jit(solution)/shard_map/mixer_forward/pallas_call | solution.py:358
  252.7 8.9 out_projection.4
  262.8 16.3 %in_projection.5 = (bf16[2,512,2048]{2,1,0:T(8,128)(2,1)}, f32[2,512,256]{2,1,0:T(8,128)}) custom-call(bf16[512,2048]{1,0:T(8,128)(2,1)} %get-tuple-element.116.normed_ref.refs_1_, bf16[4096,3328]{1,0:T(8,128)(2,1)} %bitcast.188, bf16[4096,3328]{1,0:T(8,128)(2,1)} %bitcast.189), custom_call_target="tpu_custom_call" | custom-call | flops 9663676416 | bytes 20971520 | tf_op jit(solution)/shard_map/in_projection/pallas_call | solution.py:442
  280.4 13.2 %mixer_forward.5 = (bf16[2,512,1024]{2,1,0:T(8,128)(2,1)}, f32[512,1]{1,0:T(8,128)S(1)}, f32[2,512,1024]{2,1,0:T(8,128)}, bf16[2,4,128,1024]{3,2,1,0:T(8,128)(2,1)}, f32[128,2048]{1,0:T(8,128)}) custom-call(bf16[2,512,2048]{2,1,0:T(8,128)(2,1)} %get-tuple-element.117.refs_0_.refs_11_, f32[2,512,256]{2,1,0:T(8,128)S(1)} %copy-done.12, ...), custom_call_target="tpu_custom_call" | custom-call | flops 6291456000 | bytes 14680064 | tf_op jit(solution)/shard_map/mixer_forward/pallas_call | solution.py:358
  295.3 9.3 out_projection.5
  304.6 10.7 collective-permute-done.4
  327.4 34.1 %all-gather.2.cloned.1.call-done.main_ref.thin_ref.first_ref.second_ref.weight_ref.refs_0_.refs_1_.refs_2_.refs_3_.refs_4_.refs_5_ = bf16[4096,3328]{1,0:T(8,128)(2,1)} async-done(((bf16[256,3328]{1,0:T(8,128)(2,1)}), bf16[4096,3328]{1,0:T(8,128)(2,1)}) %all-gather.2.cloned.1.call-update) | async-done | bytes 27262992 | tf_op jit(solution)/shard_map/all_gather | solution.py:1068
  366.9 15.7 %in_projection.6 = (bf16[2,512,2048]{2,1,0:T(8,128)(2,1)}, f32[2,512,256]{2,1,0:T(8,128)}) custom-call(bf16[512,2048]{1,0:T(8,128)(2,1)} %multiply_convert_fusion.3.normed_ref.refs_0_, bf16[4096,3328]{1,0:T(8,128)(2,1)} %all-gather.2.cloned.1.call-done.main_ref.thin_ref.first_ref.second_ref.weight_ref.refs_0_.refs_1_.refs_2_.refs_3_.refs_4_.refs_5_, ...), custom_call_target="tpu_custom_call" | custom-call | flops 9663676416 | bytes 20971520 | tf_op jit(solution)/shard_map/in_projection/pallas_call | solution.py:442
  383.9 12.9 %mixer_forward.6 = (bf16[2,512,1024]{2,1,0:T(8,128)(2,1)S(1)}, f32[512,1]{1,0:T(8,128)S(1)}, f32[2,512,1024]{2,1,0:T(8,128)}, bf16[2,4,128,1024]{3,2,1,0:T(8,128)(2,1)}, f32[128,2048]{1,0:T(8,128)S(1)}) custom-call(bf16[2,512,2048]{2,1,0:T(8,128)(2,1)} %get-tuple-element.124.refs_0_.refs_8_.refs_13_.refs_11_, f32[2,512,256]{2,1,0:T(8,128)S(1)} %copy-done.13, ...), custom_call_target="tpu_custom_call" | custom-call | flops 6291456000 | bytes 14680064 | tf_op jit(solution)/shard_map/mixer_forward/pallas_call | solution.py:358
  399.6 9.0 out_projection.6
  422.2 15.8 %in_projection.7 = (bf16[2,512,2048]{2,1,0:T(8,128)(2,1)}, f32[2,512,256]{2,1,0:T(8,128)}) custom-call(bf16[512,2048]{1,0:T(8,128)(2,1)} %multiply_convert_fusion.2.normed_ref.refs_1_, bf16[4096,3328]{1,0:T(8,128)(2,1)} %all-gather.2.cloned.1.call-done.main_ref.thin_ref.first_ref.second_ref.weight_ref.refs_0_.refs_1_.refs_2_.refs_3_.refs_4_.refs_5_, ...), custom_call_target="tpu_custom_call" | custom-call | flops 9663676416 | bytes 20971520 | tf_op jit(solution)/shard_map/in_projection/pallas_call | solution.py:442
  439.3 13.3 %mixer_forward.7 = (bf16[2,512,1024]{2,1,0:T(8,128)(2,1)}, f32[512,1]{1,0:T(8,128)S(1)}, f32[2,512,1024]{2,1,0:T(8,128)}, bf16[2,4,128,1024]{3,2,1,0:T(8,128)(2,1)}, f32[128,2048]{1,0:T(8,128)}) custom-call(bf16[2,512,2048]{2,1,0:T(8,128)(2,1)} %get-tuple-element.131.refs_0_.refs_11_, f32[2,512,256]{2,1,0:T(8,128)S(1)} %copy-done.15, ...), custom_call_target="tpu_custom_call" | custom-call | flops 6291456000 | bytes 14680064 | tf_op jit(solution)/shard_map/mixer_forward/pallas_call | solution.py:358
  466.3 9.5 mixed_gradient.4
  476.2 9.1 mixed_gradient.5
  495.3 14.5 %stacked_product.2 = bf16[2,1024,1024]{2,1,0:T(8,128)(2,1)} custom-call(s32[1]{0:T(128)} %bitcast.37.core_ref, bf16[512,2048]{1,0:T(8,128)(2,1)} %get-tuple-element.146.up_ref.refs_0_, bf16[512,2048]{1,0:T(8,128)(2,1)} %get-tuple-element.147.up_ref.refs_1_, bf16[512,2048]{1,0:T(8,128)(2,1)} %collective-permute-done.16.refs_2_, ...), custom_call_target="tpu_custom_call" | custom-call | flops 8589934592 | bytes 20971520 | tf_op jit(solution)/shard_map/stacked_product/pallas_call | solution.py:590
  514.6 26.9 %mixer_backward.4 = (bf16[512,4608]{1,0:T(8,128)(2,1)}, f32[128,2048]{1,0:T(8,128)}, f32[8,2048]{1,0:T(8,128)}, f32[8,256]{1,0:T(8,128)}, f32[8,2048]{1,0:T(8,12...) custom-call(bf16[2,512,2048]{2,1,0:T(8,128)(2,1)} %get-tuple-element.131.refs_0_.refs_11_, ...), custom_call_target="tpu_custom_call" | custom-call | flops 14680064000 | bytes 20971520 | tf_op jit(solution)/shard_map/mixer_backward/pallas_call | solution.py:419
  541.5 16.2 %normed_gradient.4.refs_21_ = bf16[512,2048]{1,0:T(8,128)(2,1)} custom-call(bf16[512,4608]{1,0:T(8,128)(2,1)} %get-tuple-element.156.dcolumns_ref.refs_5_, bf16[4096,3328]{1,0:T(8,128)(2,1)} %all-gather.2.cloned.1.call-done.main_ref.thin_ref.first_ref.second_ref.weight_ref.refs_0_.refs_1_.refs_2_.refs_3_.refs_4_.refs_5_, ...), custom_call_target="tpu_custom_call" | custom-call | flops 9663676416 | bytes 23592960 | tf_op jit(solution)/shard_map/normed_gradient/pallas_call | solution.py:442
  563.4 27.2 %mixer_backward.5 = (bf16[512,4608]{1,0:T(8,128)(2,1)}, f32[128,2048]{1,0:T(8,128)}, f32[8,2048]{1,0:T(8,128)}, f32[8,256]{1,0:T(8,128)}, f32[8,2048]{1,0:T(8,12...) custom-call(bf16[2,512,2048]{2,1,0:T(8,128)(2,1)} %get-tuple-element.124.refs_0_.refs_8_.refs_13_.refs_11_, ...), custom_call_target="tpu_custom_call" | custom-call | flops 14680064000 | bytes 20971520 | tf_op jit(solution)/shard_map/mixer_backward/pallas_call | solution.py:419
  606.3 16.5 %normed_gradient.5.refs_15_ = bf16[512,2048]{1,0:T(8,128)(2,1)} custom-call(bf16[512,4608]{1,0:T(8,128)(2,1)} %get-tuple-element.157.dcolumns_ref.refs_4_, bf16[4096,3328]{1,0:T(8,128)(2,1)} %all-gather.2.cloned.1.call-done.main_ref.thin_ref.first_ref.second_ref.weight_ref.refs_0_.refs_1_.refs_2_.refs_3_.refs_4_.refs_5_, ...), custom_call_target="tpu_custom_call" | custom-call | flops 9663676416 | bytes 23592960 | tf_op jit(solution)/shard_map/normed_gradient/pallas_call | solution.py:442
  625.2 163.9 %reduced_product.2 = (f32[256,2304]{1,0:T(8,128)}, f32[8,1024]{1,0:T(8,128)}, f32[8,256]{1,0:T(8,128)}) custom-call(bf16[512,2048]{1,0:T(8,128)(2,1)} %multiply_convert_fusion.3.normed_ref.refs_0_, bf16[512,2048]{1,0:T(8,128)(2,1)} %multiply_convert_fusion.2.normed_ref.refs_1_, bf16[512,2048]{1,0:T(8,128)(2,1)} %collective-permute-done.10.refs_2_, ...), custom_call_target="tpu_custom_call" | custom-call | flops 115964116992 | bytes 104857600 | tf_op jit(solution)/shard_map/reduced_product/pallas_call | solution.py:1009
  815.4 9.2 multiply_reduce_fusion.5
  852.5 9.1 mixed_gradient.7
  861.6 9.1 mixed_gradient.6
  875.5 14.6 %stacked_product.3 = bf16[2,1024,1024]{2,1,0:T(8,128)(2,1)} custom-call(s32[1]{0:T(128)} %bitcast.37.core_ref, bf16[512,2048]{1,0:T(8,128)(2,1)} %get-tuple-element.173.up_ref.refs_0_, bf16[512,2048]{1,0:T(8,128)(2,1)} %get-tuple-element.174.up_ref.refs_1_, bf16[512,2048]{1,0:T(8,128)(2,1)} %collective-permute-done.25.refs_2_, ...), custom_call_target="tpu_custom_call" | custom-call | flops 8589934592 | bytes 20971520 | tf_op jit(solution)/shard_map/stacked_product/pallas_call | solution.py:590
  894.8 27.3 %mixer_backward.6 = (bf16[512,4608]{1,0:T(8,128)(2,1)}, f32[128,2048]{1,0:T(8,128)}, f32[8,2048]{1,0:T(8,128)}, f32[8,256]{1,0:T(8,128)}, f32[8,2048]{1,0:T(8,12...) custom-call(bf16[2,512,2048]{2,1,0:T(8,128)(2,1)} %get-tuple-element.117.refs_0_.refs_11_, ...), custom_call_target="tpu_custom_call" | custom-call | flops 14680064000 | bytes 20971520 | tf_op jit(solution)/shard_map/mixer_backward/pallas_call | solution.py:419
  922.1 27.5 %mixer_backward.7 = (bf16[512,4608]{1,0:T(8,128)(2,1)}, f32[128,2048]{1,0:T(8,128)}, f32[8,2048]{1,0:T(8,128)}, f32[8,256]{1,0:T(8,128)}, f32[8,2048]{1,0:T(8,12...) custom-call(bf16[2,512,2048]{2,1,0:T(8,128)(2,1)} %get-tuple-element.111.refs_0_.refs_8_.refs_13_.refs_11_, ...), custom_call_target="tpu_custom_call" | custom-call | flops 14680064000 | bytes 20971520 | tf_op jit(solution)/shard_map/mixer_backward/pallas_call | solution.py:419
  957.5 15.9 %normed_gradient.6 = bf16[512,2048]{1,0:T(8,128)(2,1)} custom-call(bf16[512,4608]{1,0:T(8,128)(2,1)} %get-tuple-element.275.dcolumns_ref, bf16[4096,3328]{1,0:T(8,128)(2,1)} %bitcast.194, bf16[4096,3328]{1,0:T(8,128)(2,1)} %bitcast.195, bf16[4096,3328]{1,0:T(8,128)(2,1)} %bitcast.196, bf16[4096,3328]{1,0:T(8,128)(2,1)} %bitcast.197, ...), custom_call_target="tpu_custom_call" | custom-call | flops 9663676416 | bytes 23592960 | tf_op jit(solution)/shard_map/normed_gradient/pallas_call | solution.py:442
  981.8 15.9 %normed_gradient.7 = bf16[512,2048]{1,0:T(8,128)(2,1)} custom-call(bf16[512,4608]{1,0:T(8,128)(2,1)} %get-tuple-element.185.dcolumns_ref, bf16[4096,3328]{1,0:T(8,128)(2,1)} %bitcast.200, bf16[4096,3328]{1,0:T(8,128)(2,1)} %bitcast.201, bf16[4096,3328]{1,0:T(8,128)(2,1)} %bitcast.202, bf16[4096,3328]{1,0:T(8,128)(2,1)} %bitcast.203, ...), custom_call_target="tpu_custom_call" | custom-call | flops 9663676416 | bytes 23592960 | tf_op jit(solution)/shard_map/normed_gradient/pallas_call | solution.py:442
  1002.5 17.9 %collective-permute-done.29 = bf16[512,2048]{1,0:T(8,128)(2,1)} collective-permute-done((bf16[512,2048]{1,0:T(8,128)(2,1)}, bf16[512,2048]{1,0:T(8,128)(2,1)}, u32[]{:S(2)}, u32[]{:S(2)}) %collective-permute-start.29) | collective-permute-done | bytes 2097184 | tf_op jit(solution)/shard_map/ppermute | solution.py:1058
  1045.0 132.1 %reduced_product.3 = (f32[256,2304]{1,0:T(8,128)}, f32[8,1024]{1,0:T(8,128)}, f32[24,256]{1,0:T(8,128)}) custom-call(bf16[512,2048]{1,0:T(8,128)(2,1)} %get-tuple-element.338.normed_ref.refs_0_, bf16[512,2048]{1,0:T(8,128)(2,1)} %get-tuple-element.116.normed_ref.refs_1_, bf16[512,2048]{1,0:T(8,128)(2,1)} %collective-permute-done.31.refs_2_, ...), custom_call_target="tpu_custom_call" | custom-call | flops 115964116992 | bytes 104857600 | tf_op jit(solution)/shard_map/reduced_product/pallas_call | solution.py:1009
  (429 shorter events, 266.0 us)
Async XLA Ops:
  7.2 354.3 %all-gather.2.cloned.1.call-start = ((), (), s32[]{:S(2)}) async-start(), calls=%async_computation | async-start | bytes 28966912 | tf_op jit(solution)/shard_map/all_gather | solution.py:1068
  202.6 34.1 %collective-permute-start = (f32[2,6,1024]{2,1,0:T(8,128)S(1)}, f32[2,6,1024]{2,1,0:T(8,128)S(1)}, u32[]{:S(2)}, u32[]{:S(2)}) collective-permute-start(f32[2,6,1024]{2,1,0:T(8,128)S(1)} %pad_maximum_fusion.7), channel_id=1, source_target_pairs={{0,1},{1,0},{2,3},{3,2},{4,5},{5,4},{6,7},{7,6},{8,9},{9,8},{10,11... | collective-permute-start | bytes 147464 | tf_op jit(solution)/shard_map/ppermute | solution.py:1055
  203.2 32.7 %collective-permute-start.1 = (f32[2,1,3,16]{3,0,2,1:T(2,128)S(1)}, f32[2,1,3,16]{3,0,2,1:T(2,128)S(1)}, u32[]{:S(2)}, u32[]{:S(2)}) collective-permute-start(f32[2,1,3,16]{3,0,2,1:T(2,128)S(1)} %maximum_bitcast_fusion.2), channel_id=1, source_target_pairs={{0,1},{1,0},{2,3},{3,2},{4,5},{5,4},{6,7},{7,6},{8,9},{9,8},{10,11... | collective-permute-start | bytes 1160 | tf_op jit(solution)/shard_map/ppermute | solution.py:1055
  207.5 109.9 %collective-permute-start.12 = (bf16[256,2048]{1,0:T(8,128)(2,1)}, bf16[256,2048]{1,0:T(8,128)(2,1)}, u32[]{:S(2)}, u32[]{:S(2)}) collective-permute-start(bf16[256,2048]{1,0:T(8,128)(2,1)} %get-tuple-element.296), channel_id=1, source_target_pairs={{0,1},{1,0},{2,3},{3,2},{4,5},{5,4},{6,7},{7,6},{8,9},{9,8},{10,11... | collective-permute-start | bytes 3145736 | tf_op jit(solution)/shard_map/ppermute | solution.py:1055
  262.3 60.5 %collective-permute-start.3 = (bf16[512,2048]{1,0:T(8,128)(2,1)}, bf16[512,2048]{1,0:T(8,128)(2,1)}, u32[]{:S(2)}, u32[]{:S(2)}) collective-permute-start(bf16[512,2048]{1,0:T(8,128)(2,1)} %out_projection.4), channel_id=1, source_target_pairs={{0,2},{1,3},{2,0},{3,1},{4,6},{5,7},{6,4},{7,5},{8,10},{9,11},{10,... | collective-permute-start | bytes 6291464 | tf_op jit(solution)/shard_map/ppermute | solution.py:1058
  317.0 97.6 %collective-permute-start.5 = (bf16[512,2048]{1,0:T(8,128)(2,1)}, bf16[512,2048]{1,0:T(8,128)(2,1)}, u32[]{:S(2)}, u32[]{:S(2)}) collective-permute-start(bf16[512,2048]{1,0:T(8,128)(2,1)} %out_projection.5), channel_id=1, source_target_pairs={{0,2},{1,3},{2,0},{3,1},{4,6},{5,7},{6,4},{7,5},{8,10},{9,11},{10,... | collective-permute-start | bytes 6291464 | tf_op jit(solution)/shard_map/ppermute | solution.py:1058
  321.1 138.7 %collective-permute-start.13 = (bf16[512,2048]{1,0:T(8,128)(2,1)}, bf16[512,2048]{1,0:T(8,128)(2,1)}, u32[]{:S(2)}, u32[]{:S(2)}) collective-permute-start(bf16[512,2048]{1,0:T(8,128)(2,1)} %maximum_select_fusion.2), channel_id=1, source_target_pairs={{0,2},{1,3},{2,0},{3,1},{4,6},{5,7},{6,4},{7,5},{8,10},{9,11},{10,... | collective-permute-start | bytes 6291464 | tf_op jit(solution)/shard_map/ppermute | solution.py:1058
  465.3 30.0 %collective-permute-start.16 = (bf16[512,2048]{1,0:T(8,128)(2,1)}, bf16[512,2048]{1,0:T(8,128)(2,1)}, u32[]{:S(2)}, u32[]{:S(2)}) collective-permute-start(bf16[512,2048]{1,0:T(8,128)(2,1)} %get-tuple-element.146.up_ref.refs_0_), channel_id=1, source_target_pairs={{0,4},{4,0},{8,12},{12,8},{16,20},{20,16},{24,28},{28,24},{1,5},{5... | collective-permute-start | bytes 6291464 | tf_op jit(solution)/shard_map/ppermute | solution.py:1061
  465.3 30.0 %collective-permute-start.17 = (bf16[512,2048]{1,0:T(8,128)(2,1)}, bf16[512,2048]{1,0:T(8,128)(2,1)}, u32[]{:S(2)}, u32[]{:S(2)}) collective-permute-start(bf16[512,2048]{1,0:T(8,128)(2,1)} %get-tuple-element.147.up_ref.refs_1_), channel_id=1, source_target_pairs={{0,4},{4,0},{8,12},{12,8},{16,20},{20,16},{24,28},{28,24},{1,5},{5... | collective-permute-start | bytes 6291464 | tf_op jit(solution)/shard_map/ppermute | solution.py:1061
  512.9 46.6 %collective-permute-start.20 = (bf16[1024,1024]{1,0:T(8,128)(2,1)}, bf16[1024,1024]{1,0:T(8,128)(2,1)S(1)}, u32[]{:S(2)}, u32[]{:S(2)}) collective-permute-start(bf16[1024,1024]{1,0:T(8,128)(2,1)} %dynamic-slice_bitcast_fusion.1.refs_15_), channel_id=1, source_target_pairs={{0,1},{1,0},{2,3},{3,2},{4,5},{5,4},{6,7},{7,6},{8,9},{9,8},{10,11... | collective-permute-start | bytes 6291464 | tf_op jit(solution)/shard_map/ppermute | solution.py:1055
  541.4 81.6 %collective-permute-start.22 = (bf16[512,4608]{1,0:T(8,128)(2,1)}, bf16[512,4608]{1,0:T(8,128)(2,1)}, u32[]{:S(2)}, u32[]{:S(2)}) collective-permute-start(bf16[512,4608]{1,0:T(8,128)(2,1)} %get-tuple-element.156.dcolumns_ref.refs_5_), channel_id=1, source_target_pairs={{0,4},{4,0},{8,12},{12,8},{16,20},{20,16},{24,28},{28,24},{1,5},{5... | collective-permute-start | bytes 14155784 | tf_op jit(solution)/shard_map/ppermute | solution.py:1061
  590.6 34.4 %collective-permute-start.21 = (bf16[512,4608]{1,0:T(8,128)(2,1)}, bf16[512,4608]{1,0:T(8,128)(2,1)}, u32[]{:S(2)}, u32[]{:S(2)}) collective-permute-start(bf16[512,4608]{1,0:T(8,128)(2,1)} %get-tuple-element.157.dcolumns_ref.refs_4_), channel_id=1, source_target_pairs={{0,4},{4,0},{8,12},{12,8},{16,20},{20,16},{24,28},{28,24},{1,5},{5... | collective-permute-start | bytes 14155784 | tf_op jit(solution)/shard_map/ppermute | solution.py:1061
  591.4 284.2 %collective-permute-start.27 = (bf16[2,512,1024]{2,1,0:T(8,128)(2,1)}, bf16[2,512,1024]{2,1,0:T(8,128)(2,1)}, u32[]{:S(2)}, u32[]{:S(2)}) collective-permute-start(bf16[2,512,1024]{2,1,0:T(8,128)(2,1)} %get-tuple-element.113.mixed_ref.refs_4_), channel_id=1, source_target_pairs={{0,4},{4,0},{8,12},{12,8},{16,20},{20,16},{24,28},{28,24},{1,5},{5... | collective-permute-start | bytes 6291464 | tf_op jit(solution)/shard_map/ppermute | solution.py:1061
  591.8 31.0 %collective-permute-start.10 = (bf16[512,2048]{1,0:T(8,128)(2,1)}, bf16[512,2048]{1,0:T(8,128)(2,1)}, u32[]{:S(2)}, u32[]{:S(2)}) collective-permute-start(bf16[512,2048]{1,0:T(8,128)(2,1)} %multiply_convert_fusion.3.normed_ref.refs_0_), channel_id=1, source_target_pairs={{0,4},{4,0},{8,12},{12,8},{16,20},{20,16},{24,28},{28,24},{1,5},{5... | collective-permute-start | bytes 6291464 | tf_op jit(solution)/shard_map/ppermute | solution.py:1061
  591.9 31.2 %collective-permute-start.11 = (bf16[512,2048]{1,0:T(8,128)(2,1)}, bf16[512,2048]{1,0:T(8,128)(2,1)}, u32[]{:S(2)}, u32[]{:S(2)}) collective-permute-start(bf16[512,2048]{1,0:T(8,128)(2,1)} %multiply_convert_fusion.2.normed_ref.refs_1_), channel_id=1, source_target_pairs={{0,4},{4,0},{8,12},{12,8},{16,20},{20,16},{24,28},{28,24},{1,5},{5... | collective-permute-start | bytes 6291464 | tf_op jit(solution)/shard_map/ppermute | solution.py:1061
  622.9 252.7 %collective-permute-start.28 = (bf16[2,512,1024]{2,1,0:T(8,128)(2,1)}, bf16[2,512,1024]{2,1,0:T(8,128)(2,1)}, u32[]{:S(2)}, u32[]{:S(2)}) collective-permute-start(bf16[2,512,1024]{2,1,0:T(8,128)(2,1)} %get-tuple-element.120.mixed_ref.refs_5_), channel_id=1, source_target_pairs={{0,4},{4,0},{8,12},{12,8},{16,20},{20,16},{24,28},{28,24},{1,5},{5... | collective-permute-start | bytes 6291464 | tf_op jit(solution)/shard_map/ppermute | solution.py:1061
  623.0 189.6 %collective-permute-start.8 = (bf16[512,2048]{1,0:T(8,128)(2,1)}, bf16[512,2048]{1,0:T(8,128)(2,1)}, u32[]{:S(2)}, u32[]{:S(2)}) collective-permute-start(bf16[512,2048]{1,0:T(8,128)(2,1)} %broadcast_select_fusion.4), channel_id=1, source_target_pairs={{0,2},{1,3},{2,0},{3,1},{4,6},{5,7},{6,4},{7,5},{8,10},{9,11},{10,... | collective-permute-start | bytes 6291464 | tf_op jit(solution)/shard_map/ppermute | solution.py:1058
  623.1 167.0 %collective-permute-start.24 = (bf16[512,2048]{1,0:T(8,128)(2,1)S(1)}, bf16[512,2048]{1,0:T(8,128)(2,1)}, u32[]{:S(2)}, u32[]{:S(2)}) collective-permute-start(bf16[512,2048]{1,0:T(8,128)(2,1)S(1)} %copy-done.29), channel_id=1, source_target_pairs={{0,2},{1,3},{2,0},{3,1},{4,6},{5,7},{6,4},{7,5},{8,10},{9,11},{10,... | collective-permute-start | bytes 6291464 | tf_op jit(solution)/shard_map/ppermute | solution.py:1058
  625.1 179.4 %collective-permute-start.23 = (bf16[512,2048]{1,0:T(8,128)(2,1)}, bf16[512,2048]{1,0:T(8,128)(2,1)}, u32[]{:S(2)}, u32[]{:S(2)}) collective-permute-start(bf16[512,2048]{1,0:T(8,128)(2,1)} %normed_gradient.5.refs_15_), channel_id=1, source_target_pairs={{0,2},{1,3},{2,0},{3,1},{4,6},{5,7},{6,4},{7,5},{8,10},{9,11},{10,... | collective-permute-start | bytes 6291464 | tf_op jit(solution)/shard_map/ppermute | solution.py:1058
  790.1 39.8 %collective-permute-start.43 = (bf16[256,1024]{1,0:T(8,128)(2,1)}, bf16[256,1024]{1,0:T(8,128)(2,1)S(1)}, u32[]{:S(2)}, u32[]{:S(2)}) collective-permute-start(bf16[256,1024]{1,0:T(8,128)(2,1)} %get-tuple-element.292.refs_22_), channel_id=1, source_target_pairs={{0,8},{4,12},{8,16},{12,20},{16,24},{20,28},{24,0},{28,4},{1,9},{5... | collective-permute-start | bytes 1572872 | tf_op jit(solution)/shard_map/ppermute | solution.py:1065
  829.8 45.7 %collective-permute-start.26 = (bf16[512,2048]{1,0:T(8,128)(2,1)}, bf16[512,2048]{1,0:T(8,128)(2,1)}, u32[]{:S(2)}, u32[]{:S(2)}) collective-permute-start(bf16[512,2048]{1,0:T(8,128)(2,1)} %get-tuple-element.174.up_ref.refs_1_), channel_id=1, source_target_pairs={{0,4},{4,0},{8,12},{12,8},{16,20},{20,16},{24,28},{28,24},{1,5},{5... | collective-permute-start | bytes 6291464 | tf_op jit(solution)/shard_map/ppermute | solution.py:1061
  830.8 44.7 %collective-permute-start.25 = (bf16[512,2048]{1,0:T(8,128)(2,1)}, bf16[512,2048]{1,0:T(8,128)(2,1)}, u32[]{:S(2)}, u32[]{:S(2)}) collective-permute-start(bf16[512,2048]{1,0:T(8,128)(2,1)} %get-tuple-element.173.up_ref.refs_0_), channel_id=1, source_target_pairs={{0,4},{4,0},{8,12},{12,8},{16,20},{20,16},{24,28},{28,24},{1,5},{5... | collective-permute-start | bytes 6291464 | tf_op jit(solution)/shard_map/ppermute | solution.py:1061
  871.5 169.4 %collective-permute-start.31 = (bf16[512,2048]{1,0:T(8,128)(2,1)}, bf16[512,2048]{1,0:T(8,128)(2,1)}, u32[]{:S(2)}, u32[]{:S(2)}) collective-permute-start(bf16[512,2048]{1,0:T(8,128)(2,1)} %get-tuple-element.338.normed_ref.refs_0_), channel_id=1, source_target_pairs={{0,4},{4,0},{8,12},{12,8},{16,20},{20,16},{24,28},{28,24},{1,5},{5... | collective-permute-start | bytes 6291464 | tf_op jit(solution)/shard_map/ppermute | solution.py:1061
  893.3 104.5 %collective-permute-start.35 = (bf16[1024,1024]{1,0:T(8,128)(2,1)}, bf16[1024,1024]{1,0:T(8,128)(2,1)}, u32[]{:S(2)}, u32[]{:S(2)}) collective-permute-start(bf16[1024,1024]{1,0:T(8,128)(2,1)} %dynamic-slice_bitcast_fusion.refs_16_), channel_id=1, source_target_pairs={{0,1},{1,0},{2,3},{3,2},{4,5},{5,4},{6,7},{7,6},{8,9},{9,8},{10,11... | collective-permute-start | bytes 6291464 | tf_op jit(solution)/shard_map/ppermute | solution.py:1055
  973.4 47.0 %collective-permute-start.29 = (bf16[512,2048]{1,0:T(8,128)(2,1)}, bf16[512,2048]{1,0:T(8,128)(2,1)}, u32[]{:S(2)}, u32[]{:S(2)}) collective-permute-start(bf16[512,2048]{1,0:T(8,128)(2,1)} %normed_gradient.6), channel_id=1, source_target_pairs={{0,2},{1,3},{2,0},{3,1},{4,6},{5,7},{6,4},{7,5},{8,10},{9,11},{10,... | collective-permute-start | bytes 6291464 | tf_op jit(solution)/shard_map/ppermute | solution.py:1058
  979.8 64.5 %collective-permute-start.33 = (bf16[512,4608]{1,0:T(8,128)(2,1)}, bf16[512,4608]{1,0:T(8,128)(2,1)}, u32[]{:S(2)}, u32[]{:S(2)}) collective-permute-start(bf16[512,4608]{1,0:T(8,128)(2,1)} %get-tuple-element.183.refs_4_), channel_id=1, source_target_pairs={{0,4},{4,0},{8,12},{12,8},{16,20},{20,16},{24,28},{28,24},{1,5},{5... | collective-permute-start | bytes 14155784 | tf_op jit(solution)/shard_map/ppermute | solution.py:1061
  979.8 65.1 %collective-permute-start.34 = (bf16[512,4608]{1,0:T(8,128)(2,1)}, bf16[512,4608]{1,0:T(8,128)(2,1)}, u32[]{:S(2)}, u32[]{:S(2)}) collective-permute-start(bf16[512,4608]{1,0:T(8,128)(2,1)} %get-tuple-element.184.refs_5_), channel_id=1, source_target_pairs={{0,4},{4,0},{8,12},{12,8},{16,20},{20,16},{24,28},{28,24},{1,5},{5... | collective-permute-start | bytes 14155784 | tf_op jit(solution)/shard_map/ppermute | solution.py:1061
  997.7 46.6 %collective-permute-start.32 = (bf16[512,2048]{1,0:T(8,128)(2,1)}, bf16[512,2048]{1,0:T(8,128)(2,1)}, u32[]{:S(2)}, u32[]{:S(2)}) collective-permute-start(bf16[512,2048]{1,0:T(8,128)(2,1)} %get-tuple-element.116.normed_ref.refs_1_), channel_id=1, source_target_pairs={{0,4},{4,0},{8,12},{12,8},{16,20},{20,16},{24,28},{28,24},{1,5},{5... | collective-permute-start | bytes 6291464 | tf_op jit(solution)/shard_map/ppermute | solution.py:1061
  1029.7 149.9 %collective-permute-start.40 = (bf16[256,1024]{1,0:T(8,128)(2,1)}, bf16[256,1024]{1,0:T(8,128)(2,1)S(1)}, u32[]{:S(2)}, u32[]{:S(2)}) collective-permute-start(bf16[256,1024]{1,0:T(8,128)(2,1)} %get-tuple-element.288), channel_id=1, source_target_pairs={{0,8},{4,12},{8,16},{12,20},{16,24},{20,28},{24,0},{28,4},{1,9},{5... | collective-permute-start | bytes 1572872 | tf_op jit(solution)/shard_map/ppermute | solution.py:1065
  1040.9 138.7 %collective-permute-start.41 = (bf16[256,1024]{1,0:T(8,128)(2,1)}, bf16[256,1024]{1,0:T(8,128)(2,1)}, u32[]{:S(2)}, u32[]{:S(2)}) collective-permute-start(bf16[256,1024]{1,0:T(8,128)(2,1)} %get-tuple-element.287), channel_id=1, source_target_pairs={{0,16},{4,20},{8,24},{12,28},{16,0},{20,4},{24,8},{28,12},{1,17},{... | collective-permute-start | bytes 1572872 | tf_op jit(solution)/shard_map/ppermute | solution.py:1065
  1044.4 135.2 %collective-permute-start.42 = (bf16[256,1024]{1,0:T(8,128)(2,1)S(1)}, bf16[256,1024]{1,0:T(8,128)(2,1)}, u32[]{:S(2)}, u32[]{:S(2)}) collective-permute-start(bf16[256,1024]{1,0:T(8,128)(2,1)S(1)} %get-tuple-element.286), channel_id=1, source_target_pairs={{0,24},{4,28},{8,0},{12,4},{16,8},{20,12},{24,16},{28,20},{1,25},{... | collective-permute-start | bytes 1572872 | tf_op jit(solution)/shard_map/ppermute | solution.py:1065
  1044.4 142.8 %collective-permute-start.30 = (bf16[256,2048]{1,0:T(8,128)(2,1)S(1)}, bf16[256,2048]{1,0:T(8,128)(2,1)}, u32[]{:S(2)}, u32[]{:S(2)}) collective-permute-start(bf16[256,2048]{1,0:T(8,128)(2,1)S(1)} %get-tuple-element.293), channel_id=1, source_target_pairs={{0,1},{1,0},{2,3},{3,2},{4,5},{5,4},{6,7},{7,6},{8,9},{9,8},{10,11... | collective-permute-start | bytes 3145736 | tf_op jit(solution)/shard_map/ppermute | solution.py:1055
  (102 other events, 2858.8 us)
Sparse Core Ops, SparseCore 0:
  202.6 158.8 all-gather.1

commit v5 on v4

--- a/solution.py
+++ b/solution.py
@@ -379,7 +379,7 @@
         ],
         compiler_params=pltpu.CompilerParams(vmem_limit_bytes=48 * 1024 * 1024),
         cost_estimate=pl.CostEstimate(
-            flops=tokens * channels * 12000, bytes_accessed=tokens * channels * 28, transcendentals=tokens * channels * 12
+            flops=tokens * channels * 3000, bytes_accessed=tokens * channels * 8, transcendentals=tokens * channels * 3
         ),
         name="mixer_forward",
     )(*operands)
@@ -431,14 +431,14 @@
         ],
         compiler_params=pltpu.CompilerParams(vmem_limit_bytes=56 * 1024 * 1024),
         cost_estimate=pl.CostEstimate(
-            flops=tokens * channels * 28000, bytes_accessed=tokens * channels * 40, transcendentals=tokens * channels * 12
+            flops=tokens * channels * 6000, bytes_accessed=tokens * channels * 10, transcendentals=tokens * channels * 3
         ),
         name="mixer_backward",
     )(*operands)
 
 
 def product_call(kernel, grid, specs, outs, out_specs, operands, flops, name):
-    moved = sum(array.size * array.dtype.itemsize for array in operands[:1]) + flops // 512
+    moved = flops // 2048
     return pl.pallas_call(
         kernel,
         grid=grid,
@@ -446,7 +446,7 @@
         out_specs=out_specs,
         out_shape=outs,
         compiler_params=pltpu.CompilerParams(vmem_limit_bytes=60 * 1024 * 1024),
-        cost_estimate=pl.CostEstimate(flops=flops, bytes_accessed=moved, transcendentals=0),
+        cost_estimate=pl.CostEstimate(flops=flops // 3, bytes_accessed=moved, transcendentals=0),
         name=name,
     )(*operands)
 
@@ -599,8 +599,8 @@
         out_shape=jax.ShapeDtypeStruct((2, steps * row_tile, columns), BF16),
         compiler_params=pltpu.CompilerParams(vmem_limit_bytes=60 * 1024 * 1024),
         cost_estimate=pl.CostEstimate(
-            flops=4 * steps * row_tile * columns * tokens * chunks,
-            bytes_accessed=4 * steps * row_tile * columns + 2 * chunks * tokens * (2 * columns + features),
+            flops=steps * row_tile * columns * tokens * chunks,
+            bytes_accessed=steps * row_tile * columns,
             transcendentals=0,
         ),
         name="stacked_product",
@@ -984,12 +984,13 @@
         multiply(step)
         if step >= 2:
             pass_on(step - 2)
-        if step < 4:
+        if step < 3:
             small_finish(step)
-    for stage in range(chips, 4):
+    for stage in range(chips, 3):
         small_finish(stage)
     for step in range(max(0, chips - 2), chips):
         pass_on(step)
+    small_finish(3)
     for step in range(chips - 1):
         chain_copy(step).wait_send()
 
@@ -1039,6 +1040,8 @@
 
 class Place:
     def __init__(self):
+        self.last = ()
+        self.due = []
         self.members = lax.axis_size("tensor")
         self.groups = self.members // 2
         self.sequence = lax.axis_index("tensor") % 2
@@ -1051,6 +1054,17 @@
             [d * self.members + 2 * g + s for s in range(2) for d in range(copies)] for g in range(self.groups)
         ]
 
+    def now(self, v):
+        return lax.optimization_barrier((v, self.last, tuple(self.due)))[0]
+
+    def did(self, v):
+        self.last, self.due = (v,), []
+        return v
+
+    def soon(self, v):
+        self.due.append(v)
+        return v
+
     def to_pair(self, v):
         return lax.ppermute(v, "tensor", [(t, t ^ 1) for t in range(self.members)])
 
@@ -1090,22 +1104,20 @@
     def gather_chunks(self, v, chunks):
         if chunks == self.groups == 2:
             other = self.to_group(v, 1)
-            return [jnp.where(self.group == at, v, other) for at in range(2)]
+            return lambda: [jnp.where(self.group == at, v, self.now(other)) for at in range(2)]
         count = v.shape[0]
         total = jnp.zeros((count * self.groups,) + v.shape[1:], v.dtype)
         total = lax.dynamic_update_slice_in_dim(total, v, self.group * count, 0)
         for hop in range(1, self.groups):
             start = (self.group - hop) % self.groups * count
             total = lax.dynamic_update_slice_in_dim(total, self.to_group(v, hop), start, 0)
-        return jnp.split(total, chunks)
-
-    def scatter_rows(self, chunks):
-        arrived = [self.to_group(self.rows_of(chunks, hop), hop) for hop in range(1, self.groups)]
-        return self.rows_of(chunks, 0).astype(F32) + sum(piece.astype(F32) for piece in arrived)
+        return lambda: jnp.split(self.now(total), chunks)
 
     def take_sequence(self, v):
         mine = jnp.where(self.sequence == 0, v[0], v[1])
-        other = self.to_pair(jnp.where(self.sequence == 0, v[1], v[0]))
+        return mine, self.to_pair(jnp.where(self.sequence == 0, v[1], v[0]))
+
+    def in_order(self, mine, other):
         return jnp.where(self.sequence == 0, jnp.concatenate([mine, other]), jnp.concatenate([other, mine]))
 
     def give_sequence(self, v):
@@ -1114,8 +1126,8 @@
         other = self.to_pair(jnp.where(self.sequence == 0, second, first))
         return mine, other
 
-    def both_sequences(self, given, *earlier):
-        mine, other = then(given, *earlier)
+    def both_sequences(self, given):
+        mine, other = self.now(given)
         mine, other = mine.astype(F32), other.astype(F32)
         return jnp.where(self.sequence == 0, jnp.stack([mine, other]), jnp.stack([other, mine]))
 
@@ -1130,124 +1142,204 @@
 
 class WeightSum:
 
-    def __init__(self, place, features, columns):
+    def __init__(self, place, features, columns, far_features=None, far_columns=None):
         self.place = place
-        self.lhs = list(features) + [place.to_core(part) for part in features]
-        self.rhs = list(columns) + [place.to_core(part) for part in columns]
-
-    def to_pair(self, *earlier):
+        self.lhs = list(features) + (far_features or [place.to_core(part) for part in features])
+        self.rhs = list(columns) + (far_columns or [place.to_core(part) for part in columns])
+
+    def to_pair(self):
         place = self.place
-        self.lhs = list(then(tuple(self.lhs), *earlier))
         rows = self.lhs[0].shape[1] // (2 * place.chips)
-        self.stack = stacked_product(self.lhs, self.rhs, (rows, place.core.astype(jnp.int32)[None]))
-        other = lax.dynamic_index_in_dim(self.stack, 1 - self.place.sequence, 0, keepdims=False)
-        self.landed = self.place.to_pair(other)
-        return other
+        lhs = list(place.now(tuple(self.lhs)))
+        self.stack = place.did(stacked_product(lhs, self.rhs, (rows, place.core.astype(jnp.int32)[None])))
+        other = place.soon(lax.dynamic_index_in_dim(self.stack, 1 - place.sequence, 0, keepdims=False))
+        self.landed = place.to_pair(other)
 
     def to_chips(self):
         place = self.place
         own = lax.dynamic_index_in_dim(self.stack, place.sequence, 0, keepdims=False)
-        total = (own.astype(F32) + self.landed.astype(F32)).astype(BF16)
+        total = (own.astype(F32) + place.now(self.landed).astype(F32)).astype(BF16)
         pieces = total.reshape(place.chips, -1, total.shape[1])
         self.kept = lax.dynamic_index_in_dim(pieces, place.chip, 0, keepdims=False)
         hops = range(1, place.chips)
         self.sent = [
             lax.dynamic_index_in_dim(pieces, (place.chip + hop) % place.chips, 0, keepdims=False) for hop in hops
         ]
-        self.arrived = [place.to_chip(piece, hop) for piece, hop in zip(self.sent, hops)]
-        return self.sent
-
-    def total(self, *earlier):
-        kept, arrived = then((self.kept, tuple(self.arrived)), *earlier)
-        return added(kept, arrived)
-
-
-def norm_scale(stream):
-    return lax.rsqrt(jnp.mean(stream * stream, axis=-1, keepdims=True) + EPSILON)
-
-
-def block_forward(place, incoming, weights, tables, heads, inner, final):
-    gathered, gain, own, thin = weights
-    kept = {"update": []}
-    for key in ("stream", "normed", "columns", "small", "mixed", "y", "saved", "scale", "share"):
-        kept[key] = []
-    earlier = None
-    for at in range(PIECES):
-        stream = incoming(at, *kept["share"][-1:])
-        part = (stream * norm_scale(stream) * gain).astype(BF16)
-        if at:
-            part = then(part, kept["share"][at - 1])
-        columns, small = in_projection(part, gathered, own, thin)
-        mixed, square, y, saved, state = mixer_forward(columns, small, tables, heads, earlier)
-        earlier = (state, columns, small)
-        scale = lax.rsqrt(place.add_groups(square) / inner + EPSILON)
-        share = then(out_projection(mixed, gathered, own), scale)
-        results = (stream, part, columns, small, mixed, y, saved, scale, share)
-        names = ("stream", "normed", "columns", "small", "mixed", "y", "saved", "scale", "share")
-        for key, value in zip(names, results):
-            kept[key].append(value)
-    shares, scales = kept["share"], kept["scale"]
-    if final:
-        after = place.rows_of(kept["stream"], 0) + place.scatter_rows(shares) * place.rows_of(scales, 0)
-    else:
-        arrived = [place.sent_to_groups(share) for share in shares]
-
-        def after(at, *earlier):
-            update = added(shares[at], then(tuple(arrived[at]), *earlier) if earlier else arrived[at])
-            kept["update"].append(update)
-            return kept["stream"][at] + update * scales[at]
-
-    return after, kept
-
-
-def norm_backward(stream, grad, grad_normed, gain):
-    row_scale = norm_scale(stream)
-    unit = stream * row_scale
-    lifted = grad_normed * gain
-    back = grad + row_scale * (lifted - unit * jnp.mean(lifted * unit, axis=-1, keepdims=True))
-    return back, jnp.sum(grad_normed * unit, axis=0)
+        self.arrived = [place.to_chip(place.soon(piece), hop) for piece, hop in zip(self.sent, hops)]
+
+    def total(self):
+        return added(self.kept, self.place.now(tuple(self.arrived)))
+
+
+def norm_rows(row_args, fixed_args, outs, kernel, name, choice=None):
+    tokens = row_args[0].shape[0]
+    block = min(128, tokens)
+
+    def by_rows(cols):
+        return pl.BlockSpec((block, cols), lambda i, *_: (i, 0))
+
+    def fixed(shape):
+        return pl.BlockSpec(shape, lambda i, *_: (0, 0))
+
+    scalars = [] if choice is None else [choice]
+    return pl.pallas_call(
+        kernel,
+        grid_spec=pltpu.PrefetchScalarGridSpec(
+            num_scalar_prefetch=len(scalars),
+            grid=(tokens // block,),
+            in_specs=[by_rows(array.shape[1]) for array in row_args] + [fixed(array.shape) for array in fixed_args],
+            out_specs=[by_rows(shape[1]) if shape[0] == tokens else fixed(shape) for shape, _ in outs],
+        ),
+        out_shape=[jax.ShapeDtypeStruct(shape, dtype) for shape, dtype in outs],
+        compiler_params=pltpu.CompilerParams(vmem_limit_bytes=48 * 1024 * 1024),
+        cost_estimate=pl.CostEstimate(
+            flops=20 * row_args[0].size, bytes_accessed=sum(array.size * array.dtype.itemsize for array in row_args), transcendentals=0
+        ),
+        name=name,
+    )(*scalars, *row_args, *fixed_args)
+
+
+def normed_rows(stream, gain):
+    row_scale = lax.rsqrt(jnp.mean(stream * stream, axis=1, keepdims=True) + EPSILON)
+    return stream * row_scale, row_scale
+
+
+def norm_forward(stream, gain, share=None, arrived=(), scale=None):
+    shape = stream.shape
+
+    def plain(stream_ref, gain_ref, normed_ref):
+        normed_ref[...] = (normed_rows(stream_ref[...].astype(F32), None)[0] * gain_ref[...]).astype(BF16)
+
+    def updated(*refs):
+        stream_ref, scale_ref, share_ref = refs[:3]
+        gain_ref, out_ref, normed_ref = refs[-3:]
+        update = share_ref[...].astype(F32)
+        for ref in refs[3:-3]:
+            update = update + ref[...].astype(F32)
+        rows = stream_ref[...].astype(F32) + update * scale_ref[...]
+        out_ref[...] = rows
+        normed_ref[...] = (normed_rows(rows, None)[0] * gain_ref[...]).astype(BF16)
+
+    if share is None:
+        return stream, norm_rows([stream], [gain], [(shape, BF16)], plain, "norm_forward")[0]
+    outs = [(shape, F32), (shape, BF16)]
+    return norm_rows([stream, scale, share, *arrived], [gain], outs, updated, "norm_forward")
+
+
+def norm_backward(streams, grads, share, arrived, gain, choice=None, entry=None, inner=None):
+    features = gain.shape[1]
+    tokens = share.shape[0]
+    pick = 0 if choice is None else 1
+    scale, parts = entry if entry else (None, ())
+
+    def kernel(*refs):
+        choice_ref, refs = (refs[0], refs[1:]) if pick else (None, refs)
+
+        def chosen(pair):
+            return pair[0][...].astype(F32) if not pick else jnp.where(choice_ref[0] == 0, pair[0][...].astype(F32), pair[1][...].astype(F32))
+
+        count = 1 + pick
+        stream, grad = chosen(refs[:count]), chosen(refs[count : 2 * count])
+        refs = refs[2 * count :]
+        grad_normed = refs[0][...].astype(F32)
+        for ref in refs[1 : 1 + len(arrived)]:
+            grad_normed = grad_normed + ref[...].astype(F32)
+        refs = refs[1 + len(arrived) :]
+        if entry:
+            scale_ref, part_refs, refs = refs[0], refs[1 : 1 + len(parts)], refs[1 + len(parts) :]
+        gain_ref, grad_ref, sum_ref = refs[:3]
+        unit, row_scale = normed_rows(stream, None)
+        lifted = grad_normed * gain_ref[...]
+        grad = grad + row_scale * (lifted - unit * jnp.mean(lifted * unit, axis=1, keepdims=True))
+        grad_ref[...] = grad
+
+        @pl.when(pl.program_id(0) == 0)
+        def _():
+            sum_ref[...] = jnp.zeros_like(sum_ref)
+
+        sum_ref[0:1] += jnp.sum(grad_normed * unit, axis=0, keepdims=True)
+        if entry:
+            up_ref, pull_ref = refs[3:5]
+            row = scale_ref[...]
+            up = (grad * row).astype(BF16)
+            up_ref[...] = up
+            update = sum(ref[...].astype(F32) for ref in part_refs)
+            pull_ref[...] = jnp.sum(up.astype(F32) * update, axis=1, keepdims=True) * (row * row / inner)
+
+    outs = [((tokens, features), F32), ((8, features), F32)]
+    rows = [*streams, *grads, share, *arrived]
+    if entry:
+        outs += [((tokens, features), BF16), ((tokens, 1), F32)]
+        rows += [scale, *parts]
+    return norm_rows(rows, [gain], outs, kernel, "norm_backward", choice)
+
+
+class Forward:
+    def __init__(self, place, weights, tables, heads, inner):
+        self.place, self.weights, self.tables, self.heads, self.inner = place, weights, tables, heads, inner
+        self.kept = {}
+        self.earlier = None
+
+    def keep(self, **values):
+        for key, value in values.items():
+            self.kept.setdefault(key, []).append(value)
+
+    def chunk(self, stream, normed):
+        place, (gathered, _, own, thin) = self.place, self.weights
+        columns, small = in_projection(place.now(normed), gathered, own, thin)
+        mixed, square, y, saved, state = mixer_forward(columns, small, self.tables, self.heads, self.earlier)
+        self.earlier = (state, columns, small)
+        squares = [square] + place.sent_to_groups(square)
+        share = place.did(out_projection(place.now(mixed), gathered, own))
+        self.keep(stream=stream, normed=normed, columns=columns, small=small, mixed=mixed, y=y, saved=saved)
+        self.keep(squares=squares, share=share, sent=place.sent_to_groups(share))
+
+    def scale(self, at):
+        if "scale" not in self.kept:
+            self.kept["scale"] = [None] * PIECES
+        if self.kept["scale"][at] is None:
+            square = sum(self.place.now(tuple(self.kept["squares"][at])))
+            self.kept["scale"][at] = lax.rsqrt(square / self.inner + EPSILON)
+        return self.kept["scale"][at]
 
 
 class Backward:
-    def __init__(self, place, weights, tables, heads, inner, kept, final):
-        self.final = final
+    def __init__(self, place, weights, tables, heads, inner, kept):
         self.place, self.weights, self.tables, self.heads, self.inner, self.kept = place, weights, tables, heads, inner, kept
-        chunks = len(kept["normed"])
-        self.ups, self.grad_mixed, self.pulls = [None] * chunks, [None] * chunks, [None] * chunks
-        self.dcolumns, self.shares = [None] * chunks, [None] * chunks
+        self.ups, self.grad_mixed, self.pulls = [None] * PIECES, [None] * PIECES, [None] * PIECES
+        self.dcolumns, self.shares = [None] * PIECES, [None] * PIECES
         self.carried = None
 
-    def enter(self, at, grad):
+    def enter(self, at, up, pull=None):
         gathered, _, own, _ = self.weights
-        scale = self.kept["scale"][at]
-        self.ups[at] = (grad * scale).astype(BF16)
-        self.grad_mixed[at], pull = mixed_gradient(self.ups[at], gathered, own, self.kept["mixed"][at])
-        if not self.final:
-            pull = jnp.sum(self.ups[at].astype(F32) * self.kept["update"][at], axis=-1, keepdims=True)
-        else:
-            pull = self.place.add_groups(pull)
-        self.pulls[at] = pull * (scale * scale / self.inner)
-
-    def mix(self, at, after=()):
-        kept = self.kept
+        self.ups[at] = up
+        self.grad_mixed[at], sums = mixed_gradient(self.place.now(up), gathered, own, self.kept["mixed"][at])
+        self.place.did(self.grad_mixed[at])
+        self.pulls[at] = [sums] + self.place.sent_to_groups(sums) if pull is None else pull
+
+    def mix(self, at):
+        kept, place = self.kept, self.place
+        pull = self.pulls[at]
+        if isinstance(pull, list):
+            scale = kept["scale"][at]
+            pull = sum(place.now(tuple(pull))) * (scale * scale / self.inner)
         result = mixer_backward(
             kept["columns"][at],
             kept["small"][at],
             kept["y"][at],
             kept["saved"][at],
             self.grad_mixed[at],
-            self.pulls[at],
+            place.now(pull),
             self.tables,
             self.heads,
             (kept["columns"][at - 1], kept["small"][at - 1]) if at else None,
             self.carried,
-            after,
         )
-        self.dcolumns[at], self.carried = result[0], result[1:]
+        self.dcolumns[at], self.carried = place.did(result[0]), result[1:]
 
     def share(self, columns):
         gathered, _, own, thin = self.weights
-        return normed_gradient(columns, gathered, own, thin)
+        return self.place.did(normed_gradient(self.place.now(columns), gathered, own, thin))
 
 
 def local(
@@ -1291,13 +1383,8 @@
             gathered = place.gather_owners(block)
         else:
             gathered, sequence_rows = gathered_first(place, block, hidden)
-        gain = gathered[: gathered.shape[0] // 2, -1].astype(F32)
+        gain = gathered[: gathered.shape[0] // 2, -1].astype(F32)[None]
         weights.append((gathered, gain, own_cols, half + 128))
-
-    chunks = [stream.astype(F32) for stream in jnp.split(sequence_rows, PIECES)]
-
-    def streams(at, *earlier):
-        return chunks[at]
 
     per_channel = place.both(jnp.concatenate([channel_taps, inner_gain[:, None]], axis=1), 2)
     per_head = jnp.stack([step_bias, decay_log, skip_gain], axis=1)
@@ -1315,20 +1402,41 @@
             head += [pair, jnp.zeros((6, 128), F32)]
         tables.append((chan, taps, jnp.concatenate(head), expand, tri))
 
+    rows_in = jnp.split(sequence_rows, PIECES)
     kept = []
     for layer in range(layers):
         final = layer == layers - 1
-        if layer == 0:
-            last_up = place.take_sequence(then(cotangent, chunks))
-            last_up = place.gather_chunks(last_up, PIECES)
-        streams, saved = block_forward(place, streams, weights[layer], tables[layer], heads, inner, final)
-        kept.append(saved)
-    mixed_out = place.give_sequence(streams)
-
-    grads = [part.astype(F32) for part in last_up]
+        gathered, gain = weights[layer][:2]
+        if layer:
+            weights[layer] = (place.now(gathered),) + weights[layer][1:]
+            before = kept[-1]
+            for at in range(PIECES):
+                place.soon(previous.scale(at))
+        forward = Forward(place, weights[layer], tables[layer], heads, inner)
+        for at in range(PIECES):
+            if layer:
+                landed = list(place.now(tuple(before["sent"][at])))
+                before.setdefault("update", []).append([before["share"][at], *landed])
+                stream, normed = norm_forward(
+                    before["stream"][at], gain, before["share"][at], landed, previous.scale(at)
+                )
+            else:
+                stream, normed = norm_forward(place.now(rows_in[at]), gain)
+            if final and at == 0:
+                taken = place.take_sequence(then(cotangent, normed))
+            forward.chunk(stream, normed)
+            if final and at == 0:
+                last_up = place.gather_chunks(place.in_order(*place.now(taken)), PIECES)
+        kept.append(forward.kept)
+        previous = forward
+    for at in range(PIECES):
+        previous.scale(at)
+    shares = kept[-1]["share"]
+    mixed_sent = [place.to_group(place.soon(place.rows_of(shares, hop)), hop) for hop in range(1, place.groups)]
+    grads = last_up()
     in_sums, out_sums, gain_grads, carried = [None] * layers, [None] * layers, [0.0] * layers, [None] * layers
     half_totals, common_totals = [None] * layers, [None] * layers
-    pending, held = None, ()
+    pending = None
 
     def small_sums(layer):
         gchan, gtaps, ghead = carried[layer]
@@ -1341,73 +1449,97 @@
 
     for layer in reversed(range(layers)):
         final = layer == layers - 1
-        back = Backward(place, weights[layer], tables[layer], heads, inner, kept[layer], final)
+        back = Backward(place, weights[layer], tables[layer], heads, inner, kept[layer])
         for at in reversed(range(PIECES)):
-            if not final:
-                share, arrived = pending[at]
-                before = (in_sums[layer + 1].owned,) if at == PIECES - 1 else (back.ups[at + 1],)
-                grad_normed = added(share, then(tuple(arrived), *before))
-                grads[at], gain_grad = norm_backward(
-                    kept[layer + 1]["stream"][at], grads[at], grad_normed, weights[layer + 1][1]
-                )
-                gain_grads[layer + 1] = gain_grads[layer + 1] + jnp.where(place.group == 0, gain_grad, 0.0)
-            back.enter(at, grads[at])
+            scale = kept[layer]["scale"][at]
+            if final:
+                back.enter(at, (grads[at].astype(F32) * scale).astype(BF16))
+                continue
+            share, arrived = pending[at]
+            grads[at], gain_grad, up, pull = norm_backward(
+                [kept[layer + 1]["stream"][at]],
+                [grads[at]],
+                share,
+                list(place.now(tuple(arrived))),
+                weights[layer + 1][1],
+                None,
+                (scale, kept[layer]["update"][at]),
+                inner,
+            )
+            gain_grads[layer + 1] = gain_grads[layer + 1] + jnp.where(place.group == 0, gain_grad[0], 0.0)
+            back.enter(at, up, pull)
         normed, mixed = kept[layer]["normed"], kept[layer]["mixed"]
         out_sum = out_sums[layer] = WeightSum(place, back.ups, mixed)
-        held += (out_sum.to_pair(),)
+        far_normed = [place.to_core(part) for part in normed]
+        out_sum.to_pair()
+        far_columns, pending = [None] * PIECES, [None] * PIECES
         for at in reversed(range(PIECES)):
-            back.mix(at, held)
-            held = ()
+            back.mix(at)
+            far_columns[at] = place.to_core(back.dcolumns[at])
+            if at == PIECES - 1:
+                for later in out_sums[layer + 1 :]:
+                    later.owned = later.total()
             if layer:
-                back.shares[at] = back.share(back.dcolumns[at])
-                held = (back.shares[at],)
+                share = back.share(back.dcolumns[at])
+                pending[at] = (share, place.sent_to_groups(share))
                 if at == PIECES - 1:
-                    held += tuple(out_sum.to_chips())
+                    out_sum.to_chips()
         carried[layer] = back.carried[3:]
-        in_sum = in_sums[layer] = WeightSum(place, normed, back.dcolumns)
+        in_sum = in_sums[layer] = WeightSum(place, normed, back.dcolumns, far_normed, far_columns)
         if layer:
-            pending = [(share, place.sent_to_groups(share)) for share in back.shares]
             halves, common = small_sums(layer)
-            halves = then(halves, *back.shares)
             in_sum.owned, half_totals[layer], common_totals[layer] = reduced_product(
-                place, in_sum.lhs, in_sum.rhs, halves, common, layer
+                place, in_sum.lhs, in_sum.rhs, place.now(halves), common, layer
             )
+            place.did(in_sum.owned)
+            if final:
+                own_rows = place.rows_of(kept[-1]["stream"], 0).astype(F32)
+                update = added(place.rows_of(shares, 0), place.now(tuple(mixed_sent)))
+                mixed_out = place.give_sequence(own_rows + update * place.rows_of(kept[-1]["scale"], 0))
             continue
+        mixed_out = place.both_sequences(mixed_out)
         if PIECES == place.groups:
             sent = [back.share(place.rows_of(back.dcolumns, hop)) for hop in range(1, place.groups)]
-            own = back.share(then(place.rows_of(back.dcolumns, 0), *sent))
+            arrived = [place.to_group(piece, hop) for hop, piece in enumerate(sent, 1)]
+            own = back.share(place.rows_of(back.dcolumns, 0))
         else:
-            shares = [back.share(columns) for columns in back.dcolumns]
-            sent = [place.rows_of(shares, hop) for hop in range(1, place.groups)]
-            own = place.rows_of(shares, 0)
-        arrived = [place.to_group(piece, hop) for hop, piece in enumerate(sent, 1)]
-        out_sent = out_sum.to_chips()
-        grad, gain_grads[layer] = norm_backward(
-            place.rows_of(kept[layer]["stream"], 0), place.rows_of(grads, 0), added(own, arrived), weights[layer][1]
-        )
+            done = [back.share(columns) for columns in back.dcolumns]
+            arrived = [place.to_group(place.rows_of(done, hop), hop) for hop in range(1, place.groups)]
+            own = place.rows_of(done, 0)
+        out_sum.to_chips()
+        stream_parts, grad_parts, choice = kept[layer]["stream"], grads, place.group.astype(jnp.int32)[None]
+        if PIECES != place.groups:
+            stream_parts, grad_parts, choice = [place.rows_of(stream_parts, 0)], [place.rows_of(grads, 0)], None
+        arrived = list(place.now(tuple(arrived)))
+        grad, gain_grad = norm_backward(stream_parts, grad_parts, own, arrived, weights[layer][1], choice)
+        place.did(grad)
+        gain_grads[layer] = gain_grad[0]
     grad_hidden = place.give_sequence(grad)
 
     halves, common = small_sums(0)
     gains = jnp.stack(gain_grads).reshape(-1, shared)
     common = jnp.concatenate([common, gains, jnp.zeros((-gains.shape[0] % 8, shared), F32)])
-    common = then(common, *out_sent)
+    common = then(place.now(common), *out_sums[0].sent)
     in_sums[0].owned, half_totals[0], common_totals[0] = reduced_product(
         place, in_sum.lhs, in_sum.rhs, halves, common, 0
     )
+    place.did(in_sums[0].owned)
+    out_sums[0].owned = out_sums[0].total()
     gain_total = common_totals[0][8 : 8 + gains.shape[0]].reshape(layers, -1)
 
+    state_parts = jnp.concatenate([in_sum.owned[:, main : main + half] for in_sum in in_sums])
+    state_parts = place.both(place.add_groups(place.now(state_parts)), 1).reshape(layers, rows, shared)
     outs = []
     for layer in range(layers):
         per_channel_part = half_totals[layer]
         gain_part = lax.dynamic_slice_in_dim(gain_total[layer], lax.axis_index("dp") * rows, rows, 0)
         taps_part = common_totals[layer][:5]
-        in_owned, out_owned = in_sums[layer].owned, out_sums[layer].total(in_sums[layer].owned)
-        state_part = place.both(place.add_groups(in_owned[:, main : main + half]), 1)
+        in_owned, out_owned = in_sums[layer].owned, out_sums[layer].owned
         outs.append(
             (
                 gain_part,
                 jnp.stack([in_owned[:, :own_cols], in_owned[:, own_cols:main]]),
-                state_part,
+                state_parts[layer],
                 in_owned[:, main + half : main + half + heads],
                 per_channel_part[:5],
                 taps_part,
@@ -1418,8 +1550,7 @@
                 out_owned.T,
             )
         )
-    mixed_out = place.both_sequences(mixed_out, in_sums[-1].owned)
-    grad_hidden = place.both_sequences(grad_hidden, in_sums[0].owned)
+    grad_hidden = place.both_sequences(grad_hidden)
     return (mixed_out, grad_hidden) + tuple(jnp.stack(parts) for parts in zip(*outs))
 
 

time: 1220 us -> 1170 us (0.959)
  other arithmetic: 132 us -> 69.3 us
  waiting for transfers between devices: 90.9 us -> 66.4 us
  local copies, waits for them, and re-layouts: 59.1 us -> 77.2 us
  Pallas kernels: 867 us -> 880 us
    reduce_sum x8 -> x0, other arithmetic: 44.1 us -> none  [the longest x2 15.8 us: enter(): jnp.sum(self.ups[at].astype(F32) * self.kept['update'][at], axis=-1, keep...]
    pallas_call x0 -> x7, Pallas kernels: none -> 41.6 us  [norm_rows(): pl.pallas_call(kernel, grid_spec=pltpu.PrefetchScalarGridSpec(num_scalar_...]
    pallas_call x2, Pallas kernels: 296 us -> 268 us  [reduced_product(): pl.pallas_call(functools.partial(reduce_kernel, chips, groups, orders, pa...]
    dynamic_slice x0 -> x8, local copies, waits for them, and re-layouts: none -> 12.7 us  [the longest x6 10.3 us: to_chips(): lax.dynamic_index_in_dim(pieces, (place.chip + hop) % place.chips, 0, kee...]
    convert_element_type x9 -> x5, other arithmetic: 25.3 us -> 14.5 us  [the longest x2 5.75 us: to_chips(): total = (own.astype(F32) + place.now(self.landed).astype(F32)).astype(BF16)]
    ppermute x15 -> x14, waiting for transfers between devices: 45.7 us -> 35 us  [to_group(): lax.ppermute(v, 'tensor', [(t, (t + 2 * hop) % self.members) for t in ran...]
    unnamed x188 -> x174, local copies, waits for them, and re-layouts: 17.9 us -> 27.3 us
  transfers between devices with their start and end apart: 47 -> 45, of which waited for: 11 -> 10; matrix products, arithmetic and copies ran while one was open for 13% -> 9% of each run, Pallas kernels for 56% -> 59%
where the time goes in v5:
time: 1170 us; the launch traced here: 1160 us
  Pallas kernels  880 us (75%)
  local copies, waits for them, and re-layouts  77.2 us (7%)
  other arithmetic  69.3 us (6%)
  waiting for transfers between devices  66.4 us (6%)
  starting transfers between devices  49.5 us (4%)
  between operations  15.8 us (1%)
    pallas_call x2, Pallas kernels, reduced_product(): pl.pallas_call(functools.partial(reduce_kernel, chips, groups, orders, pa...  268 us
    pallas_call x16, Pallas kernels, product_call(): pl.pallas_call(kernel, grid=grid, in_specs=specs, out_specs=out_specs, ou...  200 us
    pallas_call x1, Pallas kernels, gathered_first(): pl.pallas_call(functools.partial(gather_kernel, chips, groups), in_specs=...  180 us
    pallas_call x4, Pallas kernels, mixer_backward(): pl.pallas_call(functools.partial(backward_kernel, early is None, carried...  109 us
    pallas_call x4, Pallas kernels, mixer_forward(): pl.pallas_call(functools.partial(forward_kernel, earlier is None, heads),...  52.4 us
    pallas_call x7, Pallas kernels, norm_rows(): pl.pallas_call(kernel, grid_spec=pltpu.PrefetchScalarGridSpec(num_scalar_...  41.6 us
    ppermute x14, waiting for transfers between devices, to_group(): lax.ppermute(v, 'tensor', [(t, (t + 2 * hop) % self.members) for t in ran...  35 us
    pallas_call x2, Pallas kernels, stacked_product(): pl.pallas_call(kernel, grid_spec=pltpu.PrefetchScalarGridSpec(num_scalar_...  29.7 us
  transfers between devices with their start and end apart: 45, of which 10 were waited for; matrix products, arithmetic and copies ran while one was open for 9% of the time, Pallas kernels for 59%

profile of v5, /device:TPU:0, one launch (start us, length us, event | category | flops | bytes accessed | tf_op | source)
XLA Modules:
  0.0 1158.1 jit_solution(7953635192367201367)
XLA Ops:
  16.7 179.8 %gathered_first.1 = (bf16[2,8,256,3328]{3,2,1,0:T(8,128)(2,1)}, bf16[4,256,2048]{2,1,0:T(8,128)(2,1)}) custom-call(bf16[256,3328]{1,0:T(8,128)(2,1)} %concatenate.93.block_ref, bf16[2,256,2048]{2,1,0:T(8,128)(2,1)} %hidden_ref.1), custom_call_target="tpu_custom_call" | custom-call | bytes 314572800 | tf_op jit(solution)/shard_map/gathered_first/pallas_call | solution.py:809
  211.9 16.0 %in_projection.4 = (bf16[2,512,2048]{2,1,0:T(8,128)(2,1)}, f32[2,512,256]{2,1,0:T(8,128)}) custom-call(bf16[512,2048]{1,0:T(8,128)(2,1)} %copy-done.11, bf16[4096,3328]{1,0:T(8,128)(2,1)} %bitcast.172, bf16[4096,3328]{1,0:T(8,128)(2,1)} %bitcast.173), custom_call_target="tpu_custom_call" | custom-call | flops 3221225472 | bytes 4718592 | tf_op jit(solution)/shard_map/in_projection/pallas_call | solution.py:442
  230.1 12.7 %mixer_forward.4 = (bf16[2,512,1024]{2,1,0:T(8,128)(2,1)S(1)}, f32[512,1]{1,0:T(8,128)S(1)}, f32[2,512,1024]{2,1,0:T(8,128)}, bf16[2,4,128,1024]{3,2,1,0:T(8,128)(2,1)}, f32[128,2048]{1,0:T(8,128)S(1)}) custom-call(bf16[2,512,2048]{2,1,0:T(8,128)(2,1)} %get-tuple-element.158.refs_0_.refs_8_.refs_13_.refs_11_, f32[2,512,256]{2,1,0:T(8,128)S(1)} %copy-done.3, ...), custom_call_target="tpu_custom_call" | custom-call | flops 1572864000 | bytes 4194304 | tf_op jit(solution)/shard_map/mixer_forward/pallas_call | solution.py:358
  257.8 16.1 %in_projection.5 = (bf16[2,512,2048]{2,1,0:T(8,128)(2,1)}, f32[2,512,256]{2,1,0:T(8,128)}) custom-call(bf16[512,2048]{1,0:T(8,128)(2,1)} %norm_forward.5.normed_ref.refs_1_, bf16[4096,3328]{1,0:T(8,128)(2,1)} %bitcast.176, bf16[4096,3328]{1,0:T(8,128)(2,1)} %bitcast.177), custom_call_target="tpu_custom_call" | custom-call | flops 3221225472 | bytes 4718592 | tf_op jit(solution)/shard_map/in_projection/pallas_call | solution.py:442
  276.5 13.5 %mixer_forward.5 = (bf16[2,512,1024]{2,1,0:T(8,128)(2,1)}, f32[512,1]{1,0:T(8,128)S(1)}, f32[2,512,1024]{2,1,0:T(8,128)}, bf16[2,4,128,1024]{3,2,1,0:T(8,128)(2,1)}, f32[128,2048]{1,0:T(8,128)}) custom-call(bf16[2,512,2048]{2,1,0:T(8,128)(2,1)} %get-tuple-element.164.refs_0_.refs_11_, f32[2,512,256]{2,1,0:T(8,128)S(1)} %copy-done.9, ...), custom_call_target="tpu_custom_call" | custom-call | flops 1572864000 | bytes 4194304 | tf_op jit(solution)/shard_map/mixer_forward/pallas_call | solution.py:358
  291.1 9.0 out_projection.5.refs_2_.refs_5_
  314.0 25.4 %all-gather.2.cloned.1.call-done.main_ref.thin_ref.first_ref.second_ref.weight_ref.refs_0_.refs_1_.refs_2_.refs_3_.refs_4_.refs_5_ = bf16[4096,3328]{1,0:T(8,128)(2,1)} async-done(((bf16[256,3328]{1,0:T(8,128)(2,1)}), bf16[4096,3328]{1,0:T(8,128)(2,1)}) %all-gather.2.cloned.1.call-update) | async-done | bytes 27262992 | tf_op jit(solution)/shard_map/all_gather | solution.py:1082
  351.0 15.8 %in_projection.6 = (bf16[2,512,2048]{2,1,0:T(8,128)(2,1)}, f32[2,512,256]{2,1,0:T(8,128)}) custom-call(bf16[512,2048]{1,0:T(8,128)(2,1)} %get-tuple-element.178.normed_ref.refs_0_, bf16[4096,3328]{1,0:T(8,128)(2,1)} %all-gather.2.cloned.1.call-done.main_ref.thin_ref.first_ref.second_ref.weight_ref.refs_0_.refs_1_.refs_2_.refs_3_.refs_4_.refs_5_, ...), custom_call_target="tpu_custom_call" | custom-call | flops 3221225472 | bytes 4718592 | tf_op jit(solution)/shard_map/in_projection/pallas_call | solution.py:442
  368.0 12.9 %mixer_forward.6 = (bf16[2,512,1024]{2,1,0:T(8,128)(2,1)}, f32[512,1]{1,0:T(8,128)S(1)}, f32[2,512,1024]{2,1,0:T(8,128)}, bf16[2,4,128,1024]{3,2,1,0:T(8,128)(2,1)}, f32[128,2048]{1,0:T(8,128)S(1)}) custom-call(bf16[2,512,2048]{2,1,0:T(8,128)(2,1)} %get-tuple-element.180.refs_0_.refs_8_.refs_13_.refs_11_, f32[2,512,256]{2,1,0:T(8,128)S(1)} %copy-done.5, ...), custom_call_target="tpu_custom_call" | custom-call | flops 1572864000 | bytes 4194304 | tf_op jit(solution)/shard_map/mixer_forward/pallas_call | solution.py:358
  381.9 8.9 out_projection.6
  403.0 15.9 %in_projection.7 = (bf16[2,512,2048]{2,1,0:T(8,128)(2,1)}, f32[2,512,256]{2,1,0:T(8,128)}) custom-call(bf16[512,2048]{1,0:T(8,128)(2,1)} %get-tuple-element.187.normed_ref.refs_1_, bf16[4096,3328]{1,0:T(8,128)(2,1)} %all-gather.2.cloned.1.call-done.main_ref.thin_ref.first_ref.second_ref.weight_ref.refs_0_.refs_1_.refs_2_.refs_3_.refs_4_.refs_5_, ...), custom_call_target="tpu_custom_call" | custom-call | flops 3221225472 | bytes 4718592 | tf_op jit(solution)/shard_map/in_projection/pallas_call | solution.py:442
  421.3 13.3 %mixer_forward.7 = (bf16[2,512,1024]{2,1,0:T(8,128)(2,1)}, f32[512,1]{1,0:T(8,128)S(1)}, f32[2,512,1024]{2,1,0:T(8,128)}, bf16[2,4,128,1024]{3,2,1,0:T(8,128)(2,1)}, f32[128,2048]{1,0:T(8,128)}) custom-call(bf16[2,512,2048]{2,1,0:T(8,128)(2,1)} %get-tuple-element.188.refs_0_.refs_11_, f32[2,512,256]{2,1,0:T(8,128)S(1)} %copy-done.10, ...), custom_call_target="tpu_custom_call" | custom-call | flops 1572864000 | bytes 4194304 | tf_op jit(solution)/shard_map/mixer_forward/pallas_call | solution.py:358
  461.8 9.1 mixed_gradient.4
  470.9 9.2 mixed_gradient.5
  480.1 15.0 %stacked_product.2 = bf16[2,1024,1024]{2,1,0:T(8,128)(2,1)} custom-call(s32[1]{0:T(128)} %bitcast.37.core_ref, bf16[512,2048]{1,0:T(8,128)(2,1)} %get-tuple-element.213.up_ref.refs_0_, bf16[512,2048]{1,0:T(8,128)(2,1)} %get-tuple-element.214.up_ref.refs_1_, bf16[512,2048]{1,0:T(8,128)(2,1)} %collective-permute-done.15.refs_2_, ...), custom_call_target="tpu_custom_call" | custom-call | flops 2147483648 | bytes 1048576 | tf_op jit(solution)/shard_map/stacked_product/pallas_call | solution.py:590
  509.1 26.8 %mixer_backward.4 = (bf16[512,4608]{1,0:T(8,128)(2,1)}, f32[128,2048]{1,0:T(8,128)}, f32[8,2048]{1,0:T(8,128)}, f32[8,256]{1,0:T(8,128)}, f32[8,2048]{1,0:T(8,12...) custom-call(bf16[2,512,2048]{2,1,0:T(8,128)(2,1)} %get-tuple-element.188.refs_0_.refs_11_, ...), custom_call_target="tpu_custom_call" | custom-call | flops 3145728000 | bytes 5242880 | tf_op jit(solution)/shard_map/mixer_backward/pallas_call | solution.py:419
  536.0 16.1 %normed_gradient.4.refs_2_ = bf16[512,2048]{1,0:T(8,128)(2,1)} custom-call(bf16[512,4608]{1,0:T(8,128)(2,1)} %get-tuple-element.221.dcolumns_ref.refs_5_, bf16[4096,3328]{1,0:T(8,128)(2,1)} %all-gather.2.cloned.1.call-done.main_ref.thin_ref.first_ref.second_ref.weight_ref.refs_0_.refs_1_.refs_2_.refs_3_.refs_4_.refs_5_, ...), custom_call_target="tpu_custom_call" | custom-call | flops 3221225472 | bytes 4718592 | tf_op jit(solution)/shard_map/normed_gradient/pallas_call | solution.py:442
  563.6 27.3 %mixer_backward.5 = (bf16[512,4608]{1,0:T(8,128)(2,1)}, f32[128,2048]{1,0:T(8,128)}, f32[8,2048]{1,0:T(8,128)}, f32[8,256]{1,0:T(8,128)}, f32[8,2048]{1,0:T(8,12...) custom-call(bf16[2,512,2048]{2,1,0:T(8,128)(2,1)} %get-tuple-element.180.refs_0_.refs_8_.refs_13_.refs_11_, ...), custom_call_target="tpu_custom_call" | custom-call | flops 3145728000 | bytes 5242880 | tf_op jit(solution)/shard_map/mixer_backward/pallas_call | solution.py:419
  594.2 16.0 %normed_gradient.5.refs_2_ = bf16[512,2048]{1,0:T(8,128)(2,1)} custom-call(bf16[512,4608]{1,0:T(8,128)(2,1)} %get-tuple-element.235.dcolumns_ref.refs_4_, bf16[4096,3328]{1,0:T(8,128)(2,1)} %all-gather.2.cloned.1.call-done.main_ref.thin_ref.first_ref.second_ref.weight_ref.refs_0_.refs_1_.refs_2_.refs_3_.refs_4_.refs_5_, ...), custom_call_target="tpu_custom_call" | custom-call | flops 3221225472 | bytes 4718592 | tf_op jit(solution)/shard_map/normed_gradient/pallas_call | solution.py:442
  615.2 136.2 %reduced_product.2 = (f32[256,2304]{1,0:T(8,128)}, f32[8,1024]{1,0:T(8,128)}, f32[8,256]{1,0:T(8,128)}) custom-call(bf16[512,2048]{1,0:T(8,128)(2,1)} %get-tuple-element.178.normed_ref.refs_0_, bf16[512,2048]{1,0:T(8,128)(2,1)} %get-tuple-element.187.normed_ref.refs_1_, bf16[512,2048]{1,0:T(8,128)(2,1)} %collective-permute-done.7.refs_2_, ...), custom_call_target="tpu_custom_call" | custom-call | flops 115964116992 | bytes 104857600 | tf_op jit(solution)/shard_map/reduced_product/pallas_call | solution.py:1010
  753.0 9.2 norm_backward.3
  762.1 9.3 mixed_gradient.6
  773.1 9.3 norm_backward.4
  786.5 9.2 mixed_gradient.7
  808.4 14.7 %stacked_product.3 = bf16[2,1024,1024]{2,1,0:T(8,128)(2,1)} custom-call(s32[1]{0:T(128)} %bitcast.37.core_ref, bf16[512,2048]{1,0:T(8,128)(2,1)} %get-tuple-element.254.up_ref.refs_0_, bf16[512,2048]{1,0:T(8,128)(2,1)} %get-tuple-element.255.up_ref.refs_1_, bf16[512,2048]{1,0:T(8,128)(2,1)} %collective-permute-done.25.refs_2_, ...), custom_call_target="tpu_custom_call" | custom-call | flops 2147483648 | bytes 1048576 | tf_op jit(solution)/shard_map/stacked_product/pallas_call | solution.py:590
  826.2 26.8 %mixer_backward.6 = (bf16[512,4608]{1,0:T(8,128)(2,1)}, f32[128,2048]{1,0:T(8,128)}, f32[8,2048]{1,0:T(8,128)}, f32[8,256]{1,0:T(8,128)}, f32[8,2048]{1,0:T(8,12...) custom-call(bf16[2,512,2048]{2,1,0:T(8,128)(2,1)} %get-tuple-element.164.refs_0_.refs_11_, ...), custom_call_target="tpu_custom_call" | custom-call | flops 3145728000 | bytes 5242880 | tf_op jit(solution)/shard_map/mixer_backward/pallas_call | solution.py:419
  853.2 27.6 %mixer_backward.7 = (bf16[512,4608]{1,0:T(8,128)(2,1)}, f32[128,2048]{1,0:T(8,128)}, f32[8,2048]{1,0:T(8,128)}, f32[8,256]{1,0:T(8,128)}, f32[8,2048]{1,0:T(8,12...) custom-call(bf16[2,512,2048]{2,1,0:T(8,128)(2,1)} %get-tuple-element.158.refs_0_.refs_8_.refs_13_.refs_11_, ...), custom_call_target="tpu_custom_call" | custom-call | flops 3145728000 | bytes 5242880 | tf_op jit(solution)/shard_map/mixer_backward/pallas_call | solution.py:419
  894.9 16.2 %normed_gradient.6 = bf16[512,2048]{1,0:T(8,128)(2,1)} custom-call(bf16[512,4608]{1,0:T(8,128)(2,1)} %get-tuple-element.272.dcolumns_ref, bf16[4096,3328]{1,0:T(8,128)(2,1)} %bitcast.182, bf16[4096,3328]{1,0:T(8,128)(2,1)} %bitcast.183, bf16[4096,3328]{1,0:T(8,128)(2,1)} %bitcast.184, bf16[4096,3328]{1,0:T(8,128)(2,1)} %bitcast.185, ...), custom_call_target="tpu_custom_call" | custom-call | flops 3221225472 | bytes 4718592 | tf_op jit(solution)/shard_map/normed_gradient/pallas_call | solution.py:442
  917.4 15.9 %normed_gradient.7.refs_5_ = bf16[512,2048]{1,0:T(8,128)(2,1)} custom-call(bf16[512,4608]{1,0:T(8,128)(2,1)} %get-tuple-element.273.dcolumns_ref, bf16[4096,3328]{1,0:T(8,128)(2,1)} %bitcast.188, bf16[4096,3328]{1,0:T(8,128)(2,1)} %bitcast.189, bf16[4096,3328]{1,0:T(8,128)(2,1)} %bitcast.190, bf16[4096,3328]{1,0:T(8,128)(2,1)} %bitcast.191, ...), custom_call_target="tpu_custom_call" | custom-call | flops 3221225472 | bytes 4718592 | tf_op jit(solution)/shard_map/normed_gradient/pallas_call | solution.py:442
  951.3 10.4 collective-permute-done.29.refs_6_
  961.7 10.7 collective-permute-start.38
  992.7 131.6 %reduced_product.3 = (f32[256,2304]{1,0:T(8,128)}, f32[8,1024]{1,0:T(8,128)}, f32[24,256]{1,0:T(8,128)}) custom-call(bf16[512,2048]{1,0:T(8,128)(2,1)} %copy-done.11, bf16[512,2048]{1,0:T(8,128)(2,1)} %norm_forward.5.normed_ref.refs_1_, bf16[512,2048]{1,0:T(8,128)(2,1)} %collective-permute-done.32.refs_2_, ...), custom_call_target="tpu_custom_call" | custom-call | flops 115964116992 | bytes 104857600 | tf_op jit(solution)/shard_map/reduced_product/pallas_call | solution.py:1010
  (403 shorter events, 256.7 us)
Async XLA Ops:
  7.2 332.2 %all-gather.2.cloned.1.call-start = ((), (), s32[]{:S(2)}) async-start(), calls=%async_computation | async-start | bytes 28966912 | tf_op jit(solution)/shard_map/all_gather | solution.py:1082
  202.6 26.1 %collective-permute-start = (f32[2,6,1024]{2,1,0:T(8,128)S(1)}, f32[2,6,1024]{2,1,0:T(8,128)S(1)}, u32[]{:S(2)}, u32[]{:S(2)}) collective-permute-start(f32[2,6,1024]{2,1,0:T(8,128)S(1)} %pad_maximum_fusion.10), channel_id=1, source_target_pairs={{0,1},{1,0},{2,3},{3,2},{4,5},{5,4},{6,7},{7,6},{8,9},{9,8},{10,11... | collective-permute-start | bytes 147464 | tf_op jit(solution)/shard_map/ppermute | solution.py:1069
  203.2 24.8 %collective-permute-start.1 = (f32[2,1,3,16]{3,0,2,1:T(2,128)S(1)}, f32[2,1,3,16]{3,0,2,1:T(2,128)S(1)}, u32[]{:S(2)}, u32[]{:S(2)}) collective-permute-start(f32[2,1,3,16]{3,0,2,1:T(2,128)S(1)} %maximum_bitcast_fusion.2), channel_id=1, source_target_pairs={{0,1},{1,0},{2,3},{3,2},{4,5},{5,4},{6,7},{7,6},{8,9},{9,8},{10,11... | collective-permute-start | bytes 1160 | tf_op jit(solution)/shard_map/ppermute | solution.py:1069
  253.9 60.0 %collective-permute-start.3 = (bf16[512,2048]{1,0:T(8,128)(2,1)}, bf16[512,2048]{1,0:T(8,128)(2,1)}, u32[]{:S(2)}, u32[]{:S(2)}) collective-permute-start(bf16[512,2048]{1,0:T(8,128)(2,1)} %out_projection.4.refs_2_.refs_5_), channel_id=1, source_target_pairs={{0,2},{1,3},{2,0},{3,1},{4,6},{5,7},{6,4},{7,5},{8,10},{9,11},{10,... | collective-permute-start | bytes 6291464 | tf_op jit(solution)/shard_map/ppermute | solution.py:1072
  301.9 95.1 %collective-permute-start.5 = (bf16[512,2048]{1,0:T(8,128)(2,1)}, bf16[512,2048]{1,0:T(8,128)(2,1)}, u32[]{:S(2)}, u32[]{:S(2)}) collective-permute-start(bf16[512,2048]{1,0:T(8,128)(2,1)} %out_projection.5.refs_2_.refs_5_), channel_id=1, source_target_pairs={{0,2},{1,3},{2,0},{3,1},{4,6},{5,7},{6,4},{7,5},{8,10},{9,11},{10,... | collective-permute-start | bytes 6291464 | tf_op jit(solution)/shard_map/ppermute | solution.py:1072
  349.7 41.1 %collective-permute-start.9 = (bf16[256,2048]{1,0:T(8,128)(2,1)}, bf16[256,2048]{1,0:T(8,128)(2,1)}, u32[]{:S(2)}, u32[]{:S(2)}) collective-permute-start(bf16[256,2048]{1,0:T(8,128)(2,1)} %get-tuple-element.369), channel_id=1, source_target_pairs={{0,1},{1,0},{2,3},{3,2},{4,5},{5,4},{6,7},{7,6},{8,9},{9,8},{10,11... | collective-permute-start | bytes 3145736 | tf_op jit(solution)/shard_map/ppermute | solution.py:1069
  395.6 59.7 %collective-permute-start.10 = (bf16[512,2048]{1,0:T(8,128)(2,1)}, bf16[512,2048]{1,0:T(8,128)(2,1)}, u32[]{:S(2)}, u32[]{:S(2)}) collective-permute-start(bf16[512,2048]{1,0:T(8,128)(2,1)} %maximum_select_fusion.2), channel_id=1, source_target_pairs={{0,2},{1,3},{2,0},{3,1},{4,6},{5,7},{6,4},{7,5},{8,10},{9,11},{10,... | collective-permute-start | bytes 6291464 | tf_op jit(solution)/shard_map/ppermute | solution.py:1072
  498.2 53.9 %collective-permute-start.19 = (bf16[1024,1024]{1,0:T(8,128)(2,1)}, bf16[1024,1024]{1,0:T(8,128)(2,1)}, u32[]{:S(2)}, u32[]{:S(2)}) collective-permute-start(bf16[1024,1024]{1,0:T(8,128)(2,1)} %dynamic-slice_bitcast_fusion.1), channel_id=1, source_target_pairs={{0,1},{1,0},{2,3},{3,2},{4,5},{5,4},{6,7},{7,6},{8,9},{9,8},{10,11... | collective-permute-start | bytes 6291464 | tf_op jit(solution)/shard_map/ppermute | solution.py:1069
  500.6 61.2 %collective-permute-start.13 = (f32[512,1]{1,0:T(8,128)}, f32[512,1]{1,0:T(8,128)}, u32[]{:S(2)}, u32[]{:S(2)}) collective-permute-start(f32[512,1]{1,0:T(8,128)} %get-tuple-element.223), channel_id=1, source_target_pairs={{0,2},{1,3},{2,0},{3,1},{4,6},{5,7},{6,4},{7,5},{8,10},{9,11},{10,... | collective-permute-start | bytes 6152 | tf_op jit(solution)/shard_map/ppermute | solution.py:1072
  535.9 77.2 %collective-permute-start.21 = (bf16[512,4608]{1,0:T(8,128)(2,1)}, bf16[512,4608]{1,0:T(8,128)(2,1)}, u32[]{:S(2)}, u32[]{:S(2)}) collective-permute-start(bf16[512,4608]{1,0:T(8,128)(2,1)} %get-tuple-element.221.dcolumns_ref.refs_5_), channel_id=1, source_target_pairs={{0,4},{4,0},{8,12},{12,8},{16,20},{20,16},{24,28},{28,24},{1,5},{5... | collective-permute-start | bytes 14155784 | tf_op jit(solution)/shard_map/ppermute | solution.py:1075
  590.9 22.8 %collective-permute-start.20 = (bf16[512,4608]{1,0:T(8,128)(2,1)}, bf16[512,4608]{1,0:T(8,128)(2,1)}, u32[]{:S(2)}, u32[]{:S(2)}) collective-permute-start(bf16[512,4608]{1,0:T(8,128)(2,1)} %get-tuple-element.235.dcolumns_ref.refs_4_), channel_id=1, source_target_pairs={{0,4},{4,0},{8,12},{12,8},{16,20},{20,16},{24,28},{28,24},{1,5},{5... | collective-permute-start | bytes 14155784 | tf_op jit(solution)/shard_map/ppermute | solution.py:1075
  592.0 216.5 %collective-permute-start.28 = (bf16[2,512,1024]{2,1,0:T(8,128)(2,1)}, bf16[2,512,1024]{2,1,0:T(8,128)(2,1)}, u32[]{:S(2)}, u32[]{:S(2)}) collective-permute-start(bf16[2,512,1024]{2,1,0:T(8,128)(2,1)} %get-tuple-element.168.mixed_ref.refs_5_), channel_id=1, source_target_pairs={{0,4},{4,0},{8,12},{12,8},{16,20},{20,16},{24,28},{28,24},{1,5},{5... | collective-permute-start | bytes 6291464 | tf_op jit(solution)/shard_map/ppermute | solution.py:1075
  611.2 197.2 %collective-permute-start.27 = (bf16[2,512,1024]{2,1,0:T(8,128)(2,1)}, bf16[2,512,1024]{2,1,0:T(8,128)(2,1)}, u32[]{:S(2)}, u32[]{:S(2)}) collective-permute-start(bf16[2,512,1024]{2,1,0:T(8,128)(2,1)} %copy-done.7), channel_id=1, source_target_pairs={{0,4},{4,0},{8,12},{12,8},{16,20},{20,16},{24,28},{28,24},{1,5},{5... | collective-permute-start | bytes 6291464 | tf_op jit(solution)/shard_map/ppermute | solution.py:1075
  611.7 187.0 %collective-permute-start.6 = (bf16[512,2048]{1,0:T(8,128)(2,1)}, bf16[512,2048]{1,0:T(8,128)(2,1)}, u32[]{:S(2)}, u32[]{:S(2)}) collective-permute-start(bf16[512,2048]{1,0:T(8,128)(2,1)} %broadcast_select_fusion.4), channel_id=1, source_target_pairs={{0,2},{1,3},{2,0},{3,1},{4,6},{5,7},{6,4},{7,5},{8,10},{9,11},{10,... | collective-permute-start | bytes 6291464 | tf_op jit(solution)/shard_map/ppermute | solution.py:1072
  613.1 138.2 %collective-permute-start.24 = (bf16[512,2048]{1,0:T(8,128)(2,1)}, bf16[512,2048]{1,0:T(8,128)(2,1)}, u32[]{:S(2)}, u32[]{:S(2)}) collective-permute-start(bf16[512,2048]{1,0:T(8,128)(2,1)} %normed_gradient.4.refs_2_), channel_id=1, source_target_pairs={{0,2},{1,3},{2,0},{3,1},{4,6},{5,7},{6,4},{7,5},{8,10},{9,11},{10,... | collective-permute-start | bytes 6291464 | tf_op jit(solution)/shard_map/ppermute | solution.py:1072
  613.7 157.8 %collective-permute-start.23 = (bf16[512,2048]{1,0:T(8,128)(2,1)}, bf16[512,2048]{1,0:T(8,128)(2,1)}, u32[]{:S(2)}, u32[]{:S(2)}) collective-permute-start(bf16[512,2048]{1,0:T(8,128)(2,1)} %normed_gradient.5.refs_2_), channel_id=1, source_target_pairs={{0,2},{1,3},{2,0},{3,1},{4,6},{5,7},{6,4},{7,5},{8,10},{9,11},{10,... | collective-permute-start | bytes 6291464 | tf_op jit(solution)/shard_map/ppermute | solution.py:1072
  782.4 24.9 %collective-permute-start.25 = (bf16[512,2048]{1,0:T(8,128)(2,1)}, bf16[512,2048]{1,0:T(8,128)(2,1)}, u32[]{:S(2)}, u32[]{:S(2)}) collective-permute-start(bf16[512,2048]{1,0:T(8,128)(2,1)} %get-tuple-element.254.up_ref.refs_0_), channel_id=1, source_target_pairs={{0,4},{4,0},{8,12},{12,8},{16,20},{20,16},{24,28},{28,24},{1,5},{5... | collective-permute-start | bytes 6291464 | tf_op jit(solution)/shard_map/ppermute | solution.py:1075
  782.4 26.0 %collective-permute-start.26 = (bf16[512,2048]{1,0:T(8,128)(2,1)}, bf16[512,2048]{1,0:T(8,128)(2,1)}, u32[]{:S(2)}, u32[]{:S(2)}) collective-permute-start(bf16[512,2048]{1,0:T(8,128)(2,1)} %get-tuple-element.255.up_ref.refs_1_), channel_id=1, source_target_pairs={{0,4},{4,0},{8,12},{12,8},{16,20},{20,16},{24,28},{28,24},{1,5},{5... | collective-permute-start | bytes 6291464 | tf_op jit(solution)/shard_map/ppermute | solution.py:1075
  798.6 94.0 %collective-permute-start.41 = (bf16[256,1024]{0,1:T(8,128)(2,1)}, bf16[256,1024]{0,1:T(8,128)(2,1)}, u32[]{:S(2)}, u32[]{:S(2)}) collective-permute-start(bf16[256,1024]{0,1:T(8,128)(2,1)} %bitcast.41), channel_id=1, source_target_pairs={{0,8},{4,12},{8,16},{12,20},{16,24},{20,28},{24,0},{28,4},{1,9},{5... | collective-permute-start | bytes 1572872 | tf_op jit(solution)/shard_map/ppermute | solution.py:1079
  807.2 81.4 %collective-permute-start.22 = (bf16[256,2048]{1,0:T(8,128)(2,1)}, bf16[256,2048]{1,0:T(8,128)(2,1)}, u32[]{:S(2)}, u32[]{:S(2)}) collective-permute-start(bf16[256,2048]{1,0:T(8,128)(2,1)} %get-tuple-element.367), channel_id=1, source_target_pairs={{0,1},{1,0},{2,3},{3,2},{4,5},{5,4},{6,7},{7,6},{8,9},{9,8},{10,11... | collective-permute-start | bytes 3145736 | tf_op jit(solution)/shard_map/ppermute | solution.py:1069
  853.1 139.7 %collective-permute-start.35 = (bf16[512,4608]{1,0:T(8,128)(2,1)}, bf16[512,4608]{1,0:T(8,128)(2,1)}, u32[]{:S(2)}, u32[]{:S(2)}) collective-permute-start(bf16[512,4608]{1,0:T(8,128)(2,1)} %get-tuple-element.259.refs_5_), channel_id=1, source_target_pairs={{0,4},{4,0},{8,12},{12,8},{16,20},{20,16},{24,28},{28,24},{1,5},{5... | collective-permute-start | bytes 14155784 | tf_op jit(solution)/shard_map/ppermute | solution.py:1075
  880.8 110.1 %collective-permute-start.34 = (bf16[512,4608]{1,0:T(8,128)(2,1)}, bf16[512,4608]{1,0:T(8,128)(2,1)}, u32[]{:S(2)}, u32[]{:S(2)}) collective-permute-start(bf16[512,4608]{1,0:T(8,128)(2,1)} %get-tuple-element.267.refs_4_), channel_id=1, source_target_pairs={{0,4},{4,0},{8,12},{12,8},{16,20},{20,16},{24,28},{28,24},{1,5},{5... | collective-permute-start | bytes 14155784 | tf_op jit(solution)/shard_map/ppermute | solution.py:1075
  887.8 47.9 %collective-permute-start.30 = (bf16[1024,1024]{1,0:T(8,128)(2,1)}, bf16[1024,1024]{1,0:T(8,128)(2,1)}, u32[]{:S(2)}, u32[]{:S(2)}) collective-permute-start(bf16[1024,1024]{1,0:T(8,128)(2,1)} %dynamic-slice_bitcast_fusion), channel_id=1, source_target_pairs={{0,1},{1,0},{2,3},{3,2},{4,5},{5,4},{6,7},{7,6},{8,9},{9,8},{10,11... | collective-permute-start | bytes 6291464 | tf_op jit(solution)/shard_map/ppermute | solution.py:1069
  888.6 27.2 %collective-permute-start.42 = (bf16[256,1024]{0,1:T(8,128)(2,1)}, bf16[256,1024]{0,1:T(8,128)(2,1)}, u32[]{:S(2)}, u32[]{:S(2)}) collective-permute-start(bf16[256,1024]{0,1:T(8,128)(2,1)} %bitcast.42), channel_id=1, source_target_pairs={{0,16},{4,20},{8,24},{12,28},{16,0},{20,4},{24,8},{28,12},{1,17},{... | collective-permute-start | bytes 1572872 | tf_op jit(solution)/shard_map/ppermute | solution.py:1079
  892.6 24.7 %collective-permute-start.43 = (bf16[256,1024]{0,1:T(8,128)(2,1)S(1)}, bf16[256,1024]{0,1:T(8,128)(2,1)S(1)}, u32[]{:S(2)}, u32[]{:S(2)}) collective-permute-start(bf16[256,1024]{0,1:T(8,128)(2,1)S(1)} %bitcast.204), channel_id=1, source_target_pairs={{0,24},{4,28},{8,0},{12,4},{16,8},{20,12},{24,16},{28,20},{1,25},{... | collective-permute-start | bytes 1572872 | tf_op jit(solution)/shard_map/ppermute | solution.py:1079
  915.8 45.9 %collective-permute-start.29 = (bf16[512,2048]{1,0:T(8,128)(2,1)}, bf16[512,2048]{1,0:T(8,128)(2,1)}, u32[]{:S(2)}, u32[]{:S(2)}) collective-permute-start(bf16[512,2048]{1,0:T(8,128)(2,1)} %normed_gradient.6), channel_id=1, source_target_pairs={{0,2},{1,3},{2,0},{3,1},{4,6},{5,7},{6,4},{7,5},{8,10},{9,11},{10,... | collective-permute-start | bytes 6291464 | tf_op jit(solution)/shard_map/ppermute | solution.py:1072
  917.3 70.1 %collective-permute-start.32 = (bf16[512,2048]{1,0:T(8,128)(2,1)}, bf16[512,2048]{1,0:T(8,128)(2,1)}, u32[]{:S(2)}, u32[]{:S(2)}) collective-permute-start(bf16[512,2048]{1,0:T(8,128)(2,1)} %copy-done.11), channel_id=1, source_target_pairs={{0,4},{4,0},{8,12},{12,8},{16,20},{20,16},{24,28},{28,24},{1,5},{5... | collective-permute-start | bytes 6291464 | tf_op jit(solution)/shard_map/ppermute | solution.py:1075
  935.7 55.2 %collective-permute-start.33 = (bf16[512,2048]{1,0:T(8,128)(2,1)}, bf16[512,2048]{1,0:T(8,128)(2,1)}, u32[]{:S(2)}, u32[]{:S(2)}) collective-permute-start(bf16[512,2048]{1,0:T(8,128)(2,1)} %norm_forward.5.normed_ref.refs_1_), channel_id=1, source_target_pairs={{0,4},{4,0},{8,12},{12,8},{16,20},{20,16},{24,28},{28,24},{1,5},{5... | collective-permute-start | bytes 6291464 | tf_op jit(solution)/shard_map/ppermute | solution.py:1075
  961.7 164.4 %collective-permute-start.38 = (bf16[256,1024]{0,1:T(8,128)(2,1)}, bf16[256,1024]{0,1:T(8,128)(2,1)}, u32[]{:S(2)}, u32[]{:S(2)}) collective-permute-start(bf16[256,1024]{0,1:T(8,128)(2,1)} %bitcast.206), channel_id=1, source_target_pairs={{0,8},{4,12},{8,16},{12,20},{16,24},{20,28},{24,0},{28,4},{1,9},{5... | collective-permute-start | bytes 1572872 | tf_op jit(solution)/shard_map/ppermute | solution.py:1079
  987.4 138.7 %collective-permute-start.39 = (bf16[256,1024]{0,1:T(8,128)(2,1)}, bf16[256,1024]{0,1:T(8,128)(2,1)S(1)}, u32[]{:S(2)}, u32[]{:S(2)}) collective-permute-start(bf16[256,1024]{0,1:T(8,128)(2,1)} %bitcast.55), channel_id=1, source_target_pairs={{0,16},{4,20},{8,24},{12,28},{16,0},{20,4},{24,8},{28,12},{1,17},{... | collective-permute-start | bytes 1572872 | tf_op jit(solution)/shard_map/ppermute | solution.py:1079
  990.8 135.3 %collective-permute-start.40 = (bf16[256,1024]{0,1:T(8,128)(2,1)S(1)}, bf16[256,1024]{0,1:T(8,128)(2,1)}, u32[]{:S(2)}, u32[]{:S(2)}) collective-permute-start(bf16[256,1024]{0,1:T(8,128)(2,1)S(1)} %bitcast.205), channel_id=1, source_target_pairs={{0,24},{4,28},{8,0},{12,4},{16,8},{20,12},{24,16},{28,20},{1,25},{... | collective-permute-start | bytes 1572872 | tf_op jit(solution)/shard_map/ppermute | solution.py:1079
  990.9 142.7 %collective-permute-start.31 = (bf16[256,2048]{1,0:T(8,128)(2,1)}, bf16[256,2048]{1,0:T(8,128)(2,1)S(1)}, u32[]{:S(2)}, u32[]{:S(2)}) collective-permute-start(bf16[256,2048]{1,0:T(8,128)(2,1)} %get-tuple-element.365), channel_id=1, source_target_pairs={{0,1},{1,0},{2,3},{3,2},{4,5},{5,4},{6,7},{7,6},{8,9},{9,8},{10,11... | collective-permute-start | bytes 3145736 | tf_op jit(solution)/shard_map/ppermute | solution.py:1069
  (94 other events, 2107.9 us)
Sparse Core Ops, SparseCore 0:
  202.6 136.7 all-gather.1

commit v6 on v5

--- a/solution.py
+++ b/solution.py
@@ -11,6 +11,8 @@
 CHUNK = 128
 PIECES = 2
 GROUP_LANES = 256
+SMALL_COST = pl.CostEstimate(flops=1000, bytes_accessed=1000, transcendentals=0)
+LARGE_COST = pl.CostEstimate(flops=10**11, bytes_accessed=10**8, transcendentals=0)
 LOG2E = 1.4426950408889634
 F32 = jnp.float32
 BF16 = jnp.bfloat16
@@ -378,9 +380,7 @@
             pltpu.VMEM((CHUNK + 8, shared), F32),
         ],
         compiler_params=pltpu.CompilerParams(vmem_limit_bytes=48 * 1024 * 1024),
-        cost_estimate=pl.CostEstimate(
-            flops=tokens * channels * 3000, bytes_accessed=tokens * channels * 8, transcendentals=tokens * channels * 3
-        ),
+        cost_estimate=SMALL_COST,
         name="mixer_forward",
     )(*operands)
 
@@ -430,15 +430,12 @@
             pltpu.VMEM((CHUNK + 8, shared), F32),
         ],
         compiler_params=pltpu.CompilerParams(vmem_limit_bytes=56 * 1024 * 1024),
-        cost_estimate=pl.CostEstimate(
-            flops=tokens * channels * 6000, bytes_accessed=tokens * channels * 10, transcendentals=tokens * channels * 3
-        ),
+        cost_estimate=SMALL_COST,
         name="mixer_backward",
     )(*operands)
 
 
-def product_call(kernel, grid, specs, outs, out_specs, operands, flops, name):
-    moved = flops // 2048
+def product_call(kernel, grid, specs, outs, out_specs, operands, name, cost=SMALL_COST):
     return pl.pallas_call(
         kernel,
         grid=grid,
@@ -446,7 +443,7 @@
         out_specs=out_specs,
         out_shape=outs,
         compiler_params=pltpu.CompilerParams(vmem_limit_bytes=60 * 1024 * 1024),
-        cost_estimate=pl.CostEstimate(flops=flops // 3, bytes_accessed=moved, transcendentals=0),
+        cost_estimate=cost,
         name=name,
     )(*operands)
 
@@ -476,7 +473,6 @@
             pl.BlockSpec((1, tokens, thin), lambda s, n: (s, 0, 0)),
         ],
         (normed, gathered, gathered),
-        4 * tokens * features * (2 * own + thin),
         "in_projection",
     )
 
@@ -501,7 +497,6 @@
         jax.ShapeDtypeStruct((tokens, features), BF16),
         pl.BlockSpec((tokens, tile), lambda n: (0, n)),
         (mixed, gathered, gathered),
-        4 * tokens * features * own,
         "out_projection",
     )
 
@@ -533,7 +528,6 @@
         [jax.ShapeDtypeStruct((2, tokens, own), BF16), jax.ShapeDtypeStruct((tokens, 1), F32)],
         [pl.BlockSpec((1, tokens, own), lambda s: (s, 0, 0)), pl.BlockSpec((tokens, 1), lambda s: (0, 0))],
         (up, gathered, mixed),
-        4 * tokens * features * own,
         "mixed_gradient",
     )
 
@@ -563,8 +557,8 @@
         jax.ShapeDtypeStruct((tokens, features), BF16),
         pl.BlockSpec((tokens, tile), lambda n: (0, n)),
         (dcolumns,) + (gathered,) * 6,
-        2 * tokens * features * columns,
         "normed_gradient",
+        LARGE_COST,
     )
 
 
@@ -598,11 +592,7 @@
         ),
         out_shape=jax.ShapeDtypeStruct((2, steps * row_tile, columns), BF16),
         compiler_params=pltpu.CompilerParams(vmem_limit_bytes=60 * 1024 * 1024),
-        cost_estimate=pl.CostEstimate(
-            flops=steps * row_tile * columns * tokens * chunks,
-            bytes_accessed=steps * row_tile * columns,
-            transcendentals=0,
-        ),
+        cost_estimate=LARGE_COST,
         name="stacked_product",
     )(core, *lhs, *rhs)
 
@@ -820,7 +810,7 @@
             dma((2 * groups,)), dma((members,)), dma((2,)),
         ],
         compiler_params=pltpu.CompilerParams(collective_id=1, has_side_effects=True),
-        cost_estimate=pl.CostEstimate(flops=0, bytes_accessed=300 * 1024 * 1024, transcendentals=0),
+        cost_estimate=SMALL_COST,
         name="gathered_first",
     )(block, hidden)
     return both.reshape(-1, block.shape[1]), stream.reshape(-1, hidden.shape[2])
@@ -1031,9 +1021,7 @@
         compiler_params=pltpu.CompilerParams(
             collective_id=2 + number, has_side_effects=True, vmem_limit_bytes=60 * 1024 * 1024
         ),
-        cost_estimate=pl.CostEstimate(
-            flops=24 * chips * rows * columns * parts * lhs[0].shape[0], bytes_accessed=100 * 1024 * 1024, transcendentals=0
-        ),
+        cost_estimate=LARGE_COST,
         name="reduced_product",
     )(*lhs, *rhs, halves, common)
 
@@ -1078,6 +1066,10 @@
         count = 2 * self.chips
         return lax.ppermute(v, "dp", [(t, (t + 2 * hop) % count) for t in range(count)])
 
+    def scatter_owners(self, v):
+        v = v.reshape(-1, v.shape[-1])
+        return lax.psum_scatter(v, ("dp", "tensor"), scatter_dimension=0, axis_index_groups=self.owners, tiled=True)
+
     def gather_owners(self, v):
         return lax.all_gather(v, ("dp", "tensor"), axis=0, axis_index_groups=self.owners, tiled=True)
 
@@ -1140,6 +1132,10 @@
     return v.astype(F32) + sum(piece.astype(F32) for piece in arrived)
 
 
+class Owned:
+    pass
+
+
 class WeightSum:
 
     def __init__(self, place, features, columns, far_features=None, far_columns=None):
@@ -1192,9 +1188,7 @@
         ),
         out_shape=[jax.ShapeDtypeStruct(shape, dtype) for shape, dtype in outs],
         compiler_params=pltpu.CompilerParams(vmem_limit_bytes=48 * 1024 * 1024),
-        cost_estimate=pl.CostEstimate(
-            flops=20 * row_args[0].size, bytes_accessed=sum(array.size * array.dtype.itemsize for array in row_args), transcendentals=0
-        ),
+        cost_estimate=SMALL_COST,
         name=name,
     )(*scalars, *row_args, *fixed_args)
 
@@ -1435,8 +1429,7 @@
     mixed_sent = [place.to_group(place.soon(place.rows_of(shares, hop)), hop) for hop in range(1, place.groups)]
     grads = last_up()
     in_sums, out_sums, gain_grads, carried = [None] * layers, [None] * layers, [0.0] * layers, [None] * layers
-    half_totals, common_totals = [None] * layers, [None] * layers
-    pending = None
+    pending, waiting = None, []
 
     def small_sums(layer):
         gchan, gtaps, ghead = carried[layer]
@@ -1470,33 +1463,34 @@
             back.enter(at, up, pull)
         normed, mixed = kept[layer]["normed"], kept[layer]["mixed"]
         out_sum = out_sums[layer] = WeightSum(place, back.ups, mixed)
-        far_normed = [place.to_core(part) for part in normed]
         out_sum.to_pair()
+        if layer == 0:
+            far_normed = [place.to_core(part) for part in normed]
         far_columns, pending = [None] * PIECES, [None] * PIECES
         for at in reversed(range(PIECES)):
             back.mix(at)
-            far_columns[at] = place.to_core(back.dcolumns[at])
+            if layer == 0:
+                far_columns[at] = place.to_core(back.dcolumns[at])
             if at == PIECES - 1:
                 for later in out_sums[layer + 1 :]:
                     later.owned = later.total()
+                if layer == 0:
+                    own_rows = place.rows_of(kept[-1]["stream"], 0).astype(F32)
+                    update = added(place.rows_of(shares, 0), place.now(tuple(mixed_sent)))
+                    mixed_out = place.give_sequence(own_rows + update * place.rows_of(kept[-1]["scale"], 0))
             if layer:
                 share = back.share(back.dcolumns[at])
                 pending[at] = (share, place.sent_to_groups(share))
                 if at == PIECES - 1:
                     out_sum.to_chips()
         carried[layer] = back.carried[3:]
+        waiting.append(small_sums(layer))
+        if layer:
+            in_sum = in_sums[layer] = Owned()
+            stack = place.did(stacked_product(list(place.now(tuple(normed))), back.dcolumns))
+            in_sum.owned = place.scatter_owners(stack).astype(F32)
+            continue
         in_sum = in_sums[layer] = WeightSum(place, normed, back.dcolumns, far_normed, far_columns)
-        if layer:
-            halves, common = small_sums(layer)
-            in_sum.owned, half_totals[layer], common_totals[layer] = reduced_product(
-                place, in_sum.lhs, in_sum.rhs, place.now(halves), common, layer
-            )
-            place.did(in_sum.owned)
-            if final:
-                own_rows = place.rows_of(kept[-1]["stream"], 0).astype(F32)
-                update = added(place.rows_of(shares, 0), place.now(tuple(mixed_sent)))
-                mixed_out = place.give_sequence(own_rows + update * place.rows_of(kept[-1]["scale"], 0))
-            continue
         mixed_out = place.both_sequences(mixed_out)
         if PIECES == place.groups:
             sent = [back.share(place.rows_of(back.dcolumns, hop)) for hop in range(1, place.groups)]
@@ -1516,24 +1510,22 @@
         gain_grads[layer] = gain_grad[0]
     grad_hidden = place.give_sequence(grad)
 
-    halves, common = small_sums(0)
+    halves = jnp.concatenate([part for part, _ in reversed(waiting)], axis=1)
     gains = jnp.stack(gain_grads).reshape(-1, shared)
-    common = jnp.concatenate([common, gains, jnp.zeros((-gains.shape[0] % 8, shared), F32)])
-    common = then(place.now(common), *out_sums[0].sent)
-    in_sums[0].owned, half_totals[0], common_totals[0] = reduced_product(
-        place, in_sum.lhs, in_sum.rhs, halves, common, 0
-    )
+    common = [part for _, part in reversed(waiting)] + [gains, jnp.zeros((-gains.shape[0] % 8, shared), F32)]
+    common = then(place.now(jnp.concatenate(common)), *out_sums[0].sent)
+    in_sums[0].owned, half_total, common_total = reduced_product(place, in_sum.lhs, in_sum.rhs, halves, common, 0)
     place.did(in_sums[0].owned)
     out_sums[0].owned = out_sums[0].total()
-    gain_total = common_totals[0][8 : 8 + gains.shape[0]].reshape(layers, -1)
+    gain_total = common_total[8 * layers : 8 * layers + gains.shape[0]].reshape(layers, -1)
 
     state_parts = jnp.concatenate([in_sum.owned[:, main : main + half] for in_sum in in_sums])
     state_parts = place.both(place.add_groups(place.now(state_parts)), 1).reshape(layers, rows, shared)
     outs = []
     for layer in range(layers):
-        per_channel_part = half_totals[layer]
+        per_channel_part = half_total[8 * layer : 8 * layer + 8]
         gain_part = lax.dynamic_slice_in_dim(gain_total[layer], lax.axis_index("dp") * rows, rows, 0)
-        taps_part = common_totals[layer][:5]
+        taps_part = common_total[8 * layer : 8 * layer + 5]
         in_owned, out_owned = in_sums[layer].owned, out_sums[layer].owned
         outs.append(
             (

time: 1170 us -> 1060 us (0.906)
  Pallas kernels: 880 us -> 783 us
    pallas_call x2 -> x1, Pallas kernels: 268 us -> 139 us  [reduced_product(): pl.pallas_call(functools.partial(reduce_kernel, chips, groups, orders, pa...]
    pallas_call x2 -> x3, Pallas kernels: 29.7 us -> 58 us  [stacked_product(): pl.pallas_call(kernel, grid_spec=pltpu.PrefetchScalarGridSpec(num_scalar_...]
    ppermute x8, waiting for transfers between devices: 1.2 us -> 17.4 us  [to_pair(): return lax.ppermute(v, 'tensor', [(t, t ^ 1) for t in range(self.members)])]
  transfers between devices with their start and end apart: 45 -> 42, of which waited for: 10 -> 11; matrix products, arithmetic and copies ran while one was open for 9% -> 9% of each run, Pallas kernels for 59% -> 57%
where the time goes in v6:
time: 1060 us
  Pallas kernels  783 us (74%)
  waiting for transfers between devices  77 us (7%)
  local copies, waits for them, and re-layouts  75.4 us (7%)
  other arithmetic  67.9 us (6%)
  starting transfers between devices  38.5 us (4%)
  between operations  15.5 us (1%)
    pallas_call x16, Pallas kernels, product_call(): pl.pallas_call(kernel, grid=grid, in_specs=specs, out_specs=out_specs, ou...  201 us
    pallas_call x1, Pallas kernels, gathered_first(): pl.pallas_call(functools.partial(gather_kernel, chips, groups), in_specs=...  180 us
    pallas_call x1, Pallas kernels, reduced_product(): pl.pallas_call(functools.partial(reduce_kernel, chips, groups, orders, pa...  139 us
    pallas_call x4, Pallas kernels, mixer_backward(): pl.pallas_call(functools.partial(backward_kernel, early is None, carried...  110 us
    pallas_call x3, Pallas kernels, stacked_product(): pl.pallas_call(kernel, grid_spec=pltpu.PrefetchScalarGridSpec(num_scalar_...  58 us
    pallas_call x4, Pallas kernels, mixer_forward(): pl.pallas_call(functools.partial(forward_kernel, earlier is None, heads),...  52.5 us
    pallas_call x7, Pallas kernels, norm_rows(): pl.pallas_call(kernel, grid_spec=pltpu.PrefetchScalarGridSpec(num_scalar_...  42.4 us
    ppermute x14, waiting for transfers between devices, to_group(): lax.ppermute(v, 'tensor', [(t, (t + 2 * hop) % self.members) for t in ran...  32.6 us
  transfers between devices with their start and end apart: 42, of which 11 were waited for; matrix products, arithmetic and copies ran while one was open for 9% of the time, Pallas kernels for 57%

profile of v6, /device:TPU:0, one launch (start us, length us, event | category | flops | bytes accessed | tf_op | source)
XLA Modules:
  0.0 1057.0 jit_solution(4821526686850328523)
XLA Ops:
  16.7 179.8 %gathered_first.1 = (bf16[2,8,256,3328]{3,2,1,0:T(8,128)(2,1)}, bf16[4,256,2048]{2,1,0:T(8,128)(2,1)}) custom-call(bf16[256,3328]{1,0:T(8,128)(2,1)} %concatenate.96.block_ref, bf16[2,256,2048]{2,1,0:T(8,128)(2,1)} %hidden_ref.1), custom_call_target="tpu_custom_call" | custom-call | flops 1000 | bytes 1000 | tf_op jit(solution)/shard_map/gathered_first/pallas_call | solution.py:799
  212.7 16.1 %in_projection.4 = (bf16[2,512,2048]{2,1,0:T(8,128)(2,1)}, f32[2,512,256]{2,1,0:T(8,128)}) custom-call(bf16[512,2048]{1,0:T(8,128)(2,1)} %norm_forward.4.normed_ref.refs_0_, bf16[4096,3328]{1,0:T(8,128)(2,1)} %bitcast.173, bf16[4096,3328]{1,0:T(8,128)(2,1)} %bitcast.174), custom_call_target="tpu_custom_call" | custom-call | flops 1000 | bytes 1000 | tf_op jit(solution)/shard_map/in_projection/pallas_call | solution.py:439
  231.0 12.8 %mixer_forward.4 = (bf16[2,512,1024]{2,1,0:T(8,128)(2,1)}, f32[512,1]{1,0:T(8,128)S(1)}, f32[2,512,1024]{2,1,0:T(8,128)}, bf16[2,4,128,1024]{3,2,1,0:T(8,128)(2,1)}, f32[128,2048]{1,0:T(8,128)S(1)}) custom-call(bf16[2,512,2048]{2,1,0:T(8,128)(2,1)} %get-tuple-element.156.refs_0_.refs_8_.refs_13_.refs_11_, f32[2,512,256]{2,1,0:T(8,128)S(1)} %copy-done, ...), custom_call_target="tpu_custom_call" | custom-call | flops 1000 | bytes 1000 | tf_op jit(solution)/shard_map/mixer_forward/pallas_call | solution.py:360
  257.9 16.1 %in_projection.5 = (bf16[2,512,2048]{2,1,0:T(8,128)(2,1)}, f32[2,512,256]{2,1,0:T(8,128)}) custom-call(bf16[512,2048]{1,0:T(8,128)(2,1)} %norm_forward.5.normed_ref.refs_1_, bf16[4096,3328]{1,0:T(8,128)(2,1)} %bitcast.177, bf16[4096,3328]{1,0:T(8,128)(2,1)} %bitcast.178), custom_call_target="tpu_custom_call" | custom-call | flops 1000 | bytes 1000 | tf_op jit(solution)/shard_map/in_projection/pallas_call | solution.py:439
  276.7 13.3 %mixer_forward.5 = (bf16[2,512,1024]{2,1,0:T(8,128)(2,1)}, f32[512,1]{1,0:T(8,128)S(1)}, f32[2,512,1024]{2,1,0:T(8,128)}, bf16[2,4,128,1024]{3,2,1,0:T(8,128)(2,1)}, f32[128,2048]{1,0:T(8,128)}) custom-call(bf16[2,512,2048]{2,1,0:T(8,128)(2,1)} %get-tuple-element.162.refs_0_.refs_11_, f32[2,512,256]{2,1,0:T(8,128)S(1)} %copy-done.10, ...), custom_call_target="tpu_custom_call" | custom-call | flops 1000 | bytes 1000 | tf_op jit(solution)/shard_map/mixer_forward/pallas_call | solution.py:360
  290.7 9.0 out_projection.5.refs_2_.refs_5_
  312.5 26.9 %all-gather.2.cloned.1.call-done.main_ref.thin_ref.first_ref.second_ref.weight_ref.refs_0_.refs_1_.refs_2_.refs_3_.refs_4_.refs_5_ = bf16[4096,3328]{1,0:T(8,128)(2,1)} async-done(((bf16[256,3328]{1,0:T(8,128)(2,1)}), bf16[4096,3328]{1,0:T(8,128)(2,1)}) %all-gather.2.cloned.1.call-update) | async-done | bytes 27262992 | tf_op jit(solution)/shard_map/all_gather | solution.py:1074
  352.4 15.8 %in_projection.6 = (bf16[2,512,2048]{2,1,0:T(8,128)(2,1)}, f32[2,512,256]{2,1,0:T(8,128)}) custom-call(bf16[512,2048]{1,0:T(8,128)(2,1)} %copy-done.16, bf16[4096,3328]{1,0:T(8,128)(2,1)} %all-gather.2.cloned.1.call-done.main_ref.thin_ref.first_ref.second_ref.weight_ref.refs_0_.refs_1_.refs_2_.refs_3_.refs_4_.refs_5_, ...), custom_call_target="tpu_custom_call" | custom-call | flops 1000 | bytes 1000 | tf_op jit(solution)/shard_map/in_projection/pallas_call | solution.py:439
  369.5 12.8 %mixer_forward.6 = (bf16[2,512,1024]{2,1,0:T(8,128)(2,1)}, f32[512,1]{1,0:T(8,128)S(1)}, f32[2,512,1024]{2,1,0:T(8,128)}, bf16[2,4,128,1024]{3,2,1,0:T(8,128)(2,1)}, f32[128,2048]{1,0:T(8,128)S(1)}) custom-call(bf16[2,512,2048]{2,1,0:T(8,128)(2,1)} %get-tuple-element.178.refs_0_.refs_8_.refs_13_.refs_11_, f32[2,512,256]{2,1,0:T(8,128)S(1)} %copy-done.2, ...), custom_call_target="tpu_custom_call" | custom-call | flops 1000 | bytes 1000 | tf_op jit(solution)/shard_map/mixer_forward/pallas_call | solution.py:360
  405.3 15.9 %in_projection.7 = (bf16[2,512,2048]{2,1,0:T(8,128)(2,1)}, f32[2,512,256]{2,1,0:T(8,128)}) custom-call(bf16[512,2048]{1,0:T(8,128)(2,1)} %copy-done.17, bf16[4096,3328]{1,0:T(8,128)(2,1)} %all-gather.2.cloned.1.call-done.main_ref.thin_ref.first_ref.second_ref.weight_ref.refs_0_.refs_1_.refs_2_.refs_3_.refs_4_.refs_5_, ...), custom_call_target="tpu_custom_call" | custom-call | flops 1000 | bytes 1000 | tf_op jit(solution)/shard_map/in_projection/pallas_call | solution.py:439
  422.5 13.5 %mixer_forward.7 = (bf16[2,512,1024]{2,1,0:T(8,128)(2,1)}, f32[512,1]{1,0:T(8,128)S(1)}, f32[2,512,1024]{2,1,0:T(8,128)}, bf16[2,4,128,1024]{3,2,1,0:T(8,128)(2,1)}, f32[128,2048]{1,0:T(8,128)}) custom-call(bf16[2,512,2048]{2,1,0:T(8,128)(2,1)} %get-tuple-element.186.refs_0_.refs_11_, f32[2,512,256]{2,1,0:T(8,128)S(1)} %copy-done.11, ...), custom_call_target="tpu_custom_call" | custom-call | flops 1000 | bytes 1000 | tf_op jit(solution)/shard_map/mixer_forward/pallas_call | solution.py:360
  436.0 9.0 out_projection.7
  464.6 9.1 mixed_gradient.4
  473.7 9.2 mixed_gradient.5
  485.0 14.6 %stacked_product.3 = bf16[2,1024,1024]{2,1,0:T(8,128)(2,1)} custom-call(s32[1]{0:T(128)} %bitcast.37.core_ref, bf16[512,2048]{1,0:T(8,128)(2,1)} %get-tuple-element.210.up_ref.refs_0_, bf16[512,2048]{1,0:T(8,128)(2,1)} %get-tuple-element.211.up_ref.refs_1_, bf16[512,2048]{1,0:T(8,128)(2,1)} %collective-permute-done.12.refs_2_, ...), custom_call_target="tpu_custom_call" | custom-call | flops 99999997952 | bytes 100000000 | tf_op jit(solution)/shard_map/stacked_product/pallas_call | solution.py:584
  504.4 27.2 %mixer_backward.4 = (bf16[512,4608]{1,0:T(8,128)(2,1)}, f32[128,2048]{1,0:T(8,128)}, f32[8,2048]{1,0:T(8,128)}, f32[8,256]{1,0:T(8,128)}, f32[8,2048]{1,0:T(8,12...) custom-call(bf16[2,512,2048]{2,1,0:T(8,128)(2,1)} %get-tuple-element.186.refs_0_.refs_11_, ...), custom_call_target="tpu_custom_call" | custom-call | flops 1000 | bytes 1000 | tf_op jit(solution)/shard_map/mixer_backward/pallas_call | solution.py:419
  531.6 16.0 %normed_gradient.4.refs_2_ = bf16[512,2048]{1,0:T(8,128)(2,1)} custom-call(bf16[512,4608]{1,0:T(8,128)(2,1)} %get-tuple-element.218.dcolumns_ref.refs_3_, bf16[4096,3328]{1,0:T(8,128)(2,1)} %all-gather.2.cloned.1.call-done.main_ref.thin_ref.first_ref.second_ref.weight_ref.refs_0_.refs_1_.refs_2_.refs_3_.refs_4_.refs_5_, ...), custom_call_target="tpu_custom_call" | custom-call | flops 99999997952 | bytes 100000000 | tf_op jit(solution)/shard_map/normed_gradient/pallas_call | solution.py:439
  562.8 27.4 %mixer_backward.5 = (bf16[512,4608]{1,0:T(8,128)(2,1)}, f32[128,2048]{1,0:T(8,128)}, f32[8,2048]{1,0:T(8,128)}, f32[8,256]{1,0:T(8,128)}, f32[8,2048]{1,0:T(8,12...) custom-call(bf16[2,512,2048]{2,1,0:T(8,128)(2,1)} %get-tuple-element.178.refs_0_.refs_8_.refs_13_.refs_11_, ...), custom_call_target="tpu_custom_call" | custom-call | flops 1000 | bytes 1000 | tf_op jit(solution)/shard_map/mixer_backward/pallas_call | solution.py:419
  590.2 16.3 %normed_gradient.5.refs_2_ = bf16[512,2048]{1,0:T(8,128)(2,1)} custom-call(bf16[512,4608]{1,0:T(8,128)(2,1)} %get-tuple-element.233.dcolumns_ref.refs_2_, bf16[4096,3328]{1,0:T(8,128)(2,1)} %all-gather.2.cloned.1.call-done.main_ref.thin_ref.first_ref.second_ref.weight_ref.refs_0_.refs_1_.refs_2_.refs_3_.refs_4_.refs_5_, ...), custom_call_target="tpu_custom_call" | custom-call | flops 99999997952 | bytes 100000000 | tf_op jit(solution)/shard_map/normed_gradient/pallas_call | solution.py:439
  607.9 26.8 %stacked_product.4 = bf16[2,2048,2304]{2,1,0:T(8,128)(2,1)} custom-call(s32[1]{0:T(128)} %constant.178.clone.1.core_ref, bf16[512,2048]{1,0:T(8,128)(2,1)} %copy-done.16, bf16[512,2048]{1,0:T(8,128)(2,1)} %copy-done.17, bf16[512,4608]{1,0:T(8,128)(2,1)} %get-tuple-element.233.dcolumns_ref.refs_2_, bf16[512,4608]{1,0:T(8,128)(2,1)} %get-tuple-element.218.dcolumns_ref.refs_3_), custom_call_target="tpu_custom_call" | custom-call | flops 99999997952 | bytes 100000000 | tf_op jit(solution)/shard_map/stacked_product/pallas_call | solution.py:584
  636.3 9.2 norm_backward.3
  646.2 9.5 mixed_gradient.6
  655.7 9.3 norm_backward.4
  670.2 9.1 mixed_gradient.7
  685.3 16.6 %stacked_product.5 = bf16[2,1024,1024]{2,1,0:T(8,128)(2,1)} custom-call(s32[1]{0:T(128)} %bitcast.37.core_ref, bf16[512,2048]{1,0:T(8,128)(2,1)} %get-tuple-element.245.up_ref.refs_0_, bf16[512,2048]{1,0:T(8,128)(2,1)} %get-tuple-element.246.up_ref.refs_1_, bf16[512,2048]{1,0:T(8,128)(2,1)} %collective-permute-done.20.refs_2_, ...), custom_call_target="tpu_custom_call" | custom-call | flops 99999997952 | bytes 100000000 | tf_op jit(solution)/shard_map/stacked_product/pallas_call | solution.py:584
  705.8 27.7 %mixer_backward.6 = (bf16[512,4608]{1,0:T(8,128)(2,1)}, f32[128,2048]{1,0:T(8,128)}, f32[8,2048]{1,0:T(8,128)}, f32[8,256]{1,0:T(8,128)}, f32[8,2048]{1,0:T(8,12...) custom-call(bf16[2,512,2048]{2,1,0:T(8,128)(2,1)} %get-tuple-element.162.refs_0_.refs_11_, ...), custom_call_target="tpu_custom_call" | custom-call | flops 1000 | bytes 1000 | tf_op jit(solution)/shard_map/mixer_backward/pallas_call | solution.py:419
  733.5 28.0 %mixer_backward.7 = (bf16[512,4608]{1,0:T(8,128)(2,1)}, f32[128,2048]{1,0:T(8,128)}, f32[8,2048]{1,0:T(8,128)}, f32[8,256]{1,0:T(8,128)}, f32[8,2048]{1,0:T(8,12...) custom-call(bf16[2,512,2048]{2,1,0:T(8,128)(2,1)} %get-tuple-element.156.refs_0_.refs_8_.refs_13_.refs_11_, ...), custom_call_target="tpu_custom_call" | custom-call | flops 1000 | bytes 1000 | tf_op jit(solution)/shard_map/mixer_backward/pallas_call | solution.py:419
  768.1 16.1 %normed_gradient.6 = bf16[512,2048]{1,0:T(8,128)(2,1)} custom-call(bf16[512,4608]{1,0:T(8,128)(2,1)} %get-tuple-element.267.dcolumns_ref, bf16[4096,3328]{1,0:T(8,128)(2,1)} %bitcast.183, bf16[4096,3328]{1,0:T(8,128)(2,1)} %bitcast.184, bf16[4096,3328]{1,0:T(8,128)(2,1)} %bitcast.185, bf16[4096,3328]{1,0:T(8,128)(2,1)} %bitcast.186, ...), custom_call_target="tpu_custom_call" | custom-call | flops 99999997952 | bytes 100000000 | tf_op jit(solution)/shard_map/normed_gradient/pallas_call | solution.py:439
  790.8 16.1 %normed_gradient.7.refs_5_ = bf16[512,2048]{1,0:T(8,128)(2,1)} custom-call(bf16[512,4608]{1,0:T(8,128)(2,1)} %get-tuple-element.268.dcolumns_ref, bf16[4096,3328]{1,0:T(8,128)(2,1)} %bitcast.189, bf16[4096,3328]{1,0:T(8,128)(2,1)} %bitcast.190, bf16[4096,3328]{1,0:T(8,128)(2,1)} %bitcast.191, bf16[4096,3328]{1,0:T(8,128)(2,1)} %bitcast.192, ...), custom_call_target="tpu_custom_call" | custom-call | flops 99999997952 | bytes 100000000 | tf_op jit(solution)/shard_map/normed_gradient/pallas_call | solution.py:439
  813.0 14.7 %collective-permute-done.24 = bf16[256,2048]{1,0:T(8,128)(2,1)S(1)} collective-permute-done((bf16[256,2048]{1,0:T(8,128)(2,1)S(1)}, bf16[256,2048]{1,0:T(8,128)(2,1)S(1)}, u32[]{:S(2)}, u32[]{:S(2)}) %collective-permute-start.24) | collective-permute-done | bytes 1048608 | tf_op jit(solution)/shard_map/ppermute | solution.py:1057
  841.5 13.3 %collective-permute-done.25.refs_6_ = bf16[512,2048]{1,0:T(8,128)(2,1)} collective-permute-done((bf16[512,2048]{1,0:T(8,128)(2,1)}, bf16[512,2048]{1,0:T(8,128)(2,1)}, u32[]{:S(2)}, u32[]{:S(2)}) %collective-permute-start.25) | collective-permute-done | bytes 2097184 | tf_op jit(solution)/shard_map/ppermute | solution.py:1060
  875.3 138.9 %reduced_product.1 = (f32[256,2304]{1,0:T(8,128)}, f32[16,1024]{1,0:T(8,128)}, f32[32,256]{1,0:T(8,128)}) custom-call(bf16[512,2048]{1,0:T(8,128)(2,1)} %norm_forward.4.normed_ref.refs_0_, bf16[512,2048]{1,0:T(8,128)(2,1)} %norm_forward.5.normed_ref.refs_1_, bf16[512,2048]{1,0:T(8,128)(2,1)} %collective-permute-done.28.refs_2_, ...), custom_call_target="tpu_custom_call" | custom-call | flops 99999997952 | bytes 100000000 | tf_op jit(solution)/shard_map/reduced_product/pallas_call | solution.py:1000
  (392 shorter events, 245.6 us)
Async XLA Ops:
  7.2 332.2 %all-gather.2.cloned.1.call-start = ((), (), s32[]{:S(2)}) async-start(), calls=%async_computation.1 | async-start | bytes 28966912 | tf_op jit(solution)/shard_map/all_gather | solution.py:1074
  202.5 831.6 %reduce-scatter.2.cloned.1.call-start = ((), (), s32[]{:S(2)}) async-start(), calls=%async_computation.2 | async-start | bytes 20054016 | tf_op jit(solution)/shard_map/reduce_scatter | solution.py:1071
  202.6 26.9 %collective-permute-start = (f32[2,6,1024]{2,1,0:T(8,128)S(1)}, f32[2,6,1024]{2,1,0:T(8,128)S(1)}, u32[]{:S(2)}, u32[]{:S(2)}) collective-permute-start(f32[2,6,1024]{2,1,0:T(8,128)S(1)} %pad_maximum_fusion.10), channel_id=1, source_target_pairs={{0,1},{1,0},{2,3},{3,2},{4,5},{5,4},{6,7},{7,6},{8,9},{9,8},{10,11... | collective-permute-start | bytes 147464 | tf_op jit(solution)/shard_map/ppermute | solution.py:1057
  203.3 25.6 %collective-permute-start.1 = (f32[2,1,3,16]{3,0,2,1:T(2,128)S(1)}, f32[2,1,3,16]{3,0,2,1:T(2,128)S(1)}, u32[]{:S(2)}, u32[]{:S(2)}) collective-permute-start(f32[2,1,3,16]{3,0,2,1:T(2,128)S(1)} %maximum_bitcast_fusion.2), channel_id=1, source_target_pairs={{0,1},{1,0},{2,3},{3,2},{4,5},{5,4},{6,7},{7,6},{8,9},{9,8},{10,11... | collective-permute-start | bytes 1160 | tf_op jit(solution)/shard_map/ppermute | solution.py:1057
  253.6 58.9 %collective-permute-start.3 = (bf16[512,2048]{1,0:T(8,128)(2,1)}, bf16[512,2048]{1,0:T(8,128)(2,1)}, u32[]{:S(2)}, u32[]{:S(2)}) collective-permute-start(bf16[512,2048]{1,0:T(8,128)(2,1)} %out_projection.4.refs_2_.refs_5_), channel_id=1, source_target_pairs={{0,2},{1,3},{2,0},{3,1},{4,6},{5,7},{6,4},{7,5},{8,10},{9,11},{10,... | collective-permute-start | bytes 6291464 | tf_op jit(solution)/shard_map/ppermute | solution.py:1060
  255.1 52.9 %collective-permute-start.2 = (f32[512,1]{1,0:T(8,128)S(1)}, f32[512,1]{1,0:T(8,128)}, u32[]{:S(2)}, u32[]{:S(2)}) collective-permute-start(f32[512,1]{1,0:T(8,128)S(1)} %get-tuple-element.167), channel_id=1, source_target_pairs={{0,2},{1,3},{2,0},{3,1},{4,6},{5,7},{6,4},{7,5},{8,10},{9,11},{10,... | collective-permute-start | bytes 6152 | tf_op jit(solution)/shard_map/ppermute | solution.py:1060
  349.7 42.5 %collective-permute-start.7 = (bf16[256,2048]{1,0:T(8,128)(2,1)}, bf16[256,2048]{1,0:T(8,128)(2,1)}, u32[]{:S(2)}, u32[]{:S(2)}) collective-permute-start(bf16[256,2048]{1,0:T(8,128)(2,1)} %get-tuple-element.367), channel_id=1, source_target_pairs={{0,1},{1,0},{2,3},{3,2},{4,5},{5,4},{6,7},{7,6},{8,9},{9,8},{10,11... | collective-permute-start | bytes 3145736 | tf_op jit(solution)/shard_map/ppermute | solution.py:1057
  350.9 47.8 %collective-permute-start.5 = (bf16[512,2048]{1,0:T(8,128)(2,1)}, bf16[512,2048]{1,0:T(8,128)(2,1)}, u32[]{:S(2)}, u32[]{:S(2)}) collective-permute-start(bf16[512,2048]{1,0:T(8,128)(2,1)} %out_projection.5.refs_2_.refs_5_), channel_id=1, source_target_pairs={{0,2},{1,3},{2,0},{3,1},{4,6},{5,7},{6,4},{7,5},{8,10},{9,11},{10,... | collective-permute-start | bytes 6291464 | tf_op jit(solution)/shard_map/ppermute | solution.py:1060
  396.9 61.8 %collective-permute-start.8 = (bf16[512,2048]{1,0:T(8,128)(2,1)}, bf16[512,2048]{1,0:T(8,128)(2,1)}, u32[]{:S(2)}, u32[]{:S(2)}) collective-permute-start(bf16[512,2048]{1,0:T(8,128)(2,1)} %maximum_select_fusion.2), channel_id=1, source_target_pairs={{0,2},{1,3},{2,0},{3,1},{4,6},{5,7},{6,4},{7,5},{8,10},{9,11},{10,... | collective-permute-start | bytes 6291464 | tf_op jit(solution)/shard_map/ppermute | solution.py:1060
  463.6 20.9 %collective-permute-start.12 = (bf16[512,2048]{1,0:T(8,128)(2,1)}, bf16[512,2048]{1,0:T(8,128)(2,1)}, u32[]{:S(2)}, u32[]{:S(2)}) collective-permute-start(bf16[512,2048]{1,0:T(8,128)(2,1)} %get-tuple-element.210.up_ref.refs_0_), channel_id=1, source_target_pairs={{0,4},{4,0},{8,12},{12,8},{16,20},{20,16},{24,28},{28,24},{1,5},{5... | collective-permute-start | bytes 6291464 | tf_op jit(solution)/shard_map/ppermute | solution.py:1063
  463.6 21.4 %collective-permute-start.13 = (bf16[512,2048]{1,0:T(8,128)(2,1)}, bf16[512,2048]{1,0:T(8,128)(2,1)}, u32[]{:S(2)}, u32[]{:S(2)}) collective-permute-start(bf16[512,2048]{1,0:T(8,128)(2,1)} %get-tuple-element.211.up_ref.refs_1_), channel_id=1, source_target_pairs={{0,4},{4,0},{8,12},{12,8},{16,20},{20,16},{24,28},{28,24},{1,5},{5... | collective-permute-start | bytes 6291464 | tf_op jit(solution)/shard_map/ppermute | solution.py:1063
  464.1 20.9 %collective-permute-start.15 = (bf16[2,512,1024]{2,1,0:T(8,128)(2,1)}, bf16[2,512,1024]{2,1,0:T(8,128)(2,1)}, u32[]{:S(2)}, u32[]{:S(2)}) collective-permute-start(bf16[2,512,1024]{2,1,0:T(8,128)(2,1)} %get-tuple-element.190.mixed_ref.refs_5_), channel_id=1, source_target_pairs={{0,4},{4,0},{8,12},{12,8},{16,20},{20,16},{24,28},{28,24},{1,5},{5... | collective-permute-start | bytes 6291464 | tf_op jit(solution)/shard_map/ppermute | solution.py:1063
  484.5 76.6 %collective-permute-start.17 = (f32[512,1]{1,0:T(8,128)}, f32[512,1]{1,0:T(8,128)}, u32[]{:S(2)}, u32[]{:S(2)}) collective-permute-start(f32[512,1]{1,0:T(8,128)} %get-tuple-element.223), channel_id=1, source_target_pairs={{0,2},{1,3},{2,0},{3,1},{4,6},{5,7},{6,4},{7,5},{8,10},{9,11},{10,... | collective-permute-start | bytes 6152 | tf_op jit(solution)/shard_map/ppermute | solution.py:1060
  502.7 47.4 %collective-permute-start.18 = (bf16[1024,1024]{1,0:T(8,128)(2,1)}, bf16[1024,1024]{1,0:T(8,128)(2,1)}, u32[]{:S(2)}, u32[]{:S(2)}) collective-permute-start(bf16[1024,1024]{1,0:T(8,128)(2,1)} %dynamic-slice_bitcast_fusion.1), channel_id=1, source_target_pairs={{0,1},{1,0},{2,3},{3,2},{4,5},{5,4},{6,7},{7,6},{8,9},{9,8},{10,11... | collective-permute-start | bytes 6291464 | tf_op jit(solution)/shard_map/ppermute | solution.py:1057
  547.6 87.1 %collective-permute-start.16 = (bf16[512,2048]{1,0:T(8,128)(2,1)}, bf16[512,2048]{1,0:T(8,128)(2,1)}, u32[]{:S(2)}, u32[]{:S(2)}) collective-permute-start(bf16[512,2048]{1,0:T(8,128)(2,1)} %normed_gradient.4.refs_2_), channel_id=1, source_target_pairs={{0,2},{1,3},{2,0},{3,1},{4,6},{5,7},{6,4},{7,5},{8,10},{9,11},{10,... | collective-permute-start | bytes 6291464 | tf_op jit(solution)/shard_map/ppermute | solution.py:1060
  606.5 49.2 %collective-permute-start.19 = (bf16[512,2048]{1,0:T(8,128)(2,1)}, bf16[512,2048]{1,0:T(8,128)(2,1)}, u32[]{:S(2)}, u32[]{:S(2)}) collective-permute-start(bf16[512,2048]{1,0:T(8,128)(2,1)} %normed_gradient.5.refs_2_), channel_id=1, source_target_pairs={{0,2},{1,3},{2,0},{3,1},{4,6},{5,7},{6,4},{7,5},{8,10},{9,11},{10,... | collective-permute-start | bytes 6291464 | tf_op jit(solution)/shard_map/ppermute | solution.py:1060
  646.2 33.8 %collective-permute-start.21 = (bf16[512,2048]{1,0:T(8,128)(2,1)}, bf16[512,2048]{1,0:T(8,128)(2,1)}, u32[]{:S(2)}, u32[]{:S(2)}) collective-permute-start(bf16[512,2048]{1,0:T(8,128)(2,1)} %get-tuple-element.246.up_ref.refs_1_), channel_id=1, source_target_pairs={{0,4},{4,0},{8,12},{12,8},{16,20},{20,16},{24,28},{28,24},{1,5},{5... | collective-permute-start | bytes 6291464 | tf_op jit(solution)/shard_map/ppermute | solution.py:1063
  666.7 117.5 %collective-permute-start.6 = (bf16[512,2048]{1,0:T(8,128)(2,1)}, bf16[512,2048]{1,0:T(8,128)(2,1)}, u32[]{:S(2)}, u32[]{:S(2)}) collective-permute-start(bf16[512,2048]{1,0:T(8,128)(2,1)} %broadcast_select_fusion.4), channel_id=1, source_target_pairs={{0,2},{1,3},{2,0},{3,1},{4,6},{5,7},{6,4},{7,5},{8,10},{9,11},{10,... | collective-permute-start | bytes 6291464 | tf_op jit(solution)/shard_map/ppermute | solution.py:1060
  680.0 109.2 %collective-permute-start.37 = (bf16[256,1024]{0,1:T(8,128)(2,1)}, bf16[256,1024]{0,1:T(8,128)(2,1)}, u32[]{:S(2)}, u32[]{:S(2)}) collective-permute-start(bf16[256,1024]{0,1:T(8,128)(2,1)} %bitcast.41), channel_id=1, source_target_pairs={{0,8},{4,12},{8,16},{12,20},{16,24},{20,28},{24,0},{28,4},{1,9},{5... | collective-permute-start | bytes 1572872 | tf_op jit(solution)/shard_map/ppermute | solution.py:1067
  681.5 108.3 %collective-permute-start.38 = (bf16[256,1024]{0,1:T(8,128)(2,1)}, bf16[256,1024]{0,1:T(8,128)(2,1)}, u32[]{:S(2)}, u32[]{:S(2)}) collective-permute-start(bf16[256,1024]{0,1:T(8,128)(2,1)} %bitcast.42), channel_id=1, source_target_pairs={{0,16},{4,20},{8,24},{12,28},{16,0},{20,4},{24,8},{28,12},{1,17},{... | collective-permute-start | bytes 1572872 | tf_op jit(solution)/shard_map/ppermute | solution.py:1067
  683.2 123.7 %collective-permute-start.39 = (bf16[256,1024]{0,1:T(8,128)(2,1)}, bf16[256,1024]{0,1:T(8,128)(2,1)}, u32[]{:S(2)}, u32[]{:S(2)}) collective-permute-start(bf16[256,1024]{0,1:T(8,128)(2,1)} %bitcast.43), channel_id=1, source_target_pairs={{0,24},{4,28},{8,0},{12,4},{16,8},{20,12},{24,16},{28,20},{1,25},{... | collective-permute-start | bytes 1572872 | tf_op jit(solution)/shard_map/ppermute | solution.py:1067
  705.0 122.9 %collective-permute-start.26 = (bf16[1024,1024]{1,0:T(8,128)(2,1)}, bf16[1024,1024]{1,0:T(8,128)(2,1)}, u32[]{:S(2)}, u32[]{:S(2)}) collective-permute-start(bf16[1024,1024]{1,0:T(8,128)(2,1)} %dynamic-slice_bitcast_fusion), channel_id=1, source_target_pairs={{0,1},{1,0},{2,3},{3,2},{4,5},{5,4},{6,7},{7,6},{8,9},{9,8},{10,11... | collective-permute-start | bytes 6291464 | tf_op jit(solution)/shard_map/ppermute | solution.py:1057
  784.2 89.7 %collective-permute-start.30 = (bf16[512,4608]{1,0:T(8,128)(2,1)}, bf16[512,4608]{1,0:T(8,128)(2,1)}, u32[]{:S(2)}, u32[]{:S(2)}) collective-permute-start(bf16[512,4608]{1,0:T(8,128)(2,1)} %get-tuple-element.262.refs_4_), channel_id=1, source_target_pairs={{0,4},{4,0},{8,12},{12,8},{16,20},{20,16},{24,28},{28,24},{1,5},{5... | collective-permute-start | bytes 14155784 | tf_op jit(solution)/shard_map/ppermute | solution.py:1063
  789.2 86.1 %collective-permute-start.31 = (bf16[512,4608]{1,0:T(8,128)(2,1)}, bf16[512,4608]{1,0:T(8,128)(2,1)}, u32[]{:S(2)}, u32[]{:S(2)}) collective-permute-start(bf16[512,4608]{1,0:T(8,128)(2,1)} %get-tuple-element.250.refs_5_), channel_id=1, source_target_pairs={{0,4},{4,0},{8,12},{12,8},{16,20},{20,16},{24,28},{28,24},{1,5},{5... | collective-permute-start | bytes 14155784 | tf_op jit(solution)/shard_map/ppermute | solution.py:1063
  789.9 37.8 %collective-permute-start.24 = (bf16[256,2048]{1,0:T(8,128)(2,1)S(1)}, bf16[256,2048]{1,0:T(8,128)(2,1)S(1)}, u32[]{:S(2)}, u32[]{:S(2)}) collective-permute-start(bf16[256,2048]{1,0:T(8,128)(2,1)S(1)} %get-tuple-element.365), channel_id=1, source_target_pairs={{0,1},{1,0},{2,3},{3,2},{4,5},{5,4},{6,7},{7,6},{8,9},{9,8},{10,11... | collective-permute-start | bytes 3145736 | tf_op jit(solution)/shard_map/ppermute | solution.py:1057
  806.9 47.8 %collective-permute-start.25 = (bf16[512,2048]{1,0:T(8,128)(2,1)}, bf16[512,2048]{1,0:T(8,128)(2,1)}, u32[]{:S(2)}, u32[]{:S(2)}) collective-permute-start(bf16[512,2048]{1,0:T(8,128)(2,1)} %normed_gradient.6), channel_id=1, source_target_pairs={{0,2},{1,3},{2,0},{3,1},{4,6},{5,7},{6,4},{7,5},{8,10},{9,11},{10,... | collective-permute-start | bytes 6291464 | tf_op jit(solution)/shard_map/ppermute | solution.py:1060
  827.7 42.3 %collective-permute-start.28 = (bf16[512,2048]{1,0:T(8,128)(2,1)}, bf16[512,2048]{1,0:T(8,128)(2,1)}, u32[]{:S(2)}, u32[]{:S(2)}) collective-permute-start(bf16[512,2048]{1,0:T(8,128)(2,1)} %norm_forward.4.normed_ref.refs_0_), channel_id=1, source_target_pairs={{0,4},{4,0},{8,12},{12,8},{16,20},{20,16},{24,28},{28,24},{1,5},{5... | collective-permute-start | bytes 6291464 | tf_op jit(solution)/shard_map/ppermute | solution.py:1063
  827.9 43.5 %collective-permute-start.29 = (bf16[512,2048]{1,0:T(8,128)(2,1)}, bf16[512,2048]{1,0:T(8,128)(2,1)}, u32[]{:S(2)}, u32[]{:S(2)}) collective-permute-start(bf16[512,2048]{1,0:T(8,128)(2,1)} %norm_forward.5.normed_ref.refs_1_), channel_id=1, source_target_pairs={{0,4},{4,0},{8,12},{12,8},{16,20},{20,16},{24,28},{28,24},{1,5},{5... | collective-permute-start | bytes 6291464 | tf_op jit(solution)/shard_map/ppermute | solution.py:1063
  854.7 160.4 %collective-permute-start.34 = (bf16[256,1024]{0,1:T(8,128)(2,1)}, bf16[256,1024]{0,1:T(8,128)(2,1)}, u32[]{:S(2)}, u32[]{:S(2)}) collective-permute-start(bf16[256,1024]{0,1:T(8,128)(2,1)} %bitcast.205), channel_id=1, source_target_pairs={{0,8},{4,12},{8,16},{12,20},{16,24},{20,28},{24,0},{28,4},{1,9},{5... | collective-permute-start | bytes 1572872 | tf_op jit(solution)/shard_map/ppermute | solution.py:1067
  869.9 145.1 %collective-permute-start.35 = (bf16[256,1024]{0,1:T(8,128)(2,1)}, bf16[256,1024]{0,1:T(8,128)(2,1)S(1)}, u32[]{:S(2)}, u32[]{:S(2)}) collective-permute-start(bf16[256,1024]{0,1:T(8,128)(2,1)} %bitcast.53), channel_id=1, source_target_pairs={{0,16},{4,20},{8,24},{12,28},{16,0},{20,4},{24,8},{28,12},{1,17},{... | collective-permute-start | bytes 1572872 | tf_op jit(solution)/shard_map/ppermute | solution.py:1067
  871.5 143.6 %collective-permute-start.36 = (bf16[256,1024]{0,1:T(8,128)(2,1)S(1)}, bf16[256,1024]{0,1:T(8,128)(2,1)S(1)}, u32[]{:S(2)}, u32[]{:S(2)}) collective-permute-start(bf16[256,1024]{0,1:T(8,128)(2,1)S(1)} %bitcast.204), channel_id=1, source_target_pairs={{0,24},{4,28},{8,0},{12,4},{16,8},{20,12},{24,16},{28,20},{1,25},{... | collective-permute-start | bytes 1572872 | tf_op jit(solution)/shard_map/ppermute | solution.py:1067
  873.9 148.0 %collective-permute-start.27 = (bf16[256,2048]{1,0:T(8,128)(2,1)}, bf16[256,2048]{1,0:T(8,128)(2,1)S(1)}, u32[]{:S(2)}, u32[]{:S(2)}) collective-permute-start(bf16[256,2048]{1,0:T(8,128)(2,1)} %get-tuple-element.363), channel_id=1, source_target_pairs={{0,1},{1,0},{2,3},{3,2},{4,5},{5,4},{6,7},{7,6},{8,9},{9,8},{10,11... | collective-permute-start | bytes 3145736 | tf_op jit(solution)/shard_map/ppermute | solution.py:1057
  (91 other events, 1950.0 us)
Sparse Core Ops, SparseCore 0:
  202.6 136.7 all-gather.1
  668.4 270.1 reduce-scatter.1

commit v7 on v6

--- a/solution.py
+++ b/solution.py
@@ -1491,7 +1491,6 @@
             in_sum.owned = place.scatter_owners(stack).astype(F32)
             continue
         in_sum = in_sums[layer] = WeightSum(place, normed, back.dcolumns, far_normed, far_columns)
-        mixed_out = place.both_sequences(mixed_out)
         if PIECES == place.groups:
             sent = [back.share(place.rows_of(back.dcolumns, hop)) for hop in range(1, place.groups)]
             arrived = [place.to_group(piece, hop) for hop, piece in enumerate(sent, 1)]
@@ -1542,6 +1541,7 @@
                 out_owned.T,
             )
         )
+    mixed_out = place.both_sequences(mixed_out)
     grad_hidden = place.both_sequences(grad_hidden)
     return (mixed_out, grad_hidden) + tuple(jnp.stack(parts) for parts in zip(*outs))
 

time: 1060 us -> 1070 us (level)
    ppermute x8, waiting for transfers between devices: 17.4 us -> 3.93 us  [to_pair(): return lax.ppermute(v, 'tensor', [(t, t ^ 1) for t in range(self.members)])]
    ppermute x14, waiting for transfers between devices: 32.6 us -> 43.9 us  [to_group(): lax.ppermute(v, 'tensor', [(t, (t + 2 * hop) % self.members) for t in ran...]
    unnamed x174 -> x178, local copies, waits for them, and re-layouts: 27 us -> 29.3 us
  transfers between devices with their start and end apart: 42 -> 42, of which waited for: 11 -> 10; matrix products, arithmetic and copies ran while one was open for 9% -> 9% of each run, Pallas kernels for 57% -> 57%
where the time goes in v7:
time: 1070 us
  Pallas kernels  790 us (74%)
  local copies, waits for them, and re-layouts  79.1 us (7%)
  waiting for transfers between devices  74.7 us (7%)
  other arithmetic  70.6 us (7%)
  starting transfers between devices  36.1 us (3%)
  between operations  15.5 us (1%)
    pallas_call x16, Pallas kernels, product_call(): pl.pallas_call(kernel, grid=grid, in_specs=specs, out_specs=out_specs, ou...  201 us
    pallas_call x1, Pallas kernels, gathered_first(): pl.pallas_call(functools.partial(gather_kernel, chips, groups), in_specs=...  180 us
    pallas_call x1, Pallas kernels, reduced_product(): pl.pallas_call(functools.partial(reduce_kernel, chips, groups, orders, pa...  147 us
    pallas_call x4, Pallas kernels, mixer_backward(): pl.pallas_call(functools.partial(backward_kernel, early is None, carried...  110 us
    pallas_call x3, Pallas kernels, stacked_product(): pl.pallas_call(kernel, grid_spec=pltpu.PrefetchScalarGridSpec(num_scalar_...  58 us
    pallas_call x4, Pallas kernels, mixer_forward(): pl.pallas_call(functools.partial(forward_kernel, earlier is None, heads),...  52.4 us
    ppermute x14, waiting for transfers between devices, to_group(): lax.ppermute(v, 'tensor', [(t, (t + 2 * hop) % self.members) for t in ran...  43.9 us
    pallas_call x7, Pallas kernels, norm_rows(): pl.pallas_call(kernel, grid_spec=pltpu.PrefetchScalarGridSpec(num_scalar_...  42.4 us
  transfers between devices with their start and end apart: 42, of which 10 were waited for; matrix products, arithmetic and copies ran while one was open for 9% of the time, Pallas kernels for 57%

profile of v7, /device:TPU:0, one launch (start us, length us, event | category | flops | bytes accessed | tf_op | source)
XLA Modules:
  0.0 1066.3 jit_solution(15744660348763806555)
XLA Ops:
  16.7 179.8 %gathered_first.1 = (bf16[2,8,256,3328]{3,2,1,0:T(8,128)(2,1)}, bf16[4,256,2048]{2,1,0:T(8,128)(2,1)}) custom-call(bf16[256,3328]{1,0:T(8,128)(2,1)} %concatenate.96.block_ref, bf16[2,256,2048]{2,1,0:T(8,128)(2,1)} %hidden_ref.1), custom_call_target="tpu_custom_call" | custom-call | flops 1000 | bytes 1000 | tf_op jit(solution)/shard_map/gathered_first/pallas_call | solution.py:799
  212.7 16.1 %in_projection.4 = (bf16[2,512,2048]{2,1,0:T(8,128)(2,1)}, f32[2,512,256]{2,1,0:T(8,128)}) custom-call(bf16[512,2048]{1,0:T(8,128)(2,1)} %norm_forward.4.normed_ref.refs_0_, bf16[4096,3328]{1,0:T(8,128)(2,1)} %bitcast.173, bf16[4096,3328]{1,0:T(8,128)(2,1)} %bitcast.174), custom_call_target="tpu_custom_call" | custom-call | flops 1000 | bytes 1000 | tf_op jit(solution)/shard_map/in_projection/pallas_call | solution.py:439
  231.0 12.8 %mixer_forward.4 = (bf16[2,512,1024]{2,1,0:T(8,128)(2,1)}, f32[512,1]{1,0:T(8,128)S(1)}, f32[2,512,1024]{2,1,0:T(8,128)}, bf16[2,4,128,1024]{3,2,1,0:T(8,128)(2,1)}, f32[128,2048]{1,0:T(8,128)S(1)}) custom-call(bf16[2,512,2048]{2,1,0:T(8,128)(2,1)} %get-tuple-element.156.refs_0_.refs_8_.refs_13_.refs_11_, f32[2,512,256]{2,1,0:T(8,128)S(1)} %copy-done, ...), custom_call_target="tpu_custom_call" | custom-call | flops 1000 | bytes 1000 | tf_op jit(solution)/shard_map/mixer_forward/pallas_call | solution.py:360
  257.9 16.1 %in_projection.5 = (bf16[2,512,2048]{2,1,0:T(8,128)(2,1)}, f32[2,512,256]{2,1,0:T(8,128)}) custom-call(bf16[512,2048]{1,0:T(8,128)(2,1)} %norm_forward.5.normed_ref.refs_1_, bf16[4096,3328]{1,0:T(8,128)(2,1)} %bitcast.177, bf16[4096,3328]{1,0:T(8,128)(2,1)} %bitcast.178), custom_call_target="tpu_custom_call" | custom-call | flops 1000 | bytes 1000 | tf_op jit(solution)/shard_map/in_projection/pallas_call | solution.py:439
  276.7 13.3 %mixer_forward.5 = (bf16[2,512,1024]{2,1,0:T(8,128)(2,1)}, f32[512,1]{1,0:T(8,128)S(1)}, f32[2,512,1024]{2,1,0:T(8,128)}, bf16[2,4,128,1024]{3,2,1,0:T(8,128)(2,1)}, f32[128,2048]{1,0:T(8,128)}) custom-call(bf16[2,512,2048]{2,1,0:T(8,128)(2,1)} %get-tuple-element.162.refs_0_.refs_11_, f32[2,512,256]{2,1,0:T(8,128)S(1)} %copy-done.10, ...), custom_call_target="tpu_custom_call" | custom-call | flops 1000 | bytes 1000 | tf_op jit(solution)/shard_map/mixer_forward/pallas_call | solution.py:360
  290.7 9.0 out_projection.5.refs_2_.refs_5_
  312.5 26.9 %all-gather.2.cloned.1.call-done.main_ref.thin_ref.first_ref.second_ref.weight_ref.refs_0_.refs_1_.refs_2_.refs_3_.refs_4_.refs_5_ = bf16[4096,3328]{1,0:T(8,128)(2,1)} async-done(((bf16[256,3328]{1,0:T(8,128)(2,1)}), bf16[4096,3328]{1,0:T(8,128)(2,1)}) %all-gather.2.cloned.1.call-update) | async-done | bytes 27262992 | tf_op jit(solution)/shard_map/all_gather | solution.py:1074
  352.4 15.8 %in_projection.6 = (bf16[2,512,2048]{2,1,0:T(8,128)(2,1)}, f32[2,512,256]{2,1,0:T(8,128)}) custom-call(bf16[512,2048]{1,0:T(8,128)(2,1)} %copy-done.16, bf16[4096,3328]{1,0:T(8,128)(2,1)} %all-gather.2.cloned.1.call-done.main_ref.thin_ref.first_ref.second_ref.weight_ref.refs_0_.refs_1_.refs_2_.refs_3_.refs_4_.refs_5_, ...), custom_call_target="tpu_custom_call" | custom-call | flops 1000 | bytes 1000 | tf_op jit(solution)/shard_map/in_projection/pallas_call | solution.py:439
  369.5 12.8 %mixer_forward.6 = (bf16[2,512,1024]{2,1,0:T(8,128)(2,1)}, f32[512,1]{1,0:T(8,128)S(1)}, f32[2,512,1024]{2,1,0:T(8,128)}, bf16[2,4,128,1024]{3,2,1,0:T(8,128)(2,1)}, f32[128,2048]{1,0:T(8,128)S(1)}) custom-call(bf16[2,512,2048]{2,1,0:T(8,128)(2,1)} %get-tuple-element.178.refs_0_.refs_8_.refs_13_.refs_11_, f32[2,512,256]{2,1,0:T(8,128)S(1)} %copy-done.2, ...), custom_call_target="tpu_custom_call" | custom-call | flops 1000 | bytes 1000 | tf_op jit(solution)/shard_map/mixer_forward/pallas_call | solution.py:360
  383.3 8.9 out_projection.6
  405.3 15.9 %in_projection.7 = (bf16[2,512,2048]{2,1,0:T(8,128)(2,1)}, f32[2,512,256]{2,1,0:T(8,128)}) custom-call(bf16[512,2048]{1,0:T(8,128)(2,1)} %copy-done.17, bf16[4096,3328]{1,0:T(8,128)(2,1)} %all-gather.2.cloned.1.call-done.main_ref.thin_ref.first_ref.second_ref.weight_ref.refs_0_.refs_1_.refs_2_.refs_3_.refs_4_.refs_5_, ...), custom_call_target="tpu_custom_call" | custom-call | flops 1000 | bytes 1000 | tf_op jit(solution)/shard_map/in_projection/pallas_call | solution.py:439
  422.5 13.4 %mixer_forward.7 = (bf16[2,512,1024]{2,1,0:T(8,128)(2,1)}, f32[512,1]{1,0:T(8,128)S(1)}, f32[2,512,1024]{2,1,0:T(8,128)}, bf16[2,4,128,1024]{3,2,1,0:T(8,128)(2,1)}, f32[128,2048]{1,0:T(8,128)}) custom-call(bf16[2,512,2048]{2,1,0:T(8,128)(2,1)} %get-tuple-element.186.refs_0_.refs_11_, f32[2,512,256]{2,1,0:T(8,128)S(1)} %copy-done.11, ...), custom_call_target="tpu_custom_call" | custom-call | flops 1000 | bytes 1000 | tf_op jit(solution)/shard_map/mixer_forward/pallas_call | solution.py:360
  435.9 9.0 out_projection.7
  464.6 9.1 mixed_gradient.4
  473.7 9.2 mixed_gradient.5
  485.0 14.6 %stacked_product.3 = bf16[2,1024,1024]{2,1,0:T(8,128)(2,1)} custom-call(s32[1]{0:T(128)} %bitcast.37.core_ref, bf16[512,2048]{1,0:T(8,128)(2,1)} %get-tuple-element.210.up_ref.refs_0_, bf16[512,2048]{1,0:T(8,128)(2,1)} %get-tuple-element.211.up_ref.refs_1_, bf16[512,2048]{1,0:T(8,128)(2,1)} %collective-permute-done.12.refs_2_, ...), custom_call_target="tpu_custom_call" | custom-call | flops 99999997952 | bytes 100000000 | tf_op jit(solution)/shard_map/stacked_product/pallas_call | solution.py:584
  504.3 27.3 %mixer_backward.4 = (bf16[512,4608]{1,0:T(8,128)(2,1)}, f32[128,2048]{1,0:T(8,128)}, f32[8,2048]{1,0:T(8,128)}, f32[8,256]{1,0:T(8,128)}, f32[8,2048]{1,0:T(8,12...) custom-call(bf16[2,512,2048]{2,1,0:T(8,128)(2,1)} %get-tuple-element.186.refs_0_.refs_11_, ...), custom_call_target="tpu_custom_call" | custom-call | flops 1000 | bytes 1000 | tf_op jit(solution)/shard_map/mixer_backward/pallas_call | solution.py:419
  531.6 16.0 %normed_gradient.4.refs_2_ = bf16[512,2048]{1,0:T(8,128)(2,1)} custom-call(bf16[512,4608]{1,0:T(8,128)(2,1)} %get-tuple-element.218.dcolumns_ref.refs_3_, bf16[4096,3328]{1,0:T(8,128)(2,1)} %all-gather.2.cloned.1.call-done.main_ref.thin_ref.first_ref.second_ref.weight_ref.refs_0_.refs_1_.refs_2_.refs_3_.refs_4_.refs_5_, ...), custom_call_target="tpu_custom_call" | custom-call | flops 99999997952 | bytes 100000000 | tf_op jit(solution)/shard_map/normed_gradient/pallas_call | solution.py:439
  562.7 27.4 %mixer_backward.5 = (bf16[512,4608]{1,0:T(8,128)(2,1)}, f32[128,2048]{1,0:T(8,128)}, f32[8,2048]{1,0:T(8,128)}, f32[8,256]{1,0:T(8,128)}, f32[8,2048]{1,0:T(8,12...) custom-call(bf16[2,512,2048]{2,1,0:T(8,128)(2,1)} %get-tuple-element.178.refs_0_.refs_8_.refs_13_.refs_11_, ...), custom_call_target="tpu_custom_call" | custom-call | flops 1000 | bytes 1000 | tf_op jit(solution)/shard_map/mixer_backward/pallas_call | solution.py:419
  590.1 16.0 %normed_gradient.5.refs_2_ = bf16[512,2048]{1,0:T(8,128)(2,1)} custom-call(bf16[512,4608]{1,0:T(8,128)(2,1)} %get-tuple-element.233.dcolumns_ref.refs_2_, bf16[4096,3328]{1,0:T(8,128)(2,1)} %all-gather.2.cloned.1.call-done.main_ref.thin_ref.first_ref.second_ref.weight_ref.refs_0_.refs_1_.refs_2_.refs_3_.refs_4_.refs_5_, ...), custom_call_target="tpu_custom_call" | custom-call | flops 99999997952 | bytes 100000000 | tf_op jit(solution)/shard_map/normed_gradient/pallas_call | solution.py:439
  607.6 26.8 %stacked_product.4 = bf16[2,2048,2304]{2,1,0:T(8,128)(2,1)} custom-call(s32[1]{0:T(128)} %constant.178.clone.1.core_ref, bf16[512,2048]{1,0:T(8,128)(2,1)} %copy-done.16, bf16[512,2048]{1,0:T(8,128)(2,1)} %copy-done.17, bf16[512,4608]{1,0:T(8,128)(2,1)} %get-tuple-element.233.dcolumns_ref.refs_2_, bf16[512,4608]{1,0:T(8,128)(2,1)} %get-tuple-element.218.dcolumns_ref.refs_3_), custom_call_target="tpu_custom_call" | custom-call | flops 99999997952 | bytes 100000000 | tf_op jit(solution)/shard_map/stacked_product/pallas_call | solution.py:584
  636.0 9.3 norm_backward.3
  645.9 9.4 mixed_gradient.6
  655.3 9.2 norm_backward.4
  669.8 9.1 mixed_gradient.7
  684.9 16.6 %stacked_product.5 = bf16[2,1024,1024]{2,1,0:T(8,128)(2,1)} custom-call(s32[1]{0:T(128)} %bitcast.37.core_ref, bf16[512,2048]{1,0:T(8,128)(2,1)} %get-tuple-element.245.up_ref.refs_0_, bf16[512,2048]{1,0:T(8,128)(2,1)} %get-tuple-element.246.up_ref.refs_1_, bf16[512,2048]{1,0:T(8,128)(2,1)} %collective-permute-done.20.refs_2_, ...), custom_call_target="tpu_custom_call" | custom-call | flops 99999997952 | bytes 100000000 | tf_op jit(solution)/shard_map/stacked_product/pallas_call | solution.py:584
  705.5 27.6 %mixer_backward.6 = (bf16[512,4608]{1,0:T(8,128)(2,1)}, f32[128,2048]{1,0:T(8,128)}, f32[8,2048]{1,0:T(8,128)}, f32[8,256]{1,0:T(8,128)}, f32[8,2048]{1,0:T(8,12...) custom-call(bf16[2,512,2048]{2,1,0:T(8,128)(2,1)} %get-tuple-element.162.refs_0_.refs_11_, ...), custom_call_target="tpu_custom_call" | custom-call | flops 1000 | bytes 1000 | tf_op jit(solution)/shard_map/mixer_backward/pallas_call | solution.py:419
  733.1 28.0 %mixer_backward.7 = (bf16[512,4608]{1,0:T(8,128)(2,1)}, f32[128,2048]{1,0:T(8,128)}, f32[8,2048]{1,0:T(8,128)}, f32[8,256]{1,0:T(8,128)}, f32[8,2048]{1,0:T(8,12...) custom-call(bf16[2,512,2048]{2,1,0:T(8,128)(2,1)} %get-tuple-element.156.refs_0_.refs_8_.refs_13_.refs_11_, ...), custom_call_target="tpu_custom_call" | custom-call | flops 1000 | bytes 1000 | tf_op jit(solution)/shard_map/mixer_backward/pallas_call | solution.py:419
  767.8 16.0 %normed_gradient.6 = bf16[512,2048]{1,0:T(8,128)(2,1)} custom-call(bf16[512,4608]{1,0:T(8,128)(2,1)} %get-tuple-element.271.dcolumns_ref, bf16[4096,3328]{1,0:T(8,128)(2,1)} %bitcast.183, bf16[4096,3328]{1,0:T(8,128)(2,1)} %bitcast.184, bf16[4096,3328]{1,0:T(8,128)(2,1)} %bitcast.185, bf16[4096,3328]{1,0:T(8,128)(2,1)} %bitcast.186, ...), custom_call_target="tpu_custom_call" | custom-call | flops 99999997952 | bytes 100000000 | tf_op jit(solution)/shard_map/normed_gradient/pallas_call | solution.py:439
  784.4 16.3 %normed_gradient.7.refs_5_ = bf16[512,2048]{1,0:T(8,128)(2,1)} custom-call(bf16[512,4608]{1,0:T(8,128)(2,1)} %get-tuple-element.272.dcolumns_ref, bf16[4096,3328]{1,0:T(8,128)(2,1)} %bitcast.189, bf16[4096,3328]{1,0:T(8,128)(2,1)} %bitcast.190, bf16[4096,3328]{1,0:T(8,128)(2,1)} %bitcast.191, bf16[4096,3328]{1,0:T(8,128)(2,1)} %bitcast.192, ...), custom_call_target="tpu_custom_call" | custom-call | flops 99999997952 | bytes 100000000 | tf_op jit(solution)/shard_map/normed_gradient/pallas_call | solution.py:439
  824.7 24.4 %collective-permute-done.29.refs_6_ = bf16[512,2048]{1,0:T(8,128)(2,1)} collective-permute-done((bf16[512,2048]{1,0:T(8,128)(2,1)}, bf16[512,2048]{1,0:T(8,128)(2,1)}, u32[]{:S(2)}, u32[]{:S(2)}) %collective-permute-start.29) | collective-permute-done | bytes 2097184 | tf_op jit(solution)/shard_map/ppermute | solution.py:1060
  871.7 146.8 %reduced_product.1 = (f32[256,2304]{1,0:T(8,128)}, f32[16,1024]{1,0:T(8,128)}, f32[32,256]{1,0:T(8,128)}) custom-call(bf16[512,2048]{1,0:T(8,128)(2,1)} %norm_forward.4.normed_ref.refs_0_, bf16[512,2048]{1,0:T(8,128)(2,1)} %norm_forward.5.normed_ref.refs_1_, bf16[512,2048]{1,0:T(8,128)(2,1)} %collective-permute-done.25.refs_2_, ...), custom_call_target="tpu_custom_call" | custom-call | flops 99999997952 | bytes 100000000 | tf_op jit(solution)/shard_map/reduced_product/pallas_call | solution.py:1000
  (396 shorter events, 242.0 us)
Async XLA Ops:
  7.2 332.2 %all-gather.2.cloned.1.call-start = ((), (), s32[]{:S(2)}) async-start(), calls=%async_computation.1 | async-start | bytes 28966912 | tf_op jit(solution)/shard_map/all_gather | solution.py:1074
  202.5 840.9 %reduce-scatter.2.cloned.1.call-start = ((), (), s32[]{:S(2)}) async-start(), calls=%async_computation.2 | async-start | bytes 20054016 | tf_op jit(solution)/shard_map/reduce_scatter | solution.py:1071
  202.6 26.9 %collective-permute-start = (f32[2,6,1024]{2,1,0:T(8,128)S(1)}, f32[2,6,1024]{2,1,0:T(8,128)S(1)}, u32[]{:S(2)}, u32[]{:S(2)}) collective-permute-start(f32[2,6,1024]{2,1,0:T(8,128)S(1)} %pad_maximum_fusion.10), channel_id=1, source_target_pairs={{0,1},{1,0},{2,3},{3,2},{4,5},{5,4},{6,7},{7,6},{8,9},{9,8},{10,11... | collective-permute-start | bytes 147464 | tf_op jit(solution)/shard_map/ppermute | solution.py:1057
  203.3 25.6 %collective-permute-start.1 = (f32[2,1,3,16]{3,0,2,1:T(2,128)S(1)}, f32[2,1,3,16]{3,0,2,1:T(2,128)S(1)}, u32[]{:S(2)}, u32[]{:S(2)}) collective-permute-start(f32[2,1,3,16]{3,0,2,1:T(2,128)S(1)} %maximum_bitcast_fusion.2), channel_id=1, source_target_pairs={{0,1},{1,0},{2,3},{3,2},{4,5},{5,4},{6,7},{7,6},{8,9},{9,8},{10,11... | collective-permute-start | bytes 1160 | tf_op jit(solution)/shard_map/ppermute | solution.py:1057
  253.6 58.8 %collective-permute-start.3 = (bf16[512,2048]{1,0:T(8,128)(2,1)}, bf16[512,2048]{1,0:T(8,128)(2,1)}, u32[]{:S(2)}, u32[]{:S(2)}) collective-permute-start(bf16[512,2048]{1,0:T(8,128)(2,1)} %out_projection.4.refs_2_.refs_5_), channel_id=1, source_target_pairs={{0,2},{1,3},{2,0},{3,1},{4,6},{5,7},{6,4},{7,5},{8,10},{9,11},{10,... | collective-permute-start | bytes 6291464 | tf_op jit(solution)/shard_map/ppermute | solution.py:1060
  255.2 52.9 %collective-permute-start.2 = (f32[512,1]{1,0:T(8,128)S(1)}, f32[512,1]{1,0:T(8,128)}, u32[]{:S(2)}, u32[]{:S(2)}) collective-permute-start(f32[512,1]{1,0:T(8,128)S(1)} %get-tuple-element.167), channel_id=1, source_target_pairs={{0,2},{1,3},{2,0},{3,1},{4,6},{5,7},{6,4},{7,5},{8,10},{9,11},{10,... | collective-permute-start | bytes 6152 | tf_op jit(solution)/shard_map/ppermute | solution.py:1060
  349.7 42.5 %collective-permute-start.7 = (bf16[256,2048]{1,0:T(8,128)(2,1)}, bf16[256,2048]{1,0:T(8,128)(2,1)}, u32[]{:S(2)}, u32[]{:S(2)}) collective-permute-start(bf16[256,2048]{1,0:T(8,128)(2,1)} %get-tuple-element.367), channel_id=1, source_target_pairs={{0,1},{1,0},{2,3},{3,2},{4,5},{5,4},{6,7},{7,6},{8,9},{9,8},{10,11... | collective-permute-start | bytes 3145736 | tf_op jit(solution)/shard_map/ppermute | solution.py:1057
  350.9 47.8 %collective-permute-start.5 = (bf16[512,2048]{1,0:T(8,128)(2,1)}, bf16[512,2048]{1,0:T(8,128)(2,1)}, u32[]{:S(2)}, u32[]{:S(2)}) collective-permute-start(bf16[512,2048]{1,0:T(8,128)(2,1)} %out_projection.5.refs_2_.refs_5_), channel_id=1, source_target_pairs={{0,2},{1,3},{2,0},{3,1},{4,6},{5,7},{6,4},{7,5},{8,10},{9,11},{10,... | collective-permute-start | bytes 6291464 | tf_op jit(solution)/shard_map/ppermute | solution.py:1060
  397.0 61.6 %collective-permute-start.8 = (bf16[512,2048]{1,0:T(8,128)(2,1)}, bf16[512,2048]{1,0:T(8,128)(2,1)}, u32[]{:S(2)}, u32[]{:S(2)}) collective-permute-start(bf16[512,2048]{1,0:T(8,128)(2,1)} %maximum_select_fusion.2), channel_id=1, source_target_pairs={{0,2},{1,3},{2,0},{3,1},{4,6},{5,7},{6,4},{7,5},{8,10},{9,11},{10,... | collective-permute-start | bytes 6291464 | tf_op jit(solution)/shard_map/ppermute | solution.py:1060
  463.5 20.9 %collective-permute-start.12 = (bf16[512,2048]{1,0:T(8,128)(2,1)}, bf16[512,2048]{1,0:T(8,128)(2,1)}, u32[]{:S(2)}, u32[]{:S(2)}) collective-permute-start(bf16[512,2048]{1,0:T(8,128)(2,1)} %get-tuple-element.210.up_ref.refs_0_), channel_id=1, source_target_pairs={{0,4},{4,0},{8,12},{12,8},{16,20},{20,16},{24,28},{28,24},{1,5},{5... | collective-permute-start | bytes 6291464 | tf_op jit(solution)/shard_map/ppermute | solution.py:1063
  463.6 21.4 %collective-permute-start.13 = (bf16[512,2048]{1,0:T(8,128)(2,1)}, bf16[512,2048]{1,0:T(8,128)(2,1)}, u32[]{:S(2)}, u32[]{:S(2)}) collective-permute-start(bf16[512,2048]{1,0:T(8,128)(2,1)} %get-tuple-element.211.up_ref.refs_1_), channel_id=1, source_target_pairs={{0,4},{4,0},{8,12},{12,8},{16,20},{20,16},{24,28},{28,24},{1,5},{5... | collective-permute-start | bytes 6291464 | tf_op jit(solution)/shard_map/ppermute | solution.py:1063
  464.1 20.9 %collective-permute-start.15 = (bf16[2,512,1024]{2,1,0:T(8,128)(2,1)}, bf16[2,512,1024]{2,1,0:T(8,128)(2,1)}, u32[]{:S(2)}, u32[]{:S(2)}) collective-permute-start(bf16[2,512,1024]{2,1,0:T(8,128)(2,1)} %get-tuple-element.190.mixed_ref.refs_5_), channel_id=1, source_target_pairs={{0,4},{4,0},{8,12},{12,8},{16,20},{20,16},{24,28},{28,24},{1,5},{5... | collective-permute-start | bytes 6291464 | tf_op jit(solution)/shard_map/ppermute | solution.py:1063
  484.4 76.5 %collective-permute-start.17 = (f32[512,1]{1,0:T(8,128)}, f32[512,1]{1,0:T(8,128)}, u32[]{:S(2)}, u32[]{:S(2)}) collective-permute-start(f32[512,1]{1,0:T(8,128)} %get-tuple-element.223), channel_id=1, source_target_pairs={{0,2},{1,3},{2,0},{3,1},{4,6},{5,7},{6,4},{7,5},{8,10},{9,11},{10,... | collective-permute-start | bytes 6152 | tf_op jit(solution)/shard_map/ppermute | solution.py:1060
  502.7 47.4 %collective-permute-start.18 = (bf16[1024,1024]{1,0:T(8,128)(2,1)}, bf16[1024,1024]{1,0:T(8,128)(2,1)}, u32[]{:S(2)}, u32[]{:S(2)}) collective-permute-start(bf16[1024,1024]{1,0:T(8,128)(2,1)} %dynamic-slice_bitcast_fusion.1), channel_id=1, source_target_pairs={{0,1},{1,0},{2,3},{3,2},{4,5},{5,4},{6,7},{7,6},{8,9},{9,8},{10,11... | collective-permute-start | bytes 6291464 | tf_op jit(solution)/shard_map/ppermute | solution.py:1057
  547.6 86.8 %collective-permute-start.16 = (bf16[512,2048]{1,0:T(8,128)(2,1)}, bf16[512,2048]{1,0:T(8,128)(2,1)}, u32[]{:S(2)}, u32[]{:S(2)}) collective-permute-start(bf16[512,2048]{1,0:T(8,128)(2,1)} %normed_gradient.4.refs_2_), channel_id=1, source_target_pairs={{0,2},{1,3},{2,0},{3,1},{4,6},{5,7},{6,4},{7,5},{8,10},{9,11},{10,... | collective-permute-start | bytes 6291464 | tf_op jit(solution)/shard_map/ppermute | solution.py:1060
  606.1 49.2 %collective-permute-start.19 = (bf16[512,2048]{1,0:T(8,128)(2,1)}, bf16[512,2048]{1,0:T(8,128)(2,1)}, u32[]{:S(2)}, u32[]{:S(2)}) collective-permute-start(bf16[512,2048]{1,0:T(8,128)(2,1)} %normed_gradient.5.refs_2_), channel_id=1, source_target_pairs={{0,2},{1,3},{2,0},{3,1},{4,6},{5,7},{6,4},{7,5},{8,10},{9,11},{10,... | collective-permute-start | bytes 6291464 | tf_op jit(solution)/shard_map/ppermute | solution.py:1060
  645.9 33.6 %collective-permute-start.21 = (bf16[512,2048]{1,0:T(8,128)(2,1)}, bf16[512,2048]{1,0:T(8,128)(2,1)}, u32[]{:S(2)}, u32[]{:S(2)}) collective-permute-start(bf16[512,2048]{1,0:T(8,128)(2,1)} %get-tuple-element.246.up_ref.refs_1_), channel_id=1, source_target_pairs={{0,4},{4,0},{8,12},{12,8},{16,20},{20,16},{24,28},{28,24},{1,5},{5... | collective-permute-start | bytes 6291464 | tf_op jit(solution)/shard_map/ppermute | solution.py:1063
  666.3 134.6 %collective-permute-start.6 = (bf16[512,2048]{1,0:T(8,128)(2,1)}, bf16[512,2048]{1,0:T(8,128)(2,1)}, u32[]{:S(2)}, u32[]{:S(2)}) collective-permute-start(bf16[512,2048]{1,0:T(8,128)(2,1)} %broadcast_select_fusion.4), channel_id=1, source_target_pairs={{0,2},{1,3},{2,0},{3,1},{4,6},{5,7},{6,4},{7,5},{8,10},{9,11},{10,... | collective-permute-start | bytes 6291464 | tf_op jit(solution)/shard_map/ppermute | solution.py:1060
  679.6 104.2 %collective-permute-start.37 = (bf16[256,1024]{0,1:T(8,128)(2,1)}, bf16[256,1024]{0,1:T(8,128)(2,1)}, u32[]{:S(2)}, u32[]{:S(2)}) collective-permute-start(bf16[256,1024]{0,1:T(8,128)(2,1)} %bitcast.41), channel_id=1, source_target_pairs={{0,8},{4,12},{8,16},{12,20},{16,24},{20,28},{24,0},{28,4},{1,9},{5... | collective-permute-start | bytes 1572872 | tf_op jit(solution)/shard_map/ppermute | solution.py:1067
  681.1 102.8 %collective-permute-start.38 = (bf16[256,1024]{0,1:T(8,128)(2,1)}, bf16[256,1024]{0,1:T(8,128)(2,1)}, u32[]{:S(2)}, u32[]{:S(2)}) collective-permute-start(bf16[256,1024]{0,1:T(8,128)(2,1)} %bitcast.42), channel_id=1, source_target_pairs={{0,16},{4,20},{8,24},{12,28},{16,0},{20,4},{24,8},{28,12},{1,17},{... | collective-permute-start | bytes 1572872 | tf_op jit(solution)/shard_map/ppermute | solution.py:1067
  682.8 117.9 %collective-permute-start.39 = (bf16[256,1024]{0,1:T(8,128)(2,1)}, bf16[256,1024]{0,1:T(8,128)(2,1)}, u32[]{:S(2)}, u32[]{:S(2)}) collective-permute-start(bf16[256,1024]{0,1:T(8,128)(2,1)} %bitcast.43), channel_id=1, source_target_pairs={{0,24},{4,28},{8,0},{12,4},{16,8},{20,12},{24,16},{28,20},{1,25},{... | collective-permute-start | bytes 1572872 | tf_op jit(solution)/shard_map/ppermute | solution.py:1067
  704.7 106.0 %collective-permute-start.30 = (bf16[1024,1024]{1,0:T(8,128)(2,1)}, bf16[1024,1024]{1,0:T(8,128)(2,1)}, u32[]{:S(2)}, u32[]{:S(2)}) collective-permute-start(bf16[1024,1024]{1,0:T(8,128)(2,1)} %dynamic-slice_bitcast_fusion), channel_id=1, source_target_pairs={{0,1},{1,0},{2,3},{3,2},{4,5},{5,4},{6,7},{7,6},{8,9},{9,8},{10,11... | collective-permute-start | bytes 6291464 | tf_op jit(solution)/shard_map/ppermute | solution.py:1057
  783.8 83.7 %collective-permute-start.27 = (bf16[512,4608]{1,0:T(8,128)(2,1)}, bf16[512,4608]{1,0:T(8,128)(2,1)}, u32[]{:S(2)}, u32[]{:S(2)}) collective-permute-start(bf16[512,4608]{1,0:T(8,128)(2,1)} %get-tuple-element.262.refs_4_), channel_id=1, source_target_pairs={{0,4},{4,0},{8,12},{12,8},{16,20},{20,16},{24,28},{28,24},{1,5},{5... | collective-permute-start | bytes 14155784 | tf_op jit(solution)/shard_map/ppermute | solution.py:1063
  783.9 86.8 %collective-permute-start.28 = (bf16[512,4608]{1,0:T(8,128)(2,1)}, bf16[512,4608]{1,0:T(8,128)(2,1)}, u32[]{:S(2)}, u32[]{:S(2)}) collective-permute-start(bf16[512,4608]{1,0:T(8,128)(2,1)} %get-tuple-element.250.refs_5_), channel_id=1, source_target_pairs={{0,4},{4,0},{8,12},{12,8},{16,20},{20,16},{24,28},{28,24},{1,5},{5... | collective-permute-start | bytes 14155784 | tf_op jit(solution)/shard_map/ppermute | solution.py:1063
  800.7 66.0 %collective-permute-start.25 = (bf16[512,2048]{1,0:T(8,128)(2,1)}, bf16[512,2048]{1,0:T(8,128)(2,1)}, u32[]{:S(2)}, u32[]{:S(2)}) collective-permute-start(bf16[512,2048]{1,0:T(8,128)(2,1)} %norm_forward.4.normed_ref.refs_0_), channel_id=1, source_target_pairs={{0,4},{4,0},{8,12},{12,8},{16,20},{20,16},{24,28},{28,24},{1,5},{5... | collective-permute-start | bytes 6291464 | tf_op jit(solution)/shard_map/ppermute | solution.py:1063
  800.9 48.3 %collective-permute-start.29 = (bf16[512,2048]{1,0:T(8,128)(2,1)}, bf16[512,2048]{1,0:T(8,128)(2,1)}, u32[]{:S(2)}, u32[]{:S(2)}) collective-permute-start(bf16[512,2048]{1,0:T(8,128)(2,1)} %normed_gradient.6), channel_id=1, source_target_pairs={{0,2},{1,3},{2,0},{3,1},{4,6},{5,7},{6,4},{7,5},{8,10},{9,11},{10,... | collective-permute-start | bytes 6291464 | tf_op jit(solution)/shard_map/ppermute | solution.py:1060
  810.7 56.1 %collective-permute-start.26 = (bf16[512,2048]{1,0:T(8,128)(2,1)}, bf16[512,2048]{1,0:T(8,128)(2,1)}, u32[]{:S(2)}, u32[]{:S(2)}) collective-permute-start(bf16[512,2048]{1,0:T(8,128)(2,1)} %norm_forward.5.normed_ref.refs_1_), channel_id=1, source_target_pairs={{0,4},{4,0},{8,12},{12,8},{16,20},{20,16},{24,28},{28,24},{1,5},{5... | collective-permute-start | bytes 6291464 | tf_op jit(solution)/shard_map/ppermute | solution.py:1063
  849.1 177.0 %collective-permute-start.24 = (bf16[256,2048]{1,0:T(8,128)(2,1)}, bf16[256,2048]{1,0:T(8,128)(2,1)}, u32[]{:S(2)}, u32[]{:S(2)}) collective-permute-start(bf16[256,2048]{1,0:T(8,128)(2,1)} %get-tuple-element.365), channel_id=1, source_target_pairs={{0,1},{1,0},{2,3},{3,2},{4,5},{5,4},{6,7},{7,6},{8,9},{9,8},{10,11... | collective-permute-start | bytes 3145736 | tf_op jit(solution)/shard_map/ppermute | solution.py:1057
  866.7 152.7 %collective-permute-start.34 = (bf16[256,1024]{0,1:T(8,128)(2,1)}, bf16[256,1024]{0,1:T(8,128)(2,1)S(1)}, u32[]{:S(2)}, u32[]{:S(2)}) collective-permute-start(bf16[256,1024]{0,1:T(8,128)(2,1)} %bitcast.52), channel_id=1, source_target_pairs={{0,8},{4,12},{8,16},{12,20},{16,24},{20,28},{24,0},{28,4},{1,9},{5... | collective-permute-start | bytes 1572872 | tf_op jit(solution)/shard_map/ppermute | solution.py:1067
  866.7 152.7 %collective-permute-start.35 = (bf16[256,1024]{0,1:T(8,128)(2,1)}, bf16[256,1024]{0,1:T(8,128)(2,1)S(1)}, u32[]{:S(2)}, u32[]{:S(2)}) collective-permute-start(bf16[256,1024]{0,1:T(8,128)(2,1)} %bitcast.53), channel_id=1, source_target_pairs={{0,16},{4,20},{8,24},{12,28},{16,0},{20,4},{24,8},{28,12},{1,17},{... | collective-permute-start | bytes 1572872 | tf_op jit(solution)/shard_map/ppermute | solution.py:1067
  867.5 151.9 %collective-permute-start.36 = (bf16[256,1024]{0,1:T(8,128)(2,1)S(1)}, bf16[256,1024]{0,1:T(8,128)(2,1)}, u32[]{:S(2)}, u32[]{:S(2)}) collective-permute-start(bf16[256,1024]{0,1:T(8,128)(2,1)S(1)} %bitcast.204), channel_id=1, source_target_pairs={{0,24},{4,28},{8,0},{12,4},{16,8},{20,12},{24,16},{28,20},{1,25},{... | collective-permute-start | bytes 1572872 | tf_op jit(solution)/shard_map/ppermute | solution.py:1067
  870.6 155.5 %collective-permute-start.31 = (bf16[256,2048]{1,0:T(8,128)(2,1)}, bf16[256,2048]{1,0:T(8,128)(2,1)S(1)}, u32[]{:S(2)}, u32[]{:S(2)}) collective-permute-start(bf16[256,2048]{1,0:T(8,128)(2,1)} %get-tuple-element.363), channel_id=1, source_target_pairs={{0,1},{1,0},{2,3},{3,2},{4,5},{5,4},{6,7},{7,6},{8,9},{9,8},{10,11... | collective-permute-start | bytes 3145736 | tf_op jit(solution)/shard_map/ppermute | solution.py:1057
  (93 other events, 1885.0 us)
Sparse Core Ops, SparseCore 0:
  202.6 136.7 all-gather.1
  668.0 249.8 reduce-scatter.1
